TPU v7x, 32 devices: a whole 2x2x4 slice. The times are simulated.
32 devices in a mesh: seq: 8 (over y, x, core), head: 4 (over z).
Axes of the slice: x: 2, y: 2, z: 4, core: 2. Of those that a mesh axis runs over, the one named last changes fastest.
Arguments:
- query_rows: bfloat16 [4096, 2048], P(('seq', 'head')), may hold values from -48 to 48
- key_rows: bfloat16 [4096, 1024], P(('seq', 'head')), may hold values from -16 to 16
- saved_value_rows: bfloat16 [4096, 1024], P(('seq', 'head')), may hold values from -6 to 6
- out_grad: bfloat16 [4096, 2048], P(('seq', 'head')), may hold values from -6 to 6
Outputs:
- query_grad: bfloat16 [4096, 2048], P(('seq', 'head'))
- key_grad: bfloat16 [4096, 1024], P(('seq', 'head'))
- value_grad: bfloat16 [4096, 1024], P(('seq', 'head'))
All inputs are finite; a program needn't handle non-finite values.
Results may differ from a plain program's by a relative error of at most 0.013.
Values may be sent and summed in bfloat16 or wider, within the bound.
No kernel may reach another device: no remote copies, remote signals or barrier semaphores. Data moves between devices by JAX's collectives and lax.ppermute only.
A program may use at most 64 MiB of HBM per device.

v0:
```python
import jax
import jax.numpy as jnp
from jax import lax
from jax.sharding import PartitionSpec as P

HEAD_SIZE = 128
W = 1024


score_scale = 168.0 ** (-0.5)
masked_value = -1e30
contract_last = (((1,), (1,)), ((), ()))
contract_first = (((0,), (0,)), ((), ()))


def shifted(value, axis, steps):
    count = lax.axis_size(axis)
    first, last = (max(0, -steps), min(count, count - steps))
    return lax.ppermute(value, axis, [(source, source + steps) for source in range(first, last)])


def on_device(query_rows, key_rows, saved_value_rows, out_grad):
    queries, keys_mine, values_mine, grads_out = (
        lax.all_to_all(query_rows, "head", split_axis=1, concat_axis=0, tiled=True),
        lax.all_to_all(key_rows, "head", split_axis=1, concat_axis=0, tiled=True),
        lax.all_to_all(saved_value_rows, "head", split_axis=1, concat_axis=0, tiled=True),
        lax.all_to_all(out_grad, "head", split_axis=1, concat_axis=0, tiled=True),
    )
    shard_rows = queries.shape[0]
    head_count = queries.shape[1] // HEAD_SIZE
    group_count = keys_mine.shape[1] // HEAD_SIZE
    keys_near, values_near = shifted((keys_mine, values_mine), "seq", 1)
    keys_far, values_far = shifted((keys_mine, values_mine), "seq", 2)
    keys_all = jnp.concatenate([keys_far, keys_near, keys_mine], 0)
    values_all = jnp.concatenate([values_far, values_near, values_mine], 0)
    anchor = lax.axis_index("seq") * shard_rows
    query_pos = anchor + jnp.arange(shard_rows, dtype=jnp.int32)
    key_pos = anchor - 2 * shard_rows + jnp.arange(3 * shard_rows, dtype=jnp.int32)
    distance = query_pos[:, None] - key_pos[None, :]
    visible = (distance >= 0) & (distance < W) & (key_pos[None, :] >= 0)
    zero_block = jnp.zeros((3 * shard_rows, HEAD_SIZE), jnp.float32)
    key_parts = [zero_block] * group_count
    value_parts = [zero_block] * group_count
    query_parts = []
    for q_head in range(head_count):
        kv_group = q_head // 2
        query_head = queries[:, q_head * HEAD_SIZE : (q_head + 1) * HEAD_SIZE]
        grad_head = grads_out[:, q_head * HEAD_SIZE : (q_head + 1) * HEAD_SIZE]
        key_head = keys_all[:, kv_group * HEAD_SIZE : (kv_group + 1) * HEAD_SIZE]
        value_head = values_all[:, kv_group * HEAD_SIZE : (kv_group + 1) * HEAD_SIZE]
        scores = (
            lax.dot_general(query_head, key_head, contract_last, preferred_element_type=jnp.float32)
            * score_scale
        )
        scores = jnp.where(visible, scores, masked_value)
        row_max = jnp.max(scores, axis=1, keepdims=True)
        weights = jnp.exp(scores - row_max)
        attention = weights / jnp.sum(weights, axis=1, keepdims=True)
        attention_low = attention.astype(jnp.bfloat16)
        prob_grad = lax.dot_general(
            grad_head, value_head, contract_last, preferred_element_type=jnp.float32
        )
        row_delta = jnp.sum(attention * prob_grad, axis=1, keepdims=True)
        score_grad = (score_scale * attention * (prob_grad - row_delta)).astype(jnp.bfloat16)
        query_parts.append(
            jnp.dot(score_grad, key_head, preferred_element_type=jnp.float32).astype(jnp.bfloat16)
        )
        key_parts[kv_group] = key_parts[kv_group] + lax.dot_general(
            score_grad, query_head, contract_first, preferred_element_type=jnp.float32
        )
        value_parts[kv_group] = value_parts[kv_group] + lax.dot_general(
            attention_low, grad_head, contract_first, preferred_element_type=jnp.float32
        )
    query_grad = jnp.concatenate(query_parts, 1)
    key_sums = jnp.concatenate(key_parts, 1)
    value_sums = jnp.concatenate(value_parts, 1)
    key_own = key_sums[2 * shard_rows :]
    value_own = value_sums[2 * shard_rows :]
    key_before = key_sums[shard_rows : 2 * shard_rows]
    value_before = value_sums[shard_rows : 2 * shard_rows]
    key_earlier = key_sums[:shard_rows]
    value_earlier = value_sums[:shard_rows]
    back_near = (
        shifted(key_before.astype(jnp.bfloat16), "seq", -1).astype(key_before.dtype),
        shifted(value_before.astype(jnp.bfloat16), "seq", -1).astype(value_before.dtype),
    )
    back_far = (
        shifted(key_earlier.astype(jnp.bfloat16), "seq", -2).astype(key_earlier.dtype),
        shifted(value_earlier.astype(jnp.bfloat16), "seq", -2).astype(value_earlier.dtype),
    )
    key_total = key_own + back_near[0] + back_far[0]
    value_total = value_own + back_near[1] + back_far[1]
    key_grad = key_total.astype(jnp.bfloat16)
    value_grad = value_total.astype(jnp.bfloat16)
    return (
        lax.all_to_all(query_grad, "head", split_axis=0, concat_axis=1, tiled=True),
        lax.all_to_all(key_grad, "head", split_axis=0, concat_axis=1, tiled=True),
        lax.all_to_all(value_grad, "head", split_axis=0, concat_axis=1, tiled=True),
    )


def solution(mesh):
    in_specs = (
        P(("seq", "head"), None),
        P(("seq", "head"), None),
        P(("seq", "head"), None),
        P(("seq", "head"), None),
    )
    out_specs = (P(("seq", "head"), None), P(("seq", "head"), None), P(("seq", "head"), None))
    return jax.shard_map(
        on_device, mesh=mesh, in_specs=in_specs, out_specs=out_specs, check_vma=False
    )
```

profile of v0, /device:TPU:6, one launch (start us, length us, event | category | flops | bytes accessed | tf_op | source)
XLA Modules:
  0.0 143.2 jit_solution(3949290689685771612)
XLA Ops:
  0.6 1.8 %copy.28 = bf16[128,1024]{0,1:T(8,128)(2,1)} copy(bf16[128,1024]{1,0:T(8,128)(2,1)} %param.6) | data formatting | bytes 524288 | tf_op args[2]
  2.5 4.9 %all-to-all-start.2 = ((bf16[128,4,256]{0,2,1:T(8,128)(2,1)}), bf16[128,4,256]{0,2,1:T(8,128)(2,1)S(1)}, u32[]{:S(2)}, u32[]{:S(2)}) async-start(bf16[128,4,256]{0,2,1:T(8,128)(2,1)} %bitcast.7), calls=%async_computation.2 | async-start | bytes 524288 | tf_op jit(solution)/shard_map/all_to_all | solution.py:26
  7.4 1.8 %copy.24 = bf16[128,1024]{0,1:T(8,128)(2,1)} copy(bf16[128,1024]{1,0:T(8,128)(2,1)} %param.5) | data formatting | bytes 524288 | tf_op args[1]
  9.1 7.1 %all-to-all-done.2 = bf16[128,4,256]{0,2,1:T(8,128)(2,1)S(1)} async-done(((bf16[128,4,256]{0,2,1:T(8,128)(2,1)}), bf16[128,4,256]{0,2,1:T(8,128)(2,1)S(1)}, u32[]{:S(2)}, u32[]{:S(2)}) %all-to-all-start.2) | async-done | bytes 262176 | tf_op jit(solution)/shard_map/all_to_all | solution.py:26
  16.3 3.4 %all-to-all-start = ((bf16[128,4,256]{0,2,1:T(8,128)(2,1)}), bf16[128,4,256]{0,2,1:T(8,128)(2,1)S(1)}, u32[]{:S(2)}, u32[]{:S(2)}) async-start(bf16[128,4,256]{0,2,1:T(8,128)(2,1)} %bitcast), calls=%async_computation | async-start | bytes 524288 | tf_op jit(solution)/shard_map/all_to_all | solution.py:25
  19.7 2.0 %copy.26 = bf16[128,2048]{0,1:T(8,128)(2,1)} copy(bf16[128,2048]{1,0:T(8,128)(2,1)} %param.4) | data formatting | bytes 1048576 | tf_op args[0]
  21.9 1.9 %collective-permute-start.3 = (bf16[512,256]{1,0:T(8,128)(2,1)S(1)}, bf16[512,256]{1,0:T(8,128)(2,1)S(1)}, u32[]{:S(2)}, u32[]{:S(2)}) collective-permute-start(bf16[512,256]{1,0:T(8,128)(2,1)S(1)} %bitcast.82), channel_id=1, source_target_pairs={{0,4},{4,8},{8,12},{12,16},{16,20},{20,24},{24,28},{1,5},{5,9},{9,... | collective-permute-start | bytes 786440 | tf_op jit(solution)/shard_map/ppermute | solution.py:19
  23.8 1.3 collective-permute-start.2
  25.1 1.6 %all-to-all-done = bf16[128,4,256]{0,2,1:T(8,128)(2,1)S(1)} async-done(((bf16[128,4,256]{0,2,1:T(8,128)(2,1)}), bf16[128,4,256]{0,2,1:T(8,128)(2,1)S(1)}, u32[]{:S(2)}, u32[]{:S(2)}) %all-to-all-start) | async-done | bytes 262176 | tf_op jit(solution)/shard_map/all_to_all | solution.py:25
  26.7 3.5 %all-to-all-start.1 = ((bf16[128,4,512]{0,2,1:T(8,128)(2,1)}), bf16[128,4,512]{0,2,1:T(8,128)(2,1)S(1)}, u32[]{:S(2)}, u32[]{:S(2)}) async-start(bf16[128,4,512]{0,2,1:T(8,128)(2,1)} %bitcast.3), calls=%async_computation.1 | async-start | bytes 1048576 | tf_op jit(solution)/shard_map/all_to_all | solution.py:24
  30.4 1.9 %collective-permute-start.1 = (bf16[512,256]{1,0:T(8,128)(2,1)S(1)}, bf16[512,256]{1,0:T(8,128)(2,1)S(1)}, u32[]{:S(2)}, u32[]{:S(2)}) collective-permute-start(bf16[512,256]{1,0:T(8,128)(2,1)S(1)} %bitcast.85), channel_id=1, source_target_pairs={{0,4},{4,8},{8,12},{12,16},{16,20},{20,24},{24,28},{1,5},{5,9},{9,... | collective-permute-start | bytes 786440 | tf_op jit(solution)/shard_map/ppermute | solution.py:19
  32.3 1.3 collective-permute-start
  33.6 1.0 copy.30
  35.0 0.9 pad_maximum_fusion.3
  35.9 2.5 %collective-permute-done.1 = bf16[512,256]{1,0:T(8,128)(2,1)S(1)} collective-permute-done((bf16[512,256]{1,0:T(8,128)(2,1)S(1)}, bf16[512,256]{1,0:T(8,128)(2,1)S(1)}, u32[]{:S(2)}, u32[]{:S(2)}) %collective-permute-start.1) | collective-permute-done | bytes 262176 | tf_op jit(solution)/shard_map/ppermute | solution.py:19
  38.4 5.6 %collective-permute-done = bf16[512,256]{1,0:T(8,128)(2,1)S(1)} collective-permute-done((bf16[512,256]{1,0:T(8,128)(2,1)S(1)}, bf16[512,256]{1,0:T(8,128)(2,1)S(1)}, u32[]{:S(2)}, u32[]{:S(2)}) %collective-permute-start) | collective-permute-done | bytes 262176 | tf_op jit(solution)/shard_map/ppermute | solution.py:19
  44.1 4.8 %all-to-all-start.3 = ((bf16[128,4,512]{0,2,1:T(8,128)(2,1)}), bf16[128,4,512]{0,2,1:T(8,128)(2,1)}, u32[]{:S(2)}, u32[]{:S(2)}) async-start(bf16[128,4,512]{0,2,1:T(8,128)(2,1)} %bitcast.10), calls=%async_computation.3 | async-start | bytes 1048576 | tf_op jit(solution)/shard_map/all_to_all | solution.py:27
  49.1 3.1 %fusion.72 = (f32[512]{0:T(512)S(1)}, f32[512,1536]{0,1:T(8,128)}) fusion(bf16[512,512]{1,0:T(8,128)(2,1)S(1)} %bitcast.68, bf16[1536,256]{1,0:T(8,128)(2,1)S(1)} %pad_maximum_fusion.2, pred[1536]{0:T(1024)(128)(4,1)S(1)} %broadcast_compare_fusion, s32[1536]{0:T(1024)S(1)} %iota_add_fusion, s32[512]{0:T(512)S(1)} %iota_add_fusion.1), kind=kOutput, calls=%fused_computation.113 | convolution fusion | flops 207617536 | bytes 3684352 | tf_op jit(solution)/shard_map/dot_general | solution.py:52
  52.2 3.1 %fusion.73 = (f32[512]{0:T(512)S(1)}, f32[512,1536]{0,1:T(8,128)}) fusion(bf16[512,512]{1,0:T(8,128)(2,1)S(1)} %bitcast.69, bf16[1536,256]{1,0:T(8,128)(2,1)S(1)} %pad_maximum_fusion.2, pred[1536]{0:T(1024)(128)(4,1)S(1)} %broadcast_compare_fusion, s32[1536]{0:T(1024)S(1)} %iota_add_fusion, s32[512]{0:T(512)S(1)} %iota_add_fusion.1), kind=kOutput, calls=%fused_computation.114 | convolution fusion | flops 207617536 | bytes 3684352 | tf_op jit(solution)/shard_map/dot_general | solution.py:52
  55.3 2.6 %fusion.74 = (f32[512]{0:T(512)S(1)}, f32[512,1536]{0,1:T(8,128)S(1)}) fusion(bf16[512,512]{1,0:T(8,128)(2,1)} %bitcast.70, bf16[1536,256]{1,0:T(8,128)(2,1)} %copy-done.10, pred[1536]{0:T(1024)(128)(4,1)S(1)} %broadcast_compare_fusion, s32[1536]{0:T(1024)S(1)} %iota_add_fusion, s32[512]{0:T(512)S(1)} %iota_add_fusion.1), kind=kOutput, calls=%fused_computation.115 | convolution fusion | flops 207617536 | bytes 3681792 | tf_op jit(solution)/shard_map/dot_general | solution.py:52
  57.9 4.0 %fusion.75 = (f32[512]{0:T(512)S(1)}, f32[512,1536]{0,1:T(8,128)}) fusion(bf16[512,512]{1,0:T(8,128)(2,1)} %bitcast.71, bf16[1536,256]{1,0:T(8,128)(2,1)S(1)} %copy-done.11, pred[1536]{0:T(1024)(128)(4,1)S(1)} %broadcast_compare_fusion, s32[1536]{0:T(1024)S(1)} %iota_add_fusion, s32[512]{0:T(512)S(1)} %iota_add_fusion.1), kind=kOutput, calls=%fused_computation.116 | convolution fusion | flops 207617536 | bytes 3684352 | tf_op jit(solution)/shard_map/dot_general | solution.py:52
  61.9 1.5 %all-to-all-done.3 = bf16[128,4,512]{0,2,1:T(8,128)(2,1)} async-done(((bf16[128,4,512]{0,2,1:T(8,128)(2,1)}), bf16[128,4,512]{0,2,1:T(8,128)(2,1)}, u32[]{:S(2)}, u32[]{:S(2)}) %all-to-all-start.3) | async-done | bytes 524320 | tf_op jit(solution)/shard_map/all_to_all | solution.py:27
  63.5 2.0 %copy.31 = bf16[4,128,512]{2,1,0:T(8,128)(2,1)} copy(bf16[4,128,512]{1,2,0:T(8,128)(2,1)} %bitcast.11) | data formatting | bytes 1048576 | tf_op jit(solution)/shard_map/all_to_all | solution.py:27
  65.5 2.5 %fusion.15 = f32[512]{0:T(512)S(1)} fusion(f32[512,1536]{0,1:T(8,128)} %get-tuple-element.15, f32[512]{0:T(512)S(1)} %get-tuple-element.14), kind=kLoop, calls=%fused_computation.37 | loop fusion | flops 1572352 | bytes 3149824 | tf_op jit(solution)/shard_map/reduce_sum | solution.py:58
  68.3 1.7 %fusion.21 = f32[1536,128]{0,1:T(8,128)S(1)} fusion(bf16[512,512]{1,0:T(8,128)(2,1)} %bitcast.88, f32[512,1536]{0,1:T(8,128)S(1)} %copy-done.1, f32[512]{0:T(512)S(1)} %fusion.15, f32[512]{0:T(512)S(1)} %get-tuple-element.14), kind=kOutput, calls=%fused_computation.53 | convolution fusion | flops 203685888 | bytes 4067328 | tf_op jit(solution)/shard_map/dot_general | solution.py:71
  70.1 0.7 multiply_reduce_fusion.1
  70.8 1.2 copy-done
  72.5 0.7 fusion.24
  73.2 0.7 multiply_reduce_fusion.3
  74.0 1.2 copy-done.2
  75.1 0.5 fusion.17
  75.6 0.7 multiply_reduce_fusion
  76.4 0.9 multiply_convert_fusion
  77.9 0.7 convolution_add_fusion
  78.7 0.9 multiply_convert_fusion.1
  79.7 0.7 fusion.54
  80.4 0.7 convolution_add_fusion.2
  81.0 0.5 fusion.13
  81.5 0.7 multiply_reduce_fusion.2
  82.3 0.7 convolution_add_fusion.1
  83.1 4.2 %collective-permute-start.6 = (bf16[512,256]{0,1:T(8,128)(2,1)S(1)}, bf16[512,256]{0,1:T(8,128)(2,1)S(1)}, u32[]{:S(2)}, u32[]{:S(2)}) collective-permute-start(bf16[512,256]{0,1:T(8,128)(2,1)S(1)} %get-tuple-element.6), channel_id=1, source_target_pairs={{4,0},{8,4},{12,8},{16,12},{20,16},{24,20},{28,24},{5,1},{9,5},{13... | collective-permute-start | bytes 786440 | tf_op jit(solution)/shard_map/ppermute | solution.py:19
  87.3 4.7 %collective-permute-start.7 = (bf16[512,256]{0,1:T(8,128)(2,1)S(1)}, bf16[512,256]{0,1:T(8,128)(2,1)S(1)}, u32[]{:S(2)}, u32[]{:S(2)}) collective-permute-start(bf16[512,256]{0,1:T(8,128)(2,1)S(1)} %get-tuple-element.7), channel_id=1, source_target_pairs={{8,0},{12,4},{16,8},{20,12},{24,16},{28,20},{9,1},{13,5},{17,9},{2... | collective-permute-start | bytes 786440 | tf_op jit(solution)/shard_map/ppermute | solution.py:19
  92.0 0.9 multiply_convert_fusion.3
  92.9 0.6 fusion.63
  93.5 0.9 multiply_convert_fusion.2
  94.4 0.7 convolution_add_fusion.3
  95.2 0.8 fusion.71
  96.0 2.8 %collective-permute-start.4 = (bf16[512,256]{0,1:T(8,128)(2,1)}, bf16[512,256]{0,1:T(8,128)(2,1)}, u32[]{:S(2)}, u32[]{:S(2)}) collective-permute-start(bf16[512,256]{0,1:T(8,128)(2,1)} %get-tuple-element.8), channel_id=1, source_target_pairs={{4,0},{8,4},{12,8},{16,12},{20,16},{24,20},{28,24},{5,1},{9,5},{13... | collective-permute-start | bytes 786440 | tf_op jit(solution)/shard_map/ppermute | solution.py:19
  98.9 3.1 %collective-permute-start.5 = (bf16[512,256]{0,1:T(8,128)(2,1)}, bf16[512,256]{0,1:T(8,128)(2,1)}, u32[]{:S(2)}, u32[]{:S(2)}) collective-permute-start(bf16[512,256]{0,1:T(8,128)(2,1)} %get-tuple-element.9), channel_id=1, source_target_pairs={{8,0},{12,4},{16,8},{20,12},{24,16},{28,20},{9,1},{13,5},{17,9},{2... | collective-permute-start | bytes 786440 | tf_op jit(solution)/shard_map/ppermute | solution.py:19
  102.0 1.1 convolution_convert_fusion.1
  103.1 0.8 copy_bitcast_fusion.1
  103.9 3.5 %all-to-all-start.6 = ((bf16[4,128,256]{1,2,0:T(8,128)(2,1)}), bf16[4,128,256]{1,2,0:T(8,128)(2,1)S(1)}, u32[]{:S(2)}, u32[]{:S(2)}) async-start(bf16[4,128,256]{1,2,0:T(8,128)(2,1)} %copy_bitcast_fusion.1), calls=%async_computation.6 | async-start | bytes 524288 | tf_op jit(solution)/shard_map/all_to_all | solution.py:98
  107.5 2.5 %convolution_convert_fusion.3 = bf16[512,128]{0,1:T(8,128)(2,1)} fusion(bf16[512,1536]{0,1:T(8,128)(2,1)} %copy-done.7, bf16[1536,256]{1,0:T(8,128)(2,1)} %copy-done.10), kind=kOutput, calls=%fused_computation.61 | convolution fusion | flops 201392128 | bytes 2097152 | tf_op jit(solution)/shard_map/dot_general | solution.py:66
  110.0 1.8 %copy_bitcast_fusion.2 = bf16[4,128,256]{1,2,0:T(8,128)(2,1)} fusion(bf16[512,256]{0,1:T(8,128)(2,1)} %collective-permute-done.5, bf16[512,256]{0,1:T(8,128)(2,1)} %collective-permute-done.4, f32[1536,128]{0,1:T(8,128)S(1)} %copy-done.4, f32[1536,128]{0,1:T(8,128)S(1)} %convolution_add_fusion.3), kind=kLoop, calls=%fused_computation.79 | loop fusion | flops 786432 | bytes 2359296 | tf_op jit(solution)/shard_map/all_to_all | solution.py:97
  111.8 4.8 %all-to-all-done.6 = bf16[4,128,256]{1,2,0:T(8,128)(2,1)S(1)} async-done(((bf16[4,128,256]{1,2,0:T(8,128)(2,1)}), bf16[4,128,256]{1,2,0:T(8,128)(2,1)S(1)}, u32[]{:S(2)}, u32[]{:S(2)}) %all-to-all-start.6) | async-done | bytes 262176 | tf_op jit(solution)/shard_map/all_to_all | solution.py:98
  116.6 3.4 %all-to-all-start.5 = ((bf16[4,128,256]{1,2,0:T(8,128)(2,1)}), bf16[4,128,256]{1,2,0:T(8,128)(2,1)S(1)}, u32[]{:S(2)}, u32[]{:S(2)}) async-start(bf16[4,128,256]{1,2,0:T(8,128)(2,1)} %copy_bitcast_fusion.2), calls=%async_computation.5 | async-start | bytes 524288 | tf_op jit(solution)/shard_map/all_to_all | solution.py:97
  120.1 1.4 convolution_convert_fusion.2
  121.5 1.9 %copy_bitcast_fusion = bf16[4,128,512]{1,2,0:T(8,128)(2,1)} fusion(bf16[512,128]{0,1:T(8,128)(2,1)S(1)} %convolution_convert_fusion, bf16[512,128]{0,1:T(8,128)(2,1)} %convolution_convert_fusion.1, bf16[512,128]{0,1:T(8,128)(2,1)S(1)} %convolution_convert_fusion.2, bf16[512,128]{0,1:T(8,128)(2,1)} %convolution_convert_fusion.3), kind=kLoop, calls=%fused_computation.72 | loop fusion | flops 2097152 | bytes 1048576 | tf_op jit(solution)/shard_map/all_to_all | solution.py:96
  123.3 3.6 %all-to-all-done.5 = bf16[4,128,256]{1,2,0:T(8,128)(2,1)S(1)} async-done(((bf16[4,128,256]{1,2,0:T(8,128)(2,1)}), bf16[4,128,256]{1,2,0:T(8,128)(2,1)S(1)}, u32[]{:S(2)}, u32[]{:S(2)}) %all-to-all-start.5) | async-done | bytes 262176 | tf_op jit(solution)/shard_map/all_to_all | solution.py:97
  126.9 3.5 %all-to-all-start.4 = ((bf16[4,128,512]{1,2,0:T(8,128)(2,1)}), bf16[4,128,512]{1,2,0:T(8,128)(2,1)S(1)}, u32[]{:S(2)}, u32[]{:S(2)}) async-start(bf16[4,128,512]{1,2,0:T(8,128)(2,1)} %copy_bitcast_fusion), calls=%async_computation.4 | async-start | bytes 1048576 | tf_op jit(solution)/shard_map/all_to_all | solution.py:96
  130.4 0.9 copy.37
  131.3 0.8 copy.36
  132.1 10.0 %all-to-all-done.4 = bf16[4,128,512]{1,2,0:T(8,128)(2,1)S(1)} async-done(((bf16[4,128,512]{1,2,0:T(8,128)(2,1)}), bf16[4,128,512]{1,2,0:T(8,128)(2,1)S(1)}, u32[]{:S(2)}, u32[]{:S(2)}) %all-to-all-start.4) | async-done | bytes 524320 | tf_op jit(solution)/shard_map/all_to_all | solution.py:96
  142.1 1.0 copy.35
  (49 shorter events, 2.8 us)
Async XLA Ops:
  0.6 33.0 %copy-start.14 = (bf16[128,2048]{1,0:T(8,128)(2,1)S(1)}, bf16[128,2048]{1,0:T(8,128)(2,1)}, u32[]{:S(2)}) copy-start(bf16[128,2048]{1,0:T(8,128)(2,1)} %param.7) | copy-start | bytes 1572868
  2.5 13.8 %all-to-all-start.2 = ((bf16[128,4,256]{0,2,1:T(8,128)(2,1)}), bf16[128,4,256]{0,2,1:T(8,128)(2,1)S(1)}, u32[]{:S(2)}, u32[]{:S(2)}) async-start(bf16[128,4,256]{0,2,1:T(8,128)(2,1)} %bitcast.7), calls=%async_computation.2 | async-start | bytes 524288 | tf_op jit(solution)/shard_map/all_to_all | solution.py:26
  16.3 10.4 %all-to-all-start = ((bf16[128,4,256]{0,2,1:T(8,128)(2,1)}), bf16[128,4,256]{0,2,1:T(8,128)(2,1)S(1)}, u32[]{:S(2)}, u32[]{:S(2)}) async-start(bf16[128,4,256]{0,2,1:T(8,128)(2,1)} %bitcast), calls=%async_computation | async-start | bytes 524288 | tf_op jit(solution)/shard_map/all_to_all | solution.py:25
  21.9 12.7 %collective-permute-start.3 = (bf16[512,256]{1,0:T(8,128)(2,1)S(1)}, bf16[512,256]{1,0:T(8,128)(2,1)S(1)}, u32[]{:S(2)}, u32[]{:S(2)}) collective-permute-start(bf16[512,256]{1,0:T(8,128)(2,1)S(1)} %bitcast.82), channel_id=1, source_target_pairs={{0,4},{4,8},{8,12},{12,16},{16,20},{20,24},{24,28},{1,5},{5,9},{9,... | collective-permute-start | bytes 786440 | tf_op jit(solution)/shard_map/ppermute | solution.py:19
  23.8 11.1 %collective-permute-start.2 = (bf16[512,256]{1,0:T(8,128)(2,1)S(1)}, bf16[512,256]{1,0:T(8,128)(2,1)S(1)}, u32[]{:S(2)}, u32[]{:S(2)}) collective-permute-start(bf16[512,256]{1,0:T(8,128)(2,1)S(1)} %bitcast.83), channel_id=1, source_target_pairs={{0,8},{4,12},{8,16},{12,20},{16,24},{20,28},{1,9},{5,13},{9,17},{1... | collective-permute-start | bytes 786440 | tf_op jit(solution)/shard_map/ppermute | solution.py:19
  26.7 17.4 %all-to-all-start.1 = ((bf16[128,4,512]{0,2,1:T(8,128)(2,1)}), bf16[128,4,512]{0,2,1:T(8,128)(2,1)S(1)}, u32[]{:S(2)}, u32[]{:S(2)}) async-start(bf16[128,4,512]{0,2,1:T(8,128)(2,1)} %bitcast.3), calls=%async_computation.1 | async-start | bytes 1048576 | tf_op jit(solution)/shard_map/all_to_all | solution.py:24
  30.4 8.0 %collective-permute-start.1 = (bf16[512,256]{1,0:T(8,128)(2,1)S(1)}, bf16[512,256]{1,0:T(8,128)(2,1)S(1)}, u32[]{:S(2)}, u32[]{:S(2)}) collective-permute-start(bf16[512,256]{1,0:T(8,128)(2,1)S(1)} %bitcast.85), channel_id=1, source_target_pairs={{0,4},{4,8},{8,12},{12,16},{16,20},{20,24},{24,28},{1,5},{5,9},{9,... | collective-permute-start | bytes 786440 | tf_op jit(solution)/shard_map/ppermute | solution.py:19
  32.3 11.7 %collective-permute-start = (bf16[512,256]{1,0:T(8,128)(2,1)S(1)}, bf16[512,256]{1,0:T(8,128)(2,1)S(1)}, u32[]{:S(2)}, u32[]{:S(2)}) collective-permute-start(bf16[512,256]{1,0:T(8,128)(2,1)S(1)} %bitcast.86), channel_id=1, source_target_pairs={{0,8},{4,12},{8,16},{12,20},{16,24},{20,28},{1,9},{5,13},{9,17},{1... | collective-permute-start | bytes 786440 | tf_op jit(solution)/shard_map/ppermute | solution.py:19
  44.1 8.1 %copy-start.10 = (bf16[1536,256]{1,0:T(8,128)(2,1)}, bf16[1536,256]{1,0:T(8,128)(2,1)S(1)}, u32[]{:S(2)}) copy-start(bf16[1536,256]{1,0:T(8,128)(2,1)S(1)} %pad_maximum_fusion.2) | copy-start | bytes 2359300
  44.1 19.4 %all-to-all-start.3 = ((bf16[128,4,512]{0,2,1:T(8,128)(2,1)}), bf16[128,4,512]{0,2,1:T(8,128)(2,1)}, u32[]{:S(2)}, u32[]{:S(2)}) async-start(bf16[128,4,512]{0,2,1:T(8,128)(2,1)} %bitcast.10), calls=%async_computation.3 | async-start | bytes 1048576 | tf_op jit(solution)/shard_map/all_to_all | solution.py:27
  49.1 3.1 %copy-start.8 = (bf16[4,128,512]{2,1,0:T(8,128)(2,1)}, bf16[4,128,512]{2,1,0:T(8,128)(2,1)S(1)}, u32[]{:S(2)}) copy-start(bf16[4,128,512]{2,1,0:T(8,128)(2,1)S(1)} %copy.27) | copy-start | bytes 1572868
  55.3 2.6 %copy-start.11 = (bf16[1536,256]{1,0:T(8,128)(2,1)S(1)}, bf16[1536,256]{1,0:T(8,128)(2,1)}, u32[]{:S(2)}) copy-start(bf16[1536,256]{1,0:T(8,128)(2,1)} %copy-done.10) | copy-start | bytes 2359300
  65.5 2.8 %copy-start.1 = (f32[512,1536]{0,1:T(8,128)S(1)}, f32[512,1536]{0,1:T(8,128)}, u32[]{:S(2)}) copy-start(f32[512,1536]{0,1:T(8,128)} %get-tuple-element.15) | copy-start | bytes 9437188
  68.3 1.8 %copy-start.13 = (bf16[1536,256]{1,0:T(8,128)(2,1)S(1)}, bf16[1536,256]{1,0:T(8,128)(2,1)}, u32[]{:S(2)}) copy-start(bf16[1536,256]{1,0:T(8,128)(2,1)} %pad_maximum_fusion.3) | copy-start | bytes 2359300
  68.3 1.8 %copy-start.15 = (bf16[4,128,512]{2,1,0:T(8,128)(2,1)S(1)}, bf16[4,128,512]{2,1,0:T(8,128)(2,1)}, u32[]{:S(2)}) copy-start(bf16[4,128,512]{2,1,0:T(8,128)(2,1)} %copy.31) | copy-start | bytes 1572868
  70.1 1.9 %copy-start = (f32[512,1536]{0,1:T(8,128)S(1)}, f32[512,1536]{0,1:T(8,128)}, u32[]{:S(2)}) copy-start(f32[512,1536]{0,1:T(8,128)} %get-tuple-element.23) | copy-start | bytes 9437188
  73.2 1.9 %copy-start.2 = (f32[512,1536]{0,1:T(8,128)S(1)}, f32[512,1536]{0,1:T(8,128)}, u32[]{:S(2)}) copy-start(f32[512,1536]{0,1:T(8,128)} %get-tuple-element.11) | copy-start | bytes 9437188
  76.4 1.1 copy-start.12
  78.7 1.0 copy-start.9
  81.0 14.1 %copy-start.3 = (f32[1536,128]{0,1:T(8,128)}, f32[1536,128]{0,1:T(8,128)S(1)}, u32[]{:S(2)}) copy-start(f32[1536,128]{0,1:T(8,128)S(1)} %convolution_add_fusion.2) | copy-start | bytes 2359300
  83.1 20.0 %collective-permute-start.6 = (bf16[512,256]{0,1:T(8,128)(2,1)S(1)}, bf16[512,256]{0,1:T(8,128)(2,1)S(1)}, u32[]{:S(2)}, u32[]{:S(2)}) collective-permute-start(bf16[512,256]{0,1:T(8,128)(2,1)S(1)} %get-tuple-element.6), channel_id=1, source_target_pairs={{4,0},{8,4},{12,8},{16,12},{20,16},{24,20},{28,24},{5,1},{9,5},{13... | collective-permute-start | bytes 786440 | tf_op jit(solution)/shard_map/ppermute | solution.py:19
  87.3 15.8 %collective-permute-start.7 = (bf16[512,256]{0,1:T(8,128)(2,1)S(1)}, bf16[512,256]{0,1:T(8,128)(2,1)S(1)}, u32[]{:S(2)}, u32[]{:S(2)}) collective-permute-start(bf16[512,256]{0,1:T(8,128)(2,1)S(1)} %get-tuple-element.7), channel_id=1, source_target_pairs={{8,0},{12,4},{16,8},{20,12},{24,16},{28,20},{9,1},{13,5},{17,9},{2... | collective-permute-start | bytes 786440 | tf_op jit(solution)/shard_map/ppermute | solution.py:19
  92.9 1.5 %copy-start.7 = (bf16[512,1536]{0,1:T(8,128)(2,1)}, bf16[512,1536]{0,1:T(8,128)(2,1)S(1)}, u32[]{:S(2)}) copy-start(bf16[512,1536]{0,1:T(8,128)(2,1)S(1)} %multiply_convert_fusion.3) | copy-start | bytes 4718596
  94.4 1.6 %copy-start.5 = (bf16[512,1536]{0,1:T(8,128)(2,1)}, bf16[512,1536]{0,1:T(8,128)(2,1)S(1)}, u32[]{:S(2)}) copy-start(bf16[512,1536]{0,1:T(8,128)(2,1)S(1)} %multiply_convert_fusion.2) | copy-start | bytes 4718596
  96.0 13.9 %collective-permute-start.4 = (bf16[512,256]{0,1:T(8,128)(2,1)}, bf16[512,256]{0,1:T(8,128)(2,1)}, u32[]{:S(2)}, u32[]{:S(2)}) collective-permute-start(bf16[512,256]{0,1:T(8,128)(2,1)} %get-tuple-element.8), channel_id=1, source_target_pairs={{4,0},{8,4},{12,8},{16,12},{20,16},{24,20},{28,24},{5,1},{9,5},{13... | collective-permute-start | bytes 786440 | tf_op jit(solution)/shard_map/ppermute | solution.py:19
  98.9 11.1 %collective-permute-start.5 = (bf16[512,256]{0,1:T(8,128)(2,1)}, bf16[512,256]{0,1:T(8,128)(2,1)}, u32[]{:S(2)}, u32[]{:S(2)}) collective-permute-start(bf16[512,256]{0,1:T(8,128)(2,1)} %get-tuple-element.9), channel_id=1, source_target_pairs={{8,0},{12,4},{16,8},{20,12},{24,16},{28,20},{9,1},{13,5},{17,9},{2... | collective-permute-start | bytes 786440 | tf_op jit(solution)/shard_map/ppermute | solution.py:19
  103.1 6.9 %copy-start.4 = (f32[1536,128]{0,1:T(8,128)S(1)}, f32[1536,128]{0,1:T(8,128)}, u32[]{:S(2)}) copy-start(f32[1536,128]{0,1:T(8,128)} %copy-done.3) | copy-start | bytes 2359300
  103.9 16.2 %copy-start.6 = (bf16[512,1536]{0,1:T(8,128)(2,1)S(1)}, bf16[512,1536]{0,1:T(8,128)(2,1)}, u32[]{:S(2)}) copy-start(bf16[512,1536]{0,1:T(8,128)(2,1)} %copy-done.5) | copy-start | bytes 4718596
  103.9 12.7 %all-to-all-start.6 = ((bf16[4,128,256]{1,2,0:T(8,128)(2,1)}), bf16[4,128,256]{1,2,0:T(8,128)(2,1)S(1)}, u32[]{:S(2)}, u32[]{:S(2)}) async-start(bf16[4,128,256]{1,2,0:T(8,128)(2,1)} %copy_bitcast_fusion.1), calls=%async_computation.6 | async-start | bytes 524288 | tf_op jit(solution)/shard_map/all_to_all | solution.py:98
  116.6 10.3 %all-to-all-start.5 = ((bf16[4,128,256]{1,2,0:T(8,128)(2,1)}), bf16[4,128,256]{1,2,0:T(8,128)(2,1)S(1)}, u32[]{:S(2)}, u32[]{:S(2)}) async-start(bf16[4,128,256]{1,2,0:T(8,128)(2,1)} %copy_bitcast_fusion.2), calls=%async_computation.5 | async-start | bytes 524288 | tf_op jit(solution)/shard_map/all_to_all | solution.py:97
  126.9 15.2 %all-to-all-start.4 = ((bf16[4,128,512]{1,2,0:T(8,128)(2,1)}), bf16[4,128,512]{1,2,0:T(8,128)(2,1)S(1)}, u32[]{:S(2)}, u32[]{:S(2)}) async-start(bf16[4,128,512]{1,2,0:T(8,128)(2,1)} %copy_bitcast_fusion), calls=%async_computation.4 | async-start | bytes 1048576 | tf_op jit(solution)/shard_map/all_to_all | solution.py:96
where the time goes:
time: 144 us; the launch traced here: 143 us
  starting transfers between devices  48.3 us (34%)
  waiting for transfers between devices  37.2 us (26%)
  matrix products  27.6 us (19%)
  local copies, waits for them, and re-layouts  15.9 us (11%)
  other arithmetic  13.1 us (9%)
    ppermute x8, starting transfers between devices, shifted(): lax.ppermute(value, axis, [(source, source + steps) for source in range(f...  21.3 us
    dot_general x4, matrix products, on_device(): lax.dot_general(query_head, key_head, contract_last, preferred_element_ty...  12.8 us
    unnamed x39, local copies, waits for them, and re-layouts  12.5 us
    all_to_all x1, waiting for transfers between devices, on_device(): lax.all_to_all(query_grad, 'head', split_axis=0, concat_axis=1, tiled=True)  10 us
    ppermute x8, waiting for transfers between devices, shifted(): lax.ppermute(value, axis, [(source, source + steps) for source in range(f...  8.46 us
    all_to_all x1, waiting for transfers between devices, on_device(): lax.all_to_all(saved_value_rows, 'head', split_axis=1, concat_axis=0, til...  7.13 us
    dot_general x4, matrix products, on_device(): jnp.dot(score_grad, key_head, preferred_element_type=jnp.float32)  5.43 us
    all_to_all x1, starting transfers between devices, on_device(): lax.all_to_all(saved_value_rows, 'head', split_axis=1, concat_axis=0, til...  4.87 us
  transfers between devices with their start and end apart: 15, of which 9 were waited for; matrix products, arithmetic and copies ran while one was open for 24% of the time, Pallas kernels for 0%

commit v1 on v0

v1 whole, which is shorter than its diff:
```python
import functools

import jax
import jax.numpy as jnp
from jax import lax
from jax.experimental import pallas as pl
from jax.experimental.pallas import tpu as pltpu
from jax.sharding import Mesh
from jax.sharding import PartitionSpec as P

HEAD_SIZE = 128
BLOCK = 128
LOG2_E = 1.4426950408889634

score_scale = 168.0 ** (-0.5)
masked_value = -1e30
contract_last = (((1,), (1,)), ((), ()))
VMEM_SPEC = pl.BlockSpec(memory_space=pltpu.VMEM)
SMEM_SPEC = pl.BlockSpec(memory_space=pltpu.SMEM)
GROUP = ("core", "head")


def pack_kernel(groups, a_ref, b_ref, out_ref):
    width = a_ref.shape[1] // groups
    for g in range(groups):
        out_ref[g, :, :width] = a_ref[:, g * width : (g + 1) * width]
        out_ref[g, :, width:] = b_ref[:, g * width : (g + 1) * width]


def packed(a, b, groups):
    rows, columns = a.shape
    width = columns // groups
    out = pl.pallas_call(
        functools.partial(pack_kernel, groups),
        out_shape=jax.ShapeDtypeStruct((groups, rows, 2 * width), a.dtype),
        in_specs=[VMEM_SPEC] * 2,
        out_specs=VMEM_SPEC,
        compiler_params=pltpu.CompilerParams(vmem_limit_bytes=16 * 2**20),
        cost_estimate=pl.CostEstimate(flops=0, bytes_accessed=8 * rows * columns, transcendentals=0),
    )(a, b)
    return out.reshape(groups * rows, 2 * width)


def unpack_one_kernel(groups, in_ref, out_ref):
    width = in_ref.shape[2]
    for g in range(groups):
        out_ref[:, g * width : (g + 1) * width] = in_ref[g]


def unpacked_one(a, groups):
    rows = a.shape[0] // groups
    width = a.shape[1]
    return pl.pallas_call(
        functools.partial(unpack_one_kernel, groups),
        out_shape=jax.ShapeDtypeStruct((rows, groups * width), a.dtype),
        in_specs=[VMEM_SPEC],
        out_specs=VMEM_SPEC,
        compiler_params=pltpu.CompilerParams(vmem_limit_bytes=16 * 2**20),
        cost_estimate=pl.CostEstimate(flops=0, bytes_accessed=4 * a.size, transcendentals=0),
    )(a.reshape(groups, rows, width))


def unpack_two_kernel(groups, in_ref, first_ref, second_ref):
    width = in_ref.shape[2] // 2
    for g in range(groups):
        first_ref[:, g * width : (g + 1) * width] = in_ref[g, :, :width]
        second_ref[:, g * width : (g + 1) * width] = in_ref[g, :, width:]


def unpacked_two(a, groups):
    rows = a.shape[0] // groups
    width = a.shape[1] // 2
    shape = jax.ShapeDtypeStruct((rows, groups * width), a.dtype)
    return pl.pallas_call(
        functools.partial(unpack_two_kernel, groups),
        out_shape=(shape, shape),
        in_specs=[VMEM_SPEC],
        out_specs=(VMEM_SPEC, VMEM_SPEC),
        compiler_params=pltpu.CompilerParams(vmem_limit_bytes=16 * 2**20),
        cost_estimate=pl.CostEstimate(flops=0, bytes_accessed=4 * a.size, transcendentals=0),
    )(a.reshape(groups, rows, 2 * width))


def attention_kernel(
    first_ref, qd_ref, own_ref, prev_ref, dq_ref, own_grad_ref, prev_grad_ref,
    own_kt_ref, prev_kt_ref, dk_prev_ref, dv_prev_ref,
):
    d = HEAD_SIZE
    positions = qd_ref.shape[0]
    steps = positions // BLOCK
    bias = jnp.where(first_ref[0] == 1, masked_value, 0.0).astype(jnp.float32)
    own_kt_ref[...] = own_ref[:, :d].T
    prev_kt_ref[...] = prev_ref[:, :d].T
    key_row = lax.broadcasted_iota(jnp.int32, (BLOCK, 2 * BLOCK), 0)
    query_row = lax.broadcasted_iota(jnp.int32, (BLOCK, 2 * BLOCK), 1) % BLOCK
    own_seen = key_row <= query_row
    for i in range(steps):
        low, high = i * BLOCK, (i + 1) * BLOCK
        q = jnp.concatenate([qd_ref[low:high, :d], qd_ref[low:high, d : 2 * d]], 0)
        g = jnp.concatenate([qd_ref[low:high, 2 * d : 3 * d], qd_ref[low:high, 3 * d :]], 0)
        dot_t = lambda a, b: lax.dot_general(a, b, contract_last, preferred_element_type=jnp.float32)
        s_own = dot_t(own_ref[:high, :d], q)
        s_prev = dot_t(prev_ref[low:, :d], q) + bias
        p_own = dot_t(own_ref[:high, d:], g)
        p_prev = dot_t(prev_ref[low:, d:], g)
        s_diag = jnp.where(own_seen, s_own[low:], s_prev[:BLOCK])
        p_diag = jnp.where(own_seen, p_own[low:], p_prev[:BLOCK])
        s = [s_own[:low]] * (i > 0) + [s_diag] + [s_prev[BLOCK:]] * (i < steps - 1)
        dp = [p_own[:low]] * (i > 0) + [p_diag] + [p_prev[BLOCK:]] * (i < steps - 1)
        s = jnp.concatenate(s, 0)
        dp = jnp.concatenate(dp, 0)
        top = jnp.max(s, axis=0, keepdims=True)
        w = jnp.exp2((s - top) * (score_scale * LOG2_E))
        inverse = 1.0 / jnp.sum(w, axis=0, keepdims=True)
        delta = jnp.sum(w * dp, axis=0, keepdims=True) * inverse
        attention = w * inverse
        ds = (attention * (dp - delta)).astype(jnp.bfloat16)
        low_attention = attention.astype(jnp.bfloat16)
        zero = jnp.zeros((BLOCK, 2 * BLOCK), jnp.bfloat16)
        ds_diag, at_diag = ds[low:high], low_attention[low:high]
        ds_own = jnp.concatenate([ds[:low]] * (i > 0) + [jnp.where(own_seen, ds_diag, zero)], 0)
        ds_prev = jnp.concatenate([jnp.where(own_seen, zero, ds_diag)] + [ds[high:]] * (i < steps - 1), 0)
        at_own = jnp.concatenate([low_attention[:low]] * (i > 0) + [jnp.where(own_seen, at_diag, zero)], 0)
        at_prev = jnp.concatenate(
            [jnp.where(own_seen, zero, at_diag)] + [low_attention[high:]] * (i < steps - 1), 0
        )
        dot = lambda a, b: jnp.dot(a, b, preferred_element_type=jnp.float32)
        dq_t = dot(own_kt_ref[:, :high], ds_own) + dot(prev_kt_ref[:, low:], ds_prev)
        dq_t = dq_t * score_scale
        dq_ref[low:high, :d] = dq_t[:, :BLOCK].T.astype(jnp.bfloat16)
        dq_ref[low:high, d:] = dq_t[:, BLOCK:].T.astype(jnp.bfloat16)
        dk_own, dk_prev = dot(ds_own, q), dot(ds_prev, q)
        dv_own, dv_prev = dot(at_own, g), dot(at_prev, g)
        if i > 0:
            own_grad_ref[:low, :d] += dk_own[:low]
            own_grad_ref[:low, d:] += dv_own[:low]
            dk_prev_ref[low:] += dk_prev
            dv_prev_ref[low:] += dv_prev
        else:
            dk_prev_ref[...] = dk_prev
            dv_prev_ref[...] = dv_prev
        own_grad_ref[low:high, :d] = dk_own[low:]
        own_grad_ref[low:high, d:] = dv_own[low:]
    own_grad_ref[:, :d] = own_grad_ref[:, :d] * score_scale
    prev_grad_ref[:, :d] = (dk_prev_ref[...] * score_scale).astype(jnp.bfloat16)
    prev_grad_ref[:, d:] = dv_prev_ref[...].astype(jnp.bfloat16)


def attention_backward(first, qd, own, prev):
    positions = qd.shape[0]
    d = HEAD_SIZE
    return pl.pallas_call(
        attention_kernel,
        out_shape=(
            jax.ShapeDtypeStruct((positions, 2 * d), jnp.bfloat16),
            jax.ShapeDtypeStruct((positions, 2 * d), jnp.float32),
            jax.ShapeDtypeStruct((positions, 2 * d), jnp.bfloat16),
        ),
        in_specs=[SMEM_SPEC] + [VMEM_SPEC] * 3,
        out_specs=(VMEM_SPEC,) * 3,
        scratch_shapes=[
            pltpu.VMEM((d, positions), jnp.bfloat16),
            pltpu.VMEM((d, positions), jnp.bfloat16),
            pltpu.VMEM((positions, d), jnp.float32),
            pltpu.VMEM((positions, d), jnp.float32),
        ],
        compiler_params=pltpu.CompilerParams(vmem_limit_bytes=48 * 2**20),
        cost_estimate=pl.CostEstimate(
            flops=20 * positions * positions * d, bytes_accessed=12 * positions * d, transcendentals=2 * positions**2
        ),
    )(first, qd, own, prev)


def add_kernel(own_ref, back_ref, out_ref):
    out_ref[...] = (own_ref[...] + back_ref[...].astype(jnp.float32)).astype(jnp.bfloat16)


def added(own, back):
    return pl.pallas_call(
        add_kernel,
        out_shape=jax.ShapeDtypeStruct(back.shape, back.dtype),
        in_specs=[VMEM_SPEC] * 2,
        out_specs=VMEM_SPEC,
        compiler_params=pltpu.CompilerParams(vmem_limit_bytes=16 * 2**20),
    )(own, back)


def exchanged(value):
    return lax.all_to_all(value, GROUP, split_axis=0, concat_axis=0, tiled=True)


def on_device(groups, query_rows, key_rows, saved_value_rows, out_grad):
    chips = lax.axis_size("chip")
    first = (lax.axis_index("chip") == 0).astype(jnp.int32).reshape(1)
    own = exchanged(packed(key_rows, saved_value_rows, groups))
    prev = lax.ppermute(own, "chip", [(c, c + 1) for c in range(chips - 1)])
    qd = exchanged(packed(query_rows, out_grad, groups))
    dq, own_grad, prev_grad = attention_backward(first, qd, own, prev)
    back = lax.ppermute(prev_grad, "chip", [(c + 1, c) for c in range(chips - 1)])
    query_grad = unpacked_one(exchanged(dq), groups)
    key_grad, value_grad = unpacked_two(exchanged(added(own_grad, back)), groups)
    return query_grad, key_grad, value_grad


def solution(mesh):
    heads = mesh.shape["head"]
    devices = mesh.devices.reshape(-1, 2, heads)
    fine_mesh = Mesh(devices, ("chip", "core", "head"))
    rows = P(("chip", "core", "head"), None)
    return jax.shard_map(
        functools.partial(on_device, 2 * heads),
        mesh=fine_mesh,
        in_specs=(rows,) * 4,
        out_specs=(rows,) * 3,
        check_vma=False,
    )
```

time: 144 us -> 107 us (0.74)
  the two profiles are of different devices: /device:TPU:6 before, /device:TPU:0 now
where the time goes in v1:
time: 107 us
  waiting for transfers between devices  65.3 us (61%)
  starting transfers between devices  23.1 us (22%)
  Pallas kernels  15 us (14%)
  local copies, waits for them, and re-layouts  2.69 us (3%)
    all_to_all x4, waiting for transfers between devices, exchanged(): return lax.all_to_all(value, GROUP, split_axis=0, concat_axis=0, tiled=True)  38.7 us
    all_to_all x4, starting transfers between devices, exchanged(): return lax.all_to_all(value, GROUP, split_axis=0, concat_axis=0, tiled=True)  18.4 us
    ppermute x1, waiting for transfers between devices, on_device(): lax.ppermute(prev_grad, 'chip', [(c + 1, c) for c in range(chips - 1)])  14.9 us
    ppermute x1, waiting for transfers between devices, on_device(): prev = lax.ppermute(own, 'chip', [(c, c + 1) for c in range(chips - 1)])  11.7 us
    pallas_call x1, Pallas kernels, attention_backward(): pl.pallas_call(attention_kernel, out_shape=(jax.ShapeDtypeStruct((positio...  10.3 us
    ppermute x1, starting transfers between devices, on_device(): prev = lax.ppermute(own, 'chip', [(c, c + 1) for c in range(chips - 1)])  3.43 us
    unnamed x12, local copies, waits for them, and re-layouts  2.69 us
  transfers between devices with their start and end apart: 6, of which 5 were waited for; matrix products, arithmetic and copies ran while one was open for 0% of the time, Pallas kernels for 3%

profile of v1, /device:TPU:0, one launch (start us, length us, event | category | flops | bytes accessed | tf_op | source)
XLA Modules:
  0.0 106.7 jit_solution(7341797793464085875)
XLA Ops:
  0.6 0.0 copy-start.2
  0.6 0.9 copy-done.2
  1.6 0.0 copy-start.3
  1.6 0.9 copy-done.3
  2.5 0.9 shard_map.68
  3.4 0.0 copy-start
  3.4 0.0 copy-start.1
  3.4 6.5 %all-to-all-start.1 = ((bf16[8,128,256]{2,1,0:T(8,128)(2,1)}), bf16[8,128,256]{2,1,0:T(8,128)(2,1)S(1)}, u32[]{:S(2)}, u32[]{:S(2)}) async-start(bf16[8,128,256]{2,1,0:T(8,128)(2,1)} %shard_map.68), calls=%async_computation.1 | async-start | bytes 1048576 | tf_op jit(solution)/shard_map/all_to_all | solution.py:189
  9.9 0.0 copy-done
  9.9 0.0 copy-done.1
  9.9 1.1 %shard_map.67 = bf16[8,128,512]{2,1,0:T(8,128)(2,1)} custom-call(bf16[128,2048]{1,0:T(8,128)(2,1)S(1)} %copy-done, bf16[128,2048]{1,0:T(8,128)(2,1)S(1)} %copy-done.1), custom_call_target="tpu_custom_call" | custom-call | bytes 2097152 | tf_op jit(solution)/shard_map/pallas_call | solution.py:33
  11.0 13.8 %all-to-all-done.1 = bf16[8,128,256]{2,1,0:T(8,128)(2,1)S(1)} async-done(((bf16[8,128,256]{2,1,0:T(8,128)(2,1)}), bf16[8,128,256]{2,1,0:T(8,128)(2,1)S(1)}, u32[]{:S(2)}, u32[]{:S(2)}) %all-to-all-start.1) | async-done | bytes 524320 | tf_op jit(solution)/shard_map/all_to_all | solution.py:189
  24.8 3.6 %all-to-all-start = ((bf16[8,128,512]{2,1,0:T(8,128)(2,1)}), bf16[8,128,512]{2,1,0:T(8,128)(2,1)S(1)}, u32[]{:S(2)}, u32[]{:S(2)}) async-start(bf16[8,128,512]{2,1,0:T(8,128)(2,1)} %shard_map.67), calls=%async_computation | async-start | bytes 2097152 | tf_op jit(solution)/shard_map/all_to_all | solution.py:189
  28.3 3.4 %collective-permute-start = (bf16[1024,256]{1,0:T(8,128)(2,1)S(1)}, bf16[1024,256]{1,0:T(8,128)(2,1)S(1)}, u32[]{:S(2)}, u32[]{:S(2)}) collective-permute-start(bf16[1024,256]{1,0:T(8,128)(2,1)S(1)} %bitcast.6), channel_id=1, source_target_pairs={{0,8},{8,16},{16,24},{1,9},{9,17},{17,25},{2,10},{10,18},{18,26},{... | collective-permute-start | bytes 1572872 | tf_op jit(solution)/shard_map/ppermute | solution.py:196
  31.8 11.7 %collective-permute-done.prev_ref = bf16[1024,256]{1,0:T(8,128)(2,1)S(1)} collective-permute-done((bf16[1024,256]{1,0:T(8,128)(2,1)S(1)}, bf16[1024,256]{1,0:T(8,128)(2,1)S(1)}, u32[]{:S(2)}, u32[]{:S(2)}) %collective-permute-start) | collective-permute-done | bytes 524320 | tf_op jit(solution)/shard_map/ppermute | solution.py:196
  43.5 10.9 %all-to-all-done = bf16[8,128,512]{2,1,0:T(8,128)(2,1)S(1)} async-done(((bf16[8,128,512]{2,1,0:T(8,128)(2,1)}), bf16[8,128,512]{2,1,0:T(8,128)(2,1)S(1)}, u32[]{:S(2)}, u32[]{:S(2)}) %all-to-all-start) | async-done | bytes 1048608 | tf_op jit(solution)/shard_map/all_to_all | solution.py:189
  54.4 10.3 %shard_map.69 = (bf16[1024,256]{1,0:T(8,128)(2,1)}, f32[1024,256]{1,0:T(8,128)S(1)}, bf16[1024,256]{1,0:T(8,128)(2,1)S(1)}) custom-call(s32[1]{0:T(128)} %bitcast.first_ref, bf16[1024,512]{1,0:T(8,128)(2,1)S(1)} %bitcast.5, bf16[1024,256]{1,0:T(8,128)(2,1)S(1)} %bitcast.7, bf16[1024,256]{1,0:T(8,128)(2,1)S(1)} %collective-permute-done.prev_ref), custom_call_target="tpu_custom_call" | custom-call | flops 2684354560 | bytes 1572864 | tf_op jit(solution)/shard_map/pallas_call | solution.py:152
  64.7 0.0 copy-start.4
  64.7 0.8 copy-done.4
  65.5 0.0 copy-start.5
  65.5 3.6 %all-to-all-start.2 = ((bf16[8,128,256]{2,1,0:T(8,128)(2,1)}), bf16[8,128,256]{2,1,0:T(8,128)(2,1)S(1)}, u32[]{:S(2)}, u32[]{:S(2)}) async-start(bf16[8,128,256]{2,1,0:T(8,128)(2,1)} %bitcast.3), calls=%async_computation.2 | async-start | bytes 1048576 | tf_op jit(solution)/shard_map/all_to_all | solution.py:189
  69.1 0.0 copy-done.5
  69.1 1.3 %collective-permute-start.1 = (bf16[1024,256]{1,0:T(8,128)(2,1)S(1)}, bf16[1024,256]{1,0:T(8,128)(2,1)S(1)}, u32[]{:S(2)}, u32[]{:S(2)}) collective-permute-start(bf16[1024,256]{1,0:T(8,128)(2,1)S(1)} %copy-done.5), channel_id=1, source_target_pairs={{8,0},{16,8},{24,16},{9,1},{17,9},{25,17},{10,2},{18,10},{26,18},{... | collective-permute-start | bytes 1572872 | tf_op jit(solution)/shard_map/ppermute | solution.py:199
  70.4 14.9 %collective-permute-done.1.back_ref = bf16[1024,256]{1,0:T(8,128)(2,1)S(1)} collective-permute-done((bf16[1024,256]{1,0:T(8,128)(2,1)S(1)}, bf16[1024,256]{1,0:T(8,128)(2,1)S(1)}, u32[]{:S(2)}, u32[]{:S(2)}) %collective-permute-start.1) | collective-permute-done | bytes 524320 | tf_op jit(solution)/shard_map/ppermute | solution.py:199
  85.3 0.9 shard_map.71
  86.2 0.0 all-to-all-done.2.in_ref
  86.2 4.7 %all-to-all-start.3 = ((bf16[8,128,256]{2,1,0:T(8,128)(2,1)}), bf16[8,128,256]{2,1,0:T(8,128)(2,1)S(1)}, u32[]{:S(2)}, u32[]{:S(2)}) async-start(bf16[8,128,256]{2,1,0:T(8,128)(2,1)} %bitcast.4), calls=%async_computation.3 | async-start | bytes 1048576 | tf_op jit(solution)/shard_map/all_to_all | solution.py:189
  90.9 0.8 shard_map.70
  91.7 14.0 %all-to-all-done.3.in_ref = bf16[8,128,256]{2,1,0:T(8,128)(2,1)S(1)} async-done(((bf16[8,128,256]{2,1,0:T(8,128)(2,1)}), bf16[8,128,256]{2,1,0:T(8,128)(2,1)S(1)}, u32[]{:S(2)}, u32[]{:S(2)}) %all-to-all-start.3) | async-done | bytes 524320 | tf_op jit(solution)/shard_map/all_to_all | solution.py:189
  105.8 0.9 shard_map.72
Async XLA Ops:
  0.6 1.0 copy-start.2
  1.6 0.9 copy-start.3
  3.4 6.5 %copy-start = (bf16[128,2048]{1,0:T(8,128)(2,1)S(1)}, bf16[128,2048]{1,0:T(8,128)(2,1)}, u32[]{:S(2)}) copy-start(bf16[128,2048]{1,0:T(8,128)(2,1)} %a_ref.2) | copy-start | bytes 1572868
  3.4 6.5 %copy-start.1 = (bf16[128,2048]{1,0:T(8,128)(2,1)S(1)}, bf16[128,2048]{1,0:T(8,128)(2,1)}, u32[]{:S(2)}) copy-start(bf16[128,2048]{1,0:T(8,128)(2,1)} %b_ref.2) | copy-start | bytes 1572868
  3.4 21.3 %all-to-all-start.1 = ((bf16[8,128,256]{2,1,0:T(8,128)(2,1)}), bf16[8,128,256]{2,1,0:T(8,128)(2,1)S(1)}, u32[]{:S(2)}, u32[]{:S(2)}) async-start(bf16[8,128,256]{2,1,0:T(8,128)(2,1)} %shard_map.68), calls=%async_computation.1 | async-start | bytes 1048576 | tf_op jit(solution)/shard_map/all_to_all | solution.py:189
  24.8 29.6 %all-to-all-start = ((bf16[8,128,512]{2,1,0:T(8,128)(2,1)}), bf16[8,128,512]{2,1,0:T(8,128)(2,1)S(1)}, u32[]{:S(2)}, u32[]{:S(2)}) async-start(bf16[8,128,512]{2,1,0:T(8,128)(2,1)} %shard_map.67), calls=%async_computation | async-start | bytes 2097152 | tf_op jit(solution)/shard_map/all_to_all | solution.py:189
  28.3 15.2 %collective-permute-start = (bf16[1024,256]{1,0:T(8,128)(2,1)S(1)}, bf16[1024,256]{1,0:T(8,128)(2,1)S(1)}, u32[]{:S(2)}, u32[]{:S(2)}) collective-permute-start(bf16[1024,256]{1,0:T(8,128)(2,1)S(1)} %bitcast.6), channel_id=1, source_target_pairs={{0,8},{8,16},{16,24},{1,9},{9,17},{17,25},{2,10},{10,18},{18,26},{... | collective-permute-start | bytes 1572872 | tf_op jit(solution)/shard_map/ppermute | solution.py:196
  64.7 0.8 copy-start.4
  65.5 3.6 %copy-start.5 = (bf16[1024,256]{1,0:T(8,128)(2,1)S(1)}, bf16[1024,256]{1,0:T(8,128)(2,1)}, u32[]{:S(2)}) copy-start(bf16[1024,256]{1,0:T(8,128)(2,1)} %copy-done.4) | copy-start | bytes 1572868
  65.5 20.7 %all-to-all-start.2 = ((bf16[8,128,256]{2,1,0:T(8,128)(2,1)}), bf16[8,128,256]{2,1,0:T(8,128)(2,1)S(1)}, u32[]{:S(2)}, u32[]{:S(2)}) async-start(bf16[8,128,256]{2,1,0:T(8,128)(2,1)} %bitcast.3), calls=%async_computation.2 | async-start | bytes 1048576 | tf_op jit(solution)/shard_map/all_to_all | solution.py:189
  69.1 16.2 %collective-permute-start.1 = (bf16[1024,256]{1,0:T(8,128)(2,1)S(1)}, bf16[1024,256]{1,0:T(8,128)(2,1)S(1)}, u32[]{:S(2)}, u32[]{:S(2)}) collective-permute-start(bf16[1024,256]{1,0:T(8,128)(2,1)S(1)} %copy-done.5), channel_id=1, source_target_pairs={{8,0},{16,8},{24,16},{9,1},{17,9},{25,17},{10,2},{18,10},{26,18},{... | collective-permute-start | bytes 1572872 | tf_op jit(solution)/shard_map/ppermute | solution.py:199
  86.2 19.6 %all-to-all-start.3 = ((bf16[8,128,256]{2,1,0:T(8,128)(2,1)}), bf16[8,128,256]{2,1,0:T(8,128)(2,1)S(1)}, u32[]{:S(2)}, u32[]{:S(2)}) async-start(bf16[8,128,256]{2,1,0:T(8,128)(2,1)} %bitcast.4), calls=%async_computation.3 | async-start | bytes 1048576 | tf_op jit(solution)/shard_map/all_to_all | solution.py:189

commit v2 on v1

v2 whole, which is shorter than its diff:
```python
import functools

import jax
import jax.numpy as jnp
from jax import lax
from jax.experimental import pallas as pl
from jax.experimental.pallas import tpu as pltpu
from jax.sharding import Mesh
from jax.sharding import PartitionSpec as P

HEAD_SIZE = 128
BLOCK = 128
LOG2_E = 1.4426950408889634

score_scale = 168.0 ** (-0.5)
masked_value = -1e30
contract_last = (((1,), (1,)), ((), ()))
VMEM_SPEC = pl.BlockSpec(memory_space=pltpu.VMEM)
SMEM_SPEC = pl.BlockSpec(memory_space=pltpu.SMEM)


def call(kernel, out_shape, operands, scratch=(), flops=0, transcendentals=0, vmem=16):
    outs = out_shape if isinstance(out_shape, tuple) else (out_shape,)
    moved = sum(a.size * a.dtype.itemsize for a in operands + outs)
    return pl.pallas_call(
        kernel,
        out_shape=out_shape,
        in_specs=[SMEM_SPEC] + [VMEM_SPEC] * (len(operands) - 1),
        out_specs=jax.tree.map(lambda _: VMEM_SPEC, out_shape),
        scratch_shapes=list(scratch),
        compiler_params=pltpu.CompilerParams(vmem_limit_bytes=vmem * 2**20),
        cost_estimate=pl.CostEstimate(flops=flops, bytes_accessed=moved, transcendentals=transcendentals),
    )(*operands)


def shape_of(dtype, *shape):
    return jax.ShapeDtypeStruct(shape, dtype)


def at(start, size):
    return pl.ds(pl.multiple_of(start, size), size)


def pack_kv_kernel(heads, place_ref, k_ref, v_ref, out_ref):
    core = place_ref[1]
    d = HEAD_SIZE
    for z in range(heads):
        mine, other = at((2 * z + core) * d, d), at((2 * z + 1 - core) * d, d)
        out_ref[z, :, :d] = k_ref[:, mine]
        out_ref[z, :, d : 2 * d] = v_ref[:, mine]
        out_ref[z, :, 2 * d : 3 * d] = k_ref[:, other]
        out_ref[z, :, 3 * d :] = v_ref[:, other]


def pack_qd_kernel(heads, place_ref, q_ref, g_ref, *out_refs):
    core, head = place_ref[1], place_ref[2]
    width = 2 * HEAD_SIZE
    for n, out_ref in enumerate(out_refs):
        step, flip = n // 2, n % 2
        z = lax.rem(head + step, heads)
        c = 1 - core if flip else core
        columns = at((2 * z + c) * width, width)
        out_ref[:, :width] = q_ref[:, columns]
        out_ref[:, width:] = g_ref[:, columns]


def unpack_dq_kernel(heads, place_ref, *refs):
    core, head = place_ref[1], place_ref[2]
    width = 2 * HEAD_SIZE
    in_refs, out_ref = refs[:-1], refs[-1]
    for n, in_ref in enumerate(in_refs):
        step, flip = n // 2, n % 2
        z = lax.rem(head + heads - step, heads)
        c = 1 - core if flip else core
        out_ref[:, at((2 * z + c) * width, width)] = in_ref[...]


def unpack_kv_kernel(heads, place_ref, in_ref, k_ref, v_ref):
    core = place_ref[1]
    d = HEAD_SIZE
    for z in range(heads):
        mine, other = at((2 * z + core) * d, d), at((2 * z + 1 - core) * d, d)
        k_ref[:, mine] = in_ref[z, :, :d]
        v_ref[:, mine] = in_ref[z, :, d : 2 * d]
        k_ref[:, other] = in_ref[z, :, 2 * d : 3 * d]
        v_ref[:, other] = in_ref[z, :, 3 * d :]


def add_kernel(place_ref, own_ref, near_ref, sibling_ref, far_ref, out_ref):
    width = 2 * HEAD_SIZE
    wide = lambda ref: ref[...].astype(jnp.float32)
    out_ref[:, :width] = (own_ref[...] + wide(near_ref)).astype(jnp.bfloat16)
    out_ref[:, width:] = (wide(sibling_ref) + wide(far_ref)).astype(jnp.bfloat16)


def attention_kernel(heads, place_ref, mine_ref, sibling_ref, near_ref, far_ref, *refs):
    d = HEAD_SIZE
    count = 2 * heads
    block_refs, refs = refs[:count], refs[count:]
    dq_refs, refs = refs[:count], refs[count:]
    own_mine_ref, own_other_ref, prev_mine_ref, prev_other_ref = refs[:4]
    qd_ref, own_ref, prev_ref, dq_ref, own_kt_ref, prev_kt_ref, own_grad_ref, prev_grad_ref = refs[4:]
    first, core, head = place_ref[0], place_ref[1], place_ref[2]
    half = heads * BLOCK
    mine, other = at(core * half, half), at((1 - core) * half, half)
    own_ref[mine] = mine_ref[:, : 2 * d]
    own_ref[other] = sibling_ref[...]
    prev_ref[mine] = near_ref[...]
    prev_ref[other] = far_ref[...]

    def rows_of(n, step):
        c = 1 - core if n % 2 else core
        return at((c * heads + lax.rem(head + step, heads)) * BLOCK, BLOCK)

    for n in range(count):
        qd_ref[rows_of(n, heads - n // 2)] = block_refs[n][...]

    bias = jnp.where(first == 1, masked_value, 0.0).astype(jnp.float32)
    own_kt_ref[...] = own_ref[:, :d].T
    prev_kt_ref[...] = prev_ref[:, :d].T
    key_row = lax.broadcasted_iota(jnp.int32, (BLOCK, 2 * BLOCK), 0)
    query_row = lax.broadcasted_iota(jnp.int32, (BLOCK, 2 * BLOCK), 1) % BLOCK
    own_seen = key_row <= query_row
    zero = jnp.zeros((BLOCK, 2 * BLOCK), jnp.bfloat16)
    dot_t = lambda a, b: lax.dot_general(a, b, contract_last, preferred_element_type=jnp.float32)
    dot = lambda a, b: jnp.dot(a, b, preferred_element_type=jnp.float32)
    for i in range(count):
        low, high = i * BLOCK, (i + 1) * BLOCK
        below, above = i > 0, i < count - 1
        q = jnp.concatenate([qd_ref[low:high, :d], qd_ref[low:high, d : 2 * d]], 0)
        g = jnp.concatenate([qd_ref[low:high, 2 * d : 3 * d], qd_ref[low:high, 3 * d :]], 0)
        s_own = dot_t(own_ref[:high, :d], q)
        s_prev = dot_t(prev_ref[low:, :d], q) + bias
        p_own = dot_t(own_ref[:high, d:], g)
        p_prev = dot_t(prev_ref[low:, d:], g)
        s_diag = jnp.where(own_seen, s_own[low:], s_prev[:BLOCK])
        p_diag = jnp.where(own_seen, p_own[low:], p_prev[:BLOCK])
        s = jnp.concatenate([s_own[:low]] * below + [s_diag] + [s_prev[BLOCK:]] * above, 0)
        dp = jnp.concatenate([p_own[:low]] * below + [p_diag] + [p_prev[BLOCK:]] * above, 0)
        top = jnp.max(s, axis=0, keepdims=True)
        w = jnp.exp2((s - top) * (score_scale * LOG2_E))
        inverse = 1.0 / jnp.sum(w, axis=0, keepdims=True)
        delta = jnp.sum(w * dp, axis=0, keepdims=True) * inverse
        attention = w * inverse
        ds = (attention * (dp - delta)).astype(jnp.bfloat16)
        low_attention = attention.astype(jnp.bfloat16)
        split = lambda x: (
            jnp.concatenate([x[:low]] * below + [jnp.where(own_seen, x[low:high], zero)], 0),
            jnp.concatenate([jnp.where(own_seen, zero, x[low:high])] + [x[high:]] * above, 0),
        )
        ds_own, ds_prev = split(ds)
        at_own, at_prev = split(low_attention)
        dq_t = dot(own_kt_ref[:, :high], ds_own) + dot(prev_kt_ref[:, low:], ds_prev)
        dq_t = dq_t * score_scale
        dq_ref[low:high, :d] = dq_t[:, :BLOCK].T.astype(jnp.bfloat16)
        dq_ref[low:high, d:] = dq_t[:, BLOCK:].T.astype(jnp.bfloat16)
        dk_own, dk_prev = dot(ds_own, q), dot(ds_prev, q)
        dv_own, dv_prev = dot(at_own, g), dot(at_prev, g)
        if below:
            own_grad_ref[:low, :d] += dk_own[:low]
            own_grad_ref[:low, d:] += dv_own[:low]
            prev_grad_ref[low:, :d] += dk_prev
            prev_grad_ref[low:, d:] += dv_prev
        else:
            prev_grad_ref[:, :d] = dk_prev
            prev_grad_ref[:, d:] = dv_prev
        own_grad_ref[low:high, :d] = dk_own[low:]
        own_grad_ref[low:high, d:] = dv_own[low:]
    for n in range(count):
        dq_refs[n][...] = dq_ref[rows_of(n, n // 2)]
    for ref, grad_ref, rows in (
        (own_mine_ref, own_grad_ref, mine),
        (own_other_ref, own_grad_ref, other),
        (prev_mine_ref, prev_grad_ref, mine),
        (prev_other_ref, prev_grad_ref, other),
    ):
        ref[:, :d] = (grad_ref[rows, :d] * score_scale).astype(ref.dtype)
        ref[:, d:] = grad_ref[rows, d:].astype(ref.dtype)


def attention_backward(heads, place, mine, sibling, near, far, blocks):
    half, d = heads * BLOCK, HEAD_SIZE
    whole = 2 * half
    low, wide = jnp.bfloat16, jnp.float32
    outs = (shape_of(low, BLOCK, 2 * d),) * (2 * heads) + (
        shape_of(wide, half, 2 * d),
        shape_of(low, half, 2 * d),
        shape_of(low, half, 2 * d),
        shape_of(low, half, 2 * d),
    )
    scratch = (
        pltpu.VMEM((whole, 4 * d), low),
        pltpu.VMEM((whole, 2 * d), low),
        pltpu.VMEM((whole, 2 * d), low),
        pltpu.VMEM((whole, 2 * d), low),
        pltpu.VMEM((d, whole), low),
        pltpu.VMEM((d, whole), low),
        pltpu.VMEM((whole, 2 * d), wide),
        pltpu.VMEM((whole, 2 * d), wide),
    )
    outs = call(
        functools.partial(attention_kernel, heads),
        outs,
        (place, mine, sibling, near, far) + tuple(blocks),
        scratch,
        20 * whole * whole * d,
        2 * whole * whole,
        48,
    )
    return outs[: 2 * heads], outs[2 * heads :]


def moved(value, chips, heads, chip_step, flip, head_step):
    index = lambda chip, core, head: (chip * 2 + core) * heads + head
    pairs = [
        (index(chip, core, head), index(chip + chip_step, core ^ flip, (head + head_step) % heads))
        for chip in range(chips)
        for core in range(2)
        for head in range(heads)
        if 0 <= chip + chip_step < chips
    ]
    return lax.ppermute(value, ("chip", "core", "head"), pairs)


def swapped_heads(value, rows):
    out = lax.all_to_all(value.reshape(-1, value.shape[-1]), "head", split_axis=0, concat_axis=0, tiled=True)
    return out


def on_device(query_rows, key_rows, saved_value_rows, out_grad):
    chips, heads = lax.axis_size("chip"), lax.axis_size("head")
    send = functools.partial(moved, chips=chips, heads=heads)
    rows, d, low = key_rows.shape[0], HEAD_SIZE, jnp.bfloat16
    place = jnp.stack(
        [(lax.axis_index("chip") == 0).astype(jnp.int32), lax.axis_index("core"), lax.axis_index("head")]
    ).astype(jnp.int32)
    kv = call(
        functools.partial(pack_kv_kernel, heads),
        shape_of(low, heads, rows, 4 * d),
        (place, key_rows, saved_value_rows),
    )
    kv = swapped_heads(kv, rows)
    other = kv[:, 2 * d :]
    sibling = send(other, chip_step=0, flip=1, head_step=0)
    near = send(kv[:, : 2 * d], chip_step=1, flip=0, head_step=0)
    far = send(other, chip_step=1, flip=1, head_step=0)
    blocks = call(
        functools.partial(pack_qd_kernel, heads),
        (shape_of(low, rows, 4 * d),) * (2 * heads),
        (place, query_rows, out_grad),
    )
    blocks = [blocks[0]] + [
        send(blocks[n], chip_step=0, flip=n % 2, head_step=n // 2) for n in range(1, 2 * heads)
    ]
    dqs, (own_mine, own_other, prev_mine, prev_other) = attention_backward(
        heads, place, kv, sibling, near, far, blocks
    )
    near_back = send(prev_mine, chip_step=-1, flip=0, head_step=0)
    far_back = send(prev_other, chip_step=-1, flip=1, head_step=0)
    sibling_back = send(own_other, chip_step=0, flip=1, head_step=0)
    dqs = [dqs[0]] + [send(dqs[n], chip_step=0, flip=n % 2, head_step=n // 2) for n in range(1, 2 * heads)]
    query_grad = call(
        functools.partial(unpack_dq_kernel, heads),
        shape_of(low, *query_rows.shape),
        (place,) + tuple(dqs),
    )
    total = call(
        add_kernel,
        shape_of(low, heads * rows, 4 * d),
        (place, own_mine, near_back, sibling_back, far_back),
    )
    total = swapped_heads(total, rows).reshape(heads, rows, 4 * d)
    key_grad, value_grad = call(
        functools.partial(unpack_kv_kernel, heads),
        (shape_of(low, *key_rows.shape),) * 2,
        (place, total),
    )
    return query_grad, key_grad, value_grad


def solution(mesh):
    heads = mesh.shape["head"]
    devices = mesh.devices.reshape(-1, 2, heads)
    fine_mesh = Mesh(devices, ("chip", "core", "head"))
    rows = P(("chip", "core", "head"), None)
    return jax.shard_map(
        on_device,
        mesh=fine_mesh,
        in_specs=(rows,) * 4,
        out_specs=(rows,) * 3,
        check_vma=False,
    )
```

time: 107 us -> 111 us (1.037)
  the two profiles are of different devices: /device:TPU:0 before, /device:TPU:13 now
where the time goes in v2:
time: 111 us; the launch traced here: 110 us
  starting transfers between devices  54.1 us (49%)
  waiting for transfers between devices  35.8 us (32%)
  Pallas kernels  16.8 us (15%)
  local copies, waits for them, and re-layouts  1.94 us (2%)
    ppermute x20, starting transfers between devices, moved(): return lax.ppermute(value, ('chip', 'core', 'head'), pairs)  42.6 us
    ppermute x20, waiting for transfers between devices, moved(): return lax.ppermute(value, ('chip', 'core', 'head'), pairs)  32.6 us
    pallas_call x6, Pallas kernels, call(): pl.pallas_call(kernel, out_shape=out_shape, in_specs=[SMEM_SPEC] + [VMEM_...  16.8 us
    all_to_all x2, starting transfers between devices, swapped_heads(): lax.all_to_all(value.reshape(-1, value.shape[-1]), 'head', split_axis=0,...  11.5 us
    all_to_all x2, waiting for transfers between devices, swapped_heads(): lax.all_to_all(value.reshape(-1, value.shape[-1]), 'head', split_axis=0,...  3.17 us
  transfers between devices with their start and end apart: 22, of which 11 were waited for; matrix products, arithmetic and copies ran while one was open for 0% of the time, Pallas kernels for 2%

profile of v2, /device:TPU:13, one launch (start us, length us, event | category | flops | bytes accessed | tf_op | source)
XLA Modules:
  0.0 109.6 jit_solution(7502828347956899531)
XLA Ops:
  0.6 0.1 pad_add_fusion.place_ref
  0.7 0.0 copy-start.2
  0.7 0.9 copy-done.2
  1.7 0.0 copy-start.3
  1.7 0.9 copy-done.3
  2.6 1.5 %shard_map.67 = bf16[4,128,512]{2,1,0:T(8,128)(2,1)} custom-call(s32[3]{0:T(128)S(1)} %pad_add_fusion.place_ref, bf16[128,1024]{1,0:T(8,128)(2,1)S(1)} %copy-done.2, bf16[128,1024]{1,0:T(8,128)(2,1)S(1)} %copy-done.3), custom_call_target="tpu_custom_call" | custom-call | bytes 1048588 | tf_op jit(solution)/shard_map/pallas_call | solution.py:25
  4.1 0.0 copy-start
  4.1 0.0 copy-start.1
  4.1 4.9 %all-to-all-start = ((bf16[4,128,512]{2,1,0:T(8,128)(2,1)}), bf16[4,128,512]{2,1,0:T(8,128)(2,1)S(1)}, u32[]{:S(2)}, u32[]{:S(2)}) async-start(bf16[4,128,512]{2,1,0:T(8,128)(2,1)} %shard_map.67), calls=%async_computation | async-start | bytes 1048576 | tf_op jit(solution)/shard_map/all_to_all | solution.py:226
  9.0 0.0 copy-done
  9.0 0.0 copy-done.1
  9.0 0.7 shard_map.68
  9.7 1.3 %collective-permute-start.3 = (bf16[128,512]{1,0:T(8,128)(2,1)S(1)}, bf16[128,512]{1,0:T(8,128)(2,1)S(1)}, u32[]{:S(2)}, u32[]{:S(2)}) collective-permute-start(bf16[128,512]{1,0:T(8,128)(2,1)S(1)} %get-tuple-element.26), channel_id=1, source_target_pairs={{0,4},{1,5},{2,6},{3,7},{4,0},{5,1},{6,2},{7,3},{8,12},{9,13},{10,... | collective-permute-start | bytes 393224 | tf_op jit(solution)/shard_map/ppermute | solution.py:222
  11.0 1.2 %collective-permute-start.4 = (bf16[128,512]{1,0:T(8,128)(2,1)S(1)}, bf16[128,512]{1,0:T(8,128)(2,1)S(1)}, u32[]{:S(2)}, u32[]{:S(2)}) collective-permute-start(bf16[128,512]{1,0:T(8,128)(2,1)S(1)} %get-tuple-element.27), channel_id=1, source_target_pairs={{0,1},{1,2},{2,3},{3,0},{4,5},{5,6},{6,7},{7,4},{8,9},{9,10},{10,1... | collective-permute-start | bytes 393224 | tf_op jit(solution)/shard_map/ppermute | solution.py:222
  12.2 1.4 %collective-permute-start.5 = (bf16[128,512]{1,0:T(8,128)(2,1)S(1)}, bf16[128,512]{1,0:T(8,128)(2,1)S(1)}, u32[]{:S(2)}, u32[]{:S(2)}) collective-permute-start(bf16[128,512]{1,0:T(8,128)(2,1)S(1)} %get-tuple-element.28), channel_id=1, source_target_pairs={{0,5},{1,6},{2,7},{3,4},{4,1},{5,2},{6,3},{7,0},{8,13},{9,14},{10,... | collective-permute-start | bytes 393224 | tf_op jit(solution)/shard_map/ppermute | solution.py:222
  13.6 1.2 %collective-permute-start.6 = (bf16[128,512]{1,0:T(8,128)(2,1)S(1)}, bf16[128,512]{1,0:T(8,128)(2,1)S(1)}, u32[]{:S(2)}, u32[]{:S(2)}) collective-permute-start(bf16[128,512]{1,0:T(8,128)(2,1)S(1)} %get-tuple-element.29), channel_id=1, source_target_pairs={{0,2},{1,3},{2,0},{3,1},{4,6},{5,7},{6,4},{7,5},{8,10},{9,11},{10,... | collective-permute-start | bytes 393224 | tf_op jit(solution)/shard_map/ppermute | solution.py:222
  14.8 1.5 %collective-permute-start.7 = (bf16[128,512]{1,0:T(8,128)(2,1)S(1)}, bf16[128,512]{1,0:T(8,128)(2,1)S(1)}, u32[]{:S(2)}, u32[]{:S(2)}) collective-permute-start(bf16[128,512]{1,0:T(8,128)(2,1)S(1)} %get-tuple-element.30), channel_id=1, source_target_pairs={{0,6},{1,7},{2,4},{3,5},{4,2},{5,3},{6,0},{7,1},{8,14},{9,15},{10,... | collective-permute-start | bytes 393224 | tf_op jit(solution)/shard_map/ppermute | solution.py:222
  16.3 3.2 %all-to-all-done = bf16[4,128,512]{2,1,0:T(8,128)(2,1)S(1)} async-done(((bf16[4,128,512]{2,1,0:T(8,128)(2,1)}), bf16[4,128,512]{2,1,0:T(8,128)(2,1)S(1)}, u32[]{:S(2)}, u32[]{:S(2)}) %all-to-all-start) | async-done | bytes 524320 | tf_op jit(solution)/shard_map/all_to_all | solution.py:226
  19.5 0.0 collective-permute-done.3.refs_1_
  19.5 3.1 %collective-permute-start.1 = (bf16[512,256]{1,0:T(8,128)(2,1)S(1)}, bf16[512,256]{1,0:T(8,128)(2,1)S(1)}, u32[]{:S(2)}, u32[]{:S(2)}) collective-permute-start(bf16[512,256]{1,0:T(8,128)(2,1)S(1)} %get-tuple-element.47), channel_id=1, source_target_pairs={{0,8},{1,9},{2,10},{3,11},{4,12},{5,13},{6,14},{7,15},{8,16},{9,17... | collective-permute-start | bytes 786440 | tf_op jit(solution)/shard_map/ppermute | solution.py:222
  22.6 0.0 collective-permute-done.4.refs_2_
  22.6 14.5 %collective-permute-start.2 = (bf16[512,256]{1,0:T(8,128)(2,1)S(1)}, bf16[512,256]{1,0:T(8,128)(2,1)S(1)}, u32[]{:S(2)}, u32[]{:S(2)}) collective-permute-start(bf16[512,256]{1,0:T(8,128)(2,1)S(1)} %get-tuple-element.48), channel_id=1, source_target_pairs={{0,12},{1,13},{2,14},{3,15},{4,8},{5,9},{6,10},{7,11},{8,20},{9,21... | collective-permute-start | bytes 786440 | tf_op jit(solution)/shard_map/ppermute | solution.py:222
  37.1 0.0 collective-permute-done.5.refs_3_
  37.1 1.1 collective-permute-start
  38.2 0.0 collective-permute-done.6.refs_4_
  38.2 4.0 %collective-permute-start.8 = (bf16[128,512]{1,0:T(8,128)(2,1)S(1)}, bf16[128,512]{1,0:T(8,128)(2,1)S(1)}, u32[]{:S(2)}, u32[]{:S(2)}) collective-permute-start(bf16[128,512]{1,0:T(8,128)(2,1)S(1)} %get-tuple-element.31), channel_id=1, source_target_pairs={{0,3},{1,0},{2,1},{3,2},{4,7},{5,4},{6,5},{7,6},{8,11},{9,8},{10,9... | collective-permute-start | bytes 393224 | tf_op jit(solution)/shard_map/ppermute | solution.py:222
  42.2 0.0 collective-permute-done.7.refs_5_
  42.2 0.0 collective-permute-start.9
  42.2 2.8 %collective-permute-done.8.refs_6_ = bf16[128,512]{1,0:T(8,128)(2,1)S(1)} collective-permute-done((bf16[128,512]{1,0:T(8,128)(2,1)S(1)}, bf16[128,512]{1,0:T(8,128)(2,1)S(1)}, u32[]{:S(2)}, u32[]{:S(2)}) %collective-permute-start.8) | collective-permute-done | bytes 131104 | tf_op jit(solution)/shard_map/ppermute | solution.py:222
  45.0 2.8 %collective-permute-done.9.refs_7_ = bf16[128,512]{1,0:T(8,128)(2,1)S(1)} collective-permute-done((bf16[128,512]{1,0:T(8,128)(2,1)S(1)}, bf16[128,512]{1,0:T(8,128)(2,1)S(1)}, u32[]{:S(2)}, u32[]{:S(2)}) %collective-permute-start.9) | collective-permute-done | bytes 131104 | tf_op jit(solution)/shard_map/ppermute | solution.py:222
  47.8 0.0 collective-permute-done.1.near_ref
  47.8 0.0 collective-permute-done.2.far_ref
  47.9 0.0 collective-permute-done.sibling_ref
  47.9 10.4 %shard_map.69 = (bf16[128,256]{1,0:T(8,128)(2,1)S(1)}, bf16[128,256]{1,0:T(8,128)(2,1)S(1)}, bf16[128,256]{1,0:T(8,128)(2,1)S(1)}, bf16[128,256]{1,0:T(8,128)(2,...) custom-call(s32[3]{0:T(128)S(1)} %pad_add_fusion.place_ref, ...), custom_call_target="tpu_custom_call" | custom-call | flops 2684354560 | bytes 4194316 | tf_op jit(solution)/shard_map/pallas_call | solution.py:25
  58.2 4.6 %collective-permute-start.17 = (bf16[512,256]{1,0:T(8,128)(2,1)S(1)}, bf16[512,256]{1,0:T(8,128)(2,1)S(1)}, u32[]{:S(2)}, u32[]{:S(2)}) collective-permute-start(bf16[512,256]{1,0:T(8,128)(2,1)S(1)} %get-tuple-element.42), channel_id=1, source_target_pairs={{8,0},{9,1},{10,2},{11,3},{12,4},{13,5},{14,6},{15,7},{16,8},{17,9... | collective-permute-start | bytes 786440 | tf_op jit(solution)/shard_map/ppermute | solution.py:222
  62.9 0.8 collective-permute-start.18
  63.7 2.1 %collective-permute-start.19 = (bf16[512,256]{1,0:T(8,128)(2,1)S(1)}, bf16[512,256]{1,0:T(8,128)(2,1)S(1)}, u32[]{:S(2)}, u32[]{:S(2)}) collective-permute-start(bf16[512,256]{1,0:T(8,128)(2,1)S(1)} %get-tuple-element.44), channel_id=1, source_target_pairs={{8,4},{9,5},{10,6},{11,7},{12,0},{13,1},{14,2},{15,3},{16,12},{17,... | collective-permute-start | bytes 786440 | tf_op jit(solution)/shard_map/ppermute | solution.py:222
  65.7 2.3 %collective-permute-done.17.near_ref = bf16[512,256]{1,0:T(8,128)(2,1)S(1)} collective-permute-done((bf16[512,256]{1,0:T(8,128)(2,1)S(1)}, bf16[512,256]{1,0:T(8,128)(2,1)S(1)}, u32[]{:S(2)}, u32[]{:S(2)}) %collective-permute-start.17) | collective-permute-done | bytes 262176 | tf_op jit(solution)/shard_map/ppermute | solution.py:222
  68.0 0.0 collective-permute-done.18.sibling_ref
  68.1 5.7 %collective-permute-done.19.far_ref = bf16[512,256]{1,0:T(8,128)(2,1)S(1)} collective-permute-done((bf16[512,256]{1,0:T(8,128)(2,1)S(1)}, bf16[512,256]{1,0:T(8,128)(2,1)S(1)}, u32[]{:S(2)}, u32[]{:S(2)}) %collective-permute-start.19) | collective-permute-done | bytes 262176 | tf_op jit(solution)/shard_map/ppermute | solution.py:222
  73.8 1.5 %shard_map.71 = bf16[512,512]{1,0:T(8,128)(2,1)} custom-call(s32[3]{0:T(128)S(1)} %pad_add_fusion.place_ref, f32[512,256]{1,0:T(8,128)S(1)} %get-tuple-element.41.own_ref, bf16[512,256]{1,0:T(8,128)(2,1)S(1)} %collective-permute-done.17.near_ref, bf16[512,256]{1,0:T(8,128)(2,1)S(1)} %collective-permute-done.18.sibling_ref, ...), custom_call_target="tpu_custom_call" | custom-call | bytes 1835020 | tf_op jit(solution)/shard_map/pallas_call | solution.py:25
  75.2 6.6 %all-to-all-start.1 = ((bf16[4,128,512]{2,1,0:T(8,128)(2,1)}), bf16[4,128,512]{2,1,0:T(8,128)(2,1)S(1)}, u32[]{:S(2)}, u32[]{:S(2)}) async-start(bf16[4,128,512]{2,1,0:T(8,128)(2,1)} %bitcast.4), calls=%async_computation.1 | async-start | bytes 1048576 | tf_op jit(solution)/shard_map/all_to_all | solution.py:226
  81.8 0.3 collective-permute-start.10
  82.1 1.2 %collective-permute-start.11 = (bf16[128,256]{1,0:T(8,128)(2,1)S(1)}, bf16[128,256]{1,0:T(8,128)(2,1)S(1)}, u32[]{:S(2)}, u32[]{:S(2)}) collective-permute-start(bf16[128,256]{1,0:T(8,128)(2,1)S(1)} %get-tuple-element.35), channel_id=1, source_target_pairs={{0,1},{1,2},{2,3},{3,0},{4,5},{5,6},{6,7},{7,4},{8,9},{9,10},{10,1... | collective-permute-start | bytes 196616 | tf_op jit(solution)/shard_map/ppermute | solution.py:222
  83.3 1.6 %collective-permute-start.12 = (bf16[128,256]{1,0:T(8,128)(2,1)S(1)}, bf16[128,256]{1,0:T(8,128)(2,1)S(1)}, u32[]{:S(2)}, u32[]{:S(2)}) collective-permute-start(bf16[128,256]{1,0:T(8,128)(2,1)S(1)} %get-tuple-element.36), channel_id=1, source_target_pairs={{0,5},{1,6},{2,7},{3,4},{4,1},{5,2},{6,3},{7,0},{8,13},{9,14},{10,... | collective-permute-start | bytes 196616 | tf_op jit(solution)/shard_map/ppermute | solution.py:222
  84.9 1.2 %collective-permute-start.13 = (bf16[128,256]{1,0:T(8,128)(2,1)S(1)}, bf16[128,256]{1,0:T(8,128)(2,1)S(1)}, u32[]{:S(2)}, u32[]{:S(2)}) collective-permute-start(bf16[128,256]{1,0:T(8,128)(2,1)S(1)} %get-tuple-element.37), channel_id=1, source_target_pairs={{0,2},{1,3},{2,0},{3,1},{4,6},{5,7},{6,4},{7,5},{8,10},{9,11},{10,... | collective-permute-start | bytes 196616 | tf_op jit(solution)/shard_map/ppermute | solution.py:222
  86.1 1.3 %collective-permute-start.14 = (bf16[128,256]{1,0:T(8,128)(2,1)S(1)}, bf16[128,256]{1,0:T(8,128)(2,1)S(1)}, u32[]{:S(2)}, u32[]{:S(2)}) collective-permute-start(bf16[128,256]{1,0:T(8,128)(2,1)S(1)} %get-tuple-element.38), channel_id=1, source_target_pairs={{0,6},{1,7},{2,4},{3,5},{4,2},{5,3},{6,0},{7,1},{8,14},{9,15},{10,... | collective-permute-start | bytes 196616 | tf_op jit(solution)/shard_map/ppermute | solution.py:222
  87.4 0.0 collective-permute-done.10.refs_1_
  87.4 0.3 collective-permute-start.15
  87.7 12.7 %collective-permute-done.11.refs_2_ = bf16[128,256]{1,0:T(8,128)(2,1)S(1)} collective-permute-done((bf16[128,256]{1,0:T(8,128)(2,1)S(1)}, bf16[128,256]{1,0:T(8,128)(2,1)S(1)}, u32[]{:S(2)}, u32[]{:S(2)}) %collective-permute-start.11) | collective-permute-done | bytes 65568 | tf_op jit(solution)/shard_map/ppermute | solution.py:222
  100.4 0.0 collective-permute-start.16
  100.4 1.4 %collective-permute-done.12.refs_3_ = bf16[128,256]{1,0:T(8,128)(2,1)S(1)} collective-permute-done((bf16[128,256]{1,0:T(8,128)(2,1)S(1)}, bf16[128,256]{1,0:T(8,128)(2,1)S(1)}, u32[]{:S(2)}, u32[]{:S(2)}) %collective-permute-start.12) | collective-permute-done | bytes 65568 | tf_op jit(solution)/shard_map/ppermute | solution.py:222
  101.8 1.4 %collective-permute-done.13.refs_4_ = bf16[128,256]{1,0:T(8,128)(2,1)S(1)} collective-permute-done((bf16[128,256]{1,0:T(8,128)(2,1)S(1)}, bf16[128,256]{1,0:T(8,128)(2,1)S(1)}, u32[]{:S(2)}, u32[]{:S(2)}) %collective-permute-start.13) | collective-permute-done | bytes 65568 | tf_op jit(solution)/shard_map/ppermute | solution.py:222
  103.2 1.4 %collective-permute-done.14.refs_5_ = bf16[128,256]{1,0:T(8,128)(2,1)S(1)} collective-permute-done((bf16[128,256]{1,0:T(8,128)(2,1)S(1)}, bf16[128,256]{1,0:T(8,128)(2,1)S(1)}, u32[]{:S(2)}, u32[]{:S(2)}) %collective-permute-start.14) | collective-permute-done | bytes 65568 | tf_op jit(solution)/shard_map/ppermute | solution.py:222
  104.6 0.5 collective-permute-done.15.refs_6_
  105.2 1.5 %collective-permute-done.16.refs_7_ = bf16[128,256]{1,0:T(8,128)(2,1)S(1)} collective-permute-done((bf16[128,256]{1,0:T(8,128)(2,1)S(1)}, bf16[128,256]{1,0:T(8,128)(2,1)S(1)}, u32[]{:S(2)}, u32[]{:S(2)}) %collective-permute-start.16) | collective-permute-done | bytes 65568 | tf_op jit(solution)/shard_map/ppermute | solution.py:222
  106.7 1.4 %shard_map.70 = bf16[128,2048]{1,0:T(8,128)(2,1)} custom-call(s32[3]{0:T(128)S(1)} %pad_add_fusion.place_ref, bf16[128,256]{1,0:T(8,128)(2,1)S(1)} %get-tuple-element.33.refs_0_, bf16[128,256]{1,0:T(8,128)(2,1)S(1)} %collective-permute-done.10.refs_1_, bf16[128,256]{1,0:T(8,128)(2,1)S(1)} %collective-permute-done.11.refs_2_, ...), custom_call_target="tpu_custom_call" | custom-call | bytes 1048588 | tf_op jit(solution)/shard_map/pallas_call | solution.py:25
  108.1 0.0 all-to-all-done.1.in_ref
  108.1 1.5 %shard_map.72 = (bf16[128,1024]{1,0:T(8,128)(2,1)}, bf16[128,1024]{1,0:T(8,128)(2,1)}) custom-call(s32[3]{0:T(128)S(1)} %pad_add_fusion.place_ref, bf16[4,128,512]{2,1,0:T(8,128)(2,1)S(1)} %all-to-all-done.1.in_ref), custom_call_target="tpu_custom_call" | custom-call | bytes 1048588 | tf_op jit(solution)/shard_map/pallas_call | solution.py:25
  (1 shorter events, 0.0 us)
Async XLA Ops:
  0.7 1.0 copy-start.2
  1.7 0.9 copy-start.3
  4.1 4.9 %copy-start = (bf16[128,2048]{1,0:T(8,128)(2,1)S(1)}, bf16[128,2048]{1,0:T(8,128)(2,1)}, u32[]{:S(2)}) copy-start(bf16[128,2048]{1,0:T(8,128)(2,1)} %q_ref.1) | copy-start | bytes 1572868
  4.1 4.9 %copy-start.1 = (bf16[128,2048]{1,0:T(8,128)(2,1)S(1)}, bf16[128,2048]{1,0:T(8,128)(2,1)}, u32[]{:S(2)}) copy-start(bf16[128,2048]{1,0:T(8,128)(2,1)} %g_ref.1) | copy-start | bytes 1572868
  4.1 15.4 %all-to-all-start = ((bf16[4,128,512]{2,1,0:T(8,128)(2,1)}), bf16[4,128,512]{2,1,0:T(8,128)(2,1)S(1)}, u32[]{:S(2)}, u32[]{:S(2)}) async-start(bf16[4,128,512]{2,1,0:T(8,128)(2,1)} %shard_map.67), calls=%async_computation | async-start | bytes 1048576 | tf_op jit(solution)/shard_map/all_to_all | solution.py:226
  9.7 9.8 %collective-permute-start.3 = (bf16[128,512]{1,0:T(8,128)(2,1)S(1)}, bf16[128,512]{1,0:T(8,128)(2,1)S(1)}, u32[]{:S(2)}, u32[]{:S(2)}) collective-permute-start(bf16[128,512]{1,0:T(8,128)(2,1)S(1)} %get-tuple-element.26), channel_id=1, source_target_pairs={{0,4},{1,5},{2,6},{3,7},{4,0},{5,1},{6,2},{7,3},{8,12},{9,13},{10,... | collective-permute-start | bytes 393224 | tf_op jit(solution)/shard_map/ppermute | solution.py:222
  11.0 11.6 %collective-permute-start.4 = (bf16[128,512]{1,0:T(8,128)(2,1)S(1)}, bf16[128,512]{1,0:T(8,128)(2,1)S(1)}, u32[]{:S(2)}, u32[]{:S(2)}) collective-permute-start(bf16[128,512]{1,0:T(8,128)(2,1)S(1)} %get-tuple-element.27), channel_id=1, source_target_pairs={{0,1},{1,2},{2,3},{3,0},{4,5},{5,6},{6,7},{7,4},{8,9},{9,10},{10,1... | collective-permute-start | bytes 393224 | tf_op jit(solution)/shard_map/ppermute | solution.py:222
  12.2 24.9 %collective-permute-start.5 = (bf16[128,512]{1,0:T(8,128)(2,1)S(1)}, bf16[128,512]{1,0:T(8,128)(2,1)S(1)}, u32[]{:S(2)}, u32[]{:S(2)}) collective-permute-start(bf16[128,512]{1,0:T(8,128)(2,1)S(1)} %get-tuple-element.28), channel_id=1, source_target_pairs={{0,5},{1,6},{2,7},{3,4},{4,1},{5,2},{6,3},{7,0},{8,13},{9,14},{10,... | collective-permute-start | bytes 393224 | tf_op jit(solution)/shard_map/ppermute | solution.py:222
  13.6 24.6 %collective-permute-start.6 = (bf16[128,512]{1,0:T(8,128)(2,1)S(1)}, bf16[128,512]{1,0:T(8,128)(2,1)S(1)}, u32[]{:S(2)}, u32[]{:S(2)}) collective-permute-start(bf16[128,512]{1,0:T(8,128)(2,1)S(1)} %get-tuple-element.29), channel_id=1, source_target_pairs={{0,2},{1,3},{2,0},{3,1},{4,6},{5,7},{6,4},{7,5},{8,10},{9,11},{10,... | collective-permute-start | bytes 393224 | tf_op jit(solution)/shard_map/ppermute | solution.py:222
  14.8 27.4 %collective-permute-start.7 = (bf16[128,512]{1,0:T(8,128)(2,1)S(1)}, bf16[128,512]{1,0:T(8,128)(2,1)S(1)}, u32[]{:S(2)}, u32[]{:S(2)}) collective-permute-start(bf16[128,512]{1,0:T(8,128)(2,1)S(1)} %get-tuple-element.30), channel_id=1, source_target_pairs={{0,6},{1,7},{2,4},{3,5},{4,2},{5,3},{6,0},{7,1},{8,14},{9,15},{10,... | collective-permute-start | bytes 393224 | tf_op jit(solution)/shard_map/ppermute | solution.py:222
  19.5 28.4 %collective-permute-start.1 = (bf16[512,256]{1,0:T(8,128)(2,1)S(1)}, bf16[512,256]{1,0:T(8,128)(2,1)S(1)}, u32[]{:S(2)}, u32[]{:S(2)}) collective-permute-start(bf16[512,256]{1,0:T(8,128)(2,1)S(1)} %get-tuple-element.47), channel_id=1, source_target_pairs={{0,8},{1,9},{2,10},{3,11},{4,12},{5,13},{6,14},{7,15},{8,16},{9,17... | collective-permute-start | bytes 786440 | tf_op jit(solution)/shard_map/ppermute | solution.py:222
  22.6 25.2 %collective-permute-start.2 = (bf16[512,256]{1,0:T(8,128)(2,1)S(1)}, bf16[512,256]{1,0:T(8,128)(2,1)S(1)}, u32[]{:S(2)}, u32[]{:S(2)}) collective-permute-start(bf16[512,256]{1,0:T(8,128)(2,1)S(1)} %get-tuple-element.48), channel_id=1, source_target_pairs={{0,12},{1,13},{2,14},{3,15},{4,8},{5,9},{6,10},{7,11},{8,20},{9,21... | collective-permute-start | bytes 786440 | tf_op jit(solution)/shard_map/ppermute | solution.py:222
  37.1 10.7 %collective-permute-start = (bf16[512,256]{1,0:T(8,128)(2,1)S(1)}, bf16[512,256]{1,0:T(8,128)(2,1)S(1)}, u32[]{:S(2)}, u32[]{:S(2)}) collective-permute-start(bf16[512,256]{1,0:T(8,128)(2,1)S(1)} %get-tuple-element.48), channel_id=1, source_target_pairs={{0,4},{1,5},{2,6},{3,7},{4,0},{5,1},{6,2},{7,3},{8,12},{9,13},{10,... | collective-permute-start | bytes 786440 | tf_op jit(solution)/shard_map/ppermute | solution.py:222
  38.2 6.8 %collective-permute-start.8 = (bf16[128,512]{1,0:T(8,128)(2,1)S(1)}, bf16[128,512]{1,0:T(8,128)(2,1)S(1)}, u32[]{:S(2)}, u32[]{:S(2)}) collective-permute-start(bf16[128,512]{1,0:T(8,128)(2,1)S(1)} %get-tuple-element.31), channel_id=1, source_target_pairs={{0,3},{1,0},{2,1},{3,2},{4,7},{5,4},{6,5},{7,6},{8,11},{9,8},{10,9... | collective-permute-start | bytes 393224 | tf_op jit(solution)/shard_map/ppermute | solution.py:222
  42.2 5.7 %collective-permute-start.9 = (bf16[128,512]{1,0:T(8,128)(2,1)S(1)}, bf16[128,512]{1,0:T(8,128)(2,1)S(1)}, u32[]{:S(2)}, u32[]{:S(2)}) collective-permute-start(bf16[128,512]{1,0:T(8,128)(2,1)S(1)} %get-tuple-element.32), channel_id=1, source_target_pairs={{0,7},{1,4},{2,5},{3,6},{4,3},{5,0},{6,1},{7,2},{8,15},{9,12},{10,... | collective-permute-start | bytes 393224 | tf_op jit(solution)/shard_map/ppermute | solution.py:222
  58.2 9.8 %collective-permute-start.17 = (bf16[512,256]{1,0:T(8,128)(2,1)S(1)}, bf16[512,256]{1,0:T(8,128)(2,1)S(1)}, u32[]{:S(2)}, u32[]{:S(2)}) collective-permute-start(bf16[512,256]{1,0:T(8,128)(2,1)S(1)} %get-tuple-element.42), channel_id=1, source_target_pairs={{8,0},{9,1},{10,2},{11,3},{12,4},{13,5},{14,6},{15,7},{16,8},{17,9... | collective-permute-start | bytes 786440 | tf_op jit(solution)/shard_map/ppermute | solution.py:222
  62.9 5.2 %collective-permute-start.18 = (bf16[512,256]{1,0:T(8,128)(2,1)S(1)}, bf16[512,256]{1,0:T(8,128)(2,1)S(1)}, u32[]{:S(2)}, u32[]{:S(2)}) collective-permute-start(bf16[512,256]{1,0:T(8,128)(2,1)S(1)} %get-tuple-element.43), channel_id=1, source_target_pairs={{0,4},{1,5},{2,6},{3,7},{4,0},{5,1},{6,2},{7,3},{8,12},{9,13},{10,... | collective-permute-start | bytes 786440 | tf_op jit(solution)/shard_map/ppermute | solution.py:222
  63.7 10.1 %collective-permute-start.19 = (bf16[512,256]{1,0:T(8,128)(2,1)S(1)}, bf16[512,256]{1,0:T(8,128)(2,1)S(1)}, u32[]{:S(2)}, u32[]{:S(2)}) collective-permute-start(bf16[512,256]{1,0:T(8,128)(2,1)S(1)} %get-tuple-element.44), channel_id=1, source_target_pairs={{8,4},{9,5},{10,6},{11,7},{12,0},{13,1},{14,2},{15,3},{16,12},{17,... | collective-permute-start | bytes 786440 | tf_op jit(solution)/shard_map/ppermute | solution.py:222
  75.2 32.9 %all-to-all-start.1 = ((bf16[4,128,512]{2,1,0:T(8,128)(2,1)}), bf16[4,128,512]{2,1,0:T(8,128)(2,1)S(1)}, u32[]{:S(2)}, u32[]{:S(2)}) async-start(bf16[4,128,512]{2,1,0:T(8,128)(2,1)} %bitcast.4), calls=%async_computation.1 | async-start | bytes 1048576 | tf_op jit(solution)/shard_map/all_to_all | solution.py:226
  81.8 5.6 %collective-permute-start.10 = (bf16[128,256]{1,0:T(8,128)(2,1)S(1)}, bf16[128,256]{1,0:T(8,128)(2,1)S(1)}, u32[]{:S(2)}, u32[]{:S(2)}) collective-permute-start(bf16[128,256]{1,0:T(8,128)(2,1)S(1)} %get-tuple-element.34), channel_id=1, source_target_pairs={{0,4},{1,5},{2,6},{3,7},{4,0},{5,1},{6,2},{7,3},{8,12},{9,13},{10,... | collective-permute-start | bytes 196616 | tf_op jit(solution)/shard_map/ppermute | solution.py:222
  82.1 18.3 %collective-permute-start.11 = (bf16[128,256]{1,0:T(8,128)(2,1)S(1)}, bf16[128,256]{1,0:T(8,128)(2,1)S(1)}, u32[]{:S(2)}, u32[]{:S(2)}) collective-permute-start(bf16[128,256]{1,0:T(8,128)(2,1)S(1)} %get-tuple-element.35), channel_id=1, source_target_pairs={{0,1},{1,2},{2,3},{3,0},{4,5},{5,6},{6,7},{7,4},{8,9},{9,10},{10,1... | collective-permute-start | bytes 196616 | tf_op jit(solution)/shard_map/ppermute | solution.py:222
  83.3 18.5 %collective-permute-start.12 = (bf16[128,256]{1,0:T(8,128)(2,1)S(1)}, bf16[128,256]{1,0:T(8,128)(2,1)S(1)}, u32[]{:S(2)}, u32[]{:S(2)}) collective-permute-start(bf16[128,256]{1,0:T(8,128)(2,1)S(1)} %get-tuple-element.36), channel_id=1, source_target_pairs={{0,5},{1,6},{2,7},{3,4},{4,1},{5,2},{6,3},{7,0},{8,13},{9,14},{10,... | collective-permute-start | bytes 196616 | tf_op jit(solution)/shard_map/ppermute | solution.py:222
  84.9 18.4 %collective-permute-start.13 = (bf16[128,256]{1,0:T(8,128)(2,1)S(1)}, bf16[128,256]{1,0:T(8,128)(2,1)S(1)}, u32[]{:S(2)}, u32[]{:S(2)}) collective-permute-start(bf16[128,256]{1,0:T(8,128)(2,1)S(1)} %get-tuple-element.37), channel_id=1, source_target_pairs={{0,2},{1,3},{2,0},{3,1},{4,6},{5,7},{6,4},{7,5},{8,10},{9,11},{10,... | collective-permute-start | bytes 196616 | tf_op jit(solution)/shard_map/ppermute | solution.py:222
  86.1 18.6 %collective-permute-start.14 = (bf16[128,256]{1,0:T(8,128)(2,1)S(1)}, bf16[128,256]{1,0:T(8,128)(2,1)S(1)}, u32[]{:S(2)}, u32[]{:S(2)}) collective-permute-start(bf16[128,256]{1,0:T(8,128)(2,1)S(1)} %get-tuple-element.38), channel_id=1, source_target_pairs={{0,6},{1,7},{2,4},{3,5},{4,2},{5,3},{6,0},{7,1},{8,14},{9,15},{10,... | collective-permute-start | bytes 196616 | tf_op jit(solution)/shard_map/ppermute | solution.py:222
  87.4 17.8 %collective-permute-start.15 = (bf16[128,256]{1,0:T(8,128)(2,1)S(1)}, bf16[128,256]{1,0:T(8,128)(2,1)S(1)}, u32[]{:S(2)}, u32[]{:S(2)}) collective-permute-start(bf16[128,256]{1,0:T(8,128)(2,1)S(1)} %get-tuple-element.39), channel_id=1, source_target_pairs={{0,3},{1,0},{2,1},{3,2},{4,7},{5,4},{6,5},{7,6},{8,11},{9,8},{10,9... | collective-permute-start | bytes 196616 | tf_op jit(solution)/shard_map/ppermute | solution.py:222
  100.4 6.2 %collective-permute-start.16 = (bf16[128,256]{1,0:T(8,128)(2,1)S(1)}, bf16[128,256]{1,0:T(8,128)(2,1)S(1)}, u32[]{:S(2)}, u32[]{:S(2)}) collective-permute-start(bf16[128,256]{1,0:T(8,128)(2,1)S(1)} %get-tuple-element.40), channel_id=1, source_target_pairs={{0,7},{1,4},{2,5},{3,6},{4,3},{5,0},{6,1},{7,2},{8,15},{9,12},{10,... | collective-permute-start | bytes 196616 | tf_op jit(solution)/shard_map/ppermute | solution.py:222

commit v3 on v2

v3 whole, which is shorter than its diff:
```python
import functools

import jax
import jax.numpy as jnp
from jax import lax
from jax.experimental import pallas as pl
from jax.experimental.pallas import tpu as pltpu
from jax.sharding import Mesh
from jax.sharding import PartitionSpec as P

HEAD_SIZE = 128
BLOCK = 128
LOG2_E = 1.4426950408889634

score_scale = 168.0 ** (-0.5)
masked_value = -1e30
contract_last = (((1,), (1,)), ((), ()))
VMEM_SPEC = pl.BlockSpec(memory_space=pltpu.VMEM)
SMEM_SPEC = pl.BlockSpec(memory_space=pltpu.SMEM)


def call(kernel, out_shape, operands, scratch=(), flops=0, transcendentals=0, vmem=16, spec=VMEM_SPEC):
    outs = out_shape if isinstance(out_shape, tuple) else (out_shape,)
    moved = sum(a.size * a.dtype.itemsize for a in operands + outs)
    return pl.pallas_call(
        kernel,
        out_shape=out_shape,
        in_specs=[SMEM_SPEC] + [spec] * (len(operands) - 1),
        out_specs=jax.tree.map(lambda _: spec, out_shape),
        scratch_shapes=list(scratch),
        compiler_params=pltpu.CompilerParams(vmem_limit_bytes=vmem * 2**20),
        cost_estimate=pl.CostEstimate(flops=flops, bytes_accessed=moved, transcendentals=transcendentals),
    )(*operands)


def copy_call(kernel, copies, out_shape, operands):
    spec = pl.BlockSpec(memory_space=pltpu.HBM)
    return call(kernel, out_shape, operands, (pltpu.SemaphoreType.DMA((copies,)),), spec=spec)


def shape_of(dtype, *shape):
    return jax.ShapeDtypeStruct(shape, dtype)


def at(start, size):
    return pl.ds(pl.multiple_of(start, size), size)


def copied(sems, pairs):
    copies = [pltpu.make_async_copy(src, dst, sems.at[n]) for n, (src, dst) in enumerate(pairs)]
    for copy in copies:
        copy.start()
    for copy in copies:
        copy.wait()


def pack_kv_kernel(heads, place_ref, k_ref, v_ref, out_ref, sems):
    core = place_ref[1]
    d = HEAD_SIZE
    pairs = []
    for z in range(heads):
        for n, g in enumerate((2 * z + core, 2 * z + 1 - core)):
            columns = at(g * d, d)
            pairs.append((k_ref.at[:, columns], out_ref.at[z, :, pl.ds(2 * n * d, d)]))
            pairs.append((v_ref.at[:, columns], out_ref.at[z, :, pl.ds((2 * n + 1) * d, d)]))
    copied(sems, pairs)


def pack_qd_kernel(heads, place_ref, q_ref, g_ref, mine_ref, other_ref, sems):
    core = place_ref[1]
    width = 2 * HEAD_SIZE
    pairs = []
    for ref, c in ((other_ref, 1 - core), (mine_ref, core)):
        for z in range(heads):
            columns = at((2 * z + c) * width, width)
            pairs.append((q_ref.at[:, columns], ref.at[z, :, pl.ds(0, width)]))
            pairs.append((g_ref.at[:, columns], ref.at[z, :, pl.ds(width, width)]))
    copied(sems, pairs)


def merge_rows_kernel(heads, place_ref, mine_ref, other_ref, out_ref):
    core = place_ref[1]
    for z in range(heads):
        out_ref[z, at(core * BLOCK, BLOCK)] = mine_ref[z]
        out_ref[z, at((1 - core) * BLOCK, BLOCK)] = other_ref[z]


def merge_columns_kernel(heads, place_ref, mine_ref, other_ref, out_ref):
    core = place_ref[1]
    width = 2 * HEAD_SIZE
    for z in range(heads):
        out_ref[z, :, at(core * width, width)] = mine_ref[z]
        out_ref[z, :, at((1 - core) * width, width)] = other_ref[z]


def unpack_dq_kernel(heads, place_ref, in_ref, out_ref, sems):
    width = 4 * HEAD_SIZE
    copied(sems, [(in_ref.at[z], out_ref.at[:, pl.ds(z * width, width)]) for z in range(heads)])


def unpack_kv_kernel(heads, place_ref, in_ref, k_ref, v_ref, sems):
    core = place_ref[1]
    d = HEAD_SIZE
    pairs = []
    for z in range(heads):
        for n, g in enumerate((2 * z + core, 2 * z + 1 - core)):
            columns = at(g * d, d)
            pairs.append((in_ref.at[z, :, pl.ds(2 * n * d, d)], k_ref.at[:, columns]))
            pairs.append((in_ref.at[z, :, pl.ds((2 * n + 1) * d, d)], v_ref.at[:, columns]))
    copied(sems, pairs)


def add_kernel(place_ref, own_ref, near_ref, sibling_ref, far_ref, out_ref):
    width = 2 * HEAD_SIZE
    wide = lambda ref: ref[...].astype(jnp.float32)
    out_ref[:, :width] = (own_ref[...] + wide(near_ref)).astype(jnp.bfloat16)
    out_ref[:, width:] = (wide(sibling_ref) + wide(far_ref)).astype(jnp.bfloat16)


def attention_kernel(heads, place_ref, mine_ref, sibling_ref, near_ref, far_ref, blocks_ref, *refs):
    d = HEAD_SIZE
    count = 2 * heads
    dq_mine_ref, dq_other_ref, own_mine_ref, own_other_ref, prev_mine_ref, prev_other_ref = refs[:6]
    qd_ref, own_ref, prev_ref, dq_ref, own_kt_ref, prev_kt_ref, own_grad_ref, prev_grad_ref = refs[6:]
    first, core = place_ref[0], place_ref[1]
    half = heads * BLOCK
    mine, other = at(core * half, half), at((1 - core) * half, half)
    own_ref[mine] = mine_ref[:, : 2 * d]
    own_ref[other] = sibling_ref[...]
    prev_ref[mine] = near_ref[...]
    prev_ref[other] = far_ref[...]
    for c in range(2):
        for z in range(heads):
            start = (c * heads + z) * BLOCK
            qd_ref[start : start + BLOCK] = blocks_ref[z, c * BLOCK : (c + 1) * BLOCK]
    bias = jnp.where(first == 1, masked_value, 0.0).astype(jnp.float32)
    own_kt_ref[...] = own_ref[:, :d].T
    prev_kt_ref[...] = prev_ref[:, :d].T
    key_row = lax.broadcasted_iota(jnp.int32, (BLOCK, 2 * BLOCK), 0)
    query_row = lax.broadcasted_iota(jnp.int32, (BLOCK, 2 * BLOCK), 1) % BLOCK
    own_seen = key_row <= query_row
    zero = jnp.zeros((BLOCK, 2 * BLOCK), jnp.bfloat16)
    dot_t = lambda a, b: lax.dot_general(a, b, contract_last, preferred_element_type=jnp.float32)
    dot = lambda a, b: jnp.dot(a, b, preferred_element_type=jnp.float32)
    for i in range(count):
        low, high = i * BLOCK, (i + 1) * BLOCK
        below, above = i > 0, i < count - 1
        q = jnp.concatenate([qd_ref[low:high, :d], qd_ref[low:high, d : 2 * d]], 0)
        g = jnp.concatenate([qd_ref[low:high, 2 * d : 3 * d], qd_ref[low:high, 3 * d :]], 0)
        s_own = dot_t(own_ref[:high, :d], q)
        s_prev = dot_t(prev_ref[low:, :d], q) + bias
        p_own = dot_t(own_ref[:high, d:], g)
        p_prev = dot_t(prev_ref[low:, d:], g)
        s_diag = jnp.where(own_seen, s_own[low:], s_prev[:BLOCK])
        p_diag = jnp.where(own_seen, p_own[low:], p_prev[:BLOCK])
        s = jnp.concatenate([s_own[:low]] * below + [s_diag] + [s_prev[BLOCK:]] * above, 0)
        dp = jnp.concatenate([p_own[:low]] * below + [p_diag] + [p_prev[BLOCK:]] * above, 0)
        top = jnp.max(s, axis=0, keepdims=True)
        w = jnp.exp2((s - top) * (score_scale * LOG2_E))
        inverse = 1.0 / jnp.sum(w, axis=0, keepdims=True)
        delta = jnp.sum(w * dp, axis=0, keepdims=True) * inverse
        attention = w * inverse
        ds = (attention * (dp - delta)).astype(jnp.bfloat16)
        low_attention = attention.astype(jnp.bfloat16)
        split = lambda x: (
            jnp.concatenate([x[:low]] * below + [jnp.where(own_seen, x[low:high], zero)], 0),
            jnp.concatenate([jnp.where(own_seen, zero, x[low:high])] + [x[high:]] * above, 0),
        )
        ds_own, ds_prev = split(ds)
        at_own, at_prev = split(low_attention)
        dq_t = dot(own_kt_ref[:, :high], ds_own) + dot(prev_kt_ref[:, low:], ds_prev)
        dq_t = dq_t * score_scale
        dq_ref[low:high, :d] = dq_t[:, :BLOCK].T.astype(jnp.bfloat16)
        dq_ref[low:high, d:] = dq_t[:, BLOCK:].T.astype(jnp.bfloat16)
        dk_own, dk_prev = dot(ds_own, q), dot(ds_prev, q)
        dv_own, dv_prev = dot(at_own, g), dot(at_prev, g)
        if below:
            own_grad_ref[:low, :d] += dk_own[:low]
            own_grad_ref[:low, d:] += dv_own[:low]
            prev_grad_ref[low:, :d] += dk_prev
            prev_grad_ref[low:, d:] += dv_prev
        else:
            prev_grad_ref[:, :d] = dk_prev
            prev_grad_ref[:, d:] = dv_prev
        own_grad_ref[low:high, :d] = dk_own[low:]
        own_grad_ref[low:high, d:] = dv_own[low:]
    dq_mine_ref[...] = dq_ref[mine]
    dq_other_ref[...] = dq_ref[other]
    for ref, grad_ref, rows in (
        (own_mine_ref, own_grad_ref, mine),
        (own_other_ref, own_grad_ref, other),
        (prev_mine_ref, prev_grad_ref, mine),
        (prev_other_ref, prev_grad_ref, other),
    ):
        ref[:, :d] = (grad_ref[rows, :d] * score_scale).astype(ref.dtype)
        ref[:, d:] = grad_ref[rows, d:].astype(ref.dtype)


def attention_backward(heads, place, mine, sibling, near, far, blocks):
    half, d = heads * BLOCK, HEAD_SIZE
    whole = 2 * half
    low, wide = jnp.bfloat16, jnp.float32
    part = shape_of(low, half, 2 * d)
    outs = (part, part, shape_of(wide, half, 2 * d), part, part, part)
    scratch = (
        pltpu.VMEM((whole, 4 * d), low),
        pltpu.VMEM((whole, 2 * d), low),
        pltpu.VMEM((whole, 2 * d), low),
        pltpu.VMEM((whole, 2 * d), low),
        pltpu.VMEM((d, whole), low),
        pltpu.VMEM((d, whole), low),
        pltpu.VMEM((whole, 2 * d), wide),
        pltpu.VMEM((whole, 2 * d), wide),
    )
    return call(
        functools.partial(attention_kernel, heads),
        outs,
        (place, mine, sibling, near, far, blocks),
        scratch,
        20 * whole * whole * d,
        2 * whole * whole,
        48,
    )


def moved(value, chips, heads, chip_step, flip, head_step):
    index = lambda chip, core, head: (chip * 2 + core) * heads + head
    pairs = [
        (index(chip, core, head), index(chip + chip_step, core ^ flip, (head + head_step) % heads))
        for chip in range(chips)
        for core in range(2)
        for head in range(heads)
        if 0 <= chip + chip_step < chips
    ]
    return lax.ppermute(value, ("chip", "core", "head"), pairs)


def swapped_heads(value):
    return lax.all_to_all(value, "head", split_axis=0, concat_axis=0, tiled=True)


def on_device(query_rows, key_rows, saved_value_rows, out_grad):
    chips, heads = lax.axis_size("chip"), lax.axis_size("head")
    send = functools.partial(moved, chips=chips, heads=heads, head_step=0)
    rows, d, low = key_rows.shape[0], HEAD_SIZE, jnp.bfloat16
    bind = lambda kernel: functools.partial(kernel, heads)
    place = jnp.stack(
        [(lax.axis_index("chip") == 0).astype(jnp.int32), lax.axis_index("core"), lax.axis_index("head")]
    ).astype(jnp.int32)
    kv = copy_call(
        bind(pack_kv_kernel), 4 * heads, shape_of(low, heads, rows, 4 * d), (place, key_rows, saved_value_rows)
    )
    qd_mine, qd_other = copy_call(
        bind(pack_qd_kernel), 4 * heads, (shape_of(low, heads, rows, 4 * d),) * 2, (place, query_rows, out_grad)
    )
    kv = swapped_heads(kv).reshape(heads * rows, 4 * d)
    qd_other = send(qd_other, chip_step=0, flip=1)
    qd = call(bind(merge_rows_kernel), shape_of(low, heads, 2 * rows, 4 * d), (place, qd_mine, qd_other))
    other = kv[:, 2 * d :]
    near = send(kv[:, : 2 * d], chip_step=1, flip=0)
    far = send(other, chip_step=1, flip=1)
    sibling = send(other, chip_step=0, flip=1)
    blocks = swapped_heads(qd)
    dq_mine, dq_other, own_mine, own_other, prev_mine, prev_other = attention_backward(
        heads, place, kv, sibling, near, far, blocks
    )
    near_back = send(prev_mine, chip_step=-1, flip=0)
    far_back = send(prev_other, chip_step=-1, flip=1)
    sibling_back = send(own_other, chip_step=0, flip=1)
    dq_other = send(dq_other, chip_step=0, flip=1)
    split = lambda x: x.reshape(heads, rows, -1)
    dq = call(
        bind(merge_columns_kernel), shape_of(low, heads, rows, 4 * d), (place, split(dq_mine), split(dq_other))
    )
    query_grad = copy_call(
        bind(unpack_dq_kernel), heads, shape_of(low, *query_rows.shape), (place, swapped_heads(dq))
    )
    total = call(
        add_kernel,
        shape_of(low, heads * rows, 4 * d),
        (place, own_mine, near_back, sibling_back, far_back),
    )
    total = swapped_heads(split(total))
    key_grad, value_grad = copy_call(
        bind(unpack_kv_kernel), 4 * heads, (shape_of(low, *key_rows.shape),) * 2, (place, total)
    )
    return query_grad, key_grad, value_grad


def solution(mesh):
    heads = mesh.shape["head"]
    devices = mesh.devices.reshape(-1, 2, heads)
    fine_mesh = Mesh(devices, ("chip", "core", "head"))
    rows = P(("chip", "core", "head"), None)
    return jax.shard_map(
        on_device,
        mesh=fine_mesh,
        in_specs=(rows,) * 4,
        out_specs=(rows,) * 3,
        check_vma=False,
    )
```

time: 111 us -> 110 us (level)
  the two profiles are of different devices: /device:TPU:13 before, /device:TPU:0 now
where the time goes in v3:
time: 110 us
  waiting for transfers between devices  57.4 us (52%)
  starting transfers between devices  27.8 us (25%)
  Pallas kernels  20 us (18%)
  local copies, waits for them, and re-layouts  3.6 us (3%)
    all_to_all x4, waiting for transfers between devices, swapped_heads(): lax.all_to_all(value, 'head', split_axis=0, concat_axis=0, tiled=True)  34.9 us
    ppermute x8, waiting for transfers between devices, moved(): return lax.ppermute(value, ('chip', 'core', 'head'), pairs)  22.5 us
    pallas_call x8, Pallas kernels, call(): pl.pallas_call(kernel, out_shape=out_shape, in_specs=[SMEM_SPEC] + [spec]...  20 us
    all_to_all x4, starting transfers between devices, swapped_heads(): lax.all_to_all(value, 'head', split_axis=0, concat_axis=0, tiled=True)  17.9 us
    ppermute x8, starting transfers between devices, moved(): return lax.ppermute(value, ('chip', 'core', 'head'), pairs)  9.91 us
    unnamed x12, local copies, waits for them, and re-layouts  3.57 us
  transfers between devices with their start and end apart: 12, of which 9 were waited for; matrix products, arithmetic and copies ran while one was open for 0% of the time, Pallas kernels for 5%

profile of v3, /device:TPU:0, one launch (start us, length us, event | category | flops | bytes accessed | tf_op | source)
XLA Modules:
  0.0 109.6 jit_solution(7338859138609039245)
XLA Ops:
  0.6 0.1 pad_add_fusion.place_ref
  0.7 0.0 copy-start.2
  0.7 0.9 copy-done.2
  1.7 0.0 copy-start.3
  1.7 0.9 copy-done.3
  2.6 1.5 %shard_map.67 = bf16[4,128,512]{2,1,0:T(8,128)(2,1)} custom-call(s32[3]{0:T(128)S(1)} %pad_add_fusion.place_ref, bf16[128,1024]{1,0:T(8,128)(2,1)S(1)} %copy-done.2, bf16[128,1024]{1,0:T(8,128)(2,1)S(1)} %copy-done.3), custom_call_target="tpu_custom_call" | custom-call | bytes 1048588 | tf_op jit(solution)/shard_map/pallas_call | solution.py:25
  4.1 0.0 copy-start
  4.1 0.0 copy-start.1
  4.1 6.5 %all-to-all-start = ((bf16[4,128,512]{2,1,0:T(8,128)(2,1)}), bf16[4,128,512]{2,1,0:T(8,128)(2,1)S(1)}, u32[]{:S(2)}, u32[]{:S(2)}) async-start(bf16[4,128,512]{2,1,0:T(8,128)(2,1)} %shard_map.67), calls=%async_computation | async-start | bytes 1048576 | tf_op jit(solution)/shard_map/all_to_all | solution.py:239
  10.6 0.0 copy-done
  10.6 0.0 copy-done.1
  10.6 0.9 shard_map.68
  11.5 0.1 collective-permute-start.3
  11.5 1.9 %collective-permute-done.3.other_ref = bf16[4,128,512]{2,1,0:T(8,128)(2,1)S(1)} collective-permute-done((bf16[4,128,512]{2,1,0:T(8,128)(2,1)S(1)}, bf16[4,128,512]{2,1,0:T(8,128)(2,1)S(1)}, u32[]{:S(2)}, u32[]{:S(2)}) %collective-permute-start.3) | collective-permute-done | bytes 524320 | tf_op jit(solution)/shard_map/ppermute | solution.py:235
  13.4 1.6 %shard_map.69 = bf16[4,256,512]{2,1,0:T(8,128)(2,1)} custom-call(s32[3]{0:T(128)S(1)} %pad_add_fusion.place_ref, bf16[4,128,512]{2,1,0:T(8,128)(2,1)S(1)} %get-tuple-element.13.mine_ref, bf16[4,128,512]{2,1,0:T(8,128)(2,1)S(1)} %collective-permute-done.3.other_ref), custom_call_target="tpu_custom_call" | custom-call | bytes 2097164 | tf_op jit(solution)/shard_map/pallas_call | solution.py:25
  15.1 10.0 %all-to-all-done = bf16[4,128,512]{2,1,0:T(8,128)(2,1)S(1)} async-done(((bf16[4,128,512]{2,1,0:T(8,128)(2,1)}), bf16[4,128,512]{2,1,0:T(8,128)(2,1)S(1)}, u32[]{:S(2)}, u32[]{:S(2)}) %all-to-all-start) | async-done | bytes 524320 | tf_op jit(solution)/shard_map/all_to_all | solution.py:239
  25.1 3.5 %all-to-all-start.1 = ((bf16[4,256,512]{2,1,0:T(8,128)(2,1)}), bf16[4,256,512]{2,1,0:T(8,128)(2,1)S(1)}, u32[]{:S(2)}, u32[]{:S(2)}) async-start(bf16[4,256,512]{2,1,0:T(8,128)(2,1)} %shard_map.69), calls=%async_computation.1 | async-start | bytes 2097152 | tf_op jit(solution)/shard_map/all_to_all | solution.py:239
  28.6 3.4 %collective-permute-start.1 = (bf16[512,256]{1,0:T(8,128)(2,1)S(1)}, bf16[512,256]{1,0:T(8,128)(2,1)S(1)}, u32[]{:S(2)}, u32[]{:S(2)}) collective-permute-start(bf16[512,256]{1,0:T(8,128)(2,1)S(1)} %get-tuple-element.23), channel_id=1, source_target_pairs={{0,8},{1,9},{2,10},{3,11},{4,12},{5,13},{6,14},{7,15},{8,16},{9,17... | collective-permute-start | bytes 786440 | tf_op jit(solution)/shard_map/ppermute | solution.py:235
  32.0 1.8 %collective-permute-start.2 = (bf16[512,256]{1,0:T(8,128)(2,1)S(1)}, bf16[512,256]{1,0:T(8,128)(2,1)S(1)}, u32[]{:S(2)}, u32[]{:S(2)}) collective-permute-start(bf16[512,256]{1,0:T(8,128)(2,1)S(1)} %get-tuple-element.24), channel_id=1, source_target_pairs={{0,12},{1,13},{2,14},{3,15},{4,8},{5,9},{6,10},{7,11},{8,20},{9,21... | collective-permute-start | bytes 786440 | tf_op jit(solution)/shard_map/ppermute | solution.py:235
  33.8 1.8 %collective-permute-start = (bf16[512,256]{1,0:T(8,128)(2,1)S(1)}, bf16[512,256]{1,0:T(8,128)(2,1)S(1)}, u32[]{:S(2)}, u32[]{:S(2)}) collective-permute-start(bf16[512,256]{1,0:T(8,128)(2,1)S(1)} %get-tuple-element.24), channel_id=1, source_target_pairs={{0,4},{1,5},{2,6},{3,7},{4,0},{5,1},{6,2},{7,3},{8,12},{9,13},{10,... | collective-permute-start | bytes 786440 | tf_op jit(solution)/shard_map/ppermute | solution.py:235
  35.6 2.0 %collective-permute-done.1.near_ref = bf16[512,256]{1,0:T(8,128)(2,1)S(1)} collective-permute-done((bf16[512,256]{1,0:T(8,128)(2,1)S(1)}, bf16[512,256]{1,0:T(8,128)(2,1)S(1)}, u32[]{:S(2)}, u32[]{:S(2)}) %collective-permute-start.1) | collective-permute-done | bytes 262176 | tf_op jit(solution)/shard_map/ppermute | solution.py:235
  37.6 4.8 %collective-permute-done.2.far_ref = bf16[512,256]{1,0:T(8,128)(2,1)S(1)} collective-permute-done((bf16[512,256]{1,0:T(8,128)(2,1)S(1)}, bf16[512,256]{1,0:T(8,128)(2,1)S(1)}, u32[]{:S(2)}, u32[]{:S(2)}) %collective-permute-start.2) | collective-permute-done | bytes 262176 | tf_op jit(solution)/shard_map/ppermute | solution.py:235
  42.4 0.0 collective-permute-done.sibling_ref
  42.4 0.0 copy-start.4
  42.4 0.7 copy-done.4
  43.1 10.7 %all-to-all-done.1.blocks_ref = bf16[4,256,512]{2,1,0:T(8,128)(2,1)S(1)} async-done(((bf16[4,256,512]{2,1,0:T(8,128)(2,1)}), bf16[4,256,512]{2,1,0:T(8,128)(2,1)S(1)}, u32[]{:S(2)}, u32[]{:S(2)}) %all-to-all-start.1) | async-done | bytes 1048608 | tf_op jit(solution)/shard_map/all_to_all | solution.py:239
  53.8 0.0 copy-start.5
  53.8 0.9 copy-done.5
  54.7 10.3 %shard_map.70 = (bf16[512,256]{1,0:T(8,128)(2,1)S(1)}, bf16[512,256]{1,0:T(8,128)(2,1)S(1)}, f32[512,256]{1,0:T(8,128)S(1)}, bf16[512,256]{1,0:T(8,128)(2,1)S(1)...) custom-call(s32[3]{0:T(128)S(1)} %pad_add_fusion.place_ref, bf16[512,512]{1,0:T(8,128)(2,1)S(1)} %bitcast.8, ...), custom_call_target="tpu_custom_call" | custom-call | flops 2684354560 | bytes 4194316 | tf_op jit(solution)/shard_map/pallas_call | solution.py:25
  65.1 0.1 collective-permute-start.4
  65.2 1.5 %collective-permute-done.4 = bf16[512,256]{1,0:T(8,128)(2,1)S(1)} collective-permute-done((bf16[512,256]{1,0:T(8,128)(2,1)S(1)}, bf16[512,256]{1,0:T(8,128)(2,1)S(1)}, u32[]{:S(2)}, u32[]{:S(2)}) %collective-permute-start.4) | collective-permute-done | bytes 262176 | tf_op jit(solution)/shard_map/ppermute | solution.py:235
  66.7 1.4 %shard_map.71 = bf16[4,128,512]{2,1,0:T(8,128)(2,1)} custom-call(s32[3]{0:T(128)S(1)} %pad_add_fusion.place_ref, bf16[4,128,256]{2,1,0:T(8,128)(2,1)S(1)} %bitcast.9, bf16[4,128,256]{2,1,0:T(8,128)(2,1)S(1)} %bitcast.10), custom_call_target="tpu_custom_call" | custom-call | bytes 1048588 | tf_op jit(solution)/shard_map/pallas_call | solution.py:25
  68.1 3.5 %all-to-all-start.2 = ((bf16[4,128,512]{2,1,0:T(8,128)(2,1)}), bf16[4,128,512]{2,1,0:T(8,128)(2,1)S(1)}, u32[]{:S(2)}, u32[]{:S(2)}) async-start(bf16[4,128,512]{2,1,0:T(8,128)(2,1)} %shard_map.71), calls=%async_computation.2 | async-start | bytes 1048576 | tf_op jit(solution)/shard_map/all_to_all | solution.py:239
  71.5 1.3 %collective-permute-start.5 = (bf16[512,256]{1,0:T(8,128)(2,1)S(1)}, bf16[512,256]{1,0:T(8,128)(2,1)S(1)}, u32[]{:S(2)}, u32[]{:S(2)}) collective-permute-start(bf16[512,256]{1,0:T(8,128)(2,1)S(1)} %get-tuple-element.18), channel_id=1, source_target_pairs={{8,0},{9,1},{10,2},{11,3},{12,4},{13,5},{14,6},{15,7},{16,8},{17,9... | collective-permute-start | bytes 786440 | tf_op jit(solution)/shard_map/ppermute | solution.py:235
  72.8 0.2 collective-permute-start.6
  73.0 1.3 %collective-permute-start.7 = (bf16[512,256]{1,0:T(8,128)(2,1)S(1)}, bf16[512,256]{1,0:T(8,128)(2,1)S(1)}, u32[]{:S(2)}, u32[]{:S(2)}) collective-permute-start(bf16[512,256]{1,0:T(8,128)(2,1)S(1)} %get-tuple-element.20), channel_id=1, source_target_pairs={{8,4},{9,5},{10,6},{11,7},{12,0},{13,1},{14,2},{15,3},{16,12},{17,... | collective-permute-start | bytes 786440 | tf_op jit(solution)/shard_map/ppermute | solution.py:235
  74.3 8.3 %collective-permute-done.5.near_ref = bf16[512,256]{1,0:T(8,128)(2,1)S(1)} collective-permute-done((bf16[512,256]{1,0:T(8,128)(2,1)S(1)}, bf16[512,256]{1,0:T(8,128)(2,1)S(1)}, u32[]{:S(2)}, u32[]{:S(2)}) %collective-permute-start.5) | collective-permute-done | bytes 262176 | tf_op jit(solution)/shard_map/ppermute | solution.py:235
  82.6 0.0 collective-permute-done.6.sibling_ref
  82.6 4.0 %collective-permute-done.7.far_ref = bf16[512,256]{1,0:T(8,128)(2,1)S(1)} collective-permute-done((bf16[512,256]{1,0:T(8,128)(2,1)S(1)}, bf16[512,256]{1,0:T(8,128)(2,1)S(1)}, u32[]{:S(2)}, u32[]{:S(2)}) %collective-permute-start.7) | collective-permute-done | bytes 262176 | tf_op jit(solution)/shard_map/ppermute | solution.py:235
  86.6 1.5 %shard_map.73 = bf16[512,512]{1,0:T(8,128)(2,1)} custom-call(s32[3]{0:T(128)S(1)} %pad_add_fusion.place_ref, f32[512,256]{1,0:T(8,128)S(1)} %get-tuple-element.17.own_ref, bf16[512,256]{1,0:T(8,128)(2,1)S(1)} %collective-permute-done.5.near_ref, bf16[512,256]{1,0:T(8,128)(2,1)S(1)} %collective-permute-done.6.sibling_ref, ...), custom_call_target="tpu_custom_call" | custom-call | bytes 1835020 | tf_op jit(solution)/shard_map/pallas_call | solution.py:25
  88.1 0.0 all-to-all-done.2.in_ref
  88.1 4.4 %all-to-all-start.3 = ((bf16[4,128,512]{2,1,0:T(8,128)(2,1)}), bf16[4,128,512]{2,1,0:T(8,128)(2,1)S(1)}, u32[]{:S(2)}, u32[]{:S(2)}) async-start(bf16[4,128,512]{2,1,0:T(8,128)(2,1)} %bitcast.6), calls=%async_computation.3 | async-start | bytes 1048576 | tf_op jit(solution)/shard_map/all_to_all | solution.py:239
  92.5 1.4 %shard_map.72 = bf16[128,2048]{1,0:T(8,128)(2,1)} custom-call(s32[3]{0:T(128)S(1)} %pad_add_fusion.place_ref, bf16[4,128,512]{2,1,0:T(8,128)(2,1)S(1)} %all-to-all-done.2.in_ref), custom_call_target="tpu_custom_call" | custom-call | bytes 1048588 | tf_op jit(solution)/shard_map/pallas_call | solution.py:25
  93.9 14.2 %all-to-all-done.3.in_ref = bf16[4,128,512]{2,1,0:T(8,128)(2,1)S(1)} async-done(((bf16[4,128,512]{2,1,0:T(8,128)(2,1)}), bf16[4,128,512]{2,1,0:T(8,128)(2,1)S(1)}, u32[]{:S(2)}, u32[]{:S(2)}) %all-to-all-start.3) | async-done | bytes 524320 | tf_op jit(solution)/shard_map/all_to_all | solution.py:239
  108.1 1.5 %shard_map.74 = (bf16[128,1024]{1,0:T(8,128)(2,1)}, bf16[128,1024]{1,0:T(8,128)(2,1)}) custom-call(s32[3]{0:T(128)S(1)} %pad_add_fusion.place_ref, bf16[4,128,512]{2,1,0:T(8,128)(2,1)S(1)} %all-to-all-done.3.in_ref), custom_call_target="tpu_custom_call" | custom-call | bytes 1048588 | tf_op jit(solution)/shard_map/pallas_call | solution.py:25
  (1 shorter events, 0.0 us)
Async XLA Ops:
  0.7 1.0 copy-start.2
  1.7 0.9 copy-start.3
  4.1 6.5 %copy-start = (bf16[128,2048]{1,0:T(8,128)(2,1)S(1)}, bf16[128,2048]{1,0:T(8,128)(2,1)}, u32[]{:S(2)}) copy-start(bf16[128,2048]{1,0:T(8,128)(2,1)} %q_ref.1) | copy-start | bytes 1572868
  4.1 6.5 %copy-start.1 = (bf16[128,2048]{1,0:T(8,128)(2,1)S(1)}, bf16[128,2048]{1,0:T(8,128)(2,1)}, u32[]{:S(2)}) copy-start(bf16[128,2048]{1,0:T(8,128)(2,1)} %g_ref.1) | copy-start | bytes 1572868
  4.1 21.0 %all-to-all-start = ((bf16[4,128,512]{2,1,0:T(8,128)(2,1)}), bf16[4,128,512]{2,1,0:T(8,128)(2,1)S(1)}, u32[]{:S(2)}, u32[]{:S(2)}) async-start(bf16[4,128,512]{2,1,0:T(8,128)(2,1)} %shard_map.67), calls=%async_computation | async-start | bytes 1048576 | tf_op jit(solution)/shard_map/all_to_all | solution.py:239
  11.5 2.0 %collective-permute-start.3 = (bf16[4,128,512]{2,1,0:T(8,128)(2,1)S(1)}, bf16[4,128,512]{2,1,0:T(8,128)(2,1)S(1)}, u32[]{:S(2)}, u32[]{:S(2)}) collective-permute-start(bf16[4,128,512]{2,1,0:T(8,128)(2,1)S(1)} %get-tuple-element.14), channel_id=1, source_target_pairs={{0,4},{1,5},{2,6},{3,7},{4,0},{5,1},{6,2},{7,3},{8,12},{9,13},{10,... | collective-permute-start | bytes 1572872 | tf_op jit(solution)/shard_map/ppermute | solution.py:235
  25.1 28.7 %all-to-all-start.1 = ((bf16[4,256,512]{2,1,0:T(8,128)(2,1)}), bf16[4,256,512]{2,1,0:T(8,128)(2,1)S(1)}, u32[]{:S(2)}, u32[]{:S(2)}) async-start(bf16[4,256,512]{2,1,0:T(8,128)(2,1)} %shard_map.69), calls=%async_computation.1 | async-start | bytes 2097152 | tf_op jit(solution)/shard_map/all_to_all | solution.py:239
  28.6 9.0 %collective-permute-start.1 = (bf16[512,256]{1,0:T(8,128)(2,1)S(1)}, bf16[512,256]{1,0:T(8,128)(2,1)S(1)}, u32[]{:S(2)}, u32[]{:S(2)}) collective-permute-start(bf16[512,256]{1,0:T(8,128)(2,1)S(1)} %get-tuple-element.23), channel_id=1, source_target_pairs={{0,8},{1,9},{2,10},{3,11},{4,12},{5,13},{6,14},{7,15},{8,16},{9,17... | collective-permute-start | bytes 786440 | tf_op jit(solution)/shard_map/ppermute | solution.py:235
  32.0 10.4 %collective-permute-start.2 = (bf16[512,256]{1,0:T(8,128)(2,1)S(1)}, bf16[512,256]{1,0:T(8,128)(2,1)S(1)}, u32[]{:S(2)}, u32[]{:S(2)}) collective-permute-start(bf16[512,256]{1,0:T(8,128)(2,1)S(1)} %get-tuple-element.24), channel_id=1, source_target_pairs={{0,12},{1,13},{2,14},{3,15},{4,8},{5,9},{6,10},{7,11},{8,20},{9,21... | collective-permute-start | bytes 786440 | tf_op jit(solution)/shard_map/ppermute | solution.py:235
  33.8 8.6 %collective-permute-start = (bf16[512,256]{1,0:T(8,128)(2,1)S(1)}, bf16[512,256]{1,0:T(8,128)(2,1)S(1)}, u32[]{:S(2)}, u32[]{:S(2)}) collective-permute-start(bf16[512,256]{1,0:T(8,128)(2,1)S(1)} %get-tuple-element.24), channel_id=1, source_target_pairs={{0,4},{1,5},{2,6},{3,7},{4,0},{5,1},{6,2},{7,3},{8,12},{9,13},{10,... | collective-permute-start | bytes 786440 | tf_op jit(solution)/shard_map/ppermute | solution.py:235
  42.4 0.7 copy-start.4
  53.8 1.0 copy-start.5
  65.1 1.6 %collective-permute-start.4 = (bf16[512,256]{1,0:T(8,128)(2,1)S(1)}, bf16[512,256]{1,0:T(8,128)(2,1)S(1)}, u32[]{:S(2)}, u32[]{:S(2)}) collective-permute-start(bf16[512,256]{1,0:T(8,128)(2,1)S(1)} %get-tuple-element.16), channel_id=1, source_target_pairs={{0,4},{1,5},{2,6},{3,7},{4,0},{5,1},{6,2},{7,3},{8,12},{9,13},{10,... | collective-permute-start | bytes 786440 | tf_op jit(solution)/shard_map/ppermute | solution.py:235
  68.1 20.0 %all-to-all-start.2 = ((bf16[4,128,512]{2,1,0:T(8,128)(2,1)}), bf16[4,128,512]{2,1,0:T(8,128)(2,1)S(1)}, u32[]{:S(2)}, u32[]{:S(2)}) async-start(bf16[4,128,512]{2,1,0:T(8,128)(2,1)} %shard_map.71), calls=%async_computation.2 | async-start | bytes 1048576 | tf_op jit(solution)/shard_map/all_to_all | solution.py:239
  71.5 11.0 %collective-permute-start.5 = (bf16[512,256]{1,0:T(8,128)(2,1)S(1)}, bf16[512,256]{1,0:T(8,128)(2,1)S(1)}, u32[]{:S(2)}, u32[]{:S(2)}) collective-permute-start(bf16[512,256]{1,0:T(8,128)(2,1)S(1)} %get-tuple-element.18), channel_id=1, source_target_pairs={{8,0},{9,1},{10,2},{11,3},{12,4},{13,5},{14,6},{15,7},{16,8},{17,9... | collective-permute-start | bytes 786440 | tf_op jit(solution)/shard_map/ppermute | solution.py:235
  72.8 9.7 %collective-permute-start.6 = (bf16[512,256]{1,0:T(8,128)(2,1)S(1)}, bf16[512,256]{1,0:T(8,128)(2,1)S(1)}, u32[]{:S(2)}, u32[]{:S(2)}) collective-permute-start(bf16[512,256]{1,0:T(8,128)(2,1)S(1)} %get-tuple-element.19), channel_id=1, source_target_pairs={{0,4},{1,5},{2,6},{3,7},{4,0},{5,1},{6,2},{7,3},{8,12},{9,13},{10,... | collective-permute-start | bytes 786440 | tf_op jit(solution)/shard_map/ppermute | solution.py:235
  73.0 13.6 %collective-permute-start.7 = (bf16[512,256]{1,0:T(8,128)(2,1)S(1)}, bf16[512,256]{1,0:T(8,128)(2,1)S(1)}, u32[]{:S(2)}, u32[]{:S(2)}) collective-permute-start(bf16[512,256]{1,0:T(8,128)(2,1)S(1)} %get-tuple-element.20), channel_id=1, source_target_pairs={{8,4},{9,5},{10,6},{11,7},{12,0},{13,1},{14,2},{15,3},{16,12},{17,... | collective-permute-start | bytes 786440 | tf_op jit(solution)/shard_map/ppermute | solution.py:235
  88.1 20.0 %all-to-all-start.3 = ((bf16[4,128,512]{2,1,0:T(8,128)(2,1)}), bf16[4,128,512]{2,1,0:T(8,128)(2,1)S(1)}, u32[]{:S(2)}, u32[]{:S(2)}) async-start(bf16[4,128,512]{2,1,0:T(8,128)(2,1)} %bitcast.6), calls=%async_computation.3 | async-start | bytes 1048576 | tf_op jit(solution)/shard_map/all_to_all | solution.py:239

commit v4 on v3

--- a/solution.py
+++ b/solution.py
@@ -54,15 +54,25 @@
         copy.wait()
 
 
-def pack_kv_kernel(heads, place_ref, k_ref, v_ref, out_ref, sems):
+def onward(place_ref, heads, k):
+    return lax.rem(place_ref[2] + k, heads)
+
+
+def source(place_ref, heads, k):
+    return lax.rem(place_ref[2] + heads - k, heads)
+
+
+def pack_kv_kernel(heads, place_ref, k_ref, v_ref, *refs):
+    out_refs, sems = refs[:-1], refs[-1]
     core = place_ref[1]
     d = HEAD_SIZE
     pairs = []
-    for z in range(heads):
+    for k, out_ref in enumerate(out_refs):
+        z = onward(place_ref, heads, k)
         for n, g in enumerate((2 * z + core, 2 * z + 1 - core)):
             columns = at(g * d, d)
-            pairs.append((k_ref.at[:, columns], out_ref.at[z, :, pl.ds(2 * n * d, d)]))
-            pairs.append((v_ref.at[:, columns], out_ref.at[z, :, pl.ds((2 * n + 1) * d, d)]))
+            pairs.append((k_ref.at[:, columns], out_ref.at[:, pl.ds(2 * n * d, d)]))
+            pairs.append((v_ref.at[:, columns], out_ref.at[:, pl.ds((2 * n + 1) * d, d)]))
     copied(sems, pairs)
 
 
@@ -71,68 +81,90 @@
     width = 2 * HEAD_SIZE
     pairs = []
     for ref, c in ((other_ref, 1 - core), (mine_ref, core)):
-        for z in range(heads):
-            columns = at((2 * z + c) * width, width)
-            pairs.append((q_ref.at[:, columns], ref.at[z, :, pl.ds(0, width)]))
-            pairs.append((g_ref.at[:, columns], ref.at[z, :, pl.ds(width, width)]))
+        for k in range(heads):
+            columns = at((2 * onward(place_ref, heads, k) + c) * width, width)
+            pairs.append((q_ref.at[:, columns], ref.at[k, :, pl.ds(0, width)]))
+            pairs.append((g_ref.at[:, columns], ref.at[k, :, pl.ds(width, width)]))
     copied(sems, pairs)
 
 
-def merge_rows_kernel(heads, place_ref, mine_ref, other_ref, out_ref):
-    core = place_ref[1]
-    for z in range(heads):
-        out_ref[z, at(core * BLOCK, BLOCK)] = mine_ref[z]
-        out_ref[z, at((1 - core) * BLOCK, BLOCK)] = other_ref[z]
-
-
-def merge_columns_kernel(heads, place_ref, mine_ref, other_ref, out_ref):
-    core = place_ref[1]
+def gather_kv_kernel(heads, place_ref, *refs):
+    in_refs, (mine_ref, other_ref) = refs[:heads], refs[heads:]
     width = 2 * HEAD_SIZE
-    for z in range(heads):
-        out_ref[z, :, at(core * width, width)] = mine_ref[z]
-        out_ref[z, :, at((1 - core) * width, width)] = other_ref[z]
-
-
-def unpack_dq_kernel(heads, place_ref, in_ref, out_ref, sems):
+    for k, in_ref in enumerate(in_refs):
+        rows = at(source(place_ref, heads, k) * BLOCK, BLOCK)
+        mine_ref[rows] = in_ref[:, :width]
+        other_ref[rows] = in_ref[:, width:]
+
+
+def join_kernel(place_ref, mine_ref, sibling_ref, out_ref):
+    core = place_ref[1]
+    half = mine_ref.shape[0]
+    out_ref[at(core * half, half)] = mine_ref[...]
+    out_ref[at((1 - core) * half, half)] = sibling_ref[...]
+
+
+def merge_rows_kernel(heads, place_ref, mine_ref, other_ref, after_ref, *out_refs):
+    core = place_ref[1]
+    for k, out_ref in enumerate(out_refs):
+        out_ref[at(core * BLOCK, BLOCK)] = mine_ref[k]
+        out_ref[at((1 - core) * BLOCK, BLOCK)] = other_ref[k]
+
+
+def merge_columns_kernel(heads, place_ref, mine_ref, other_ref, *out_refs):
+    core = place_ref[1]
+    width = 2 * HEAD_SIZE
+    for k, out_ref in enumerate(out_refs):
+        rows = slice(k * BLOCK, (k + 1) * BLOCK)
+        out_ref[:, at(core * width, width)] = mine_ref[rows]
+        out_ref[:, at((1 - core) * width, width)] = other_ref[rows]
+
+
+def unpack_dq_kernel(heads, place_ref, *refs):
+    in_refs, out_ref, sems = refs[:-2], refs[-2], refs[-1]
     width = 4 * HEAD_SIZE
-    copied(sems, [(in_ref.at[z], out_ref.at[:, pl.ds(z * width, width)]) for z in range(heads)])
-
-
-def unpack_kv_kernel(heads, place_ref, in_ref, k_ref, v_ref, sems):
+    pairs = []
+    for k, in_ref in enumerate(in_refs):
+        pairs.append((in_ref, out_ref.at[:, at(source(place_ref, heads, k) * width, width)]))
+    copied(sems, pairs)
+
+
+def unpack_kv_kernel(heads, place_ref, *refs):
+    in_refs, k_ref, v_ref, sems = refs[:-3], refs[-3], refs[-2], refs[-1]
     core = place_ref[1]
     d = HEAD_SIZE
     pairs = []
-    for z in range(heads):
+    for k, in_ref in enumerate(in_refs):
+        z = source(place_ref, heads, k)
         for n, g in enumerate((2 * z + core, 2 * z + 1 - core)):
             columns = at(g * d, d)
-            pairs.append((in_ref.at[z, :, pl.ds(2 * n * d, d)], k_ref.at[:, columns]))
-            pairs.append((in_ref.at[z, :, pl.ds((2 * n + 1) * d, d)], v_ref.at[:, columns]))
+            pairs.append((in_ref.at[:, pl.ds(2 * n * d, d)], k_ref.at[:, columns]))
+            pairs.append((in_ref.at[:, pl.ds((2 * n + 1) * d, d)], v_ref.at[:, columns]))
     copied(sems, pairs)
 
 
-def add_kernel(place_ref, own_ref, near_ref, sibling_ref, far_ref, out_ref):
+def add_kernel(heads, place_ref, own_ref, near_ref, sibling_ref, far_ref, *out_refs):
     width = 2 * HEAD_SIZE
-    wide = lambda ref: ref[...].astype(jnp.float32)
-    out_ref[:, :width] = (own_ref[...] + wide(near_ref)).astype(jnp.bfloat16)
-    out_ref[:, width:] = (wide(sibling_ref) + wide(far_ref)).astype(jnp.bfloat16)
-
-
-def attention_kernel(heads, place_ref, mine_ref, sibling_ref, near_ref, far_ref, blocks_ref, *refs):
+    for k, out_ref in enumerate(out_refs):
+        rows = at(onward(place_ref, heads, k) * BLOCK, BLOCK)
+        wide = lambda ref: ref[rows].astype(jnp.float32)
+        out_ref[:, :width] = (own_ref[rows] + wide(near_ref)).astype(jnp.bfloat16)
+        out_ref[:, width:] = (wide(sibling_ref) + wide(far_ref)).astype(jnp.bfloat16)
+
+
+def attention_kernel(heads, place_ref, own_ref, prev_ref, *refs):
     d = HEAD_SIZE
     count = 2 * heads
+    block_refs, refs = refs[:heads], refs[heads:]
     dq_mine_ref, dq_other_ref, own_mine_ref, own_other_ref, prev_mine_ref, prev_other_ref = refs[:6]
-    qd_ref, own_ref, prev_ref, dq_ref, own_kt_ref, prev_kt_ref, own_grad_ref, prev_grad_ref = refs[6:]
+    qd_ref, dq_ref, own_kt_ref, prev_kt_ref, own_grad_ref, prev_grad_ref = refs[6:]
     first, core = place_ref[0], place_ref[1]
     half = heads * BLOCK
     mine, other = at(core * half, half), at((1 - core) * half, half)
-    own_ref[mine] = mine_ref[:, : 2 * d]
-    own_ref[other] = sibling_ref[...]
-    prev_ref[mine] = near_ref[...]
-    prev_ref[other] = far_ref[...]
-    for c in range(2):
-        for z in range(heads):
-            start = (c * heads + z) * BLOCK
-            qd_ref[start : start + BLOCK] = blocks_ref[z, c * BLOCK : (c + 1) * BLOCK]
+    for k, block_ref in enumerate(block_refs):
+        for c in range(2):
+            rows = at((c * heads + source(place_ref, heads, k)) * BLOCK, BLOCK)
+            qd_ref[rows] = block_ref[c * BLOCK : (c + 1) * BLOCK]
     bias = jnp.where(first == 1, masked_value, 0.0).astype(jnp.float32)
     own_kt_ref[...] = own_ref[:, :d].T
     prev_kt_ref[...] = prev_ref[:, :d].T
@@ -184,8 +216,10 @@
             prev_grad_ref[:, d:] = dv_prev
         own_grad_ref[low:high, :d] = dk_own[low:]
         own_grad_ref[low:high, d:] = dv_own[low:]
-    dq_mine_ref[...] = dq_ref[mine]
-    dq_other_ref[...] = dq_ref[other]
+    for ref, c in ((dq_mine_ref, core), (dq_other_ref, 1 - core)):
+        for k in range(heads):
+            rows = at((c * heads + onward(place_ref, heads, k)) * BLOCK, BLOCK)
+            ref[k * BLOCK : (k + 1) * BLOCK] = dq_ref[rows]
     for ref, grad_ref, rows in (
         (own_mine_ref, own_grad_ref, mine),
         (own_other_ref, own_grad_ref, other),
@@ -196,7 +230,7 @@
         ref[:, d:] = grad_ref[rows, d:].astype(ref.dtype)
 
 
-def attention_backward(heads, place, mine, sibling, near, far, blocks):
+def attention_backward(heads, place, own, prev, blocks):
     half, d = heads * BLOCK, HEAD_SIZE
     whole = 2 * half
     low, wide = jnp.bfloat16, jnp.float32
@@ -205,8 +239,6 @@
     scratch = (
         pltpu.VMEM((whole, 4 * d), low),
         pltpu.VMEM((whole, 2 * d), low),
-        pltpu.VMEM((whole, 2 * d), low),
-        pltpu.VMEM((whole, 2 * d), low),
         pltpu.VMEM((d, whole), low),
         pltpu.VMEM((d, whole), low),
         pltpu.VMEM((whole, 2 * d), wide),
@@ -215,11 +247,11 @@
     return call(
         functools.partial(attention_kernel, heads),
         outs,
-        (place, mine, sibling, near, far, blocks),
+        (place, own, prev) + tuple(blocks),
         scratch,
         20 * whole * whole * d,
         2 * whole * whole,
-        48,
+        32,
     )
 
 
@@ -235,54 +267,52 @@
     return lax.ppermute(value, ("chip", "core", "head"), pairs)
 
 
-def swapped_heads(value):
-    return lax.all_to_all(value, "head", split_axis=0, concat_axis=0, tiled=True)
-
-
 def on_device(query_rows, key_rows, saved_value_rows, out_grad):
     chips, heads = lax.axis_size("chip"), lax.axis_size("head")
-    send = functools.partial(moved, chips=chips, heads=heads, head_step=0)
+    send = functools.partial(moved, chips=chips, heads=heads)
     rows, d, low = key_rows.shape[0], HEAD_SIZE, jnp.bfloat16
     bind = lambda kernel: functools.partial(kernel, heads)
     place = jnp.stack(
         [(lax.axis_index("chip") == 0).astype(jnp.int32), lax.axis_index("core"), lax.axis_index("head")]
     ).astype(jnp.int32)
-    kv = copy_call(
-        bind(pack_kv_kernel), 4 * heads, shape_of(low, heads, rows, 4 * d), (place, key_rows, saved_value_rows)
-    )
+
+    def spread(parts):
+        order = sorted(range(1, heads), key=lambda k: -min(k, heads - k))
+        out = {k: send(parts[k], chip_step=0, flip=0, head_step=k) for k in order}
+        return (parts[0],) + tuple(out[k] for k in range(1, heads))
+
+    across = functools.partial(send, head_step=0)
+    slab = shape_of(low, rows, 4 * d)
+    kvs = spread(copy_call(bind(pack_kv_kernel), 4 * heads, (slab,) * heads, (place, key_rows, saved_value_rows)))
     qd_mine, qd_other = copy_call(
         bind(pack_qd_kernel), 4 * heads, (shape_of(low, heads, rows, 4 * d),) * 2, (place, query_rows, out_grad)
     )
-    kv = swapped_heads(kv).reshape(heads * rows, 4 * d)
-    qd_other = send(qd_other, chip_step=0, flip=1)
-    qd = call(bind(merge_rows_kernel), shape_of(low, heads, 2 * rows, 4 * d), (place, qd_mine, qd_other))
-    other = kv[:, 2 * d :]
-    near = send(kv[:, : 2 * d], chip_step=1, flip=0)
-    far = send(other, chip_step=1, flip=1)
-    sibling = send(other, chip_step=0, flip=1)
-    blocks = swapped_heads(qd)
+    qd_other = across(qd_other, chip_step=0, flip=1)
+    mine, other = call(bind(gather_kv_kernel), (shape_of(low, heads * rows, 2 * d),) * 2, (place,) + kvs)
+    sibling = across(other, chip_step=0, flip=1)
+    blocks = spread(
+        call(
+            bind(merge_rows_kernel),
+            (shape_of(low, 2 * rows, 4 * d),) * heads,
+            (place, qd_mine, qd_other, mine[:8]),
+        )
+    )
+    own = call(join_kernel, shape_of(low, 2 * heads * rows, 2 * d), (place, mine, sibling))
+    prev = across(own, chip_step=1, flip=0)
     dq_mine, dq_other, own_mine, own_other, prev_mine, prev_other = attention_backward(
-        heads, place, kv, sibling, near, far, blocks
-    )
-    near_back = send(prev_mine, chip_step=-1, flip=0)
-    far_back = send(prev_other, chip_step=-1, flip=1)
-    sibling_back = send(own_other, chip_step=0, flip=1)
-    dq_other = send(dq_other, chip_step=0, flip=1)
-    split = lambda x: x.reshape(heads, rows, -1)
-    dq = call(
-        bind(merge_columns_kernel), shape_of(low, heads, rows, 4 * d), (place, split(dq_mine), split(dq_other))
-    )
-    query_grad = copy_call(
-        bind(unpack_dq_kernel), heads, shape_of(low, *query_rows.shape), (place, swapped_heads(dq))
-    )
-    total = call(
-        add_kernel,
-        shape_of(low, heads * rows, 4 * d),
-        (place, own_mine, near_back, sibling_back, far_back),
-    )
-    total = swapped_heads(split(total))
+        heads, place, own, prev, blocks
+    )
+    near_back = across(prev_mine, chip_step=-1, flip=0)
+    far_back = across(prev_other, chip_step=-1, flip=1)
+    sibling_back = across(own_other, chip_step=0, flip=1)
+    dq_other = across(dq_other, chip_step=0, flip=1)
+    dqs = spread(call(bind(merge_columns_kernel), (slab,) * heads, (place, dq_mine, dq_other)))
+    query_grad = copy_call(bind(unpack_dq_kernel), heads, shape_of(low, *query_rows.shape), (place,) + dqs)
+    totals = spread(
+        call(bind(add_kernel), (slab,) * heads, (place, own_mine, near_back, sibling_back, far_back))
+    )
     key_grad, value_grad = copy_call(
-        bind(unpack_kv_kernel), 4 * heads, (shape_of(low, *key_rows.shape),) * 2, (place, total)
+        bind(unpack_kv_kernel), 4 * heads, (shape_of(low, *key_rows.shape),) * 2, (place,) + totals
     )
     return query_grad, key_grad, value_grad
 

time: 110 us -> 93.7 us (0.85)
  the two profiles are of different devices: /device:TPU:0 before, /device:TPU:13 now
where the time goes in v4:
time: 93.7 us; the launch traced here: 93.4 us
  waiting for transfers between devices  49.5 us (53%)
  starting transfers between devices  22.1 us (24%)
  Pallas kernels  18 us (19%)
  local copies, waits for them, and re-layouts  3 us (3%)
    ppermute x19, waiting for transfers between devices, moved(): return lax.ppermute(value, ('chip', 'core', 'head'), pairs)  49.5 us
    ppermute x19, starting transfers between devices, moved(): return lax.ppermute(value, ('chip', 'core', 'head'), pairs)  22.1 us
    pallas_call x10, Pallas kernels, call(): pl.pallas_call(kernel, out_shape=out_shape, in_specs=[SMEM_SPEC] + [spec]...  18 us
    unnamed x8, local copies, waits for them, and re-layouts  2.99 us
  transfers between devices with their start and end apart: 19, of which 11 were waited for; matrix products, arithmetic and copies ran while one was open for 0% of the time, Pallas kernels for 6%

profile of v4, /device:TPU:13, one launch (start us, length us, event | category | flops | bytes accessed | tf_op | source)
XLA Modules:
  0.0 93.4 jit_solution(14205580321135488456)
XLA Ops:
  0.6 0.0 copy-start
  0.6 0.1 pad_add_fusion.place_ref
  0.7 0.0 copy-start.2
  0.7 1.0 %copy-done.2 = bf16[128,1024]{1,0:T(8,128)(2,1)S(1)} copy-done((bf16[128,1024]{1,0:T(8,128)(2,1)S(1)}, bf16[128,1024]{1,0:T(8,128)(2,1)}, u32[]{:S(2)}) %copy-start.2) | copy-done | bytes 262168
  1.7 0.0 copy-start.3
  1.7 0.9 %copy-done.3 = bf16[128,1024]{1,0:T(8,128)(2,1)S(1)} copy-done((bf16[128,1024]{1,0:T(8,128)(2,1)S(1)}, bf16[128,1024]{1,0:T(8,128)(2,1)}, u32[]{:S(2)}) %copy-start.3) | copy-done | bytes 262168
  2.7 0.9 shard_map.67
  3.6 1.3 %collective-permute-start = (bf16[128,512]{1,0:T(8,128)(2,1)S(1)}, bf16[128,512]{1,0:T(8,128)(2,1)S(1)}, u32[]{:S(2)}, u32[]{:S(2)}) collective-permute-start(bf16[128,512]{1,0:T(8,128)(2,1)S(1)} %get-tuple-element.32), channel_id=1, source_target_pairs={{0,1},{1,2},{2,3},{3,0},{4,5},{5,6},{6,7},{7,4},{8,9},{9,10},{10,1... | collective-permute-start | bytes 393224 | tf_op jit(solution)/shard_map/ppermute | solution.py:267
  4.9 1.1 %collective-permute-start.1 = (bf16[128,512]{1,0:T(8,128)(2,1)S(1)}, bf16[128,512]{1,0:T(8,128)(2,1)S(1)}, u32[]{:S(2)}, u32[]{:S(2)}) collective-permute-start(bf16[128,512]{1,0:T(8,128)(2,1)S(1)} %get-tuple-element.33), channel_id=1, source_target_pairs={{0,2},{1,3},{2,0},{3,1},{4,6},{5,7},{6,4},{7,5},{8,10},{9,11},{10,... | collective-permute-start | bytes 393224 | tf_op jit(solution)/shard_map/ppermute | solution.py:267
  6.0 1.4 %collective-permute-start.2 = (bf16[128,512]{1,0:T(8,128)(2,1)S(1)}, bf16[128,512]{1,0:T(8,128)(2,1)S(1)}, u32[]{:S(2)}, u32[]{:S(2)}) collective-permute-start(bf16[128,512]{1,0:T(8,128)(2,1)S(1)} %get-tuple-element.34), channel_id=1, source_target_pairs={{0,3},{1,0},{2,1},{3,2},{4,7},{5,4},{6,5},{7,6},{8,11},{9,8},{10,9... | collective-permute-start | bytes 393224 | tf_op jit(solution)/shard_map/ppermute | solution.py:267
  7.4 0.0 copy-done
  7.4 0.0 copy-start.1
  7.4 1.0 %copy-done.1 = bf16[128,2048]{1,0:T(8,128)(2,1)S(1)} copy-done((bf16[128,2048]{1,0:T(8,128)(2,1)S(1)}, bf16[128,2048]{1,0:T(8,128)(2,1)}, u32[]{:S(2)}) %copy-start.1) | copy-done | bytes 524312
  8.4 0.9 shard_map.70
  9.3 1.6 %collective-permute-start.5 = (bf16[4,128,512]{2,1,0:T(8,128)(2,1)S(1)}, bf16[4,128,512]{2,1,0:T(8,128)(2,1)S(1)}, u32[]{:S(2)}, u32[]{:S(2)}) collective-permute-start(bf16[4,128,512]{2,1,0:T(8,128)(2,1)S(1)} %get-tuple-element.38), channel_id=1, source_target_pairs={{0,4},{1,5},{2,6},{3,7},{4,0},{5,1},{6,2},{7,3},{8,12},{9,13},{10,... | collective-permute-start | bytes 1572872 | tf_op jit(solution)/shard_map/ppermute | solution.py:267
  10.9 0.0 collective-permute-done.refs_1_
  10.9 4.6 %collective-permute-done.1.refs_2_ = bf16[128,512]{1,0:T(8,128)(2,1)S(1)} collective-permute-done((bf16[128,512]{1,0:T(8,128)(2,1)S(1)}, bf16[128,512]{1,0:T(8,128)(2,1)S(1)}, u32[]{:S(2)}, u32[]{:S(2)}) %collective-permute-start.1) | collective-permute-done | bytes 131104 | tf_op jit(solution)/shard_map/ppermute | solution.py:267
  15.5 2.8 %collective-permute-done.2.refs_3_ = bf16[128,512]{1,0:T(8,128)(2,1)S(1)} collective-permute-done((bf16[128,512]{1,0:T(8,128)(2,1)S(1)}, bf16[128,512]{1,0:T(8,128)(2,1)S(1)}, u32[]{:S(2)}, u32[]{:S(2)}) %collective-permute-start.2) | collective-permute-done | bytes 131104 | tf_op jit(solution)/shard_map/ppermute | solution.py:267
  18.3 0.6 shard_map.68
  18.9 0.6 collective-permute-start.3
  19.5 1.2 %collective-permute-done.3.sibling_ref = bf16[512,256]{1,0:T(8,128)(2,1)S(1)} collective-permute-done((bf16[512,256]{1,0:T(8,128)(2,1)S(1)}, bf16[512,256]{1,0:T(8,128)(2,1)S(1)}, u32[]{:S(2)}, u32[]{:S(2)}) %collective-permute-start.3) | collective-permute-done | bytes 262176 | tf_op jit(solution)/shard_map/ppermute | solution.py:267
  20.6 0.6 shard_map.69.own_ref
  21.2 3.1 %collective-permute-start.4 = (bf16[1024,256]{1,0:T(8,128)(2,1)S(1)}, bf16[1024,256]{1,0:T(8,128)(2,1)S(1)}, u32[]{:S(2)}, u32[]{:S(2)}) collective-permute-start(bf16[1024,256]{1,0:T(8,128)(2,1)S(1)} %shard_map.69.own_ref), channel_id=1, source_target_pairs={{0,8},{1,9},{2,10},{3,11},{4,12},{5,13},{6,14},{7,15},{8,16},{9,17... | collective-permute-start | bytes 1572872 | tf_op jit(solution)/shard_map/ppermute | solution.py:267
  24.3 0.0 collective-permute-done.5.other_ref
  24.4 0.6 shard_map.71
  25.0 0.1 collective-permute-start.6
  25.0 1.4 %collective-permute-start.7 = (bf16[256,512]{1,0:T(8,128)(2,1)S(1)}, bf16[256,512]{1,0:T(8,128)(2,1)S(1)}, u32[]{:S(2)}, u32[]{:S(2)}) collective-permute-start(bf16[256,512]{1,0:T(8,128)(2,1)S(1)} %get-tuple-element.41), channel_id=1, source_target_pairs={{0,2},{1,3},{2,0},{3,1},{4,6},{5,7},{6,4},{7,5},{8,10},{9,11},{10,... | collective-permute-start | bytes 786440 | tf_op jit(solution)/shard_map/ppermute | solution.py:267
  26.5 1.4 %collective-permute-start.8 = (bf16[256,512]{1,0:T(8,128)(2,1)S(1)}, bf16[256,512]{1,0:T(8,128)(2,1)S(1)}, u32[]{:S(2)}, u32[]{:S(2)}) collective-permute-start(bf16[256,512]{1,0:T(8,128)(2,1)S(1)} %get-tuple-element.42), channel_id=1, source_target_pairs={{0,3},{1,0},{2,1},{3,2},{4,7},{5,4},{6,5},{7,6},{8,11},{9,8},{10,9... | collective-permute-start | bytes 786440 | tf_op jit(solution)/shard_map/ppermute | solution.py:267
  27.9 4.4 %collective-permute-done.6.refs_1_ = bf16[256,512]{1,0:T(8,128)(2,1)S(1)} collective-permute-done((bf16[256,512]{1,0:T(8,128)(2,1)S(1)}, bf16[256,512]{1,0:T(8,128)(2,1)S(1)}, u32[]{:S(2)}, u32[]{:S(2)}) %collective-permute-start.6) | collective-permute-done | bytes 262176 | tf_op jit(solution)/shard_map/ppermute | solution.py:267
  32.2 15.0 %collective-permute-done.7.refs_2_ = bf16[256,512]{1,0:T(8,128)(2,1)S(1)} collective-permute-done((bf16[256,512]{1,0:T(8,128)(2,1)S(1)}, bf16[256,512]{1,0:T(8,128)(2,1)S(1)}, u32[]{:S(2)}, u32[]{:S(2)}) %collective-permute-start.7) | collective-permute-done | bytes 262176 | tf_op jit(solution)/shard_map/ppermute | solution.py:267
  47.2 2.8 %collective-permute-done.8.refs_3_ = bf16[256,512]{1,0:T(8,128)(2,1)S(1)} collective-permute-done((bf16[256,512]{1,0:T(8,128)(2,1)S(1)}, bf16[256,512]{1,0:T(8,128)(2,1)S(1)}, u32[]{:S(2)}, u32[]{:S(2)}) %collective-permute-start.8) | collective-permute-done | bytes 262176 | tf_op jit(solution)/shard_map/ppermute | solution.py:267
  50.0 0.0 collective-permute-done.4.prev_ref
  50.0 10.4 %shard_map.72 = (bf16[512,256]{1,0:T(8,128)(2,1)S(1)}, bf16[512,256]{1,0:T(8,128)(2,1)S(1)}, f32[512,256]{1,0:T(8,128)S(1)}, bf16[512,256]{1,0:T(8,128)(2,1)S(1)...) custom-call(s32[3]{0:T(128)S(1)} %pad_add_fusion.place_ref, bf16[1024,256]{1,0:T(8,128)(2,1)S(1)} %shard_map.69.own_ref, ...), custom_call_target="tpu_custom_call" | custom-call | flops 2684354560 | bytes 3932172 | tf_op jit(solution)/shard_map/pallas_call | solution.py:25
  60.4 0.6 collective-permute-start.9
  61.0 3.0 %collective-permute-start.13 = (bf16[512,256]{1,0:T(8,128)(2,1)S(1)}, bf16[512,256]{1,0:T(8,128)(2,1)S(1)}, u32[]{:S(2)}, u32[]{:S(2)}) collective-permute-start(bf16[512,256]{1,0:T(8,128)(2,1)S(1)} %get-tuple-element.50), channel_id=1, source_target_pairs={{8,0},{9,1},{10,2},{11,3},{12,4},{13,5},{14,6},{15,7},{16,8},{17,9... | collective-permute-start | bytes 786440 | tf_op jit(solution)/shard_map/ppermute | solution.py:267
  64.0 0.4 collective-permute-start.14
  64.4 2.3 %collective-permute-start.15 = (bf16[512,256]{1,0:T(8,128)(2,1)S(1)}, bf16[512,256]{1,0:T(8,128)(2,1)S(1)}, u32[]{:S(2)}, u32[]{:S(2)}) collective-permute-start(bf16[512,256]{1,0:T(8,128)(2,1)S(1)} %get-tuple-element.52), channel_id=1, source_target_pairs={{8,4},{9,5},{10,6},{11,7},{12,0},{13,1},{14,2},{15,3},{16,12},{17,... | collective-permute-start | bytes 786440 | tf_op jit(solution)/shard_map/ppermute | solution.py:267
  66.7 0.0 collective-permute-done.9.other_ref
  66.7 0.6 shard_map.73
  67.3 0.1 collective-permute-start.10
  67.4 1.0 %collective-permute-start.11 = (bf16[128,512]{1,0:T(8,128)(2,1)S(1)}, bf16[128,512]{1,0:T(8,128)(2,1)S(1)}, u32[]{:S(2)}, u32[]{:S(2)}) collective-permute-start(bf16[128,512]{1,0:T(8,128)(2,1)S(1)} %get-tuple-element.47), channel_id=1, source_target_pairs={{0,2},{1,3},{2,0},{3,1},{4,6},{5,7},{6,4},{7,5},{8,10},{9,11},{10,... | collective-permute-start | bytes 393224 | tf_op jit(solution)/shard_map/ppermute | solution.py:267
  68.4 2.4 %collective-permute-done.13.near_ref = bf16[512,256]{1,0:T(8,128)(2,1)S(1)} collective-permute-done((bf16[512,256]{1,0:T(8,128)(2,1)S(1)}, bf16[512,256]{1,0:T(8,128)(2,1)S(1)}, u32[]{:S(2)}, u32[]{:S(2)}) %collective-permute-start.13) | collective-permute-done | bytes 262176 | tf_op jit(solution)/shard_map/ppermute | solution.py:267
  70.8 0.0 collective-permute-start.12
  70.8 0.0 collective-permute-done.14.sibling_ref
  70.8 5.7 %collective-permute-done.15.far_ref = bf16[512,256]{1,0:T(8,128)(2,1)S(1)} collective-permute-done((bf16[512,256]{1,0:T(8,128)(2,1)S(1)}, bf16[512,256]{1,0:T(8,128)(2,1)S(1)}, u32[]{:S(2)}, u32[]{:S(2)}) %collective-permute-start.15) | collective-permute-done | bytes 262176 | tf_op jit(solution)/shard_map/ppermute | solution.py:267
  76.5 0.7 shard_map.75
  77.2 0.1 collective-permute-start.16
  77.2 1.3 %collective-permute-start.17 = (bf16[128,512]{1,0:T(8,128)(2,1)S(1)}, bf16[128,512]{1,0:T(8,128)(2,1)S(1)}, u32[]{:S(2)}, u32[]{:S(2)}) collective-permute-start(bf16[128,512]{1,0:T(8,128)(2,1)S(1)} %get-tuple-element.55), channel_id=1, source_target_pairs={{0,2},{1,3},{2,0},{3,1},{4,6},{5,7},{6,4},{7,5},{8,10},{9,11},{10,... | collective-permute-start | bytes 393224 | tf_op jit(solution)/shard_map/ppermute | solution.py:267
  78.6 0.0 collective-permute-done.10.refs_1_
  78.6 1.4 %collective-permute-start.18 = (bf16[128,512]{1,0:T(8,128)(2,1)S(1)}, bf16[128,512]{1,0:T(8,128)(2,1)S(1)}, u32[]{:S(2)}, u32[]{:S(2)}) collective-permute-start(bf16[128,512]{1,0:T(8,128)(2,1)S(1)} %get-tuple-element.56), channel_id=1, source_target_pairs={{0,3},{1,0},{2,1},{3,2},{4,7},{5,4},{6,5},{7,6},{8,11},{9,8},{10,9... | collective-permute-start | bytes 393224 | tf_op jit(solution)/shard_map/ppermute | solution.py:267
  80.0 0.0 collective-permute-done.11.refs_2_
  80.0 6.4 %collective-permute-done.12.refs_3_ = bf16[128,512]{1,0:T(8,128)(2,1)S(1)} collective-permute-done((bf16[128,512]{1,0:T(8,128)(2,1)S(1)}, bf16[128,512]{1,0:T(8,128)(2,1)S(1)}, u32[]{:S(2)}, u32[]{:S(2)}) %collective-permute-start.12) | collective-permute-done | bytes 131104 | tf_op jit(solution)/shard_map/ppermute | solution.py:267
  86.4 1.4 %shard_map.74 = bf16[128,2048]{1,0:T(8,128)(2,1)} custom-call(s32[3]{0:T(128)S(1)} %pad_add_fusion.place_ref, bf16[128,512]{1,0:T(8,128)(2,1)S(1)} %get-tuple-element.45.refs_0_, bf16[128,512]{1,0:T(8,128)(2,1)S(1)} %collective-permute-done.10.refs_1_, bf16[128,512]{1,0:T(8,128)(2,1)S(1)} %collective-permute-done.11.refs_2_, ...), custom_call_target="tpu_custom_call" | custom-call | bytes 1048588 | tf_op jit(solution)/shard_map/pallas_call | solution.py:25
  87.7 0.0 collective-permute-done.16.refs_1_
  87.7 2.2 %collective-permute-done.17.refs_2_ = bf16[128,512]{1,0:T(8,128)(2,1)S(1)} collective-permute-done((bf16[128,512]{1,0:T(8,128)(2,1)S(1)}, bf16[128,512]{1,0:T(8,128)(2,1)S(1)}, u32[]{:S(2)}, u32[]{:S(2)}) %collective-permute-start.17) | collective-permute-done | bytes 131104 | tf_op jit(solution)/shard_map/ppermute | solution.py:267
  89.9 2.1 %collective-permute-done.18.refs_3_ = bf16[128,512]{1,0:T(8,128)(2,1)S(1)} collective-permute-done((bf16[128,512]{1,0:T(8,128)(2,1)S(1)}, bf16[128,512]{1,0:T(8,128)(2,1)S(1)}, u32[]{:S(2)}, u32[]{:S(2)}) %collective-permute-start.18) | collective-permute-done | bytes 131104 | tf_op jit(solution)/shard_map/ppermute | solution.py:267
  92.0 1.5 %shard_map.76 = (bf16[128,1024]{1,0:T(8,128)(2,1)}, bf16[128,1024]{1,0:T(8,128)(2,1)}) custom-call(s32[3]{0:T(128)S(1)} %pad_add_fusion.place_ref, bf16[128,512]{1,0:T(8,128)(2,1)S(1)} %get-tuple-element.53.refs_0_, bf16[128,512]{1,0:T(8,128)(2,1)S(1)} %collective-permute-done.16.refs_1_, bf16[128,512]{1,0:T(8,128)(2,1)S(1)} %collective-permute-done.17.refs_2_, ...), custom_call_target="tpu_custom_call" | custom-call | bytes 1048588 | tf_op jit(solution)/shard_map/pallas_call | solution.py:25
  (1 shorter events, 0.0 us)
Async XLA Ops:
  0.6 6.8 %copy-start = (bf16[128,2048]{1,0:T(8,128)(2,1)S(1)}, bf16[128,2048]{1,0:T(8,128)(2,1)}, u32[]{:S(2)}) copy-start(bf16[128,2048]{1,0:T(8,128)(2,1)} %q_ref.1) | copy-start | bytes 1572868
  0.7 1.0 %copy-start.2 = (bf16[128,1024]{1,0:T(8,128)(2,1)S(1)}, bf16[128,1024]{1,0:T(8,128)(2,1)}, u32[]{:S(2)}) copy-start(bf16[128,1024]{1,0:T(8,128)(2,1)} %k_ref.1) | copy-start | bytes 786436
  1.7 0.9 %copy-start.3 = (bf16[128,1024]{1,0:T(8,128)(2,1)S(1)}, bf16[128,1024]{1,0:T(8,128)(2,1)}, u32[]{:S(2)}) copy-start(bf16[128,1024]{1,0:T(8,128)(2,1)} %v_ref.1) | copy-start | bytes 786436
  3.6 7.4 %collective-permute-start = (bf16[128,512]{1,0:T(8,128)(2,1)S(1)}, bf16[128,512]{1,0:T(8,128)(2,1)S(1)}, u32[]{:S(2)}, u32[]{:S(2)}) collective-permute-start(bf16[128,512]{1,0:T(8,128)(2,1)S(1)} %get-tuple-element.32), channel_id=1, source_target_pairs={{0,1},{1,2},{2,3},{3,0},{4,5},{5,6},{6,7},{7,4},{8,9},{9,10},{10,1... | collective-permute-start | bytes 393224 | tf_op jit(solution)/shard_map/ppermute | solution.py:267
  4.9 10.6 %collective-permute-start.1 = (bf16[128,512]{1,0:T(8,128)(2,1)S(1)}, bf16[128,512]{1,0:T(8,128)(2,1)S(1)}, u32[]{:S(2)}, u32[]{:S(2)}) collective-permute-start(bf16[128,512]{1,0:T(8,128)(2,1)S(1)} %get-tuple-element.33), channel_id=1, source_target_pairs={{0,2},{1,3},{2,0},{3,1},{4,6},{5,7},{6,4},{7,5},{8,10},{9,11},{10,... | collective-permute-start | bytes 393224 | tf_op jit(solution)/shard_map/ppermute | solution.py:267
  6.0 12.3 %collective-permute-start.2 = (bf16[128,512]{1,0:T(8,128)(2,1)S(1)}, bf16[128,512]{1,0:T(8,128)(2,1)S(1)}, u32[]{:S(2)}, u32[]{:S(2)}) collective-permute-start(bf16[128,512]{1,0:T(8,128)(2,1)S(1)} %get-tuple-element.34), channel_id=1, source_target_pairs={{0,3},{1,0},{2,1},{3,2},{4,7},{5,4},{6,5},{7,6},{8,11},{9,8},{10,9... | collective-permute-start | bytes 393224 | tf_op jit(solution)/shard_map/ppermute | solution.py:267
  7.4 1.0 %copy-start.1 = (bf16[128,2048]{1,0:T(8,128)(2,1)S(1)}, bf16[128,2048]{1,0:T(8,128)(2,1)}, u32[]{:S(2)}) copy-start(bf16[128,2048]{1,0:T(8,128)(2,1)} %g_ref.1) | copy-start | bytes 1572868
  9.3 15.0 %collective-permute-start.5 = (bf16[4,128,512]{2,1,0:T(8,128)(2,1)S(1)}, bf16[4,128,512]{2,1,0:T(8,128)(2,1)S(1)}, u32[]{:S(2)}, u32[]{:S(2)}) collective-permute-start(bf16[4,128,512]{2,1,0:T(8,128)(2,1)S(1)} %get-tuple-element.38), channel_id=1, source_target_pairs={{0,4},{1,5},{2,6},{3,7},{4,0},{5,1},{6,2},{7,3},{8,12},{9,13},{10,... | collective-permute-start | bytes 1572872 | tf_op jit(solution)/shard_map/ppermute | solution.py:267
  18.9 1.7 %collective-permute-start.3 = (bf16[512,256]{1,0:T(8,128)(2,1)S(1)}, bf16[512,256]{1,0:T(8,128)(2,1)S(1)}, u32[]{:S(2)}, u32[]{:S(2)}) collective-permute-start(bf16[512,256]{1,0:T(8,128)(2,1)S(1)} %get-tuple-element.36), channel_id=1, source_target_pairs={{0,4},{1,5},{2,6},{3,7},{4,0},{5,1},{6,2},{7,3},{8,12},{9,13},{10,... | collective-permute-start | bytes 786440 | tf_op jit(solution)/shard_map/ppermute | solution.py:267
  21.2 28.8 %collective-permute-start.4 = (bf16[1024,256]{1,0:T(8,128)(2,1)S(1)}, bf16[1024,256]{1,0:T(8,128)(2,1)S(1)}, u32[]{:S(2)}, u32[]{:S(2)}) collective-permute-start(bf16[1024,256]{1,0:T(8,128)(2,1)S(1)} %shard_map.69.own_ref), channel_id=1, source_target_pairs={{0,8},{1,9},{2,10},{3,11},{4,12},{5,13},{6,14},{7,15},{8,16},{9,17... | collective-permute-start | bytes 1572872 | tf_op jit(solution)/shard_map/ppermute | solution.py:267
  25.0 7.2 %collective-permute-start.6 = (bf16[256,512]{1,0:T(8,128)(2,1)S(1)}, bf16[256,512]{1,0:T(8,128)(2,1)S(1)}, u32[]{:S(2)}, u32[]{:S(2)}) collective-permute-start(bf16[256,512]{1,0:T(8,128)(2,1)S(1)} %get-tuple-element.40), channel_id=1, source_target_pairs={{0,1},{1,2},{2,3},{3,0},{4,5},{5,6},{6,7},{7,4},{8,9},{9,10},{10,1... | collective-permute-start | bytes 786440 | tf_op jit(solution)/shard_map/ppermute | solution.py:267
  25.0 22.2 %collective-permute-start.7 = (bf16[256,512]{1,0:T(8,128)(2,1)S(1)}, bf16[256,512]{1,0:T(8,128)(2,1)S(1)}, u32[]{:S(2)}, u32[]{:S(2)}) collective-permute-start(bf16[256,512]{1,0:T(8,128)(2,1)S(1)} %get-tuple-element.41), channel_id=1, source_target_pairs={{0,2},{1,3},{2,0},{3,1},{4,6},{5,7},{6,4},{7,5},{8,10},{9,11},{10,... | collective-permute-start | bytes 786440 | tf_op jit(solution)/shard_map/ppermute | solution.py:267
  26.5 23.6 %collective-permute-start.8 = (bf16[256,512]{1,0:T(8,128)(2,1)S(1)}, bf16[256,512]{1,0:T(8,128)(2,1)S(1)}, u32[]{:S(2)}, u32[]{:S(2)}) collective-permute-start(bf16[256,512]{1,0:T(8,128)(2,1)S(1)} %get-tuple-element.42), channel_id=1, source_target_pairs={{0,3},{1,0},{2,1},{3,2},{4,7},{5,4},{6,5},{7,6},{8,11},{9,8},{10,9... | collective-permute-start | bytes 786440 | tf_op jit(solution)/shard_map/ppermute | solution.py:267
  60.4 6.3 %collective-permute-start.9 = (bf16[512,256]{1,0:T(8,128)(2,1)S(1)}, bf16[512,256]{1,0:T(8,128)(2,1)S(1)}, u32[]{:S(2)}, u32[]{:S(2)}) collective-permute-start(bf16[512,256]{1,0:T(8,128)(2,1)S(1)} %get-tuple-element.44), channel_id=1, source_target_pairs={{0,4},{1,5},{2,6},{3,7},{4,0},{5,1},{6,2},{7,3},{8,12},{9,13},{10,... | collective-permute-start | bytes 786440 | tf_op jit(solution)/shard_map/ppermute | solution.py:267
  61.0 9.8 %collective-permute-start.13 = (bf16[512,256]{1,0:T(8,128)(2,1)S(1)}, bf16[512,256]{1,0:T(8,128)(2,1)S(1)}, u32[]{:S(2)}, u32[]{:S(2)}) collective-permute-start(bf16[512,256]{1,0:T(8,128)(2,1)S(1)} %get-tuple-element.50), channel_id=1, source_target_pairs={{8,0},{9,1},{10,2},{11,3},{12,4},{13,5},{14,6},{15,7},{16,8},{17,9... | collective-permute-start | bytes 786440 | tf_op jit(solution)/shard_map/ppermute | solution.py:267
  64.0 6.7 %collective-permute-start.14 = (bf16[512,256]{1,0:T(8,128)(2,1)S(1)}, bf16[512,256]{1,0:T(8,128)(2,1)S(1)}, u32[]{:S(2)}, u32[]{:S(2)}) collective-permute-start(bf16[512,256]{1,0:T(8,128)(2,1)S(1)} %get-tuple-element.51), channel_id=1, source_target_pairs={{0,4},{1,5},{2,6},{3,7},{4,0},{5,1},{6,2},{7,3},{8,12},{9,13},{10,... | collective-permute-start | bytes 786440 | tf_op jit(solution)/shard_map/ppermute | solution.py:267
  64.4 12.1 %collective-permute-start.15 = (bf16[512,256]{1,0:T(8,128)(2,1)S(1)}, bf16[512,256]{1,0:T(8,128)(2,1)S(1)}, u32[]{:S(2)}, u32[]{:S(2)}) collective-permute-start(bf16[512,256]{1,0:T(8,128)(2,1)S(1)} %get-tuple-element.52), channel_id=1, source_target_pairs={{8,4},{9,5},{10,6},{11,7},{12,0},{13,1},{14,2},{15,3},{16,12},{17,... | collective-permute-start | bytes 786440 | tf_op jit(solution)/shard_map/ppermute | solution.py:267
  67.3 11.3 %collective-permute-start.10 = (bf16[128,512]{1,0:T(8,128)(2,1)S(1)}, bf16[128,512]{1,0:T(8,128)(2,1)S(1)}, u32[]{:S(2)}, u32[]{:S(2)}) collective-permute-start(bf16[128,512]{1,0:T(8,128)(2,1)S(1)} %get-tuple-element.46), channel_id=1, source_target_pairs={{0,1},{1,2},{2,3},{3,0},{4,5},{5,6},{6,7},{7,4},{8,9},{9,10},{10,1... | collective-permute-start | bytes 393224 | tf_op jit(solution)/shard_map/ppermute | solution.py:267
  67.4 12.6 %collective-permute-start.11 = (bf16[128,512]{1,0:T(8,128)(2,1)S(1)}, bf16[128,512]{1,0:T(8,128)(2,1)S(1)}, u32[]{:S(2)}, u32[]{:S(2)}) collective-permute-start(bf16[128,512]{1,0:T(8,128)(2,1)S(1)} %get-tuple-element.47), channel_id=1, source_target_pairs={{0,2},{1,3},{2,0},{3,1},{4,6},{5,7},{6,4},{7,5},{8,10},{9,11},{10,... | collective-permute-start | bytes 393224 | tf_op jit(solution)/shard_map/ppermute | solution.py:267
  70.8 15.6 %collective-permute-start.12 = (bf16[128,512]{1,0:T(8,128)(2,1)S(1)}, bf16[128,512]{1,0:T(8,128)(2,1)S(1)}, u32[]{:S(2)}, u32[]{:S(2)}) collective-permute-start(bf16[128,512]{1,0:T(8,128)(2,1)S(1)} %get-tuple-element.48), channel_id=1, source_target_pairs={{0,3},{1,0},{2,1},{3,2},{4,7},{5,4},{6,5},{7,6},{8,11},{9,8},{10,9... | collective-permute-start | bytes 393224 | tf_op jit(solution)/shard_map/ppermute | solution.py:267
  77.2 10.6 %collective-permute-start.16 = (bf16[128,512]{1,0:T(8,128)(2,1)S(1)}, bf16[128,512]{1,0:T(8,128)(2,1)S(1)}, u32[]{:S(2)}, u32[]{:S(2)}) collective-permute-start(bf16[128,512]{1,0:T(8,128)(2,1)S(1)} %get-tuple-element.54), channel_id=1, source_target_pairs={{0,1},{1,2},{2,3},{3,0},{4,5},{5,6},{6,7},{7,4},{8,9},{9,10},{10,1... | collective-permute-start | bytes 393224 | tf_op jit(solution)/shard_map/ppermute | solution.py:267
  77.2 12.7 %collective-permute-start.17 = (bf16[128,512]{1,0:T(8,128)(2,1)S(1)}, bf16[128,512]{1,0:T(8,128)(2,1)S(1)}, u32[]{:S(2)}, u32[]{:S(2)}) collective-permute-start(bf16[128,512]{1,0:T(8,128)(2,1)S(1)} %get-tuple-element.55), channel_id=1, source_target_pairs={{0,2},{1,3},{2,0},{3,1},{4,6},{5,7},{6,4},{7,5},{8,10},{9,11},{10,... | collective-permute-start | bytes 393224 | tf_op jit(solution)/shard_map/ppermute | solution.py:267
  78.6 13.4 %collective-permute-start.18 = (bf16[128,512]{1,0:T(8,128)(2,1)S(1)}, bf16[128,512]{1,0:T(8,128)(2,1)S(1)}, u32[]{:S(2)}, u32[]{:S(2)}) collective-permute-start(bf16[128,512]{1,0:T(8,128)(2,1)S(1)} %get-tuple-element.56), channel_id=1, source_target_pairs={{0,3},{1,0},{2,1},{3,2},{4,7},{5,4},{6,5},{7,6},{8,11},{9,8},{10,9... | collective-permute-start | bytes 393224 | tf_op jit(solution)/shard_map/ppermute | solution.py:267

commit v5 on v4

--- a/solution.py
+++ b/solution.py
@@ -16,26 +16,24 @@
 masked_value = -1e30
 contract_last = (((1,), (1,)), ((), ()))
 VMEM_SPEC = pl.BlockSpec(memory_space=pltpu.VMEM)
+ANY_SPEC = pl.BlockSpec(memory_space=pl.ANY)
 SMEM_SPEC = pl.BlockSpec(memory_space=pltpu.SMEM)
 
 
-def call(kernel, out_shape, operands, scratch=(), flops=0, transcendentals=0, vmem=16, spec=VMEM_SPEC):
-    outs = out_shape if isinstance(out_shape, tuple) else (out_shape,)
-    moved = sum(a.size * a.dtype.itemsize for a in operands + outs)
+def call(kernel, out_shape, operands, scratch=(), flops=0, transcendentals=0, vmem=16, spec=VMEM_SPEC, out_spec=VMEM_SPEC):
     return pl.pallas_call(
         kernel,
         out_shape=out_shape,
         in_specs=[SMEM_SPEC] + [spec] * (len(operands) - 1),
-        out_specs=jax.tree.map(lambda _: spec, out_shape),
+        out_specs=jax.tree.map(lambda _: out_spec, out_shape),
         scratch_shapes=list(scratch),
         compiler_params=pltpu.CompilerParams(vmem_limit_bytes=vmem * 2**20),
-        cost_estimate=pl.CostEstimate(flops=flops, bytes_accessed=moved, transcendentals=transcendentals),
+        cost_estimate=pl.CostEstimate(flops=flops, bytes_accessed=1, transcendentals=transcendentals),
     )(*operands)
 
 
 def copy_call(kernel, copies, out_shape, operands):
-    spec = pl.BlockSpec(memory_space=pltpu.HBM)
-    return call(kernel, out_shape, operands, (pltpu.SemaphoreType.DMA((copies,)),), spec=spec)
+    return call(kernel, out_shape, operands, (pltpu.SemaphoreType.DMA((copies,)),), spec=ANY_SPEC, out_spec=ANY_SPEC)
 
 
 def shape_of(dtype, *shape):
@@ -152,15 +150,17 @@
         out_ref[:, width:] = (wide(sibling_ref) + wide(far_ref)).astype(jnp.bfloat16)
 
 
-def attention_kernel(heads, place_ref, own_ref, prev_ref, *refs):
+def attention_kernel(heads, place_ref, own_ref, near_ref, far_ref, *refs):
     d = HEAD_SIZE
     count = 2 * heads
     block_refs, refs = refs[:heads], refs[heads:]
     dq_mine_ref, dq_other_ref, own_mine_ref, own_other_ref, prev_mine_ref, prev_other_ref = refs[:6]
-    qd_ref, dq_ref, own_kt_ref, prev_kt_ref, own_grad_ref, prev_grad_ref = refs[6:]
+    qd_ref, prev_ref, dq_ref, own_kt_ref, prev_kt_ref, own_grad_ref, prev_grad_ref = refs[6:]
     first, core = place_ref[0], place_ref[1]
     half = heads * BLOCK
     mine, other = at(core * half, half), at((1 - core) * half, half)
+    prev_ref[mine] = near_ref[...]
+    prev_ref[other] = far_ref[...]
     for k, block_ref in enumerate(block_refs):
         for c in range(2):
             rows = at((c * heads + source(place_ref, heads, k)) * BLOCK, BLOCK)
@@ -230,7 +230,7 @@
         ref[:, d:] = grad_ref[rows, d:].astype(ref.dtype)
 
 
-def attention_backward(heads, place, own, prev, blocks):
+def attention_backward(heads, place, own, near, far, blocks):
     half, d = heads * BLOCK, HEAD_SIZE
     whole = 2 * half
     low, wide = jnp.bfloat16, jnp.float32
@@ -239,6 +239,7 @@
     scratch = (
         pltpu.VMEM((whole, 4 * d), low),
         pltpu.VMEM((whole, 2 * d), low),
+        pltpu.VMEM((whole, 2 * d), low),
         pltpu.VMEM((d, whole), low),
         pltpu.VMEM((d, whole), low),
         pltpu.VMEM((whole, 2 * d), wide),
@@ -247,7 +248,7 @@
     return call(
         functools.partial(attention_kernel, heads),
         outs,
-        (place, own, prev) + tuple(blocks),
+        (place, own, near, far) + tuple(blocks),
         scratch,
         20 * whole * whole * d,
         2 * whole * whole,
@@ -283,24 +284,28 @@
 
     across = functools.partial(send, head_step=0)
     slab = shape_of(low, rows, 4 * d)
-    kvs = spread(copy_call(bind(pack_kv_kernel), 4 * heads, (slab,) * heads, (place, key_rows, saved_value_rows)))
+    kvs = copy_call(bind(pack_kv_kernel), 4 * heads, (slab,) * heads, (place, key_rows, saved_value_rows))
     qd_mine, qd_other = copy_call(
-        bind(pack_qd_kernel), 4 * heads, (shape_of(low, heads, rows, 4 * d),) * 2, (place, query_rows, out_grad)
-    )
+        bind(pack_qd_kernel),
+        4 * heads,
+        (shape_of(low, heads, rows, 4 * d),) * 2,
+        (place, query_rows, out_grad),
+    )
+    kvs = spread(kvs)
     qd_other = across(qd_other, chip_step=0, flip=1)
     mine, other = call(bind(gather_kv_kernel), (shape_of(low, heads * rows, 2 * d),) * 2, (place,) + kvs)
+    near = across(mine, chip_step=1, flip=0)
+    far = across(other, chip_step=1, flip=1)
+    blocks = call(
+        bind(merge_rows_kernel),
+        (shape_of(low, 2 * rows, 4 * d),) * heads,
+        (place, qd_mine, qd_other, kvs[-1][:8]),
+    )
+    blocks = spread(blocks)
     sibling = across(other, chip_step=0, flip=1)
-    blocks = spread(
-        call(
-            bind(merge_rows_kernel),
-            (shape_of(low, 2 * rows, 4 * d),) * heads,
-            (place, qd_mine, qd_other, mine[:8]),
-        )
-    )
     own = call(join_kernel, shape_of(low, 2 * heads * rows, 2 * d), (place, mine, sibling))
-    prev = across(own, chip_step=1, flip=0)
     dq_mine, dq_other, own_mine, own_other, prev_mine, prev_other = attention_backward(
-        heads, place, own, prev, blocks
+        heads, place, own, near, far, blocks
     )
     near_back = across(prev_mine, chip_step=-1, flip=0)
     far_back = across(prev_other, chip_step=-1, flip=1)

time: 93.7 us -> 96.7 us (1.032)
  waiting for transfers between devices: 49.5 us -> 51.5 us
  starting transfers between devices: 22.1 us -> 24 us
    ppermute x19 -> x20, waiting for transfers between devices: 49.5 us -> 51.5 us  [moved(): return lax.ppermute(value, ('chip', 'core', 'head'), pairs)]
    ppermute x19 -> x20, starting transfers between devices: 22.1 us -> 24 us  [moved(): return lax.ppermute(value, ('chip', 'core', 'head'), pairs)]
  transfers between devices with their start and end apart: 19 -> 20, of which waited for: 11 -> 11; matrix products, arithmetic and copies ran while one was open for 0% -> 0% of each run, Pallas kernels for 6% -> 5%
where the time goes in v5:
time: 96.7 us; the launch traced here: 96.4 us
  waiting for transfers between devices  51.5 us (53%)
  starting transfers between devices  24 us (25%)
  Pallas kernels  17.9 us (19%)
  local copies, waits for them, and re-layouts  2.09 us (2%)
    ppermute x20, waiting for transfers between devices, moved(): return lax.ppermute(value, ('chip', 'core', 'head'), pairs)  51.5 us
    ppermute x20, starting transfers between devices, moved(): return lax.ppermute(value, ('chip', 'core', 'head'), pairs)  24 us
    pallas_call x10, Pallas kernels, call(): pl.pallas_call(kernel, out_shape=out_shape, in_specs=[SMEM_SPEC] + [spec]...  17.9 us
    unnamed x8, local copies, waits for them, and re-layouts  2.09 us
  transfers between devices with their start and end apart: 20, of which 11 were waited for; matrix products, arithmetic and copies ran while one was open for 0% of the time, Pallas kernels for 5%

profile of v5, /device:TPU:13, one launch (start us, length us, event | category | flops | bytes accessed | tf_op | source)
XLA Modules:
  0.0 96.4 jit_solution(7548823728520652343)
XLA Ops:
  0.6 0.1 pad_add_fusion.place_ref
  0.7 0.0 copy-start
  0.7 1.0 %copy-done = bf16[128,2048]{1,0:T(8,128)(2,1)S(1)} copy-done((bf16[128,2048]{1,0:T(8,128)(2,1)S(1)}, bf16[128,2048]{1,0:T(8,128)(2,1)}, u32[]{:S(2)}) %copy-start) | copy-done | bytes 524312
  1.8 0.0 copy-start.1
  1.8 1.0 %copy-done.1 = bf16[128,2048]{1,0:T(8,128)(2,1)S(1)} copy-done((bf16[128,2048]{1,0:T(8,128)(2,1)S(1)}, bf16[128,2048]{1,0:T(8,128)(2,1)}, u32[]{:S(2)}) %copy-start.1) | copy-done | bytes 524312
  2.8 0.0 copy-start.2
  2.8 0.0 copy-start.3
  2.8 0.9 shard_map.70
  3.7 0.7 collective-permute-start.6
  4.5 0.0 copy-done.2
  4.5 0.0 copy-done.3
  4.5 0.9 shard_map.67
  5.3 1.3 %collective-permute-start = (bf16[128,512]{1,0:T(8,128)(2,1)S(1)}, bf16[128,512]{1,0:T(8,128)(2,1)S(1)}, u32[]{:S(2)}, u32[]{:S(2)}) collective-permute-start(bf16[128,512]{1,0:T(8,128)(2,1)S(1)} %get-tuple-element.32), channel_id=1, source_target_pairs={{0,1},{1,2},{2,3},{3,0},{4,5},{5,6},{6,7},{7,4},{8,9},{9,10},{10,1... | collective-permute-start | bytes 393224 | tf_op jit(solution)/shard_map/ppermute | solution.py:268
  6.7 1.1 %collective-permute-start.1 = (bf16[128,512]{1,0:T(8,128)(2,1)S(1)}, bf16[128,512]{1,0:T(8,128)(2,1)S(1)}, u32[]{:S(2)}, u32[]{:S(2)}) collective-permute-start(bf16[128,512]{1,0:T(8,128)(2,1)S(1)} %get-tuple-element.33), channel_id=1, source_target_pairs={{0,2},{1,3},{2,0},{3,1},{4,6},{5,7},{6,4},{7,5},{8,10},{9,11},{10,... | collective-permute-start | bytes 393224 | tf_op jit(solution)/shard_map/ppermute | solution.py:268
  7.8 1.4 %collective-permute-start.2 = (bf16[128,512]{1,0:T(8,128)(2,1)S(1)}, bf16[128,512]{1,0:T(8,128)(2,1)S(1)}, u32[]{:S(2)}, u32[]{:S(2)}) collective-permute-start(bf16[128,512]{1,0:T(8,128)(2,1)S(1)} %get-tuple-element.34), channel_id=1, source_target_pairs={{0,3},{1,0},{2,1},{3,2},{4,7},{5,4},{6,5},{7,6},{8,11},{9,8},{10,9... | collective-permute-start | bytes 393224 | tf_op jit(solution)/shard_map/ppermute | solution.py:268
  9.2 1.3 %collective-permute-done.refs_1_ = bf16[128,512]{1,0:T(8,128)(2,1)S(1)} collective-permute-done((bf16[128,512]{1,0:T(8,128)(2,1)S(1)}, bf16[128,512]{1,0:T(8,128)(2,1)S(1)}, u32[]{:S(2)}, u32[]{:S(2)}) %collective-permute-start) | collective-permute-done | bytes 131104 | tf_op jit(solution)/shard_map/ppermute | solution.py:268
  10.5 7.5 %collective-permute-done.1.refs_2_ = bf16[128,512]{1,0:T(8,128)(2,1)S(1)} collective-permute-done((bf16[128,512]{1,0:T(8,128)(2,1)S(1)}, bf16[128,512]{1,0:T(8,128)(2,1)S(1)}, u32[]{:S(2)}, u32[]{:S(2)}) %collective-permute-start.1) | collective-permute-done | bytes 131104 | tf_op jit(solution)/shard_map/ppermute | solution.py:268
  18.0 2.1 %collective-permute-done.2.refs_3_ = bf16[128,512]{1,0:T(8,128)(2,1)S(1)} collective-permute-done((bf16[128,512]{1,0:T(8,128)(2,1)S(1)}, bf16[128,512]{1,0:T(8,128)(2,1)S(1)}, u32[]{:S(2)}, u32[]{:S(2)}) %collective-permute-start.2) | collective-permute-done | bytes 131104 | tf_op jit(solution)/shard_map/ppermute | solution.py:268
  20.1 0.6 shard_map.68
  20.7 0.5 collective-permute-start.3
  21.2 3.0 %collective-permute-start.5 = (bf16[512,256]{1,0:T(8,128)(2,1)S(1)}, bf16[512,256]{1,0:T(8,128)(2,1)S(1)}, u32[]{:S(2)}, u32[]{:S(2)}) collective-permute-start(bf16[512,256]{1,0:T(8,128)(2,1)S(1)} %get-tuple-element.36), channel_id=1, source_target_pairs={{0,12},{1,13},{2,14},{3,15},{4,8},{5,9},{6,10},{7,11},{8,20},{9,21... | collective-permute-start | bytes 786440 | tf_op jit(solution)/shard_map/ppermute | solution.py:268
  24.3 1.9 %collective-permute-start.4 = (bf16[512,256]{1,0:T(8,128)(2,1)S(1)}, bf16[512,256]{1,0:T(8,128)(2,1)S(1)}, u32[]{:S(2)}, u32[]{:S(2)}) collective-permute-start(bf16[512,256]{1,0:T(8,128)(2,1)S(1)} %get-tuple-element.35.mine_ref), channel_id=1, source_target_pairs={{0,8},{1,9},{2,10},{3,11},{4,12},{5,13},{6,14},{7,15},{8,16},{9,17... | collective-permute-start | bytes 786440 | tf_op jit(solution)/shard_map/ppermute | solution.py:268
  26.2 0.0 collective-permute-done.6.other_ref
  26.2 0.6 shard_map.71
  26.9 0.1 collective-permute-start.7
  26.9 1.4 %collective-permute-start.8 = (bf16[256,512]{1,0:T(8,128)(2,1)S(1)}, bf16[256,512]{1,0:T(8,128)(2,1)S(1)}, u32[]{:S(2)}, u32[]{:S(2)}) collective-permute-start(bf16[256,512]{1,0:T(8,128)(2,1)S(1)} %get-tuple-element.41), channel_id=1, source_target_pairs={{0,2},{1,3},{2,0},{3,1},{4,6},{5,7},{6,4},{7,5},{8,10},{9,11},{10,... | collective-permute-start | bytes 786440 | tf_op jit(solution)/shard_map/ppermute | solution.py:268
  28.3 0.0 collective-permute-done.3.sibling_ref
  28.3 1.4 %collective-permute-start.9 = (bf16[256,512]{1,0:T(8,128)(2,1)S(1)}, bf16[256,512]{1,0:T(8,128)(2,1)S(1)}, u32[]{:S(2)}, u32[]{:S(2)}) collective-permute-start(bf16[256,512]{1,0:T(8,128)(2,1)S(1)} %get-tuple-element.42), channel_id=1, source_target_pairs={{0,3},{1,0},{2,1},{3,2},{4,7},{5,4},{6,5},{7,6},{8,11},{9,8},{10,9... | collective-permute-start | bytes 786440 | tf_op jit(solution)/shard_map/ppermute | solution.py:268
  29.7 0.6 shard_map.69.own_ref
  30.3 7.0 %collective-permute-done.4.near_ref = bf16[512,256]{1,0:T(8,128)(2,1)S(1)} collective-permute-done((bf16[512,256]{1,0:T(8,128)(2,1)S(1)}, bf16[512,256]{1,0:T(8,128)(2,1)S(1)}, u32[]{:S(2)}, u32[]{:S(2)}) %collective-permute-start.4) | collective-permute-done | bytes 262176 | tf_op jit(solution)/shard_map/ppermute | solution.py:268
  37.3 0.0 collective-permute-done.5.far_ref
  37.3 0.0 collective-permute-done.7.refs_1_
  37.3 12.0 %collective-permute-done.8.refs_2_ = bf16[256,512]{1,0:T(8,128)(2,1)S(1)} collective-permute-done((bf16[256,512]{1,0:T(8,128)(2,1)S(1)}, bf16[256,512]{1,0:T(8,128)(2,1)S(1)}, u32[]{:S(2)}, u32[]{:S(2)}) %collective-permute-start.8) | collective-permute-done | bytes 262176 | tf_op jit(solution)/shard_map/ppermute | solution.py:268
  49.3 2.6 %collective-permute-done.9.refs_3_ = bf16[256,512]{1,0:T(8,128)(2,1)S(1)} collective-permute-done((bf16[256,512]{1,0:T(8,128)(2,1)S(1)}, bf16[256,512]{1,0:T(8,128)(2,1)S(1)}, u32[]{:S(2)}, u32[]{:S(2)}) %collective-permute-start.9) | collective-permute-done | bytes 262176 | tf_op jit(solution)/shard_map/ppermute | solution.py:268
  51.9 10.3 %shard_map.72 = (bf16[512,256]{1,0:T(8,128)(2,1)S(1)}, bf16[512,256]{1,0:T(8,128)(2,1)S(1)}, f32[512,256]{1,0:T(8,128)S(1)}, bf16[512,256]{1,0:T(8,128)(2,1)S(1)...) custom-call(s32[3]{0:T(128)S(1)} %pad_add_fusion.place_ref, bf16[1024,256]{1,0:T(8,128)(2,1)S(1)} %shard_map.69.own_ref, ...), custom_call_target="tpu_custom_call" | custom-call | flops 2684354560 | bytes 1 | tf_op jit(solution)/shard_map/pallas_call | solution.py:24
  62.2 0.6 collective-permute-start.10
  62.8 4.2 %collective-permute-start.14 = (bf16[512,256]{1,0:T(8,128)(2,1)S(1)}, bf16[512,256]{1,0:T(8,128)(2,1)S(1)}, u32[]{:S(2)}, u32[]{:S(2)}) collective-permute-start(bf16[512,256]{1,0:T(8,128)(2,1)S(1)} %get-tuple-element.50), channel_id=1, source_target_pairs={{8,0},{9,1},{10,2},{11,3},{12,4},{13,5},{14,6},{15,7},{16,8},{17,9... | collective-permute-start | bytes 786440 | tf_op jit(solution)/shard_map/ppermute | solution.py:268
  67.0 0.4 collective-permute-start.15
  67.4 2.3 %collective-permute-start.16 = (bf16[512,256]{1,0:T(8,128)(2,1)S(1)}, bf16[512,256]{1,0:T(8,128)(2,1)S(1)}, u32[]{:S(2)}, u32[]{:S(2)}) collective-permute-start(bf16[512,256]{1,0:T(8,128)(2,1)S(1)} %get-tuple-element.52), channel_id=1, source_target_pairs={{8,4},{9,5},{10,6},{11,7},{12,0},{13,1},{14,2},{15,3},{16,12},{17,... | collective-permute-start | bytes 786440 | tf_op jit(solution)/shard_map/ppermute | solution.py:268
  69.7 0.0 collective-permute-done.10.other_ref
  69.7 0.6 shard_map.73
  70.3 0.1 collective-permute-start.11
  70.3 1.1 %collective-permute-start.12 = (bf16[128,512]{1,0:T(8,128)(2,1)S(1)}, bf16[128,512]{1,0:T(8,128)(2,1)S(1)}, u32[]{:S(2)}, u32[]{:S(2)}) collective-permute-start(bf16[128,512]{1,0:T(8,128)(2,1)S(1)} %get-tuple-element.47), channel_id=1, source_target_pairs={{0,2},{1,3},{2,0},{3,1},{4,6},{5,7},{6,4},{7,5},{8,10},{9,11},{10,... | collective-permute-start | bytes 393224 | tf_op jit(solution)/shard_map/ppermute | solution.py:268
  71.4 1.3 %collective-permute-done.14.near_ref = bf16[512,256]{1,0:T(8,128)(2,1)S(1)} collective-permute-done((bf16[512,256]{1,0:T(8,128)(2,1)S(1)}, bf16[512,256]{1,0:T(8,128)(2,1)S(1)}, u32[]{:S(2)}, u32[]{:S(2)}) %collective-permute-start.14) | collective-permute-done | bytes 262176 | tf_op jit(solution)/shard_map/ppermute | solution.py:268
  72.7 0.1 collective-permute-start.13
  72.8 0.0 collective-permute-done.15.sibling_ref
  72.8 5.8 %collective-permute-done.16.far_ref = bf16[512,256]{1,0:T(8,128)(2,1)S(1)} collective-permute-done((bf16[512,256]{1,0:T(8,128)(2,1)S(1)}, bf16[512,256]{1,0:T(8,128)(2,1)S(1)}, u32[]{:S(2)}, u32[]{:S(2)}) %collective-permute-start.16) | collective-permute-done | bytes 262176 | tf_op jit(solution)/shard_map/ppermute | solution.py:268
  78.6 0.7 shard_map.75
  79.3 0.1 collective-permute-start.17
  79.3 1.1 %collective-permute-start.18 = (bf16[128,512]{1,0:T(8,128)(2,1)S(1)}, bf16[128,512]{1,0:T(8,128)(2,1)S(1)}, u32[]{:S(2)}, u32[]{:S(2)}) collective-permute-start(bf16[128,512]{1,0:T(8,128)(2,1)S(1)} %get-tuple-element.55), channel_id=1, source_target_pairs={{0,2},{1,3},{2,0},{3,1},{4,6},{5,7},{6,4},{7,5},{8,10},{9,11},{10,... | collective-permute-start | bytes 393224 | tf_op jit(solution)/shard_map/ppermute | solution.py:268
  80.4 0.0 collective-permute-done.11.refs_1_
  80.4 1.4 %collective-permute-start.19 = (bf16[128,512]{1,0:T(8,128)(2,1)S(1)}, bf16[128,512]{1,0:T(8,128)(2,1)S(1)}, u32[]{:S(2)}, u32[]{:S(2)}) collective-permute-start(bf16[128,512]{1,0:T(8,128)(2,1)S(1)} %get-tuple-element.56), channel_id=1, source_target_pairs={{0,3},{1,0},{2,1},{3,2},{4,7},{5,4},{6,5},{7,6},{8,11},{9,8},{10,9... | collective-permute-start | bytes 393224 | tf_op jit(solution)/shard_map/ppermute | solution.py:268
  81.8 0.0 collective-permute-done.12.refs_2_
  81.8 7.5 %collective-permute-done.13.refs_3_ = bf16[128,512]{1,0:T(8,128)(2,1)S(1)} collective-permute-done((bf16[128,512]{1,0:T(8,128)(2,1)S(1)}, bf16[128,512]{1,0:T(8,128)(2,1)S(1)}, u32[]{:S(2)}, u32[]{:S(2)}) %collective-permute-start.13) | collective-permute-done | bytes 131104 | tf_op jit(solution)/shard_map/ppermute | solution.py:268
  89.3 1.4 %shard_map.74 = bf16[128,2048]{1,0:T(8,128)(2,1)} custom-call(s32[3]{0:T(128)S(1)} %pad_add_fusion.place_ref, bf16[128,512]{1,0:T(8,128)(2,1)S(1)} %get-tuple-element.45.refs_0_, bf16[128,512]{1,0:T(8,128)(2,1)S(1)} %collective-permute-done.11.refs_1_, bf16[128,512]{1,0:T(8,128)(2,1)S(1)} %collective-permute-done.12.refs_2_, ...), custom_call_target="tpu_custom_call" | custom-call | bytes 1 | tf_op jit(solution)/shard_map/pallas_call | solution.py:24
  90.7 0.0 collective-permute-done.17.refs_1_
  90.7 2.2 %collective-permute-done.18.refs_2_ = bf16[128,512]{1,0:T(8,128)(2,1)S(1)} collective-permute-done((bf16[128,512]{1,0:T(8,128)(2,1)S(1)}, bf16[128,512]{1,0:T(8,128)(2,1)S(1)}, u32[]{:S(2)}, u32[]{:S(2)}) %collective-permute-start.18) | collective-permute-done | bytes 131104 | tf_op jit(solution)/shard_map/ppermute | solution.py:268
  92.9 2.0 %collective-permute-done.19.refs_3_ = bf16[128,512]{1,0:T(8,128)(2,1)S(1)} collective-permute-done((bf16[128,512]{1,0:T(8,128)(2,1)S(1)}, bf16[128,512]{1,0:T(8,128)(2,1)S(1)}, u32[]{:S(2)}, u32[]{:S(2)}) %collective-permute-start.19) | collective-permute-done | bytes 131104 | tf_op jit(solution)/shard_map/ppermute | solution.py:268
  94.9 1.5 %shard_map.76 = (bf16[128,1024]{1,0:T(8,128)(2,1)}, bf16[128,1024]{1,0:T(8,128)(2,1)}) custom-call(s32[3]{0:T(128)S(1)} %pad_add_fusion.place_ref, bf16[128,512]{1,0:T(8,128)(2,1)S(1)} %get-tuple-element.53.refs_0_, bf16[128,512]{1,0:T(8,128)(2,1)S(1)} %collective-permute-done.17.refs_1_, bf16[128,512]{1,0:T(8,128)(2,1)S(1)} %collective-permute-done.18.refs_2_, ...), custom_call_target="tpu_custom_call" | custom-call | bytes 1 | tf_op jit(solution)/shard_map/pallas_call | solution.py:24
  (1 shorter events, 0.0 us)
Async XLA Ops:
  0.7 1.0 %copy-start = (bf16[128,2048]{1,0:T(8,128)(2,1)S(1)}, bf16[128,2048]{1,0:T(8,128)(2,1)}, u32[]{:S(2)}) copy-start(bf16[128,2048]{1,0:T(8,128)(2,1)} %q_ref.1) | copy-start | bytes 1572868
  1.8 1.0 %copy-start.1 = (bf16[128,2048]{1,0:T(8,128)(2,1)S(1)}, bf16[128,2048]{1,0:T(8,128)(2,1)}, u32[]{:S(2)}) copy-start(bf16[128,2048]{1,0:T(8,128)(2,1)} %g_ref.1) | copy-start | bytes 1572868
  2.8 1.7 %copy-start.2 = (bf16[128,1024]{1,0:T(8,128)(2,1)S(1)}, bf16[128,1024]{1,0:T(8,128)(2,1)}, u32[]{:S(2)}) copy-start(bf16[128,1024]{1,0:T(8,128)(2,1)} %k_ref.1) | copy-start | bytes 786436
  2.8 1.7 %copy-start.3 = (bf16[128,1024]{1,0:T(8,128)(2,1)S(1)}, bf16[128,1024]{1,0:T(8,128)(2,1)}, u32[]{:S(2)}) copy-start(bf16[128,1024]{1,0:T(8,128)(2,1)} %v_ref.1) | copy-start | bytes 786436
  3.7 22.5 %collective-permute-start.6 = (bf16[4,128,512]{2,1,0:T(8,128)(2,1)S(1)}, bf16[4,128,512]{2,1,0:T(8,128)(2,1)S(1)}, u32[]{:S(2)}, u32[]{:S(2)}) collective-permute-start(bf16[4,128,512]{2,1,0:T(8,128)(2,1)S(1)} %get-tuple-element.38), channel_id=1, source_target_pairs={{0,4},{1,5},{2,6},{3,7},{4,0},{5,1},{6,2},{7,3},{8,12},{9,13},{10,... | collective-permute-start | bytes 1572872 | tf_op jit(solution)/shard_map/ppermute | solution.py:268
  5.3 5.1 %collective-permute-start = (bf16[128,512]{1,0:T(8,128)(2,1)S(1)}, bf16[128,512]{1,0:T(8,128)(2,1)S(1)}, u32[]{:S(2)}, u32[]{:S(2)}) collective-permute-start(bf16[128,512]{1,0:T(8,128)(2,1)S(1)} %get-tuple-element.32), channel_id=1, source_target_pairs={{0,1},{1,2},{2,3},{3,0},{4,5},{5,6},{6,7},{7,4},{8,9},{9,10},{10,1... | collective-permute-start | bytes 393224 | tf_op jit(solution)/shard_map/ppermute | solution.py:268
  6.7 11.3 %collective-permute-start.1 = (bf16[128,512]{1,0:T(8,128)(2,1)S(1)}, bf16[128,512]{1,0:T(8,128)(2,1)S(1)}, u32[]{:S(2)}, u32[]{:S(2)}) collective-permute-start(bf16[128,512]{1,0:T(8,128)(2,1)S(1)} %get-tuple-element.33), channel_id=1, source_target_pairs={{0,2},{1,3},{2,0},{3,1},{4,6},{5,7},{6,4},{7,5},{8,10},{9,11},{10,... | collective-permute-start | bytes 393224 | tf_op jit(solution)/shard_map/ppermute | solution.py:268
  7.8 12.3 %collective-permute-start.2 = (bf16[128,512]{1,0:T(8,128)(2,1)S(1)}, bf16[128,512]{1,0:T(8,128)(2,1)S(1)}, u32[]{:S(2)}, u32[]{:S(2)}) collective-permute-start(bf16[128,512]{1,0:T(8,128)(2,1)S(1)} %get-tuple-element.34), channel_id=1, source_target_pairs={{0,3},{1,0},{2,1},{3,2},{4,7},{5,4},{6,5},{7,6},{8,11},{9,8},{10,9... | collective-permute-start | bytes 393224 | tf_op jit(solution)/shard_map/ppermute | solution.py:268
  20.7 7.6 %collective-permute-start.3 = (bf16[512,256]{1,0:T(8,128)(2,1)S(1)}, bf16[512,256]{1,0:T(8,128)(2,1)S(1)}, u32[]{:S(2)}, u32[]{:S(2)}) collective-permute-start(bf16[512,256]{1,0:T(8,128)(2,1)S(1)} %get-tuple-element.36), channel_id=1, source_target_pairs={{0,4},{1,5},{2,6},{3,7},{4,0},{5,1},{6,2},{7,3},{8,12},{9,13},{10,... | collective-permute-start | bytes 786440 | tf_op jit(solution)/shard_map/ppermute | solution.py:268
  21.2 16.0 %collective-permute-start.5 = (bf16[512,256]{1,0:T(8,128)(2,1)S(1)}, bf16[512,256]{1,0:T(8,128)(2,1)S(1)}, u32[]{:S(2)}, u32[]{:S(2)}) collective-permute-start(bf16[512,256]{1,0:T(8,128)(2,1)S(1)} %get-tuple-element.36), channel_id=1, source_target_pairs={{0,12},{1,13},{2,14},{3,15},{4,8},{5,9},{6,10},{7,11},{8,20},{9,21... | collective-permute-start | bytes 786440 | tf_op jit(solution)/shard_map/ppermute | solution.py:268
  24.3 13.0 %collective-permute-start.4 = (bf16[512,256]{1,0:T(8,128)(2,1)S(1)}, bf16[512,256]{1,0:T(8,128)(2,1)S(1)}, u32[]{:S(2)}, u32[]{:S(2)}) collective-permute-start(bf16[512,256]{1,0:T(8,128)(2,1)S(1)} %get-tuple-element.35.mine_ref), channel_id=1, source_target_pairs={{0,8},{1,9},{2,10},{3,11},{4,12},{5,13},{6,14},{7,15},{8,16},{9,17... | collective-permute-start | bytes 786440 | tf_op jit(solution)/shard_map/ppermute | solution.py:268
  26.9 10.4 %collective-permute-start.7 = (bf16[256,512]{1,0:T(8,128)(2,1)S(1)}, bf16[256,512]{1,0:T(8,128)(2,1)S(1)}, u32[]{:S(2)}, u32[]{:S(2)}) collective-permute-start(bf16[256,512]{1,0:T(8,128)(2,1)S(1)} %get-tuple-element.40), channel_id=1, source_target_pairs={{0,1},{1,2},{2,3},{3,0},{4,5},{5,6},{6,7},{7,4},{8,9},{9,10},{10,1... | collective-permute-start | bytes 786440 | tf_op jit(solution)/shard_map/ppermute | solution.py:268
  26.9 22.4 %collective-permute-start.8 = (bf16[256,512]{1,0:T(8,128)(2,1)S(1)}, bf16[256,512]{1,0:T(8,128)(2,1)S(1)}, u32[]{:S(2)}, u32[]{:S(2)}) collective-permute-start(bf16[256,512]{1,0:T(8,128)(2,1)S(1)} %get-tuple-element.41), channel_id=1, source_target_pairs={{0,2},{1,3},{2,0},{3,1},{4,6},{5,7},{6,4},{7,5},{8,10},{9,11},{10,... | collective-permute-start | bytes 786440 | tf_op jit(solution)/shard_map/ppermute | solution.py:268
  28.3 23.6 %collective-permute-start.9 = (bf16[256,512]{1,0:T(8,128)(2,1)S(1)}, bf16[256,512]{1,0:T(8,128)(2,1)S(1)}, u32[]{:S(2)}, u32[]{:S(2)}) collective-permute-start(bf16[256,512]{1,0:T(8,128)(2,1)S(1)} %get-tuple-element.42), channel_id=1, source_target_pairs={{0,3},{1,0},{2,1},{3,2},{4,7},{5,4},{6,5},{7,6},{8,11},{9,8},{10,9... | collective-permute-start | bytes 786440 | tf_op jit(solution)/shard_map/ppermute | solution.py:268
  62.2 7.5 %collective-permute-start.10 = (bf16[512,256]{1,0:T(8,128)(2,1)S(1)}, bf16[512,256]{1,0:T(8,128)(2,1)S(1)}, u32[]{:S(2)}, u32[]{:S(2)}) collective-permute-start(bf16[512,256]{1,0:T(8,128)(2,1)S(1)} %get-tuple-element.44), channel_id=1, source_target_pairs={{0,4},{1,5},{2,6},{3,7},{4,0},{5,1},{6,2},{7,3},{8,12},{9,13},{10,... | collective-permute-start | bytes 786440 | tf_op jit(solution)/shard_map/ppermute | solution.py:268
  62.8 9.9 %collective-permute-start.14 = (bf16[512,256]{1,0:T(8,128)(2,1)S(1)}, bf16[512,256]{1,0:T(8,128)(2,1)S(1)}, u32[]{:S(2)}, u32[]{:S(2)}) collective-permute-start(bf16[512,256]{1,0:T(8,128)(2,1)S(1)} %get-tuple-element.50), channel_id=1, source_target_pairs={{8,0},{9,1},{10,2},{11,3},{12,4},{13,5},{14,6},{15,7},{16,8},{17,9... | collective-permute-start | bytes 786440 | tf_op jit(solution)/shard_map/ppermute | solution.py:268
  67.0 5.8 %collective-permute-start.15 = (bf16[512,256]{1,0:T(8,128)(2,1)S(1)}, bf16[512,256]{1,0:T(8,128)(2,1)S(1)}, u32[]{:S(2)}, u32[]{:S(2)}) collective-permute-start(bf16[512,256]{1,0:T(8,128)(2,1)S(1)} %get-tuple-element.51), channel_id=1, source_target_pairs={{0,4},{1,5},{2,6},{3,7},{4,0},{5,1},{6,2},{7,3},{8,12},{9,13},{10,... | collective-permute-start | bytes 786440 | tf_op jit(solution)/shard_map/ppermute | solution.py:268
  67.4 11.2 %collective-permute-start.16 = (bf16[512,256]{1,0:T(8,128)(2,1)S(1)}, bf16[512,256]{1,0:T(8,128)(2,1)S(1)}, u32[]{:S(2)}, u32[]{:S(2)}) collective-permute-start(bf16[512,256]{1,0:T(8,128)(2,1)S(1)} %get-tuple-element.52), channel_id=1, source_target_pairs={{8,4},{9,5},{10,6},{11,7},{12,0},{13,1},{14,2},{15,3},{16,12},{17,... | collective-permute-start | bytes 786440 | tf_op jit(solution)/shard_map/ppermute | solution.py:268
  70.3 10.1 %collective-permute-start.11 = (bf16[128,512]{1,0:T(8,128)(2,1)S(1)}, bf16[128,512]{1,0:T(8,128)(2,1)S(1)}, u32[]{:S(2)}, u32[]{:S(2)}) collective-permute-start(bf16[128,512]{1,0:T(8,128)(2,1)S(1)} %get-tuple-element.46), channel_id=1, source_target_pairs={{0,1},{1,2},{2,3},{3,0},{4,5},{5,6},{6,7},{7,4},{8,9},{9,10},{10,1... | collective-permute-start | bytes 393224 | tf_op jit(solution)/shard_map/ppermute | solution.py:268
  70.3 11.4 %collective-permute-start.12 = (bf16[128,512]{1,0:T(8,128)(2,1)S(1)}, bf16[128,512]{1,0:T(8,128)(2,1)S(1)}, u32[]{:S(2)}, u32[]{:S(2)}) collective-permute-start(bf16[128,512]{1,0:T(8,128)(2,1)S(1)} %get-tuple-element.47), channel_id=1, source_target_pairs={{0,2},{1,3},{2,0},{3,1},{4,6},{5,7},{6,4},{7,5},{8,10},{9,11},{10,... | collective-permute-start | bytes 393224 | tf_op jit(solution)/shard_map/ppermute | solution.py:268
  72.7 16.6 %collective-permute-start.13 = (bf16[128,512]{1,0:T(8,128)(2,1)S(1)}, bf16[128,512]{1,0:T(8,128)(2,1)S(1)}, u32[]{:S(2)}, u32[]{:S(2)}) collective-permute-start(bf16[128,512]{1,0:T(8,128)(2,1)S(1)} %get-tuple-element.48), channel_id=1, source_target_pairs={{0,3},{1,0},{2,1},{3,2},{4,7},{5,4},{6,5},{7,6},{8,11},{9,8},{10,9... | collective-permute-start | bytes 393224 | tf_op jit(solution)/shard_map/ppermute | solution.py:268
  79.3 11.4 %collective-permute-start.17 = (bf16[128,512]{1,0:T(8,128)(2,1)S(1)}, bf16[128,512]{1,0:T(8,128)(2,1)S(1)}, u32[]{:S(2)}, u32[]{:S(2)}) collective-permute-start(bf16[128,512]{1,0:T(8,128)(2,1)S(1)} %get-tuple-element.54), channel_id=1, source_target_pairs={{0,1},{1,2},{2,3},{3,0},{4,5},{5,6},{6,7},{7,4},{8,9},{9,10},{10,1... | collective-permute-start | bytes 393224 | tf_op jit(solution)/shard_map/ppermute | solution.py:268
  79.3 13.6 %collective-permute-start.18 = (bf16[128,512]{1,0:T(8,128)(2,1)S(1)}, bf16[128,512]{1,0:T(8,128)(2,1)S(1)}, u32[]{:S(2)}, u32[]{:S(2)}) collective-permute-start(bf16[128,512]{1,0:T(8,128)(2,1)S(1)} %get-tuple-element.55), channel_id=1, source_target_pairs={{0,2},{1,3},{2,0},{3,1},{4,6},{5,7},{6,4},{7,5},{8,10},{9,11},{10,... | collective-permute-start | bytes 393224 | tf_op jit(solution)/shard_map/ppermute | solution.py:268
  80.4 14.5 %collective-permute-start.19 = (bf16[128,512]{1,0:T(8,128)(2,1)S(1)}, bf16[128,512]{1,0:T(8,128)(2,1)S(1)}, u32[]{:S(2)}, u32[]{:S(2)}) collective-permute-start(bf16[128,512]{1,0:T(8,128)(2,1)S(1)} %get-tuple-element.56), channel_id=1, source_target_pairs={{0,3},{1,0},{2,1},{3,2},{4,7},{5,4},{6,5},{7,6},{8,11},{9,8},{10,9... | collective-permute-start | bytes 393224 | tf_op jit(solution)/shard_map/ppermute | solution.py:268

commit v6 on v5

--- a/solution.py
+++ b/solution.py
@@ -21,6 +21,8 @@
 
 
 def call(kernel, out_shape, operands, scratch=(), flops=0, transcendentals=0, vmem=16, spec=VMEM_SPEC, out_spec=VMEM_SPEC):
+    outs = out_shape if isinstance(out_shape, tuple) else (out_shape,)
+    moved = sum(a.size * a.dtype.itemsize for a in operands + outs)
     return pl.pallas_call(
         kernel,
         out_shape=out_shape,
@@ -28,7 +30,7 @@
         out_specs=jax.tree.map(lambda _: out_spec, out_shape),
         scratch_shapes=list(scratch),
         compiler_params=pltpu.CompilerParams(vmem_limit_bytes=vmem * 2**20),
-        cost_estimate=pl.CostEstimate(flops=flops, bytes_accessed=1, transcendentals=transcendentals),
+        cost_estimate=pl.CostEstimate(flops=flops, bytes_accessed=moved, transcendentals=transcendentals),
     )(*operands)
 
 
@@ -102,7 +104,7 @@
     out_ref[at((1 - core) * half, half)] = sibling_ref[...]
 
 
-def merge_rows_kernel(heads, place_ref, mine_ref, other_ref, after_ref, *out_refs):
+def merge_rows_kernel(heads, place_ref, mine_ref, other_ref, *out_refs):
     core = place_ref[1]
     for k, out_ref in enumerate(out_refs):
         out_ref[at(core * BLOCK, BLOCK)] = mine_ref[k]
@@ -150,108 +152,137 @@
         out_ref[:, width:] = (wide(sibling_ref) + wide(far_ref)).astype(jnp.bfloat16)
 
 
-def attention_kernel(heads, place_ref, own_ref, near_ref, far_ref, *refs):
+def attention_block(i, count, q, g, own_ref, prev_ref, own_kt_ref, prev_kt_ref, own_grad_ref, prev_grad_ref, bias):
     d = HEAD_SIZE
-    count = 2 * heads
-    block_refs, refs = refs[:heads], refs[heads:]
-    dq_mine_ref, dq_other_ref, own_mine_ref, own_other_ref, prev_mine_ref, prev_other_ref = refs[:6]
-    qd_ref, prev_ref, dq_ref, own_kt_ref, prev_kt_ref, own_grad_ref, prev_grad_ref = refs[6:]
-    first, core = place_ref[0], place_ref[1]
-    half = heads * BLOCK
-    mine, other = at(core * half, half), at((1 - core) * half, half)
-    prev_ref[mine] = near_ref[...]
-    prev_ref[other] = far_ref[...]
-    for k, block_ref in enumerate(block_refs):
-        for c in range(2):
-            rows = at((c * heads + source(place_ref, heads, k)) * BLOCK, BLOCK)
-            qd_ref[rows] = block_ref[c * BLOCK : (c + 1) * BLOCK]
-    bias = jnp.where(first == 1, masked_value, 0.0).astype(jnp.float32)
-    own_kt_ref[...] = own_ref[:, :d].T
-    prev_kt_ref[...] = prev_ref[:, :d].T
+    low, high = i * BLOCK, (i + 1) * BLOCK
+    below, above = i > 0, i < count - 1
     key_row = lax.broadcasted_iota(jnp.int32, (BLOCK, 2 * BLOCK), 0)
     query_row = lax.broadcasted_iota(jnp.int32, (BLOCK, 2 * BLOCK), 1) % BLOCK
     own_seen = key_row <= query_row
     zero = jnp.zeros((BLOCK, 2 * BLOCK), jnp.bfloat16)
     dot_t = lambda a, b: lax.dot_general(a, b, contract_last, preferred_element_type=jnp.float32)
     dot = lambda a, b: jnp.dot(a, b, preferred_element_type=jnp.float32)
-    for i in range(count):
-        low, high = i * BLOCK, (i + 1) * BLOCK
-        below, above = i > 0, i < count - 1
-        q = jnp.concatenate([qd_ref[low:high, :d], qd_ref[low:high, d : 2 * d]], 0)
-        g = jnp.concatenate([qd_ref[low:high, 2 * d : 3 * d], qd_ref[low:high, 3 * d :]], 0)
-        s_own = dot_t(own_ref[:high, :d], q)
-        s_prev = dot_t(prev_ref[low:, :d], q) + bias
-        p_own = dot_t(own_ref[:high, d:], g)
-        p_prev = dot_t(prev_ref[low:, d:], g)
-        s_diag = jnp.where(own_seen, s_own[low:], s_prev[:BLOCK])
-        p_diag = jnp.where(own_seen, p_own[low:], p_prev[:BLOCK])
-        s = jnp.concatenate([s_own[:low]] * below + [s_diag] + [s_prev[BLOCK:]] * above, 0)
-        dp = jnp.concatenate([p_own[:low]] * below + [p_diag] + [p_prev[BLOCK:]] * above, 0)
-        top = jnp.max(s, axis=0, keepdims=True)
-        w = jnp.exp2((s - top) * (score_scale * LOG2_E))
-        inverse = 1.0 / jnp.sum(w, axis=0, keepdims=True)
-        delta = jnp.sum(w * dp, axis=0, keepdims=True) * inverse
-        attention = w * inverse
-        ds = (attention * (dp - delta)).astype(jnp.bfloat16)
-        low_attention = attention.astype(jnp.bfloat16)
-        split = lambda x: (
-            jnp.concatenate([x[:low]] * below + [jnp.where(own_seen, x[low:high], zero)], 0),
-            jnp.concatenate([jnp.where(own_seen, zero, x[low:high])] + [x[high:]] * above, 0),
-        )
-        ds_own, ds_prev = split(ds)
-        at_own, at_prev = split(low_attention)
-        dq_t = dot(own_kt_ref[:, :high], ds_own) + dot(prev_kt_ref[:, low:], ds_prev)
-        dq_t = dq_t * score_scale
-        dq_ref[low:high, :d] = dq_t[:, :BLOCK].T.astype(jnp.bfloat16)
-        dq_ref[low:high, d:] = dq_t[:, BLOCK:].T.astype(jnp.bfloat16)
-        dk_own, dk_prev = dot(ds_own, q), dot(ds_prev, q)
-        dv_own, dv_prev = dot(at_own, g), dot(at_prev, g)
-        if below:
-            own_grad_ref[:low, :d] += dk_own[:low]
-            own_grad_ref[:low, d:] += dv_own[:low]
-            prev_grad_ref[low:, :d] += dk_prev
-            prev_grad_ref[low:, d:] += dv_prev
-        else:
-            prev_grad_ref[:, :d] = dk_prev
-            prev_grad_ref[:, d:] = dv_prev
-        own_grad_ref[low:high, :d] = dk_own[low:]
-        own_grad_ref[low:high, d:] = dv_own[low:]
-    for ref, c in ((dq_mine_ref, core), (dq_other_ref, 1 - core)):
-        for k in range(heads):
-            rows = at((c * heads + onward(place_ref, heads, k)) * BLOCK, BLOCK)
-            ref[k * BLOCK : (k + 1) * BLOCK] = dq_ref[rows]
-    for ref, grad_ref, rows in (
-        (own_mine_ref, own_grad_ref, mine),
-        (own_other_ref, own_grad_ref, other),
-        (prev_mine_ref, prev_grad_ref, mine),
-        (prev_other_ref, prev_grad_ref, other),
-    ):
-        ref[:, :d] = (grad_ref[rows, :d] * score_scale).astype(ref.dtype)
-        ref[:, d:] = grad_ref[rows, d:].astype(ref.dtype)
-
-
-def attention_backward(heads, place, own, near, far, blocks):
+    s_own = dot_t(own_ref[:high, :d], q)
+    s_prev = dot_t(prev_ref[low:, :d], q) + bias
+    p_own = dot_t(own_ref[:high, d:], g)
+    p_prev = dot_t(prev_ref[low:, d:], g)
+    s_diag = jnp.where(own_seen, s_own[low:], s_prev[:BLOCK])
+    p_diag = jnp.where(own_seen, p_own[low:], p_prev[:BLOCK])
+    s = jnp.concatenate([s_own[:low]] * below + [s_diag] + [s_prev[BLOCK:]] * above, 0)
+    dp = jnp.concatenate([p_own[:low]] * below + [p_diag] + [p_prev[BLOCK:]] * above, 0)
+    top = jnp.max(s, axis=0, keepdims=True)
+    w = jnp.exp2((s - top) * (score_scale * LOG2_E))
+    inverse = 1.0 / jnp.sum(w, axis=0, keepdims=True)
+    delta = jnp.sum(w * dp, axis=0, keepdims=True) * inverse
+    attention = w * inverse
+    ds = (attention * (dp - delta)).astype(jnp.bfloat16)
+    low_attention = attention.astype(jnp.bfloat16)
+    split = lambda x: (
+        jnp.concatenate([x[:low]] * below + [jnp.where(own_seen, x[low:high], zero)], 0),
+        jnp.concatenate([jnp.where(own_seen, zero, x[low:high])] + [x[high:]] * above, 0),
+    )
+    ds_own, ds_prev = split(ds)
+    at_own, at_prev = split(low_attention)
+    own_grad_ref[:high, d:] += dot(at_own, g)
+    prev_grad_ref[low:, d:] += dot(at_prev, g)
+    own_grad_ref[:high, :d] += dot(ds_own, q)
+    prev_grad_ref[low:, :d] += dot(ds_prev, q)
+    dq_t = dot(own_kt_ref[:, :high], ds_own) + dot(prev_kt_ref[:, low:], ds_prev)
+    return dq_t * score_scale
+
+
+def attention_kernel(heads, steps, last, place_ref, own_ref, near_ref, far_ref, *refs):
+    d = HEAD_SIZE
+    count = 2 * heads
+    half = heads * BLOCK
+    block_refs, refs = refs[: len(steps)], refs[len(steps) :]
+    if last:
+        own_so_far_ref, prev_so_far_ref, mine_so_far_ref, other_so_far_ref = refs[:4]
+        dq_mine_ref, dq_other_ref, own_mine_ref, own_other_ref, prev_mine_ref, prev_other_ref = refs[4:10]
+        qd_ref, prev_ref, own_kt_ref, prev_kt_ref, own_grad_ref, prev_grad_ref = refs[10:]
+        own_grad_ref[...] = own_so_far_ref[...]
+        prev_grad_ref[...] = prev_so_far_ref[...]
+        dq_mine_ref[...] = mine_so_far_ref[...]
+        dq_other_ref[...] = other_so_far_ref[...]
+    else:
+        dq_mine_ref, dq_other_ref, own_grad_ref, prev_grad_ref = refs[:4]
+        qd_ref, prev_ref, own_kt_ref, prev_kt_ref = refs[4:]
+        own_grad_ref[...] = jnp.zeros_like(own_grad_ref)
+        prev_grad_ref[...] = jnp.zeros_like(prev_grad_ref)
+        dq_mine_ref[...] = jnp.zeros_like(dq_mine_ref)
+        dq_other_ref[...] = jnp.zeros_like(dq_other_ref)
+    first, core, head = place_ref[0], place_ref[1], place_ref[2]
+    mine, other = at(core * half, half), at((1 - core) * half, half)
+    prev_ref[mine] = near_ref[...]
+    prev_ref[other] = far_ref[...]
+    for n, block_ref in enumerate(block_refs):
+        qd_ref[n] = block_ref[: 2 * BLOCK]
+    bias = jnp.where(first == 1, masked_value, 0.0).astype(jnp.float32)
+    own_kt_ref[...] = own_ref[:, :d].T
+    prev_kt_ref[...] = prev_ref[:, :d].T
+
+    @pl.loop(0, len(steps))
+    def _(n):
+        step = steps[0] + n
+        z_here = lax.rem(head + heads - step, heads)
+        place_out = at(lax.rem(heads - step, heads) * BLOCK, BLOCK)
+        for z in range(heads):
+
+            @pl.when(z_here == z)
+            def _():
+                for c in range(2):
+                    rows = slice(c * BLOCK, (c + 1) * BLOCK)
+                    q = jnp.concatenate([qd_ref[n, rows, :d], qd_ref[n, rows, d : 2 * d]], 0)
+                    g = jnp.concatenate([qd_ref[n, rows, 2 * d : 3 * d], qd_ref[n, rows, 3 * d :]], 0)
+                    dq_t = attention_block(
+                        c * heads + z, count, q, g, own_ref, prev_ref, own_kt_ref, prev_kt_ref,
+                        own_grad_ref, prev_grad_ref, bias,
+                    )
+                    dq = jnp.concatenate([dq_t[:, :BLOCK].T, dq_t[:, BLOCK:].T], 1).astype(jnp.bfloat16)
+
+                    @pl.when(core == c)
+                    def _():
+                        dq_mine_ref[place_out] = dq
+
+                    @pl.when(core != c)
+                    def _():
+                        dq_other_ref[place_out] = dq
+
+    if last:
+        for ref, grad_ref, rows in (
+            (prev_mine_ref, prev_grad_ref, mine),
+            (prev_other_ref, prev_grad_ref, other),
+            (own_other_ref, own_grad_ref, other),
+            (own_mine_ref, own_grad_ref, mine),
+        ):
+            ref[:, :d] = (grad_ref[rows, :d] * score_scale).astype(ref.dtype)
+            ref[:, d:] = grad_ref[rows, d:].astype(ref.dtype)
+
+
+def attention_backward(heads, steps, place, own, near, far, blocks, so_far=()):
     half, d = heads * BLOCK, HEAD_SIZE
     whole = 2 * half
     low, wide = jnp.bfloat16, jnp.float32
     part = shape_of(low, half, 2 * d)
-    outs = (part, part, shape_of(wide, half, 2 * d), part, part, part)
     scratch = (
-        pltpu.VMEM((whole, 4 * d), low),
-        pltpu.VMEM((whole, 2 * d), low),
+        pltpu.VMEM((len(steps), 2 * BLOCK, 4 * d), low),
         pltpu.VMEM((whole, 2 * d), low),
         pltpu.VMEM((d, whole), low),
         pltpu.VMEM((d, whole), low),
-        pltpu.VMEM((whole, 2 * d), wide),
-        pltpu.VMEM((whole, 2 * d), wide),
-    )
+    )
+    sums = shape_of(wide, whole, 2 * d)
+    if so_far:
+        outs = (part, part, shape_of(wide, half, 2 * d), part, part, part)
+        scratch += (pltpu.VMEM((whole, 2 * d), wide), pltpu.VMEM((whole, 2 * d), wide))
+    else:
+        outs = (part, part, sums, sums)
     return call(
-        functools.partial(attention_kernel, heads),
+        functools.partial(attention_kernel, heads, steps, bool(so_far)),
         outs,
-        (place, own, near, far) + tuple(blocks),
+        (place, own, near, far) + tuple(blocks) + tuple(so_far),
         scratch,
-        20 * whole * whole * d,
-        2 * whole * whole,
+        10 * whole * whole * d,
+        whole * whole,
         32,
     )
 
@@ -298,14 +329,18 @@
     far = across(other, chip_step=1, flip=1)
     blocks = call(
         bind(merge_rows_kernel),
-        (shape_of(low, 2 * rows, 4 * d),) * heads,
-        (place, qd_mine, qd_other, kvs[-1][:8]),
+        (shape_of(low, 2 * rows + 16, 4 * d),) * heads,
+        (place, qd_mine, qd_other),
     )
     blocks = spread(blocks)
     sibling = across(other, chip_step=0, flip=1)
     own = call(join_kernel, shape_of(low, 2 * heads * rows, 2 * d), (place, mine, sibling))
+    early, late = tuple(range(heads // 2)), tuple(range(heads // 2, heads))
+    dq_mine, dq_other, own_sums, prev_sums = attention_backward(
+        heads, early, place, own, near, far, [blocks[k] for k in early]
+    )
     dq_mine, dq_other, own_mine, own_other, prev_mine, prev_other = attention_backward(
-        heads, place, own, near, far, blocks
+        heads, late, place, own, near, far, [blocks[k] for k in late], (own_sums, prev_sums, dq_mine, dq_other)
     )
     near_back = across(prev_mine, chip_step=-1, flip=0)
     far_back = across(prev_other, chip_step=-1, flip=1)

time: 96.7 us -> 90.8 us (0.939)
  waiting for transfers between devices: 51.5 us -> 40 us
  Pallas kernels: 17.9 us -> 21.3 us
  starting transfers between devices: 24 us -> 26 us
    ppermute x20, waiting for transfers between devices: 51.5 us -> 40 us  [moved(): return lax.ppermute(value, ('chip', 'core', 'head'), pairs)]
    pallas_call x10 -> x11, Pallas kernels: 17.9 us -> 21.3 us  [call(): pl.pallas_call(kernel, out_shape=out_shape, in_specs=[SMEM_SPEC] + [spec]...]
    ppermute x20, starting transfers between devices: 24 us -> 26 us  [moved(): return lax.ppermute(value, ('chip', 'core', 'head'), pairs)]
  transfers between devices with their start and end apart: 20 -> 20, of which waited for: 11 -> 12; matrix products, arithmetic and copies ran while one was open for 0% -> 0% of each run, Pallas kernels for 5% -> 13%
where the time goes in v6:
time: 90.8 us; the launch traced here: 90.5 us
  waiting for transfers between devices  40 us (44%)
  starting transfers between devices  26 us (29%)
  Pallas kernels  21.3 us (23%)
  local copies, waits for them, and re-layouts  2.09 us (2%)
  between operations  0.97 us (1%)
    ppermute x20, waiting for transfers between devices, moved(): return lax.ppermute(value, ('chip', 'core', 'head'), pairs)  40 us
    ppermute x20, starting transfers between devices, moved(): return lax.ppermute(value, ('chip', 'core', 'head'), pairs)  26 us
    pallas_call x11, Pallas kernels, call(): pl.pallas_call(kernel, out_shape=out_shape, in_specs=[SMEM_SPEC] + [spec]...  21.3 us
    unnamed x8, local copies, waits for them, and re-layouts  2.09 us
  transfers between devices with their start and end apart: 20, of which 12 were waited for; matrix products, arithmetic and copies ran while one was open for 0% of the time, Pallas kernels for 13%

profile of v6, /device:TPU:13, one launch (start us, length us, event | category | flops | bytes accessed | tf_op | source)
XLA Modules:
  0.0 90.5 jit_solution(9480611254256186248)
XLA Ops:
  0.6 0.1 pad_add_fusion.place_ref
  0.7 0.0 copy-start
  0.7 1.0 %copy-done = bf16[128,2048]{1,0:T(8,128)(2,1)S(1)} copy-done((bf16[128,2048]{1,0:T(8,128)(2,1)S(1)}, bf16[128,2048]{1,0:T(8,128)(2,1)}, u32[]{:S(2)}) %copy-start) | copy-done | bytes 524312
  1.8 0.0 copy-start.1
  1.8 1.0 %copy-done.1 = bf16[128,2048]{1,0:T(8,128)(2,1)S(1)} copy-done((bf16[128,2048]{1,0:T(8,128)(2,1)S(1)}, bf16[128,2048]{1,0:T(8,128)(2,1)}, u32[]{:S(2)}) %copy-start.1) | copy-done | bytes 524312
  2.8 0.0 copy-start.2
  2.8 0.0 copy-start.3
  2.8 0.9 shard_map.70
  3.7 0.7 collective-permute-start.6
  4.5 0.0 copy-done.2
  4.5 0.0 copy-done.3
  4.5 0.9 shard_map.67
  5.3 1.3 %collective-permute-start = (bf16[128,512]{1,0:T(8,128)(2,1)S(1)}, bf16[128,512]{1,0:T(8,128)(2,1)S(1)}, u32[]{:S(2)}, u32[]{:S(2)}) collective-permute-start(bf16[128,512]{1,0:T(8,128)(2,1)S(1)} %get-tuple-element.36), channel_id=1, source_target_pairs={{0,1},{1,2},{2,3},{3,0},{4,5},{5,6},{6,7},{7,4},{8,9},{9,10},{10,1... | collective-permute-start | bytes 393224 | tf_op jit(solution)/shard_map/ppermute | solution.py:299
  6.7 1.1 %collective-permute-start.1 = (bf16[128,512]{1,0:T(8,128)(2,1)S(1)}, bf16[128,512]{1,0:T(8,128)(2,1)S(1)}, u32[]{:S(2)}, u32[]{:S(2)}) collective-permute-start(bf16[128,512]{1,0:T(8,128)(2,1)S(1)} %get-tuple-element.37), channel_id=1, source_target_pairs={{0,2},{1,3},{2,0},{3,1},{4,6},{5,7},{6,4},{7,5},{8,10},{9,11},{10,... | collective-permute-start | bytes 393224 | tf_op jit(solution)/shard_map/ppermute | solution.py:299
  7.8 1.4 %collective-permute-start.2 = (bf16[128,512]{1,0:T(8,128)(2,1)S(1)}, bf16[128,512]{1,0:T(8,128)(2,1)S(1)}, u32[]{:S(2)}, u32[]{:S(2)}) collective-permute-start(bf16[128,512]{1,0:T(8,128)(2,1)S(1)} %get-tuple-element.38), channel_id=1, source_target_pairs={{0,3},{1,0},{2,1},{3,2},{4,7},{5,4},{6,5},{7,6},{8,11},{9,8},{10,9... | collective-permute-start | bytes 393224 | tf_op jit(solution)/shard_map/ppermute | solution.py:299
  9.2 1.3 %collective-permute-done.refs_1_ = bf16[128,512]{1,0:T(8,128)(2,1)S(1)} collective-permute-done((bf16[128,512]{1,0:T(8,128)(2,1)S(1)}, bf16[128,512]{1,0:T(8,128)(2,1)S(1)}, u32[]{:S(2)}, u32[]{:S(2)}) %collective-permute-start) | collective-permute-done | bytes 131104 | tf_op jit(solution)/shard_map/ppermute | solution.py:299
  10.5 7.5 %collective-permute-done.1.refs_2_ = bf16[128,512]{1,0:T(8,128)(2,1)S(1)} collective-permute-done((bf16[128,512]{1,0:T(8,128)(2,1)S(1)}, bf16[128,512]{1,0:T(8,128)(2,1)S(1)}, u32[]{:S(2)}, u32[]{:S(2)}) %collective-permute-start.1) | collective-permute-done | bytes 131104 | tf_op jit(solution)/shard_map/ppermute | solution.py:299
  18.0 2.1 %collective-permute-done.2.refs_3_ = bf16[128,512]{1,0:T(8,128)(2,1)S(1)} collective-permute-done((bf16[128,512]{1,0:T(8,128)(2,1)S(1)}, bf16[128,512]{1,0:T(8,128)(2,1)S(1)}, u32[]{:S(2)}, u32[]{:S(2)}) %collective-permute-start.2) | collective-permute-done | bytes 131104 | tf_op jit(solution)/shard_map/ppermute | solution.py:299
  20.1 0.6 shard_map.68
  20.7 0.5 collective-permute-start.3
  21.2 0.0 collective-permute-done.6.other_ref
  21.2 0.6 shard_map.71
  21.9 0.1 collective-permute-start.9
  21.9 3.1 %collective-permute-start.4 = (bf16[512,256]{1,0:T(8,128)(2,1)S(1)}, bf16[512,256]{1,0:T(8,128)(2,1)S(1)}, u32[]{:S(2)}, u32[]{:S(2)}) collective-permute-start(bf16[512,256]{1,0:T(8,128)(2,1)S(1)} %get-tuple-element.39.mine_ref), channel_id=1, source_target_pairs={{0,8},{1,9},{2,10},{3,11},{4,12},{5,13},{6,14},{7,15},{8,16},{9,17... | collective-permute-start | bytes 786440 | tf_op jit(solution)/shard_map/ppermute | solution.py:299
  25.1 1.9 %collective-permute-start.5 = (bf16[512,256]{1,0:T(8,128)(2,1)S(1)}, bf16[512,256]{1,0:T(8,128)(2,1)S(1)}, u32[]{:S(2)}, u32[]{:S(2)}) collective-permute-start(bf16[512,256]{1,0:T(8,128)(2,1)S(1)} %get-tuple-element.40), channel_id=1, source_target_pairs={{0,12},{1,13},{2,14},{3,15},{4,8},{5,9},{6,10},{7,11},{8,20},{9,21... | collective-permute-start | bytes 786440 | tf_op jit(solution)/shard_map/ppermute | solution.py:299
  27.0 1.4 %collective-permute-start.7 = (bf16[272,512]{1,0:T(8,128)(2,1)S(1)}, bf16[272,512]{1,0:T(8,128)(2,1)S(1)}, u32[]{:S(2)}, u32[]{:S(2)}) collective-permute-start(bf16[272,512]{1,0:T(8,128)(2,1)S(1)} %get-tuple-element.43), channel_id=1, source_target_pairs={{0,2},{1,3},{2,0},{3,1},{4,6},{5,7},{6,4},{7,5},{8,10},{9,11},{10,... | collective-permute-start | bytes 835592 | tf_op jit(solution)/shard_map/ppermute | solution.py:299
  28.4 0.0 collective-permute-done.3.sibling_ref
  28.4 1.4 %collective-permute-start.8 = (bf16[272,512]{1,0:T(8,128)(2,1)S(1)}, bf16[272,512]{1,0:T(8,128)(2,1)S(1)}, u32[]{:S(2)}, u32[]{:S(2)}) collective-permute-start(bf16[272,512]{1,0:T(8,128)(2,1)S(1)} %get-tuple-element.44), channel_id=1, source_target_pairs={{0,3},{1,0},{2,1},{3,2},{4,7},{5,4},{6,5},{7,6},{8,11},{9,8},{10,9... | collective-permute-start | bytes 835592 | tf_op jit(solution)/shard_map/ppermute | solution.py:299
  29.9 0.6 shard_map.69.own_ref
  30.4 2.2 %collective-permute-done.4.near_ref = bf16[512,256]{1,0:T(8,128)(2,1)S(1)} collective-permute-done((bf16[512,256]{1,0:T(8,128)(2,1)S(1)}, bf16[512,256]{1,0:T(8,128)(2,1)S(1)}, u32[]{:S(2)}, u32[]{:S(2)}) %collective-permute-start.4) | collective-permute-done | bytes 262176 | tf_op jit(solution)/shard_map/ppermute | solution.py:299
  32.6 5.8 %collective-permute-done.5.far_ref = bf16[512,256]{1,0:T(8,128)(2,1)S(1)} collective-permute-done((bf16[512,256]{1,0:T(8,128)(2,1)S(1)}, bf16[512,256]{1,0:T(8,128)(2,1)S(1)}, u32[]{:S(2)}, u32[]{:S(2)}) %collective-permute-start.5) | collective-permute-done | bytes 262176 | tf_op jit(solution)/shard_map/ppermute | solution.py:299
  38.4 0.0 collective-permute-done.9.refs_1_
  38.4 6.8 %shard_map.72 = (bf16[512,256]{1,0:T(8,128)(2,1)S(1)}, bf16[512,256]{1,0:T(8,128)(2,1)S(1)}, f32[1024,256]{1,0:T(8,128)S(1)}, f32[1024,256]{1,0:T(8,128)S(1)}) custom-call(s32[3]{0:T(128)S(1)} %pad_add_fusion.place_ref, bf16[1024,256]{1,0:T(8,128)(2,1)S(1)} %shard_map.69.own_ref, bf16[512,256]{1,0:T(8,128)(2,1)S(1)} %collective-permute-done.4.near_ref, ...), custom_call_target="tpu_custom_call" | custom-call | flops 1342177280 | bytes 4227084 | tf_op jit(solution)/shard_map/pallas_call | solution.py:26
  45.2 0.9 collective-permute-done.7.refs_0_
  46.1 2.4 %collective-permute-done.8.refs_1_ = bf16[272,512]{1,0:T(8,128)(2,1)S(1)} collective-permute-done((bf16[272,512]{1,0:T(8,128)(2,1)S(1)}, bf16[272,512]{1,0:T(8,128)(2,1)S(1)}, u32[]{:S(2)}, u32[]{:S(2)}) %collective-permute-start.8) | collective-permute-done | bytes 278560 | tf_op jit(solution)/shard_map/ppermute | solution.py:299
  48.5 6.9 %shard_map.73 = (bf16[512,256]{1,0:T(8,128)(2,1)S(1)}, bf16[512,256]{1,0:T(8,128)(2,1)S(1)}, f32[512,256]{1,0:T(8,128)S(1)}, bf16[512,256]{1,0:T(8,128)(2,1)S(1)...) custom-call(s32[3]{0:T(128)S(1)} %pad_add_fusion.place_ref, bf16[1024,256]{1,0:T(8,128)(2,1)S(1)} %shard_map.69.own_ref, ...), custom_call_target="tpu_custom_call" | custom-call | flops 1342177280 | bytes 6062092 | tf_op jit(solution)/shard_map/pallas_call | solution.py:26
  55.4 0.5 collective-permute-start.10
  56.0 4.5 %collective-permute-start.14 = (bf16[512,256]{1,0:T(8,128)(2,1)S(1)}, bf16[512,256]{1,0:T(8,128)(2,1)S(1)}, u32[]{:S(2)}, u32[]{:S(2)}) collective-permute-start(bf16[512,256]{1,0:T(8,128)(2,1)S(1)} %get-tuple-element.58), channel_id=1, source_target_pairs={{8,0},{9,1},{10,2},{11,3},{12,4},{13,5},{14,6},{15,7},{16,8},{17,9... | collective-permute-start | bytes 786440 | tf_op jit(solution)/shard_map/ppermute | solution.py:299
  60.4 0.4 collective-permute-start.15
  60.8 2.2 %collective-permute-start.16 = (bf16[512,256]{1,0:T(8,128)(2,1)S(1)}, bf16[512,256]{1,0:T(8,128)(2,1)S(1)}, u32[]{:S(2)}, u32[]{:S(2)}) collective-permute-start(bf16[512,256]{1,0:T(8,128)(2,1)S(1)} %get-tuple-element.60), channel_id=1, source_target_pairs={{8,4},{9,5},{10,6},{11,7},{12,0},{13,1},{14,2},{15,3},{16,12},{17,... | collective-permute-start | bytes 786440 | tf_op jit(solution)/shard_map/ppermute | solution.py:299
  63.1 0.0 collective-permute-done.10.other_ref
  63.1 0.6 shard_map.74
  63.7 0.1 collective-permute-start.11
  63.8 1.6 %collective-permute-start.12 = (bf16[128,512]{1,0:T(8,128)(2,1)S(1)}, bf16[128,512]{1,0:T(8,128)(2,1)S(1)}, u32[]{:S(2)}, u32[]{:S(2)}) collective-permute-start(bf16[128,512]{1,0:T(8,128)(2,1)S(1)} %get-tuple-element.55), channel_id=1, source_target_pairs={{0,2},{1,3},{2,0},{3,1},{4,6},{5,7},{6,4},{7,5},{8,10},{9,11},{10,... | collective-permute-start | bytes 393224 | tf_op jit(solution)/shard_map/ppermute | solution.py:299
  65.3 0.7 collective-permute-done.14.near_ref
  66.1 0.6 collective-permute-start.13
  66.7 0.0 collective-permute-done.15.sibling_ref
  66.7 5.1 %collective-permute-done.16.far_ref = bf16[512,256]{1,0:T(8,128)(2,1)S(1)} collective-permute-done((bf16[512,256]{1,0:T(8,128)(2,1)S(1)}, bf16[512,256]{1,0:T(8,128)(2,1)S(1)}, u32[]{:S(2)}, u32[]{:S(2)}) %collective-permute-start.16) | collective-permute-done | bytes 262176 | tf_op jit(solution)/shard_map/ppermute | solution.py:299
  71.8 0.7 shard_map.76
  72.4 0.1 collective-permute-start.17
  72.5 1.6 %collective-permute-start.18 = (bf16[128,512]{1,0:T(8,128)(2,1)S(1)}, bf16[128,512]{1,0:T(8,128)(2,1)S(1)}, u32[]{:S(2)}, u32[]{:S(2)}) collective-permute-start(bf16[128,512]{1,0:T(8,128)(2,1)S(1)} %get-tuple-element.63), channel_id=1, source_target_pairs={{0,2},{1,3},{2,0},{3,1},{4,6},{5,7},{6,4},{7,5},{8,10},{9,11},{10,... | collective-permute-start | bytes 393224 | tf_op jit(solution)/shard_map/ppermute | solution.py:299
  74.1 0.0 collective-permute-done.11.refs_1_
  74.1 1.4 %collective-permute-start.19 = (bf16[128,512]{1,0:T(8,128)(2,1)S(1)}, bf16[128,512]{1,0:T(8,128)(2,1)S(1)}, u32[]{:S(2)}, u32[]{:S(2)}) collective-permute-start(bf16[128,512]{1,0:T(8,128)(2,1)S(1)} %get-tuple-element.64), channel_id=1, source_target_pairs={{0,3},{1,0},{2,1},{3,2},{4,7},{5,4},{6,5},{7,6},{8,11},{9,8},{10,9... | collective-permute-start | bytes 393224 | tf_op jit(solution)/shard_map/ppermute | solution.py:299
  75.5 0.0 collective-permute-done.12.refs_2_
  75.5 7.7 %collective-permute-done.13.refs_3_ = bf16[128,512]{1,0:T(8,128)(2,1)S(1)} collective-permute-done((bf16[128,512]{1,0:T(8,128)(2,1)S(1)}, bf16[128,512]{1,0:T(8,128)(2,1)S(1)}, u32[]{:S(2)}, u32[]{:S(2)}) %collective-permute-start.13) | collective-permute-done | bytes 131104 | tf_op jit(solution)/shard_map/ppermute | solution.py:299
  83.2 1.4 %shard_map.75 = bf16[128,2048]{1,0:T(8,128)(2,1)} custom-call(s32[3]{0:T(128)S(1)} %pad_add_fusion.place_ref, bf16[128,512]{1,0:T(8,128)(2,1)S(1)} %get-tuple-element.53.refs_0_, bf16[128,512]{1,0:T(8,128)(2,1)S(1)} %collective-permute-done.11.refs_1_, bf16[128,512]{1,0:T(8,128)(2,1)S(1)} %collective-permute-done.12.refs_2_, ...), custom_call_target="tpu_custom_call" | custom-call | bytes 1048588 | tf_op jit(solution)/shard_map/pallas_call | solution.py:26
  84.6 0.0 collective-permute-done.17.refs_1_
  84.6 1.7 %collective-permute-done.18.refs_2_ = bf16[128,512]{1,0:T(8,128)(2,1)S(1)} collective-permute-done((bf16[128,512]{1,0:T(8,128)(2,1)S(1)}, bf16[128,512]{1,0:T(8,128)(2,1)S(1)}, u32[]{:S(2)}, u32[]{:S(2)}) %collective-permute-start.18) | collective-permute-done | bytes 131104 | tf_op jit(solution)/shard_map/ppermute | solution.py:299
  86.3 2.6 %collective-permute-done.19.refs_3_ = bf16[128,512]{1,0:T(8,128)(2,1)S(1)} collective-permute-done((bf16[128,512]{1,0:T(8,128)(2,1)S(1)}, bf16[128,512]{1,0:T(8,128)(2,1)S(1)}, u32[]{:S(2)}, u32[]{:S(2)}) %collective-permute-start.19) | collective-permute-done | bytes 131104 | tf_op jit(solution)/shard_map/ppermute | solution.py:299
  88.8 1.5 %shard_map.77 = (bf16[128,1024]{1,0:T(8,128)(2,1)}, bf16[128,1024]{1,0:T(8,128)(2,1)}) custom-call(s32[3]{0:T(128)S(1)} %pad_add_fusion.place_ref, bf16[128,512]{1,0:T(8,128)(2,1)S(1)} %get-tuple-element.61.refs_0_, bf16[128,512]{1,0:T(8,128)(2,1)S(1)} %collective-permute-done.17.refs_1_, bf16[128,512]{1,0:T(8,128)(2,1)S(1)} %collective-permute-done.18.refs_2_, ...), custom_call_target="tpu_custom_call" | custom-call | bytes 1048588 | tf_op jit(solution)/shard_map/pallas_call | solution.py:26
Async XLA Ops:
  0.7 1.0 %copy-start = (bf16[128,2048]{1,0:T(8,128)(2,1)S(1)}, bf16[128,2048]{1,0:T(8,128)(2,1)}, u32[]{:S(2)}) copy-start(bf16[128,2048]{1,0:T(8,128)(2,1)} %q_ref.1) | copy-start | bytes 1572868
  1.8 1.0 %copy-start.1 = (bf16[128,2048]{1,0:T(8,128)(2,1)S(1)}, bf16[128,2048]{1,0:T(8,128)(2,1)}, u32[]{:S(2)}) copy-start(bf16[128,2048]{1,0:T(8,128)(2,1)} %g_ref.1) | copy-start | bytes 1572868
  2.8 1.7 %copy-start.2 = (bf16[128,1024]{1,0:T(8,128)(2,1)S(1)}, bf16[128,1024]{1,0:T(8,128)(2,1)}, u32[]{:S(2)}) copy-start(bf16[128,1024]{1,0:T(8,128)(2,1)} %k_ref.1) | copy-start | bytes 786436
  2.8 1.7 %copy-start.3 = (bf16[128,1024]{1,0:T(8,128)(2,1)S(1)}, bf16[128,1024]{1,0:T(8,128)(2,1)}, u32[]{:S(2)}) copy-start(bf16[128,1024]{1,0:T(8,128)(2,1)} %v_ref.1) | copy-start | bytes 786436
  3.7 17.5 %collective-permute-start.6 = (bf16[4,128,512]{2,1,0:T(8,128)(2,1)S(1)}, bf16[4,128,512]{2,1,0:T(8,128)(2,1)S(1)}, u32[]{:S(2)}, u32[]{:S(2)}) collective-permute-start(bf16[4,128,512]{2,1,0:T(8,128)(2,1)S(1)} %get-tuple-element.42), channel_id=1, source_target_pairs={{0,4},{1,5},{2,6},{3,7},{4,0},{5,1},{6,2},{7,3},{8,12},{9,13},{10,... | collective-permute-start | bytes 1572872 | tf_op jit(solution)/shard_map/ppermute | solution.py:299
  5.3 5.1 %collective-permute-start = (bf16[128,512]{1,0:T(8,128)(2,1)S(1)}, bf16[128,512]{1,0:T(8,128)(2,1)S(1)}, u32[]{:S(2)}, u32[]{:S(2)}) collective-permute-start(bf16[128,512]{1,0:T(8,128)(2,1)S(1)} %get-tuple-element.36), channel_id=1, source_target_pairs={{0,1},{1,2},{2,3},{3,0},{4,5},{5,6},{6,7},{7,4},{8,9},{9,10},{10,1... | collective-permute-start | bytes 393224 | tf_op jit(solution)/shard_map/ppermute | solution.py:299
  6.7 11.3 %collective-permute-start.1 = (bf16[128,512]{1,0:T(8,128)(2,1)S(1)}, bf16[128,512]{1,0:T(8,128)(2,1)S(1)}, u32[]{:S(2)}, u32[]{:S(2)}) collective-permute-start(bf16[128,512]{1,0:T(8,128)(2,1)S(1)} %get-tuple-element.37), channel_id=1, source_target_pairs={{0,2},{1,3},{2,0},{3,1},{4,6},{5,7},{6,4},{7,5},{8,10},{9,11},{10,... | collective-permute-start | bytes 393224 | tf_op jit(solution)/shard_map/ppermute | solution.py:299
  7.8 12.3 %collective-permute-start.2 = (bf16[128,512]{1,0:T(8,128)(2,1)S(1)}, bf16[128,512]{1,0:T(8,128)(2,1)S(1)}, u32[]{:S(2)}, u32[]{:S(2)}) collective-permute-start(bf16[128,512]{1,0:T(8,128)(2,1)S(1)} %get-tuple-element.38), channel_id=1, source_target_pairs={{0,3},{1,0},{2,1},{3,2},{4,7},{5,4},{6,5},{7,6},{8,11},{9,8},{10,9... | collective-permute-start | bytes 393224 | tf_op jit(solution)/shard_map/ppermute | solution.py:299
  20.7 7.7 %collective-permute-start.3 = (bf16[512,256]{1,0:T(8,128)(2,1)S(1)}, bf16[512,256]{1,0:T(8,128)(2,1)S(1)}, u32[]{:S(2)}, u32[]{:S(2)}) collective-permute-start(bf16[512,256]{1,0:T(8,128)(2,1)S(1)} %get-tuple-element.40), channel_id=1, source_target_pairs={{0,4},{1,5},{2,6},{3,7},{4,0},{5,1},{6,2},{7,3},{8,12},{9,13},{10,... | collective-permute-start | bytes 786440 | tf_op jit(solution)/shard_map/ppermute | solution.py:299
  21.9 16.5 %collective-permute-start.9 = (bf16[272,512]{1,0:T(8,128)(2,1)S(1)}, bf16[272,512]{1,0:T(8,128)(2,1)S(1)}, u32[]{:S(2)}, u32[]{:S(2)}) collective-permute-start(bf16[272,512]{1,0:T(8,128)(2,1)S(1)} %get-tuple-element.46), channel_id=1, source_target_pairs={{0,1},{1,2},{2,3},{3,0},{4,5},{5,6},{6,7},{7,4},{8,9},{9,10},{10,1... | collective-permute-start | bytes 835592 | tf_op jit(solution)/shard_map/ppermute | solution.py:299
  21.9 10.7 %collective-permute-start.4 = (bf16[512,256]{1,0:T(8,128)(2,1)S(1)}, bf16[512,256]{1,0:T(8,128)(2,1)S(1)}, u32[]{:S(2)}, u32[]{:S(2)}) collective-permute-start(bf16[512,256]{1,0:T(8,128)(2,1)S(1)} %get-tuple-element.39.mine_ref), channel_id=1, source_target_pairs={{0,8},{1,9},{2,10},{3,11},{4,12},{5,13},{6,14},{7,15},{8,16},{9,17... | collective-permute-start | bytes 786440 | tf_op jit(solution)/shard_map/ppermute | solution.py:299
  25.1 13.3 %collective-permute-start.5 = (bf16[512,256]{1,0:T(8,128)(2,1)S(1)}, bf16[512,256]{1,0:T(8,128)(2,1)S(1)}, u32[]{:S(2)}, u32[]{:S(2)}) collective-permute-start(bf16[512,256]{1,0:T(8,128)(2,1)S(1)} %get-tuple-element.40), channel_id=1, source_target_pairs={{0,12},{1,13},{2,14},{3,15},{4,8},{5,9},{6,10},{7,11},{8,20},{9,21... | collective-permute-start | bytes 786440 | tf_op jit(solution)/shard_map/ppermute | solution.py:299
  27.0 19.1 %collective-permute-start.7 = (bf16[272,512]{1,0:T(8,128)(2,1)S(1)}, bf16[272,512]{1,0:T(8,128)(2,1)S(1)}, u32[]{:S(2)}, u32[]{:S(2)}) collective-permute-start(bf16[272,512]{1,0:T(8,128)(2,1)S(1)} %get-tuple-element.43), channel_id=1, source_target_pairs={{0,2},{1,3},{2,0},{3,1},{4,6},{5,7},{6,4},{7,5},{8,10},{9,11},{10,... | collective-permute-start | bytes 835592 | tf_op jit(solution)/shard_map/ppermute | solution.py:299
  28.4 20.1 %collective-permute-start.8 = (bf16[272,512]{1,0:T(8,128)(2,1)S(1)}, bf16[272,512]{1,0:T(8,128)(2,1)S(1)}, u32[]{:S(2)}, u32[]{:S(2)}) collective-permute-start(bf16[272,512]{1,0:T(8,128)(2,1)S(1)} %get-tuple-element.44), channel_id=1, source_target_pairs={{0,3},{1,0},{2,1},{3,2},{4,7},{5,4},{6,5},{7,6},{8,11},{9,8},{10,9... | collective-permute-start | bytes 835592 | tf_op jit(solution)/shard_map/ppermute | solution.py:299
  55.4 7.7 %collective-permute-start.10 = (bf16[512,256]{1,0:T(8,128)(2,1)S(1)}, bf16[512,256]{1,0:T(8,128)(2,1)S(1)}, u32[]{:S(2)}, u32[]{:S(2)}) collective-permute-start(bf16[512,256]{1,0:T(8,128)(2,1)S(1)} %get-tuple-element.52), channel_id=1, source_target_pairs={{0,4},{1,5},{2,6},{3,7},{4,0},{5,1},{6,2},{7,3},{8,12},{9,13},{10,... | collective-permute-start | bytes 786440 | tf_op jit(solution)/shard_map/ppermute | solution.py:299
  56.0 10.1 %collective-permute-start.14 = (bf16[512,256]{1,0:T(8,128)(2,1)S(1)}, bf16[512,256]{1,0:T(8,128)(2,1)S(1)}, u32[]{:S(2)}, u32[]{:S(2)}) collective-permute-start(bf16[512,256]{1,0:T(8,128)(2,1)S(1)} %get-tuple-element.58), channel_id=1, source_target_pairs={{8,0},{9,1},{10,2},{11,3},{12,4},{13,5},{14,6},{15,7},{16,8},{17,9... | collective-permute-start | bytes 786440 | tf_op jit(solution)/shard_map/ppermute | solution.py:299
  60.4 6.3 %collective-permute-start.15 = (bf16[512,256]{1,0:T(8,128)(2,1)S(1)}, bf16[512,256]{1,0:T(8,128)(2,1)S(1)}, u32[]{:S(2)}, u32[]{:S(2)}) collective-permute-start(bf16[512,256]{1,0:T(8,128)(2,1)S(1)} %get-tuple-element.59), channel_id=1, source_target_pairs={{0,4},{1,5},{2,6},{3,7},{4,0},{5,1},{6,2},{7,3},{8,12},{9,13},{10,... | collective-permute-start | bytes 786440 | tf_op jit(solution)/shard_map/ppermute | solution.py:299
  60.8 10.9 %collective-permute-start.16 = (bf16[512,256]{1,0:T(8,128)(2,1)S(1)}, bf16[512,256]{1,0:T(8,128)(2,1)S(1)}, u32[]{:S(2)}, u32[]{:S(2)}) collective-permute-start(bf16[512,256]{1,0:T(8,128)(2,1)S(1)} %get-tuple-element.60), channel_id=1, source_target_pairs={{8,4},{9,5},{10,6},{11,7},{12,0},{13,1},{14,2},{15,3},{16,12},{17,... | collective-permute-start | bytes 786440 | tf_op jit(solution)/shard_map/ppermute | solution.py:299
  63.7 10.4 %collective-permute-start.11 = (bf16[128,512]{1,0:T(8,128)(2,1)S(1)}, bf16[128,512]{1,0:T(8,128)(2,1)S(1)}, u32[]{:S(2)}, u32[]{:S(2)}) collective-permute-start(bf16[128,512]{1,0:T(8,128)(2,1)S(1)} %get-tuple-element.54), channel_id=1, source_target_pairs={{0,1},{1,2},{2,3},{3,0},{4,5},{5,6},{6,7},{7,4},{8,9},{9,10},{10,1... | collective-permute-start | bytes 393224 | tf_op jit(solution)/shard_map/ppermute | solution.py:299
  63.8 11.8 %collective-permute-start.12 = (bf16[128,512]{1,0:T(8,128)(2,1)S(1)}, bf16[128,512]{1,0:T(8,128)(2,1)S(1)}, u32[]{:S(2)}, u32[]{:S(2)}) collective-permute-start(bf16[128,512]{1,0:T(8,128)(2,1)S(1)} %get-tuple-element.55), channel_id=1, source_target_pairs={{0,2},{1,3},{2,0},{3,1},{4,6},{5,7},{6,4},{7,5},{8,10},{9,11},{10,... | collective-permute-start | bytes 393224 | tf_op jit(solution)/shard_map/ppermute | solution.py:299
  66.1 17.2 %collective-permute-start.13 = (bf16[128,512]{1,0:T(8,128)(2,1)S(1)}, bf16[128,512]{1,0:T(8,128)(2,1)S(1)}, u32[]{:S(2)}, u32[]{:S(2)}) collective-permute-start(bf16[128,512]{1,0:T(8,128)(2,1)S(1)} %get-tuple-element.56), channel_id=1, source_target_pairs={{0,3},{1,0},{2,1},{3,2},{4,7},{5,4},{6,5},{7,6},{8,11},{9,8},{10,9... | collective-permute-start | bytes 393224 | tf_op jit(solution)/shard_map/ppermute | solution.py:299
  72.4 12.2 %collective-permute-start.17 = (bf16[128,512]{1,0:T(8,128)(2,1)S(1)}, bf16[128,512]{1,0:T(8,128)(2,1)S(1)}, u32[]{:S(2)}, u32[]{:S(2)}) collective-permute-start(bf16[128,512]{1,0:T(8,128)(2,1)S(1)} %get-tuple-element.62), channel_id=1, source_target_pairs={{0,1},{1,2},{2,3},{3,0},{4,5},{5,6},{6,7},{7,4},{8,9},{9,10},{10,1... | collective-permute-start | bytes 393224 | tf_op jit(solution)/shard_map/ppermute | solution.py:299
  72.5 13.8 %collective-permute-start.18 = (bf16[128,512]{1,0:T(8,128)(2,1)S(1)}, bf16[128,512]{1,0:T(8,128)(2,1)S(1)}, u32[]{:S(2)}, u32[]{:S(2)}) collective-permute-start(bf16[128,512]{1,0:T(8,128)(2,1)S(1)} %get-tuple-element.63), channel_id=1, source_target_pairs={{0,2},{1,3},{2,0},{3,1},{4,6},{5,7},{6,4},{7,5},{8,10},{9,11},{10,... | collective-permute-start | bytes 393224 | tf_op jit(solution)/shard_map/ppermute | solution.py:299
  74.1 14.7 %collective-permute-start.19 = (bf16[128,512]{1,0:T(8,128)(2,1)S(1)}, bf16[128,512]{1,0:T(8,128)(2,1)S(1)}, u32[]{:S(2)}, u32[]{:S(2)}) collective-permute-start(bf16[128,512]{1,0:T(8,128)(2,1)S(1)} %get-tuple-element.64), channel_id=1, source_target_pairs={{0,3},{1,0},{2,1},{3,2},{4,7},{5,4},{6,5},{7,6},{8,11},{9,8},{10,9... | collective-permute-start | bytes 393224 | tf_op jit(solution)/shard_map/ppermute | solution.py:299

commit v7 on v6

--- a/solution.py
+++ b/solution.py
@@ -97,50 +97,55 @@
         other_ref[rows] = in_ref[:, width:]
 
 
-def join_kernel(place_ref, mine_ref, sibling_ref, out_ref):
+def join_kernel(place_ref, mine_ref, sibling_ref, out_ref, kt_ref):
     core = place_ref[1]
     half = mine_ref.shape[0]
     out_ref[at(core * half, half)] = mine_ref[...]
     out_ref[at((1 - core) * half, half)] = sibling_ref[...]
-
-
-def merge_rows_kernel(heads, place_ref, mine_ref, other_ref, *out_refs):
+    kt_ref[...] = out_ref[:, :HEAD_SIZE].T
+
+
+def merge_rows_kernel(heads, place_ref, mine_ref, other_ref, after_ref, *out_refs):
     core = place_ref[1]
     for k, out_ref in enumerate(out_refs):
         out_ref[at(core * BLOCK, BLOCK)] = mine_ref[k]
         out_ref[at((1 - core) * BLOCK, BLOCK)] = other_ref[k]
 
 
-def merge_columns_kernel(heads, place_ref, mine_ref, other_ref, *out_refs):
+def sort_dq_kernel(heads, place_ref, *refs):
+    in_refs, (mine_ref, other_ref) = refs[:heads], refs[heads:]
+    core = place_ref[1]
+    for k, in_ref in enumerate(in_refs):
+        mine_ref[k * BLOCK : (k + 1) * BLOCK] = in_ref[at(core * BLOCK, BLOCK)]
+        other_ref[k * BLOCK : (k + 1) * BLOCK] = in_ref[at((1 - core) * BLOCK, BLOCK)]
+
+
+def unpack_dq_kernel(heads, place_ref, mine_ref, sibling_ref, out_ref, sems):
     core = place_ref[1]
     width = 2 * HEAD_SIZE
-    for k, out_ref in enumerate(out_refs):
-        rows = slice(k * BLOCK, (k + 1) * BLOCK)
-        out_ref[:, at(core * width, width)] = mine_ref[rows]
-        out_ref[:, at((1 - core) * width, width)] = other_ref[rows]
-
-
-def unpack_dq_kernel(heads, place_ref, *refs):
-    in_refs, out_ref, sems = refs[:-2], refs[-2], refs[-1]
-    width = 4 * HEAD_SIZE
     pairs = []
-    for k, in_ref in enumerate(in_refs):
-        pairs.append((in_ref, out_ref.at[:, at(source(place_ref, heads, k) * width, width)]))
+    for k in range(heads):
+        z = source(place_ref, heads, k)
+        for ref, c in ((mine_ref, core), (sibling_ref, 1 - core)):
+            rows = pl.ds(k * BLOCK, BLOCK)
+            pairs.append((ref.at[rows], out_ref.at[:, at((2 * z + c) * width, width)]))
     copied(sems, pairs)
 
 
 def unpack_kv_kernel(heads, place_ref, *refs):
-    in_refs, k_ref, v_ref, sems = refs[:-3], refs[-3], refs[-2], refs[-1]
-    core = place_ref[1]
+    in_refs, (k_ref, v_ref) = refs[:heads], refs[heads:]
+    core, head = place_ref[1], place_ref[2]
     d = HEAD_SIZE
-    pairs = []
-    for k, in_ref in enumerate(in_refs):
-        z = source(place_ref, heads, k)
-        for n, g in enumerate((2 * z + core, 2 * z + 1 - core)):
-            columns = at(g * d, d)
-            pairs.append((in_ref.at[:, pl.ds(2 * n * d, d)], k_ref.at[:, columns]))
-            pairs.append((in_ref.at[:, pl.ds((2 * n + 1) * d, d)], v_ref.at[:, columns]))
-    copied(sems, pairs)
+    for h in range(heads):
+        for c in range(2):
+
+            @pl.when((head == h) & (core == c))
+            def _():
+                for k, in_ref in enumerate(in_refs):
+                    z = (h - k) % heads
+                    for n, g in enumerate((2 * z + c, 2 * z + 1 - c)):
+                        k_ref[:, g * d : (g + 1) * d] = in_ref[:, 2 * n * d : (2 * n + 1) * d]
+                        v_ref[:, g * d : (g + 1) * d] = in_ref[:, (2 * n + 1) * d : (2 * n + 2) * d]
 
 
 def add_kernel(heads, place_ref, own_ref, near_ref, sibling_ref, far_ref, *out_refs):
@@ -191,41 +196,37 @@
     return dq_t * score_scale
 
 
-def attention_kernel(heads, steps, last, place_ref, own_ref, near_ref, far_ref, *refs):
+def attention_kernel(heads, steps, last, place_ref, own_ref, own_kt_ref, a_ref, b_ref, *refs):
     d = HEAD_SIZE
     count = 2 * heads
     half = heads * BLOCK
     block_refs, refs = refs[: len(steps)], refs[len(steps) :]
     if last:
-        own_so_far_ref, prev_so_far_ref, mine_so_far_ref, other_so_far_ref = refs[:4]
-        dq_mine_ref, dq_other_ref, own_mine_ref, own_other_ref, prev_mine_ref, prev_other_ref = refs[4:10]
-        qd_ref, prev_ref, own_kt_ref, prev_kt_ref, own_grad_ref, prev_grad_ref = refs[10:]
+        own_so_far_ref, prev_so_far_ref = refs[:2]
+        own_mine_ref, own_other_ref, prev_mine_ref, prev_other_ref = refs[2:6]
+        dq_refs, (qd_ref, dq_ref, own_grad_ref, prev_grad_ref) = refs[6:-4], refs[-4:]
+        prev_ref, prev_kt_ref = a_ref, b_ref
         own_grad_ref[...] = own_so_far_ref[...]
         prev_grad_ref[...] = prev_so_far_ref[...]
-        dq_mine_ref[...] = mine_so_far_ref[...]
-        dq_other_ref[...] = other_so_far_ref[...]
     else:
-        dq_mine_ref, dq_other_ref, own_grad_ref, prev_grad_ref = refs[:4]
-        qd_ref, prev_ref, own_kt_ref, prev_kt_ref = refs[4:]
+        prev_ref, prev_kt_ref, own_grad_ref, prev_grad_ref = refs[:4]
+        dq_refs, (qd_ref, dq_ref) = refs[4:-2], refs[-2:]
         own_grad_ref[...] = jnp.zeros_like(own_grad_ref)
         prev_grad_ref[...] = jnp.zeros_like(prev_grad_ref)
-        dq_mine_ref[...] = jnp.zeros_like(dq_mine_ref)
-        dq_other_ref[...] = jnp.zeros_like(dq_other_ref)
     first, core, head = place_ref[0], place_ref[1], place_ref[2]
     mine, other = at(core * half, half), at((1 - core) * half, half)
-    prev_ref[mine] = near_ref[...]
-    prev_ref[other] = far_ref[...]
+    if not last:
+        prev_ref[mine] = a_ref[...]
+        prev_ref[other] = b_ref[...]
+        prev_kt_ref[...] = prev_ref[:, :d].T
     for n, block_ref in enumerate(block_refs):
         qd_ref[n] = block_ref[: 2 * BLOCK]
     bias = jnp.where(first == 1, masked_value, 0.0).astype(jnp.float32)
-    own_kt_ref[...] = own_ref[:, :d].T
-    prev_kt_ref[...] = prev_ref[:, :d].T
 
     @pl.loop(0, len(steps))
     def _(n):
         step = steps[0] + n
         z_here = lax.rem(head + heads - step, heads)
-        place_out = at(lax.rem(heads - step, heads) * BLOCK, BLOCK)
         for z in range(heads):
 
             @pl.when(z_here == z)
@@ -238,16 +239,11 @@
                         c * heads + z, count, q, g, own_ref, prev_ref, own_kt_ref, prev_kt_ref,
                         own_grad_ref, prev_grad_ref, bias,
                     )
-                    dq = jnp.concatenate([dq_t[:, :BLOCK].T, dq_t[:, BLOCK:].T], 1).astype(jnp.bfloat16)
-
-                    @pl.when(core == c)
-                    def _():
-                        dq_mine_ref[place_out] = dq
-
-                    @pl.when(core != c)
-                    def _():
-                        dq_other_ref[place_out] = dq
-
+                    dq_ref[n, rows, :d] = dq_t[:, :BLOCK].T.astype(jnp.bfloat16)
+                    dq_ref[n, rows, d:] = dq_t[:, BLOCK:].T.astype(jnp.bfloat16)
+
+    for n, ref in enumerate(dq_refs):
+        ref[...] = dq_ref[n]
     if last:
         for ref, grad_ref, rows in (
             (prev_mine_ref, prev_grad_ref, mine),
@@ -259,32 +255,31 @@
             ref[:, d:] = grad_ref[rows, d:].astype(ref.dtype)
 
 
-def attention_backward(heads, steps, place, own, near, far, blocks, so_far=()):
+def attention_backward(heads, steps, place, own, prev, blocks, so_far=()):
     half, d = heads * BLOCK, HEAD_SIZE
     whole = 2 * half
     low, wide = jnp.bfloat16, jnp.float32
     part = shape_of(low, half, 2 * d)
+    sums = shape_of(wide, whole, 2 * d)
     scratch = (
         pltpu.VMEM((len(steps), 2 * BLOCK, 4 * d), low),
-        pltpu.VMEM((whole, 2 * d), low),
-        pltpu.VMEM((d, whole), low),
-        pltpu.VMEM((d, whole), low),
-    )
-    sums = shape_of(wide, whole, 2 * d)
+        pltpu.VMEM((len(steps), 2 * BLOCK, 2 * d), low),
+    )
     if so_far:
-        outs = (part, part, shape_of(wide, half, 2 * d), part, part, part)
+        outs = (shape_of(wide, half, 2 * d), part, part, part)
         scratch += (pltpu.VMEM((whole, 2 * d), wide), pltpu.VMEM((whole, 2 * d), wide))
     else:
-        outs = (part, part, sums, sums)
-    return call(
+        outs = (shape_of(low, whole, 2 * d), shape_of(low, d, whole), sums, sums)
+    outs = call(
         functools.partial(attention_kernel, heads, steps, bool(so_far)),
-        outs,
-        (place, own, near, far) + tuple(blocks) + tuple(so_far),
+        outs + (shape_of(low, 2 * BLOCK, 2 * d),) * len(steps),
+        (place,) + tuple(own) + tuple(prev) + tuple(blocks) + tuple(so_far),
         scratch,
         10 * whole * whole * d,
         whole * whole,
         32,
     )
+    return outs[:4], outs[4:]
 
 
 def moved(value, chips, heads, chip_step, flip, head_step):
@@ -330,29 +325,39 @@
     blocks = call(
         bind(merge_rows_kernel),
         (shape_of(low, 2 * rows + 16, 4 * d),) * heads,
-        (place, qd_mine, qd_other),
+        (place, qd_mine, qd_other, mine[:8]),
     )
     blocks = spread(blocks)
     sibling = across(other, chip_step=0, flip=1)
-    own = call(join_kernel, shape_of(low, 2 * heads * rows, 2 * d), (place, mine, sibling))
+    own = call(
+        join_kernel,
+        (shape_of(low, 2 * heads * rows, 2 * d), shape_of(low, d, 2 * heads * rows)),
+        (place, mine, sibling),
+    )
     early, late = tuple(range(heads // 2)), tuple(range(heads // 2, heads))
-    dq_mine, dq_other, own_sums, prev_sums = attention_backward(
-        heads, early, place, own, near, far, [blocks[k] for k in early]
-    )
-    dq_mine, dq_other, own_mine, own_other, prev_mine, prev_other = attention_backward(
-        heads, late, place, own, near, far, [blocks[k] for k in late], (own_sums, prev_sums, dq_mine, dq_other)
-    )
+    prev_and_sums, dq_early = attention_backward(heads, early, place, own, (near, far), [blocks[k] for k in early])
+    grads, dq_late = attention_backward(
+        heads, late, place, own, prev_and_sums[:2], [blocks[k] for k in late], prev_and_sums[2:]
+    )
+    own_mine, own_other, prev_mine, prev_other = grads
     near_back = across(prev_mine, chip_step=-1, flip=0)
     far_back = across(prev_other, chip_step=-1, flip=1)
     sibling_back = across(own_other, chip_step=0, flip=1)
-    dq_other = across(dq_other, chip_step=0, flip=1)
-    dqs = spread(call(bind(merge_columns_kernel), (slab,) * heads, (place, dq_mine, dq_other)))
-    query_grad = copy_call(bind(unpack_dq_kernel), heads, shape_of(low, *query_rows.shape), (place,) + dqs)
-    totals = spread(
-        call(bind(add_kernel), (slab,) * heads, (place, own_mine, near_back, sibling_back, far_back))
-    )
-    key_grad, value_grad = copy_call(
-        bind(unpack_kv_kernel), 4 * heads, (shape_of(low, *key_rows.shape),) * 2, (place,) + totals
+    back = dict(zip(early + late, dq_early + dq_late))
+    dqs = [
+        send(back[heads - k], chip_step=0, flip=0, head_step=k) if k else back[0] for k in range(heads)
+    ]
+    totals = call(bind(add_kernel), (slab,) * heads, (place, own_mine, near_back, sibling_back, far_back))
+    dq_mine, dq_other = call(
+        bind(sort_dq_kernel), (shape_of(low, heads * rows, 2 * d),) * 2, (place,) + tuple(dqs)
+    )
+    dq_sibling = across(dq_other, chip_step=0, flip=1)
+    query_grad = copy_call(
+        bind(unpack_dq_kernel), 2 * heads, shape_of(low, *query_rows.shape), (place, dq_mine, dq_sibling)
+    )
+    totals = spread(totals)
+    key_grad, value_grad = call(
+        bind(unpack_kv_kernel), (shape_of(low, *key_rows.shape),) * 2, (place,) + totals
     )
     return query_grad, key_grad, value_grad
 

time: 90.8 us -> 92.7 us (1.021); the launches traced: 90.5 us -> 91.2 us
  starting transfers between devices: 26 us -> 31.5 us
  waiting for transfers between devices: 40 us -> 36.9 us
  Pallas kernels: 21.3 us -> 19.9 us
    ppermute x20, starting transfers between devices: 26 us -> 31.5 us  [moved(): return lax.ppermute(value, ('chip', 'core', 'head'), pairs)]
    ppermute x20, waiting for transfers between devices: 40 us -> 36.9 us  [moved(): return lax.ppermute(value, ('chip', 'core', 'head'), pairs)]
    pallas_call x11, Pallas kernels: 21.3 us -> 19.9 us  [call(): pl.pallas_call(kernel, out_shape=out_shape, in_specs=[SMEM_SPEC] + [spec]...]
  transfers between devices with their start and end apart: 20 -> 20, of which waited for: 12 -> 10; matrix products, arithmetic and copies ran while one was open for 0% -> 0% of each run, Pallas kernels for 13% -> 19%
where the time goes in v7:
time: 92.7 us; the launch traced here: 91.2 us
  waiting for transfers between devices  36.9 us (40%)
  starting transfers between devices  31.5 us (34%)
  Pallas kernels  19.9 us (21%)
  local copies, waits for them, and re-layouts  2.09 us (2%)
    ppermute x20, waiting for transfers between devices, moved(): return lax.ppermute(value, ('chip', 'core', 'head'), pairs)  36.9 us
    ppermute x20, starting transfers between devices, moved(): return lax.ppermute(value, ('chip', 'core', 'head'), pairs)  31.5 us
    pallas_call x11, Pallas kernels, call(): pl.pallas_call(kernel, out_shape=out_shape, in_specs=[SMEM_SPEC] + [spec]...  19.9 us
    unnamed x8, local copies, waits for them, and re-layouts  2.09 us
  transfers between devices with their start and end apart: 20, of which 10 were waited for; matrix products, arithmetic and copies ran while one was open for 0% of the time, Pallas kernels for 19%

profile of v7, /device:TPU:13, one launch (start us, length us, event | category | flops | bytes accessed | tf_op | source)
XLA Modules:
  0.0 91.2 jit_solution(14702955015591046723)
XLA Ops:
  0.6 0.1 pad_add_fusion.place_ref
  0.7 0.0 copy-start
  0.7 1.0 %copy-done = bf16[128,2048]{1,0:T(8,128)(2,1)S(1)} copy-done((bf16[128,2048]{1,0:T(8,128)(2,1)S(1)}, bf16[128,2048]{1,0:T(8,128)(2,1)}, u32[]{:S(2)}) %copy-start) | copy-done | bytes 524312
  1.8 0.0 copy-start.1
  1.8 1.0 %copy-done.1 = bf16[128,2048]{1,0:T(8,128)(2,1)S(1)} copy-done((bf16[128,2048]{1,0:T(8,128)(2,1)S(1)}, bf16[128,2048]{1,0:T(8,128)(2,1)}, u32[]{:S(2)}) %copy-start.1) | copy-done | bytes 524312
  2.8 0.0 copy-start.2
  2.8 0.0 copy-start.3
  2.8 0.9 shard_map.70
  3.7 0.7 collective-permute-start.6
  4.5 0.0 copy-done.2
  4.5 0.0 copy-done.3
  4.5 0.9 shard_map.67
  5.3 1.3 %collective-permute-start = (bf16[128,512]{1,0:T(8,128)(2,1)S(1)}, bf16[128,512]{1,0:T(8,128)(2,1)S(1)}, u32[]{:S(2)}, u32[]{:S(2)}) collective-permute-start(bf16[128,512]{1,0:T(8,128)(2,1)S(1)} %get-tuple-element.38), channel_id=1, source_target_pairs={{0,1},{1,2},{2,3},{3,0},{4,5},{5,6},{6,7},{7,4},{8,9},{9,10},{10,1... | collective-permute-start | bytes 393224 | tf_op jit(solution)/shard_map/ppermute | solution.py:294
  6.7 1.1 %collective-permute-start.1 = (bf16[128,512]{1,0:T(8,128)(2,1)S(1)}, bf16[128,512]{1,0:T(8,128)(2,1)S(1)}, u32[]{:S(2)}, u32[]{:S(2)}) collective-permute-start(bf16[128,512]{1,0:T(8,128)(2,1)S(1)} %get-tuple-element.39), channel_id=1, source_target_pairs={{0,2},{1,3},{2,0},{3,1},{4,6},{5,7},{6,4},{7,5},{8,10},{9,11},{10,... | collective-permute-start | bytes 393224 | tf_op jit(solution)/shard_map/ppermute | solution.py:294
  7.8 1.4 %collective-permute-start.2 = (bf16[128,512]{1,0:T(8,128)(2,1)S(1)}, bf16[128,512]{1,0:T(8,128)(2,1)S(1)}, u32[]{:S(2)}, u32[]{:S(2)}) collective-permute-start(bf16[128,512]{1,0:T(8,128)(2,1)S(1)} %get-tuple-element.40), channel_id=1, source_target_pairs={{0,3},{1,0},{2,1},{3,2},{4,7},{5,4},{6,5},{7,6},{8,11},{9,8},{10,9... | collective-permute-start | bytes 393224 | tf_op jit(solution)/shard_map/ppermute | solution.py:294
  9.2 1.3 %collective-permute-done.refs_1_ = bf16[128,512]{1,0:T(8,128)(2,1)S(1)} collective-permute-done((bf16[128,512]{1,0:T(8,128)(2,1)S(1)}, bf16[128,512]{1,0:T(8,128)(2,1)S(1)}, u32[]{:S(2)}, u32[]{:S(2)}) %collective-permute-start) | collective-permute-done | bytes 131104 | tf_op jit(solution)/shard_map/ppermute | solution.py:294
  10.5 7.5 %collective-permute-done.1.refs_2_ = bf16[128,512]{1,0:T(8,128)(2,1)S(1)} collective-permute-done((bf16[128,512]{1,0:T(8,128)(2,1)S(1)}, bf16[128,512]{1,0:T(8,128)(2,1)S(1)}, u32[]{:S(2)}, u32[]{:S(2)}) %collective-permute-start.1) | collective-permute-done | bytes 131104 | tf_op jit(solution)/shard_map/ppermute | solution.py:294
  18.0 2.1 %collective-permute-done.2.refs_3_ = bf16[128,512]{1,0:T(8,128)(2,1)S(1)} collective-permute-done((bf16[128,512]{1,0:T(8,128)(2,1)S(1)}, bf16[128,512]{1,0:T(8,128)(2,1)S(1)}, u32[]{:S(2)}, u32[]{:S(2)}) %collective-permute-start.2) | collective-permute-done | bytes 131104 | tf_op jit(solution)/shard_map/ppermute | solution.py:294
  20.1 0.6 shard_map.68
  20.7 0.5 collective-permute-start.3
  21.2 0.0 collective-permute-done.6.other_ref
  21.2 0.6 shard_map.71
  21.9 0.1 collective-permute-start.7
  21.9 3.0 %collective-permute-start.5 = (bf16[512,256]{1,0:T(8,128)(2,1)S(1)}, bf16[512,256]{1,0:T(8,128)(2,1)S(1)}, u32[]{:S(2)}, u32[]{:S(2)}) collective-permute-start(bf16[512,256]{1,0:T(8,128)(2,1)S(1)} %get-tuple-element.42), channel_id=1, source_target_pairs={{0,12},{1,13},{2,14},{3,15},{4,8},{5,9},{6,10},{7,11},{8,20},{9,21... | collective-permute-start | bytes 786440 | tf_op jit(solution)/shard_map/ppermute | solution.py:294
  25.0 1.9 %collective-permute-start.4 = (bf16[512,256]{1,0:T(8,128)(2,1)S(1)}, bf16[512,256]{1,0:T(8,128)(2,1)S(1)}, u32[]{:S(2)}, u32[]{:S(2)}) collective-permute-start(bf16[512,256]{1,0:T(8,128)(2,1)S(1)} %get-tuple-element.41.mine_ref), channel_id=1, source_target_pairs={{0,8},{1,9},{2,10},{3,11},{4,12},{5,13},{6,14},{7,15},{8,16},{9,17... | collective-permute-start | bytes 786440 | tf_op jit(solution)/shard_map/ppermute | solution.py:294
  26.9 1.4 %collective-permute-start.8 = (bf16[272,512]{1,0:T(8,128)(2,1)S(1)}, bf16[272,512]{1,0:T(8,128)(2,1)S(1)}, u32[]{:S(2)}, u32[]{:S(2)}) collective-permute-start(bf16[272,512]{1,0:T(8,128)(2,1)S(1)} %get-tuple-element.52), channel_id=1, source_target_pairs={{0,2},{1,3},{2,0},{3,1},{4,6},{5,7},{6,4},{7,5},{8,10},{9,11},{10,... | collective-permute-start | bytes 835592 | tf_op jit(solution)/shard_map/ppermute | solution.py:294
  28.3 0.0 collective-permute-done.3.sibling_ref
  28.3 1.7 %collective-permute-start.9 = (bf16[272,512]{1,0:T(8,128)(2,1)S(1)}, bf16[272,512]{1,0:T(8,128)(2,1)S(1)}, u32[]{:S(2)}, u32[]{:S(2)}) collective-permute-start(bf16[272,512]{1,0:T(8,128)(2,1)S(1)} %get-tuple-element.53), channel_id=1, source_target_pairs={{0,3},{1,0},{2,1},{3,2},{4,7},{5,4},{6,5},{7,6},{8,11},{9,8},{10,9... | collective-permute-start | bytes 835592 | tf_op jit(solution)/shard_map/ppermute | solution.py:294
  30.0 0.7 shard_map.69
  30.8 2.8 %collective-permute-done.5.b_ref = bf16[512,256]{1,0:T(8,128)(2,1)S(1)} collective-permute-done((bf16[512,256]{1,0:T(8,128)(2,1)S(1)}, bf16[512,256]{1,0:T(8,128)(2,1)S(1)}, u32[]{:S(2)}, u32[]{:S(2)}) %collective-permute-start.5) | collective-permute-done | bytes 262176 | tf_op jit(solution)/shard_map/ppermute | solution.py:294
  33.6 4.4 %collective-permute-done.4.a_ref = bf16[512,256]{1,0:T(8,128)(2,1)S(1)} collective-permute-done((bf16[512,256]{1,0:T(8,128)(2,1)S(1)}, bf16[512,256]{1,0:T(8,128)(2,1)S(1)}, u32[]{:S(2)}, u32[]{:S(2)}) %collective-permute-start.4) | collective-permute-done | bytes 262176 | tf_op jit(solution)/shard_map/ppermute | solution.py:294
  38.0 0.0 collective-permute-done.7.refs_1_
  38.0 6.1 %shard_map.72 = (bf16[1024,256]{1,0:T(8,128)(2,1)S(1)}, bf16[128,1024]{1,0:T(8,128)(2,1)S(1)}, f32[1024,256]{1,0:T(8,128)S(1)}, f32[1024,256]{1,0:T(8,128)S(1)},...) custom-call(s32[3]{0:T(128)S(1)} %pad_add_fusion.place_ref, bf16[1024,256]{1,0:T(8,128)(2,1)S(1)} %get-tuple-element.43.own_ref, ...), custom_call_target="tpu_custom_call" | custom-call | flops 1342177280 | bytes 5013516 | tf_op jit(solution)/shard_map/pallas_call | solution.py:26
  44.1 2.1 %collective-permute-start.12 = (bf16[256,256]{1,0:T(8,128)(2,1)S(1)}, bf16[256,256]{1,0:T(8,128)(2,1)S(1)}, u32[]{:S(2)}, u32[]{:S(2)}) collective-permute-start(bf16[256,256]{1,0:T(8,128)(2,1)S(1)} %get-tuple-element.58), channel_id=1, source_target_pairs={{0,3},{1,0},{2,1},{3,2},{4,7},{5,4},{6,5},{7,6},{8,11},{9,8},{10,9... | collective-permute-start | bytes 393224 | tf_op jit(solution)/shard_map/ppermute | solution.py:294
  46.2 0.0 collective-permute-done.8.refs_0_
  46.2 2.3 %collective-permute-done.9.refs_1_ = bf16[272,512]{1,0:T(8,128)(2,1)S(1)} collective-permute-done((bf16[272,512]{1,0:T(8,128)(2,1)S(1)}, bf16[272,512]{1,0:T(8,128)(2,1)S(1)}, u32[]{:S(2)}, u32[]{:S(2)}) %collective-permute-start.9) | collective-permute-done | bytes 278560 | tf_op jit(solution)/shard_map/ppermute | solution.py:294
  48.5 6.0 %shard_map.73 = (f32[512,256]{1,0:T(8,128)S(1)}, bf16[512,256]{1,0:T(8,128)(2,1)S(1)}, bf16[512,256]{1,0:T(8,128)(2,1)S(1)}, bf16[512,256]{1,0:T(8,128)(2,1)S(1)...) custom-call(s32[3]{0:T(128)S(1)} %pad_add_fusion.place_ref, ...), custom_call_target="tpu_custom_call" | custom-call | flops 1342177280 | bytes 5799948 | tf_op jit(solution)/shard_map/pallas_call | solution.py:26
  54.5 0.1 collective-permute-start.10
  54.5 0.6 collective-permute-start.11
  55.2 6.7 %collective-permute-start.14 = (bf16[512,256]{1,0:T(8,128)(2,1)S(1)}, bf16[512,256]{1,0:T(8,128)(2,1)S(1)}, u32[]{:S(2)}, u32[]{:S(2)}) collective-permute-start(bf16[512,256]{1,0:T(8,128)(2,1)S(1)} %get-tuple-element.62), channel_id=1, source_target_pairs={{8,0},{9,1},{10,2},{11,3},{12,4},{13,5},{14,6},{15,7},{16,8},{17,9... | collective-permute-start | bytes 786440 | tf_op jit(solution)/shard_map/ppermute | solution.py:294
  61.9 2.3 %collective-permute-start.15 = (bf16[512,256]{1,0:T(8,128)(2,1)S(1)}, bf16[512,256]{1,0:T(8,128)(2,1)S(1)}, u32[]{:S(2)}, u32[]{:S(2)}) collective-permute-start(bf16[512,256]{1,0:T(8,128)(2,1)S(1)} %get-tuple-element.63), channel_id=1, source_target_pairs={{0,4},{1,5},{2,6},{3,7},{4,0},{5,1},{6,2},{7,3},{8,12},{9,13},{10,... | collective-permute-start | bytes 786440 | tf_op jit(solution)/shard_map/ppermute | solution.py:294
  64.2 0.0 collective-permute-done.12.refs_3_
  64.2 2.1 %collective-permute-start.16 = (bf16[512,256]{1,0:T(8,128)(2,1)S(1)}, bf16[512,256]{1,0:T(8,128)(2,1)S(1)}, u32[]{:S(2)}, u32[]{:S(2)}) collective-permute-start(bf16[512,256]{1,0:T(8,128)(2,1)S(1)} %get-tuple-element.64), channel_id=1, source_target_pairs={{8,4},{9,5},{10,6},{11,7},{12,0},{13,1},{14,2},{15,3},{16,12},{17,... | collective-permute-start | bytes 786440 | tf_op jit(solution)/shard_map/ppermute | solution.py:294
  66.3 0.0 collective-permute-done.10.refs_1_
  66.3 0.0 collective-permute-done.11.refs_2_
  66.3 0.6 shard_map.74
  66.9 0.5 collective-permute-start.13
  67.4 0.0 collective-permute-done.14.near_ref
  67.4 0.0 collective-permute-done.15.sibling_ref
  67.4 6.6 %collective-permute-done.16.far_ref = bf16[512,256]{1,0:T(8,128)(2,1)S(1)} collective-permute-done((bf16[512,256]{1,0:T(8,128)(2,1)S(1)}, bf16[512,256]{1,0:T(8,128)(2,1)S(1)}, u32[]{:S(2)}, u32[]{:S(2)}) %collective-permute-start.16) | collective-permute-done | bytes 262176 | tf_op jit(solution)/shard_map/ppermute | solution.py:294
  74.0 0.7 shard_map.76
  74.7 0.3 collective-permute-start.17
  74.9 3.5 %collective-permute-start.18 = (bf16[128,512]{1,0:T(8,128)(2,1)S(1)}, bf16[128,512]{1,0:T(8,128)(2,1)S(1)}, u32[]{:S(2)}, u32[]{:S(2)}) collective-permute-start(bf16[128,512]{1,0:T(8,128)(2,1)S(1)} %get-tuple-element.67), channel_id=1, source_target_pairs={{0,2},{1,3},{2,0},{3,1},{4,6},{5,7},{6,4},{7,5},{8,10},{9,11},{10,... | collective-permute-start | bytes 393224 | tf_op jit(solution)/shard_map/ppermute | solution.py:294
  78.5 0.0 collective-permute-start.19
  78.5 0.0 collective-permute-done.13.sibling_ref
  78.5 1.4 %shard_map.75 = bf16[128,2048]{1,0:T(8,128)(2,1)} custom-call(s32[3]{0:T(128)S(1)} %pad_add_fusion.place_ref, bf16[512,256]{1,0:T(8,128)(2,1)S(1)} %get-tuple-element.59.mine_ref, bf16[512,256]{1,0:T(8,128)(2,1)S(1)} %collective-permute-done.13.sibling_ref), custom_call_target="tpu_custom_call" | custom-call | bytes 1048588 | tf_op jit(solution)/shard_map/pallas_call | solution.py:26
  79.9 0.2 collective-permute-done.17.refs_1_
  80.1 6.9 %collective-permute-done.18.refs_2_ = bf16[128,512]{1,0:T(8,128)(2,1)S(1)} collective-permute-done((bf16[128,512]{1,0:T(8,128)(2,1)S(1)}, bf16[128,512]{1,0:T(8,128)(2,1)S(1)}, u32[]{:S(2)}, u32[]{:S(2)}) %collective-permute-start.18) | collective-permute-done | bytes 131104 | tf_op jit(solution)/shard_map/ppermute | solution.py:294
  87.0 2.7 %collective-permute-done.19.refs_3_ = bf16[128,512]{1,0:T(8,128)(2,1)S(1)} collective-permute-done((bf16[128,512]{1,0:T(8,128)(2,1)S(1)}, bf16[128,512]{1,0:T(8,128)(2,1)S(1)}, u32[]{:S(2)}, u32[]{:S(2)}) %collective-permute-start.19) | collective-permute-done | bytes 131104 | tf_op jit(solution)/shard_map/ppermute | solution.py:294
  89.7 1.5 %shard_map.77 = (bf16[128,1024]{1,0:T(8,128)(2,1)}, bf16[128,1024]{1,0:T(8,128)(2,1)}) custom-call(s32[3]{0:T(128)S(1)} %pad_add_fusion.place_ref, bf16[128,512]{1,0:T(8,128)(2,1)S(1)} %get-tuple-element.65.refs_0_, bf16[128,512]{1,0:T(8,128)(2,1)S(1)} %collective-permute-done.17.refs_1_, bf16[128,512]{1,0:T(8,128)(2,1)S(1)} %collective-permute-done.18.refs_2_, ...), custom_call_target="tpu_custom_call" | custom-call | bytes 1048588 | tf_op jit(solution)/shard_map/pallas_call | solution.py:26
  (1 shorter events, 0.0 us)
Async XLA Ops:
  0.7 1.0 %copy-start = (bf16[128,2048]{1,0:T(8,128)(2,1)S(1)}, bf16[128,2048]{1,0:T(8,128)(2,1)}, u32[]{:S(2)}) copy-start(bf16[128,2048]{1,0:T(8,128)(2,1)} %q_ref.1) | copy-start | bytes 1572868
  1.8 1.0 %copy-start.1 = (bf16[128,2048]{1,0:T(8,128)(2,1)S(1)}, bf16[128,2048]{1,0:T(8,128)(2,1)}, u32[]{:S(2)}) copy-start(bf16[128,2048]{1,0:T(8,128)(2,1)} %g_ref.1) | copy-start | bytes 1572868
  2.8 1.7 %copy-start.2 = (bf16[128,1024]{1,0:T(8,128)(2,1)S(1)}, bf16[128,1024]{1,0:T(8,128)(2,1)}, u32[]{:S(2)}) copy-start(bf16[128,1024]{1,0:T(8,128)(2,1)} %k_ref.1) | copy-start | bytes 786436
  2.8 1.7 %copy-start.3 = (bf16[128,1024]{1,0:T(8,128)(2,1)S(1)}, bf16[128,1024]{1,0:T(8,128)(2,1)}, u32[]{:S(2)}) copy-start(bf16[128,1024]{1,0:T(8,128)(2,1)} %v_ref.1) | copy-start | bytes 786436
  3.7 17.5 %collective-permute-start.6 = (bf16[4,128,512]{2,1,0:T(8,128)(2,1)S(1)}, bf16[4,128,512]{2,1,0:T(8,128)(2,1)S(1)}, u32[]{:S(2)}, u32[]{:S(2)}) collective-permute-start(bf16[4,128,512]{2,1,0:T(8,128)(2,1)S(1)} %get-tuple-element.46), channel_id=1, source_target_pairs={{0,4},{1,5},{2,6},{3,7},{4,0},{5,1},{6,2},{7,3},{8,12},{9,13},{10,... | collective-permute-start | bytes 1572872 | tf_op jit(solution)/shard_map/ppermute | solution.py:294
  5.3 5.1 %collective-permute-start = (bf16[128,512]{1,0:T(8,128)(2,1)S(1)}, bf16[128,512]{1,0:T(8,128)(2,1)S(1)}, u32[]{:S(2)}, u32[]{:S(2)}) collective-permute-start(bf16[128,512]{1,0:T(8,128)(2,1)S(1)} %get-tuple-element.38), channel_id=1, source_target_pairs={{0,1},{1,2},{2,3},{3,0},{4,5},{5,6},{6,7},{7,4},{8,9},{9,10},{10,1... | collective-permute-start | bytes 393224 | tf_op jit(solution)/shard_map/ppermute | solution.py:294
  6.7 11.3 %collective-permute-start.1 = (bf16[128,512]{1,0:T(8,128)(2,1)S(1)}, bf16[128,512]{1,0:T(8,128)(2,1)S(1)}, u32[]{:S(2)}, u32[]{:S(2)}) collective-permute-start(bf16[128,512]{1,0:T(8,128)(2,1)S(1)} %get-tuple-element.39), channel_id=1, source_target_pairs={{0,2},{1,3},{2,0},{3,1},{4,6},{5,7},{6,4},{7,5},{8,10},{9,11},{10,... | collective-permute-start | bytes 393224 | tf_op jit(solution)/shard_map/ppermute | solution.py:294
  7.8 12.3 %collective-permute-start.2 = (bf16[128,512]{1,0:T(8,128)(2,1)S(1)}, bf16[128,512]{1,0:T(8,128)(2,1)S(1)}, u32[]{:S(2)}, u32[]{:S(2)}) collective-permute-start(bf16[128,512]{1,0:T(8,128)(2,1)S(1)} %get-tuple-element.40), channel_id=1, source_target_pairs={{0,3},{1,0},{2,1},{3,2},{4,7},{5,4},{6,5},{7,6},{8,11},{9,8},{10,9... | collective-permute-start | bytes 393224 | tf_op jit(solution)/shard_map/ppermute | solution.py:294
  20.7 7.6 %collective-permute-start.3 = (bf16[512,256]{1,0:T(8,128)(2,1)S(1)}, bf16[512,256]{1,0:T(8,128)(2,1)S(1)}, u32[]{:S(2)}, u32[]{:S(2)}) collective-permute-start(bf16[512,256]{1,0:T(8,128)(2,1)S(1)} %get-tuple-element.42), channel_id=1, source_target_pairs={{0,4},{1,5},{2,6},{3,7},{4,0},{5,1},{6,2},{7,3},{8,12},{9,13},{10,... | collective-permute-start | bytes 786440 | tf_op jit(solution)/shard_map/ppermute | solution.py:294
  21.9 16.1 %collective-permute-start.7 = (bf16[272,512]{1,0:T(8,128)(2,1)S(1)}, bf16[272,512]{1,0:T(8,128)(2,1)S(1)}, u32[]{:S(2)}, u32[]{:S(2)}) collective-permute-start(bf16[272,512]{1,0:T(8,128)(2,1)S(1)} %get-tuple-element.48), channel_id=1, source_target_pairs={{0,1},{1,2},{2,3},{3,0},{4,5},{5,6},{6,7},{7,4},{8,9},{9,10},{10,1... | collective-permute-start | bytes 835592 | tf_op jit(solution)/shard_map/ppermute | solution.py:294
  21.9 11.6 %collective-permute-start.5 = (bf16[512,256]{1,0:T(8,128)(2,1)S(1)}, bf16[512,256]{1,0:T(8,128)(2,1)S(1)}, u32[]{:S(2)}, u32[]{:S(2)}) collective-permute-start(bf16[512,256]{1,0:T(8,128)(2,1)S(1)} %get-tuple-element.42), channel_id=1, source_target_pairs={{0,12},{1,13},{2,14},{3,15},{4,8},{5,9},{6,10},{7,11},{8,20},{9,21... | collective-permute-start | bytes 786440 | tf_op jit(solution)/shard_map/ppermute | solution.py:294
  25.0 13.0 %collective-permute-start.4 = (bf16[512,256]{1,0:T(8,128)(2,1)S(1)}, bf16[512,256]{1,0:T(8,128)(2,1)S(1)}, u32[]{:S(2)}, u32[]{:S(2)}) collective-permute-start(bf16[512,256]{1,0:T(8,128)(2,1)S(1)} %get-tuple-element.41.mine_ref), channel_id=1, source_target_pairs={{0,8},{1,9},{2,10},{3,11},{4,12},{5,13},{6,14},{7,15},{8,16},{9,17... | collective-permute-start | bytes 786440 | tf_op jit(solution)/shard_map/ppermute | solution.py:294
  26.9 19.3 %collective-permute-start.8 = (bf16[272,512]{1,0:T(8,128)(2,1)S(1)}, bf16[272,512]{1,0:T(8,128)(2,1)S(1)}, u32[]{:S(2)}, u32[]{:S(2)}) collective-permute-start(bf16[272,512]{1,0:T(8,128)(2,1)S(1)} %get-tuple-element.52), channel_id=1, source_target_pairs={{0,2},{1,3},{2,0},{3,1},{4,6},{5,7},{6,4},{7,5},{8,10},{9,11},{10,... | collective-permute-start | bytes 835592 | tf_op jit(solution)/shard_map/ppermute | solution.py:294
  28.3 20.1 %collective-permute-start.9 = (bf16[272,512]{1,0:T(8,128)(2,1)S(1)}, bf16[272,512]{1,0:T(8,128)(2,1)S(1)}, u32[]{:S(2)}, u32[]{:S(2)}) collective-permute-start(bf16[272,512]{1,0:T(8,128)(2,1)S(1)} %get-tuple-element.53), channel_id=1, source_target_pairs={{0,3},{1,0},{2,1},{3,2},{4,7},{5,4},{6,5},{7,6},{8,11},{9,8},{10,9... | collective-permute-start | bytes 835592 | tf_op jit(solution)/shard_map/ppermute | solution.py:294
  44.1 20.1 %collective-permute-start.12 = (bf16[256,256]{1,0:T(8,128)(2,1)S(1)}, bf16[256,256]{1,0:T(8,128)(2,1)S(1)}, u32[]{:S(2)}, u32[]{:S(2)}) collective-permute-start(bf16[256,256]{1,0:T(8,128)(2,1)S(1)} %get-tuple-element.58), channel_id=1, source_target_pairs={{0,3},{1,0},{2,1},{3,2},{4,7},{5,4},{6,5},{7,6},{8,11},{9,8},{10,9... | collective-permute-start | bytes 393224 | tf_op jit(solution)/shard_map/ppermute | solution.py:294
  54.5 11.8 %collective-permute-start.10 = (bf16[256,256]{1,0:T(8,128)(2,1)S(1)}, bf16[256,256]{1,0:T(8,128)(2,1)S(1)}, u32[]{:S(2)}, u32[]{:S(2)}) collective-permute-start(bf16[256,256]{1,0:T(8,128)(2,1)S(1)} %get-tuple-element.56), channel_id=1, source_target_pairs={{0,1},{1,2},{2,3},{3,0},{4,5},{5,6},{6,7},{7,4},{8,9},{9,10},{10,1... | collective-permute-start | bytes 393224 | tf_op jit(solution)/shard_map/ppermute | solution.py:294
  54.5 11.8 %collective-permute-start.11 = (bf16[256,256]{1,0:T(8,128)(2,1)S(1)}, bf16[256,256]{1,0:T(8,128)(2,1)S(1)}, u32[]{:S(2)}, u32[]{:S(2)}) collective-permute-start(bf16[256,256]{1,0:T(8,128)(2,1)S(1)} %get-tuple-element.57), channel_id=1, source_target_pairs={{0,2},{1,3},{2,0},{3,1},{4,6},{5,7},{6,4},{7,5},{8,10},{9,11},{10,... | collective-permute-start | bytes 393224 | tf_op jit(solution)/shard_map/ppermute | solution.py:294
  55.2 12.3 %collective-permute-start.14 = (bf16[512,256]{1,0:T(8,128)(2,1)S(1)}, bf16[512,256]{1,0:T(8,128)(2,1)S(1)}, u32[]{:S(2)}, u32[]{:S(2)}) collective-permute-start(bf16[512,256]{1,0:T(8,128)(2,1)S(1)} %get-tuple-element.62), channel_id=1, source_target_pairs={{8,0},{9,1},{10,2},{11,3},{12,4},{13,5},{14,6},{15,7},{16,8},{17,9... | collective-permute-start | bytes 786440 | tf_op jit(solution)/shard_map/ppermute | solution.py:294
  61.9 5.5 %collective-permute-start.15 = (bf16[512,256]{1,0:T(8,128)(2,1)S(1)}, bf16[512,256]{1,0:T(8,128)(2,1)S(1)}, u32[]{:S(2)}, u32[]{:S(2)}) collective-permute-start(bf16[512,256]{1,0:T(8,128)(2,1)S(1)} %get-tuple-element.63), channel_id=1, source_target_pairs={{0,4},{1,5},{2,6},{3,7},{4,0},{5,1},{6,2},{7,3},{8,12},{9,13},{10,... | collective-permute-start | bytes 786440 | tf_op jit(solution)/shard_map/ppermute | solution.py:294
  64.2 9.8 %collective-permute-start.16 = (bf16[512,256]{1,0:T(8,128)(2,1)S(1)}, bf16[512,256]{1,0:T(8,128)(2,1)S(1)}, u32[]{:S(2)}, u32[]{:S(2)}) collective-permute-start(bf16[512,256]{1,0:T(8,128)(2,1)S(1)} %get-tuple-element.64), channel_id=1, source_target_pairs={{8,4},{9,5},{10,6},{11,7},{12,0},{13,1},{14,2},{15,3},{16,12},{17,... | collective-permute-start | bytes 786440 | tf_op jit(solution)/shard_map/ppermute | solution.py:294
  66.9 11.6 %collective-permute-start.13 = (bf16[512,256]{1,0:T(8,128)(2,1)S(1)}, bf16[512,256]{1,0:T(8,128)(2,1)S(1)}, u32[]{:S(2)}, u32[]{:S(2)}) collective-permute-start(bf16[512,256]{1,0:T(8,128)(2,1)S(1)} %get-tuple-element.60), channel_id=1, source_target_pairs={{0,4},{1,5},{2,6},{3,7},{4,0},{5,1},{6,2},{7,3},{8,12},{9,13},{10,... | collective-permute-start | bytes 786440 | tf_op jit(solution)/shard_map/ppermute | solution.py:294
  74.7 5.4 %collective-permute-start.17 = (bf16[128,512]{1,0:T(8,128)(2,1)S(1)}, bf16[128,512]{1,0:T(8,128)(2,1)S(1)}, u32[]{:S(2)}, u32[]{:S(2)}) collective-permute-start(bf16[128,512]{1,0:T(8,128)(2,1)S(1)} %get-tuple-element.66), channel_id=1, source_target_pairs={{0,1},{1,2},{2,3},{3,0},{4,5},{5,6},{6,7},{7,4},{8,9},{9,10},{10,1... | collective-permute-start | bytes 393224 | tf_op jit(solution)/shard_map/ppermute | solution.py:294
  74.9 12.0 %collective-permute-start.18 = (bf16[128,512]{1,0:T(8,128)(2,1)S(1)}, bf16[128,512]{1,0:T(8,128)(2,1)S(1)}, u32[]{:S(2)}, u32[]{:S(2)}) collective-permute-start(bf16[128,512]{1,0:T(8,128)(2,1)S(1)} %get-tuple-element.67), channel_id=1, source_target_pairs={{0,2},{1,3},{2,0},{3,1},{4,6},{5,7},{6,4},{7,5},{8,10},{9,11},{10,... | collective-permute-start | bytes 393224 | tf_op jit(solution)/shard_map/ppermute | solution.py:294
  78.5 11.2 %collective-permute-start.19 = (bf16[128,512]{1,0:T(8,128)(2,1)S(1)}, bf16[128,512]{1,0:T(8,128)(2,1)S(1)}, u32[]{:S(2)}, u32[]{:S(2)}) collective-permute-start(bf16[128,512]{1,0:T(8,128)(2,1)S(1)} %get-tuple-element.68), channel_id=1, source_target_pairs={{0,3},{1,0},{2,1},{3,2},{4,7},{5,4},{6,5},{7,6},{8,11},{9,8},{10,9... | collective-permute-start | bytes 393224 | tf_op jit(solution)/shard_map/ppermute | solution.py:294

commit v8 on v7

--- a/solution.py
+++ b/solution.py
@@ -82,7 +82,7 @@
     pairs = []
     for ref, c in ((other_ref, 1 - core), (mine_ref, core)):
         for k in range(heads):
-            columns = at((2 * onward(place_ref, heads, k) + c) * width, width)
+            columns = at((2 * k + c) * width, width)
             pairs.append((q_ref.at[:, columns], ref.at[k, :, pl.ds(0, width)]))
             pairs.append((g_ref.at[:, columns], ref.at[k, :, pl.ds(width, width)]))
     copied(sems, pairs)
@@ -105,15 +105,15 @@
     kt_ref[...] = out_ref[:, :HEAD_SIZE].T
 
 
-def merge_rows_kernel(heads, place_ref, mine_ref, other_ref, after_ref, *out_refs):
-    core = place_ref[1]
-    for k, out_ref in enumerate(out_refs):
-        out_ref[at(core * BLOCK, BLOCK)] = mine_ref[k]
-        out_ref[at((1 - core) * BLOCK, BLOCK)] = other_ref[k]
+def merge_rows_kernel(heads, place_ref, mine_ref, other_ref, out_ref):
+    core = place_ref[1]
+    for z in range(heads):
+        out_ref[z, at(core * BLOCK, BLOCK)] = mine_ref[z]
+        out_ref[z, at((1 - core) * BLOCK, BLOCK)] = other_ref[z]
 
 
 def sort_dq_kernel(heads, place_ref, *refs):
-    in_refs, (mine_ref, other_ref) = refs[:heads], refs[heads:]
+    in_refs, (after_ref, mine_ref, other_ref) = refs[:heads], refs[heads:]
     core = place_ref[1]
     for k, in_ref in enumerate(in_refs):
         mine_ref[k * BLOCK : (k + 1) * BLOCK] = in_ref[at(core * BLOCK, BLOCK)]
@@ -188,95 +188,72 @@
     )
     ds_own, ds_prev = split(ds)
     at_own, at_prev = split(low_attention)
-    own_grad_ref[:high, d:] += dot(at_own, g)
-    prev_grad_ref[low:, d:] += dot(at_prev, g)
-    own_grad_ref[:high, :d] += dot(ds_own, q)
-    prev_grad_ref[low:, :d] += dot(ds_prev, q)
+    for columns, x_own, x_prev, y in ((slice(d, 2 * d), at_own, at_prev, g), (slice(0, d), ds_own, ds_prev, q)):
+        sum_own, sum_prev = dot(x_own, y), dot(x_prev, y)
+        if below:
+            own_grad_ref[:low, columns] += sum_own[:low]
+            prev_grad_ref[low:, columns] += sum_prev
+        else:
+            prev_grad_ref[:, columns] = sum_prev
+        own_grad_ref[low:high, columns] = sum_own[low:]
     dq_t = dot(own_kt_ref[:, :high], ds_own) + dot(prev_kt_ref[:, low:], ds_prev)
     return dq_t * score_scale
 
 
-def attention_kernel(heads, steps, last, place_ref, own_ref, own_kt_ref, a_ref, b_ref, *refs):
+def attention_kernel(heads, place_ref, own_ref, own_kt_ref, near_ref, far_ref, blocks_ref, *refs):
     d = HEAD_SIZE
     count = 2 * heads
     half = heads * BLOCK
-    block_refs, refs = refs[: len(steps)], refs[len(steps) :]
-    if last:
-        own_so_far_ref, prev_so_far_ref = refs[:2]
-        own_mine_ref, own_other_ref, prev_mine_ref, prev_other_ref = refs[2:6]
-        dq_refs, (qd_ref, dq_ref, own_grad_ref, prev_grad_ref) = refs[6:-4], refs[-4:]
-        prev_ref, prev_kt_ref = a_ref, b_ref
-        own_grad_ref[...] = own_so_far_ref[...]
-        prev_grad_ref[...] = prev_so_far_ref[...]
-    else:
-        prev_ref, prev_kt_ref, own_grad_ref, prev_grad_ref = refs[:4]
-        dq_refs, (qd_ref, dq_ref) = refs[4:-2], refs[-2:]
-        own_grad_ref[...] = jnp.zeros_like(own_grad_ref)
-        prev_grad_ref[...] = jnp.zeros_like(prev_grad_ref)
+    own_mine_ref, own_other_ref, prev_mine_ref, prev_other_ref = refs[:4]
+    dq_refs, refs = refs[4 : 4 + heads], refs[4 + heads :]
+    prev_ref, prev_kt_ref, dq_ref, own_grad_ref, prev_grad_ref = refs
     first, core, head = place_ref[0], place_ref[1], place_ref[2]
     mine, other = at(core * half, half), at((1 - core) * half, half)
-    if not last:
-        prev_ref[mine] = a_ref[...]
-        prev_ref[other] = b_ref[...]
-        prev_kt_ref[...] = prev_ref[:, :d].T
-    for n, block_ref in enumerate(block_refs):
-        qd_ref[n] = block_ref[: 2 * BLOCK]
+    prev_ref[mine] = near_ref[...]
+    prev_ref[other] = far_ref[...]
+    prev_kt_ref[...] = prev_ref[:, :d].T
     bias = jnp.where(first == 1, masked_value, 0.0).astype(jnp.float32)
-
-    @pl.loop(0, len(steps))
-    def _(n):
-        step = steps[0] + n
-        z_here = lax.rem(head + heads - step, heads)
-        for z in range(heads):
-
-            @pl.when(z_here == z)
-            def _():
-                for c in range(2):
-                    rows = slice(c * BLOCK, (c + 1) * BLOCK)
-                    q = jnp.concatenate([qd_ref[n, rows, :d], qd_ref[n, rows, d : 2 * d]], 0)
-                    g = jnp.concatenate([qd_ref[n, rows, 2 * d : 3 * d], qd_ref[n, rows, 3 * d :]], 0)
-                    dq_t = attention_block(
-                        c * heads + z, count, q, g, own_ref, prev_ref, own_kt_ref, prev_kt_ref,
-                        own_grad_ref, prev_grad_ref, bias,
-                    )
-                    dq_ref[n, rows, :d] = dq_t[:, :BLOCK].T.astype(jnp.bfloat16)
-                    dq_ref[n, rows, d:] = dq_t[:, BLOCK:].T.astype(jnp.bfloat16)
-
-    for n, ref in enumerate(dq_refs):
-        ref[...] = dq_ref[n]
-    if last:
-        for ref, grad_ref, rows in (
-            (prev_mine_ref, prev_grad_ref, mine),
-            (prev_other_ref, prev_grad_ref, other),
-            (own_other_ref, own_grad_ref, other),
-            (own_mine_ref, own_grad_ref, mine),
-        ):
-            ref[:, :d] = (grad_ref[rows, :d] * score_scale).astype(ref.dtype)
-            ref[:, d:] = grad_ref[rows, d:].astype(ref.dtype)
-
-
-def attention_backward(heads, steps, place, own, prev, blocks, so_far=()):
+    for i in range(count):
+        c, z = i // heads, i % heads
+        rows = slice(c * BLOCK, (c + 1) * BLOCK)
+        q = jnp.concatenate([blocks_ref[z, rows, :d], blocks_ref[z, rows, d : 2 * d]], 0)
+        g = jnp.concatenate([blocks_ref[z, rows, 2 * d : 3 * d], blocks_ref[z, rows, 3 * d :]], 0)
+        dq_t = attention_block(
+            i, count, q, g, own_ref, prev_ref, own_kt_ref, prev_kt_ref, own_grad_ref, prev_grad_ref, bias
+        )
+        dq_ref[z, rows, :d] = dq_t[:, :BLOCK].T.astype(jnp.bfloat16)
+        dq_ref[z, rows, d:] = dq_t[:, BLOCK:].T.astype(jnp.bfloat16)
+    for k, ref in enumerate(dq_refs):
+        ref[...] = dq_ref[lax.rem(head + k, heads)]
+    for ref, grad_ref, rows in (
+        (prev_mine_ref, prev_grad_ref, mine),
+        (prev_other_ref, prev_grad_ref, other),
+        (own_other_ref, own_grad_ref, other),
+        (own_mine_ref, own_grad_ref, mine),
+    ):
+        ref[:, :d] = (grad_ref[rows, :d] * score_scale).astype(ref.dtype)
+        ref[:, d:] = grad_ref[rows, d:].astype(ref.dtype)
+
+
+def attention_backward(heads, place, own, near, far, blocks):
     half, d = heads * BLOCK, HEAD_SIZE
     whole = 2 * half
     low, wide = jnp.bfloat16, jnp.float32
     part = shape_of(low, half, 2 * d)
-    sums = shape_of(wide, whole, 2 * d)
     scratch = (
-        pltpu.VMEM((len(steps), 2 * BLOCK, 4 * d), low),
-        pltpu.VMEM((len(steps), 2 * BLOCK, 2 * d), low),
-    )
-    if so_far:
-        outs = (shape_of(wide, half, 2 * d), part, part, part)
-        scratch += (pltpu.VMEM((whole, 2 * d), wide), pltpu.VMEM((whole, 2 * d), wide))
-    else:
-        outs = (shape_of(low, whole, 2 * d), shape_of(low, d, whole), sums, sums)
+        pltpu.VMEM((whole, 2 * d), low),
+        pltpu.VMEM((d, whole), low),
+        pltpu.VMEM((heads, 2 * BLOCK, 2 * d), low),
+        pltpu.VMEM((whole, 2 * d), wide),
+        pltpu.VMEM((whole, 2 * d), wide),
+    )
     outs = call(
-        functools.partial(attention_kernel, heads, steps, bool(so_far)),
-        outs + (shape_of(low, 2 * BLOCK, 2 * d),) * len(steps),
-        (place,) + tuple(own) + tuple(prev) + tuple(blocks) + tuple(so_far),
+        functools.partial(attention_kernel, heads),
+        (shape_of(wide, half, 2 * d), part, part, part) + (shape_of(low, 2 * BLOCK, 2 * d),) * heads,
+        (place,) + tuple(own) + (near, far, blocks),
         scratch,
-        10 * whole * whole * d,
-        whole * whole,
+        20 * whole * whole * d,
+        2 * whole * whole,
         32,
     )
     return outs[:4], outs[4:]
@@ -322,34 +299,23 @@
     mine, other = call(bind(gather_kv_kernel), (shape_of(low, heads * rows, 2 * d),) * 2, (place,) + kvs)
     near = across(mine, chip_step=1, flip=0)
     far = across(other, chip_step=1, flip=1)
-    blocks = call(
-        bind(merge_rows_kernel),
-        (shape_of(low, 2 * rows + 16, 4 * d),) * heads,
-        (place, qd_mine, qd_other, mine[:8]),
-    )
-    blocks = spread(blocks)
+    blocks = call(bind(merge_rows_kernel), shape_of(low, heads, 2 * rows, 4 * d), (place, qd_mine, qd_other))
+    blocks = lax.all_to_all(blocks, "head", split_axis=0, concat_axis=0, tiled=True)
     sibling = across(other, chip_step=0, flip=1)
     own = call(
         join_kernel,
         (shape_of(low, 2 * heads * rows, 2 * d), shape_of(low, d, 2 * heads * rows)),
         (place, mine, sibling),
     )
-    early, late = tuple(range(heads // 2)), tuple(range(heads // 2, heads))
-    prev_and_sums, dq_early = attention_backward(heads, early, place, own, (near, far), [blocks[k] for k in early])
-    grads, dq_late = attention_backward(
-        heads, late, place, own, prev_and_sums[:2], [blocks[k] for k in late], prev_and_sums[2:]
-    )
+    grads, dqs = attention_backward(heads, place, own, near, far, blocks)
     own_mine, own_other, prev_mine, prev_other = grads
     near_back = across(prev_mine, chip_step=-1, flip=0)
     far_back = across(prev_other, chip_step=-1, flip=1)
     sibling_back = across(own_other, chip_step=0, flip=1)
-    back = dict(zip(early + late, dq_early + dq_late))
-    dqs = [
-        send(back[heads - k], chip_step=0, flip=0, head_step=k) if k else back[0] for k in range(heads)
-    ]
+    dqs = spread(dqs)
     totals = call(bind(add_kernel), (slab,) * heads, (place, own_mine, near_back, sibling_back, far_back))
     dq_mine, dq_other = call(
-        bind(sort_dq_kernel), (shape_of(low, heads * rows, 2 * d),) * 2, (place,) + tuple(dqs)
+        bind(sort_dq_kernel), (shape_of(low, heads * rows, 2 * d),) * 2, (place,) + dqs + (near_back[:8],)
     )
     dq_sibling = across(dq_other, chip_step=0, flip=1)
     query_grad = copy_call(

time: 92.7 us -> 114 us (1.23); the launches traced: 91.2 us -> 114 us
  waiting for transfers between devices: 36.9 us -> 67.1 us
  starting transfers between devices: 31.5 us -> 24.8 us
    ppermute x20 -> x17, waiting for transfers between devices: 36.9 us -> 67.1 us  [moved(): return lax.ppermute(value, ('chip', 'core', 'head'), pairs)]
    ppermute x20 -> x17, starting transfers between devices: 31.5 us -> 20 us  [moved(): return lax.ppermute(value, ('chip', 'core', 'head'), pairs)]
    all_to_all x0 -> x1, starting transfers between devices: none -> 4.89 us  [on_device(): lax.all_to_all(blocks, 'head', split_axis=0, concat_axis=0, tiled=True)]
    pallas_call x11 -> x10, Pallas kernels: 19.9 us -> 18.8 us  [call(): pl.pallas_call(kernel, out_shape=out_shape, in_specs=[SMEM_SPEC] + [spec]...]
  transfers between devices with their start and end apart: 20 -> 18, of which waited for: 10 -> 13; matrix products, arithmetic and copies ran while one was open for 0% -> 0% of each run, Pallas kernels for 19% -> 4%
where the time goes in v8:
time: 114 us
  waiting for transfers between devices  67.1 us (59%)
  starting transfers between devices  24.8 us (22%)
  Pallas kernels  18.8 us (16%)
  local copies, waits for them, and re-layouts  2.09 us (2%)
    ppermute x17, waiting for transfers between devices, moved(): return lax.ppermute(value, ('chip', 'core', 'head'), pairs)  67.1 us
    ppermute x17, starting transfers between devices, moved(): return lax.ppermute(value, ('chip', 'core', 'head'), pairs)  20 us
    pallas_call x10, Pallas kernels, call(): pl.pallas_call(kernel, out_shape=out_shape, in_specs=[SMEM_SPEC] + [spec]...  18.8 us
    all_to_all x1, starting transfers between devices, on_device(): lax.all_to_all(blocks, 'head', split_axis=0, concat_axis=0, tiled=True)  4.89 us
  transfers between devices with their start and end apart: 18, of which 13 were waited for; matrix products, arithmetic and copies ran while one was open for 0% of the time, Pallas kernels for 4%

profile of v8, /device:TPU:13, one launch (start us, length us, event | category | flops | bytes accessed | tf_op | source)
XLA Modules:
  0.0 113.7 jit_solution(1530883004921057622)
XLA Ops:
  0.6 0.1 pad_add_fusion.place_ref
  0.7 0.0 copy-start
  0.7 1.0 copy-done
  1.8 0.0 copy-start.1
  1.8 1.0 copy-done.1
  2.8 0.9 shard_map.70
  3.7 0.7 collective-permute-start.6
  4.4 1.5 %collective-permute-done.6.other_ref = bf16[4,128,512]{2,1,0:T(8,128)(2,1)S(1)} collective-permute-done((bf16[4,128,512]{2,1,0:T(8,128)(2,1)S(1)}, bf16[4,128,512]{2,1,0:T(8,128)(2,1)S(1)}, u32[]{:S(2)}, u32[]{:S(2)}) %collective-permute-start.6) | collective-permute-done | bytes 524320 | tf_op jit(solution)/shard_map/ppermute | solution.py:271
  6.0 1.6 %shard_map.71 = bf16[4,256,512]{2,1,0:T(8,128)(2,1)} custom-call(s32[3]{0:T(128)S(1)} %pad_add_fusion.place_ref, bf16[4,128,512]{2,1,0:T(8,128)(2,1)S(1)} %get-tuple-element.37.mine_ref, bf16[4,128,512]{2,1,0:T(8,128)(2,1)S(1)} %collective-permute-done.6.other_ref), custom_call_target="tpu_custom_call" | custom-call | bytes 2097164 | tf_op jit(solution)/shard_map/pallas_call | solution.py:26
  7.6 0.0 copy-start.2
  7.6 0.0 copy-start.3
  7.6 4.9 %all-to-all-start = ((bf16[4,256,512]{2,1,0:T(8,128)(2,1)}), bf16[4,256,512]{2,1,0:T(8,128)(2,1)S(1)}, u32[]{:S(2)}, u32[]{:S(2)}) async-start(bf16[4,256,512]{2,1,0:T(8,128)(2,1)} %shard_map.71), calls=%async_computation | async-start | bytes 2097152 | tf_op jit(solution)/shard_map/all_to_all | solution.py:303
  12.5 0.0 copy-done.2
  12.5 0.0 copy-done.3
  12.5 0.9 shard_map.67
  13.4 1.2 %collective-permute-start = (bf16[128,512]{1,0:T(8,128)(2,1)S(1)}, bf16[128,512]{1,0:T(8,128)(2,1)S(1)}, u32[]{:S(2)}, u32[]{:S(2)}) collective-permute-start(bf16[128,512]{1,0:T(8,128)(2,1)S(1)} %get-tuple-element.30), channel_id=1, source_target_pairs={{0,1},{1,2},{2,3},{3,0},{4,5},{5,6},{6,7},{7,4},{8,9},{9,10},{10,1... | collective-permute-start | bytes 393224 | tf_op jit(solution)/shard_map/ppermute | solution.py:271
  14.6 1.0 collective-permute-start.1
  15.6 1.4 %collective-permute-start.2 = (bf16[128,512]{1,0:T(8,128)(2,1)S(1)}, bf16[128,512]{1,0:T(8,128)(2,1)S(1)}, u32[]{:S(2)}, u32[]{:S(2)}) collective-permute-start(bf16[128,512]{1,0:T(8,128)(2,1)S(1)} %get-tuple-element.32), channel_id=1, source_target_pairs={{0,3},{1,0},{2,1},{3,2},{4,7},{5,4},{6,5},{7,6},{8,11},{9,8},{10,9... | collective-permute-start | bytes 393224 | tf_op jit(solution)/shard_map/ppermute | solution.py:271
  17.0 26.0 %collective-permute-done.refs_1_ = bf16[128,512]{1,0:T(8,128)(2,1)S(1)} collective-permute-done((bf16[128,512]{1,0:T(8,128)(2,1)S(1)}, bf16[128,512]{1,0:T(8,128)(2,1)S(1)}, u32[]{:S(2)}, u32[]{:S(2)}) %collective-permute-start) | collective-permute-done | bytes 131104 | tf_op jit(solution)/shard_map/ppermute | solution.py:271
  43.0 2.8 %collective-permute-done.1.refs_2_ = bf16[128,512]{1,0:T(8,128)(2,1)S(1)} collective-permute-done((bf16[128,512]{1,0:T(8,128)(2,1)S(1)}, bf16[128,512]{1,0:T(8,128)(2,1)S(1)}, u32[]{:S(2)}, u32[]{:S(2)}) %collective-permute-start.1) | collective-permute-done | bytes 131104 | tf_op jit(solution)/shard_map/ppermute | solution.py:271
  45.8 2.0 %collective-permute-done.2.refs_3_ = bf16[128,512]{1,0:T(8,128)(2,1)S(1)} collective-permute-done((bf16[128,512]{1,0:T(8,128)(2,1)S(1)}, bf16[128,512]{1,0:T(8,128)(2,1)S(1)}, u32[]{:S(2)}, u32[]{:S(2)}) %collective-permute-start.2) | collective-permute-done | bytes 131104 | tf_op jit(solution)/shard_map/ppermute | solution.py:271
  47.8 0.6 shard_map.68
  48.4 1.5 %collective-permute-start.3 = (bf16[512,256]{1,0:T(8,128)(2,1)S(1)}, bf16[512,256]{1,0:T(8,128)(2,1)S(1)}, u32[]{:S(2)}, u32[]{:S(2)}) collective-permute-start(bf16[512,256]{1,0:T(8,128)(2,1)S(1)} %get-tuple-element.34), channel_id=1, source_target_pairs={{0,4},{1,5},{2,6},{3,7},{4,0},{5,1},{6,2},{7,3},{8,12},{9,13},{10,... | collective-permute-start | bytes 786440 | tf_op jit(solution)/shard_map/ppermute | solution.py:271
  49.9 3.1 %collective-permute-start.4 = (bf16[512,256]{1,0:T(8,128)(2,1)S(1)}, bf16[512,256]{1,0:T(8,128)(2,1)S(1)}, u32[]{:S(2)}, u32[]{:S(2)}) collective-permute-start(bf16[512,256]{1,0:T(8,128)(2,1)S(1)} %get-tuple-element.33.mine_ref), channel_id=1, source_target_pairs={{0,8},{1,9},{2,10},{3,11},{4,12},{5,13},{6,14},{7,15},{8,16},{9,17... | collective-permute-start | bytes 786440 | tf_op jit(solution)/shard_map/ppermute | solution.py:271
  53.0 1.9 %collective-permute-start.5 = (bf16[512,256]{1,0:T(8,128)(2,1)S(1)}, bf16[512,256]{1,0:T(8,128)(2,1)S(1)}, u32[]{:S(2)}, u32[]{:S(2)}) collective-permute-start(bf16[512,256]{1,0:T(8,128)(2,1)S(1)} %get-tuple-element.34), channel_id=1, source_target_pairs={{0,12},{1,13},{2,14},{3,15},{4,8},{5,9},{6,10},{7,11},{8,20},{9,21... | collective-permute-start | bytes 786440 | tf_op jit(solution)/shard_map/ppermute | solution.py:271
  54.9 0.0 collective-permute-done.3.sibling_ref
  54.9 0.7 shard_map.69
  55.6 4.9 %collective-permute-done.4.near_ref = bf16[512,256]{1,0:T(8,128)(2,1)S(1)} collective-permute-done((bf16[512,256]{1,0:T(8,128)(2,1)S(1)}, bf16[512,256]{1,0:T(8,128)(2,1)S(1)}, u32[]{:S(2)}, u32[]{:S(2)}) %collective-permute-start.4) | collective-permute-done | bytes 262176 | tf_op jit(solution)/shard_map/ppermute | solution.py:271
  60.6 5.7 %collective-permute-done.5.far_ref = bf16[512,256]{1,0:T(8,128)(2,1)S(1)} collective-permute-done((bf16[512,256]{1,0:T(8,128)(2,1)S(1)}, bf16[512,256]{1,0:T(8,128)(2,1)S(1)}, u32[]{:S(2)}, u32[]{:S(2)}) %collective-permute-start.5) | collective-permute-done | bytes 262176 | tf_op jit(solution)/shard_map/ppermute | solution.py:271
  66.3 0.0 all-to-all-done.blocks_ref
  66.3 10.0 %shard_map.72 = (f32[512,256]{1,0:T(8,128)S(1)}, bf16[512,256]{1,0:T(8,128)(2,1)S(1)}, bf16[512,256]{1,0:T(8,128)(2,1)S(1)}, bf16[512,256]{1,0:T(8,128)(2,1)S(1)...) custom-call(s32[3]{0:T(128)S(1)} %pad_add_fusion.place_ref, ...), custom_call_target="tpu_custom_call" | custom-call | flops 2684354560 | bytes 4194316 | tf_op jit(solution)/shard_map/pallas_call | solution.py:26
  76.3 2.2 %collective-permute-start.10 = (bf16[512,256]{1,0:T(8,128)(2,1)S(1)}, bf16[512,256]{1,0:T(8,128)(2,1)S(1)}, u32[]{:S(2)}, u32[]{:S(2)}) collective-permute-start(bf16[512,256]{1,0:T(8,128)(2,1)S(1)} %get-tuple-element.43), channel_id=1, source_target_pairs={{8,0},{9,1},{10,2},{11,3},{12,4},{13,5},{14,6},{15,7},{16,8},{17,9... | collective-permute-start | bytes 786440 | tf_op jit(solution)/shard_map/ppermute | solution.py:271
  78.5 0.6 collective-permute-start.12
  79.1 1.9 %collective-permute-start.13 = (bf16[512,256]{1,0:T(8,128)(2,1)S(1)}, bf16[512,256]{1,0:T(8,128)(2,1)S(1)}, u32[]{:S(2)}, u32[]{:S(2)}) collective-permute-start(bf16[512,256]{1,0:T(8,128)(2,1)S(1)} %get-tuple-element.48), channel_id=1, source_target_pairs={{8,4},{9,5},{10,6},{11,7},{12,0},{13,1},{14,2},{15,3},{16,12},{17,... | collective-permute-start | bytes 786440 | tf_op jit(solution)/shard_map/ppermute | solution.py:271
  81.1 0.1 collective-permute-start.7
  81.1 1.5 %collective-permute-start.8 = (bf16[256,256]{1,0:T(8,128)(2,1)S(1)}, bf16[256,256]{1,0:T(8,128)(2,1)S(1)}, u32[]{:S(2)}, u32[]{:S(2)}) collective-permute-start(bf16[256,256]{1,0:T(8,128)(2,1)S(1)} %get-tuple-element.41), channel_id=1, source_target_pairs={{0,2},{1,3},{2,0},{3,1},{4,6},{5,7},{6,4},{7,5},{8,10},{9,11},{10,... | collective-permute-start | bytes 393224 | tf_op jit(solution)/shard_map/ppermute | solution.py:271
  82.6 3.3 %collective-permute-done.10.near_ref = bf16[512,256]{1,0:T(8,128)(2,1)S(1)} collective-permute-done((bf16[512,256]{1,0:T(8,128)(2,1)S(1)}, bf16[512,256]{1,0:T(8,128)(2,1)S(1)}, u32[]{:S(2)}, u32[]{:S(2)}) %collective-permute-start.10) | collective-permute-done | bytes 262176 | tf_op jit(solution)/shard_map/ppermute | solution.py:271
  85.9 0.0 collective-permute-start.9
  85.9 0.3 collective-permute-done.7.refs_1_
  86.2 4.8 %collective-permute-done.8.refs_2_ = bf16[256,256]{1,0:T(8,128)(2,1)S(1)} collective-permute-done((bf16[256,256]{1,0:T(8,128)(2,1)S(1)}, bf16[256,256]{1,0:T(8,128)(2,1)S(1)}, u32[]{:S(2)}, u32[]{:S(2)}) %collective-permute-start.8) | collective-permute-done | bytes 131104 | tf_op jit(solution)/shard_map/ppermute | solution.py:271
  91.0 4.0 %collective-permute-done.9.refs_3_ = bf16[256,256]{1,0:T(8,128)(2,1)S(1)} collective-permute-done((bf16[256,256]{1,0:T(8,128)(2,1)S(1)}, bf16[256,256]{1,0:T(8,128)(2,1)S(1)}, u32[]{:S(2)}, u32[]{:S(2)}) %collective-permute-start.9) | collective-permute-done | bytes 131104 | tf_op jit(solution)/shard_map/ppermute | solution.py:271
  95.1 0.6 shard_map.73
  95.6 0.5 collective-permute-start.11
  96.2 0.0 collective-permute-done.12.sibling_ref
  96.2 0.0 collective-permute-done.13.far_ref
  96.2 0.7 shard_map.75
  96.8 0.1 collective-permute-start.14
  96.9 1.5 %collective-permute-start.15 = (bf16[128,512]{1,0:T(8,128)(2,1)S(1)}, bf16[128,512]{1,0:T(8,128)(2,1)S(1)}, u32[]{:S(2)}, u32[]{:S(2)}) collective-permute-start(bf16[128,512]{1,0:T(8,128)(2,1)S(1)} %get-tuple-element.51), channel_id=1, source_target_pairs={{0,2},{1,3},{2,0},{3,1},{4,6},{5,7},{6,4},{7,5},{8,10},{9,11},{10,... | collective-permute-start | bytes 393224 | tf_op jit(solution)/shard_map/ppermute | solution.py:271
  98.4 0.8 collective-permute-start.16
  99.2 2.8 %collective-permute-done.14.refs_1_ = bf16[128,512]{1,0:T(8,128)(2,1)S(1)} collective-permute-done((bf16[128,512]{1,0:T(8,128)(2,1)S(1)}, bf16[128,512]{1,0:T(8,128)(2,1)S(1)}, u32[]{:S(2)}, u32[]{:S(2)}) %collective-permute-start.14) | collective-permute-done | bytes 131104 | tf_op jit(solution)/shard_map/ppermute | solution.py:271
  102.0 6.4 %collective-permute-done.15.refs_2_ = bf16[128,512]{1,0:T(8,128)(2,1)S(1)} collective-permute-done((bf16[128,512]{1,0:T(8,128)(2,1)S(1)}, bf16[128,512]{1,0:T(8,128)(2,1)S(1)}, u32[]{:S(2)}, u32[]{:S(2)}) %collective-permute-start.15) | collective-permute-done | bytes 131104 | tf_op jit(solution)/shard_map/ppermute | solution.py:271
  108.4 2.4 %collective-permute-done.16.refs_3_ = bf16[128,512]{1,0:T(8,128)(2,1)S(1)} collective-permute-done((bf16[128,512]{1,0:T(8,128)(2,1)S(1)}, bf16[128,512]{1,0:T(8,128)(2,1)S(1)}, u32[]{:S(2)}, u32[]{:S(2)}) %collective-permute-start.16) | collective-permute-done | bytes 131104 | tf_op jit(solution)/shard_map/ppermute | solution.py:271
  110.8 1.5 %shard_map.76 = (bf16[128,1024]{1,0:T(8,128)(2,1)}, bf16[128,1024]{1,0:T(8,128)(2,1)}) custom-call(s32[3]{0:T(128)S(1)} %pad_add_fusion.place_ref, bf16[128,512]{1,0:T(8,128)(2,1)S(1)} %get-tuple-element.49.refs_0_, bf16[128,512]{1,0:T(8,128)(2,1)S(1)} %collective-permute-done.14.refs_1_, bf16[128,512]{1,0:T(8,128)(2,1)S(1)} %collective-permute-done.15.refs_2_, ...), custom_call_target="tpu_custom_call" | custom-call | bytes 1048588 | tf_op jit(solution)/shard_map/pallas_call | solution.py:26
  112.3 0.0 collective-permute-done.11.sibling_ref
  112.3 1.4 %shard_map.74 = bf16[128,2048]{1,0:T(8,128)(2,1)} custom-call(s32[3]{0:T(128)S(1)} %pad_add_fusion.place_ref, bf16[512,256]{1,0:T(8,128)(2,1)S(1)} %get-tuple-element.44.mine_ref, bf16[512,256]{1,0:T(8,128)(2,1)S(1)} %collective-permute-done.11.sibling_ref), custom_call_target="tpu_custom_call" | custom-call | bytes 1048588 | tf_op jit(solution)/shard_map/pallas_call | solution.py:26
  (1 shorter events, 0.0 us)
Async XLA Ops:
  0.7 1.0 copy-start
  1.8 1.0 copy-start.1
  3.7 2.3 %collective-permute-start.6 = (bf16[4,128,512]{2,1,0:T(8,128)(2,1)S(1)}, bf16[4,128,512]{2,1,0:T(8,128)(2,1)S(1)}, u32[]{:S(2)}, u32[]{:S(2)}) collective-permute-start(bf16[4,128,512]{2,1,0:T(8,128)(2,1)S(1)} %get-tuple-element.38), channel_id=1, source_target_pairs={{0,4},{1,5},{2,6},{3,7},{4,0},{5,1},{6,2},{7,3},{8,12},{9,13},{10,... | collective-permute-start | bytes 1572872 | tf_op jit(solution)/shard_map/ppermute | solution.py:271
  7.6 4.9 %copy-start.2 = (bf16[128,1024]{1,0:T(8,128)(2,1)S(1)}, bf16[128,1024]{1,0:T(8,128)(2,1)}, u32[]{:S(2)}) copy-start(bf16[128,1024]{1,0:T(8,128)(2,1)} %k_ref.1) | copy-start | bytes 786436
  7.6 4.9 %copy-start.3 = (bf16[128,1024]{1,0:T(8,128)(2,1)S(1)}, bf16[128,1024]{1,0:T(8,128)(2,1)}, u32[]{:S(2)}) copy-start(bf16[128,1024]{1,0:T(8,128)(2,1)} %v_ref.1) | copy-start | bytes 786436
  7.6 58.7 %all-to-all-start = ((bf16[4,256,512]{2,1,0:T(8,128)(2,1)}), bf16[4,256,512]{2,1,0:T(8,128)(2,1)S(1)}, u32[]{:S(2)}, u32[]{:S(2)}) async-start(bf16[4,256,512]{2,1,0:T(8,128)(2,1)} %shard_map.71), calls=%async_computation | async-start | bytes 2097152 | tf_op jit(solution)/shard_map/all_to_all | solution.py:303
  13.4 29.6 %collective-permute-start = (bf16[128,512]{1,0:T(8,128)(2,1)S(1)}, bf16[128,512]{1,0:T(8,128)(2,1)S(1)}, u32[]{:S(2)}, u32[]{:S(2)}) collective-permute-start(bf16[128,512]{1,0:T(8,128)(2,1)S(1)} %get-tuple-element.30), channel_id=1, source_target_pairs={{0,1},{1,2},{2,3},{3,0},{4,5},{5,6},{6,7},{7,4},{8,9},{9,10},{10,1... | collective-permute-start | bytes 393224 | tf_op jit(solution)/shard_map/ppermute | solution.py:271
  14.6 31.2 %collective-permute-start.1 = (bf16[128,512]{1,0:T(8,128)(2,1)S(1)}, bf16[128,512]{1,0:T(8,128)(2,1)S(1)}, u32[]{:S(2)}, u32[]{:S(2)}) collective-permute-start(bf16[128,512]{1,0:T(8,128)(2,1)S(1)} %get-tuple-element.31), channel_id=1, source_target_pairs={{0,2},{1,3},{2,0},{3,1},{4,6},{5,7},{6,4},{7,5},{8,10},{9,11},{10,... | collective-permute-start | bytes 393224 | tf_op jit(solution)/shard_map/ppermute | solution.py:271
  15.6 32.2 %collective-permute-start.2 = (bf16[128,512]{1,0:T(8,128)(2,1)S(1)}, bf16[128,512]{1,0:T(8,128)(2,1)S(1)}, u32[]{:S(2)}, u32[]{:S(2)}) collective-permute-start(bf16[128,512]{1,0:T(8,128)(2,1)S(1)} %get-tuple-element.32), channel_id=1, source_target_pairs={{0,3},{1,0},{2,1},{3,2},{4,7},{5,4},{6,5},{7,6},{8,11},{9,8},{10,9... | collective-permute-start | bytes 393224 | tf_op jit(solution)/shard_map/ppermute | solution.py:271
  48.4 6.5 %collective-permute-start.3 = (bf16[512,256]{1,0:T(8,128)(2,1)S(1)}, bf16[512,256]{1,0:T(8,128)(2,1)S(1)}, u32[]{:S(2)}, u32[]{:S(2)}) collective-permute-start(bf16[512,256]{1,0:T(8,128)(2,1)S(1)} %get-tuple-element.34), channel_id=1, source_target_pairs={{0,4},{1,5},{2,6},{3,7},{4,0},{5,1},{6,2},{7,3},{8,12},{9,13},{10,... | collective-permute-start | bytes 786440 | tf_op jit(solution)/shard_map/ppermute | solution.py:271
  49.9 10.7 %collective-permute-start.4 = (bf16[512,256]{1,0:T(8,128)(2,1)S(1)}, bf16[512,256]{1,0:T(8,128)(2,1)S(1)}, u32[]{:S(2)}, u32[]{:S(2)}) collective-permute-start(bf16[512,256]{1,0:T(8,128)(2,1)S(1)} %get-tuple-element.33.mine_ref), channel_id=1, source_target_pairs={{0,8},{1,9},{2,10},{3,11},{4,12},{5,13},{6,14},{7,15},{8,16},{9,17... | collective-permute-start | bytes 786440 | tf_op jit(solution)/shard_map/ppermute | solution.py:271
  53.0 13.3 %collective-permute-start.5 = (bf16[512,256]{1,0:T(8,128)(2,1)S(1)}, bf16[512,256]{1,0:T(8,128)(2,1)S(1)}, u32[]{:S(2)}, u32[]{:S(2)}) collective-permute-start(bf16[512,256]{1,0:T(8,128)(2,1)S(1)} %get-tuple-element.34), channel_id=1, source_target_pairs={{0,12},{1,13},{2,14},{3,15},{4,8},{5,9},{6,10},{7,11},{8,20},{9,21... | collective-permute-start | bytes 786440 | tf_op jit(solution)/shard_map/ppermute | solution.py:271
  76.3 9.5 %collective-permute-start.10 = (bf16[512,256]{1,0:T(8,128)(2,1)S(1)}, bf16[512,256]{1,0:T(8,128)(2,1)S(1)}, u32[]{:S(2)}, u32[]{:S(2)}) collective-permute-start(bf16[512,256]{1,0:T(8,128)(2,1)S(1)} %get-tuple-element.43), channel_id=1, source_target_pairs={{8,0},{9,1},{10,2},{11,3},{12,4},{13,5},{14,6},{15,7},{16,8},{17,9... | collective-permute-start | bytes 786440 | tf_op jit(solution)/shard_map/ppermute | solution.py:271
  78.5 17.7 %collective-permute-start.12 = (bf16[512,256]{1,0:T(8,128)(2,1)S(1)}, bf16[512,256]{1,0:T(8,128)(2,1)S(1)}, u32[]{:S(2)}, u32[]{:S(2)}) collective-permute-start(bf16[512,256]{1,0:T(8,128)(2,1)S(1)} %get-tuple-element.47), channel_id=1, source_target_pairs={{0,4},{1,5},{2,6},{3,7},{4,0},{5,1},{6,2},{7,3},{8,12},{9,13},{10,... | collective-permute-start | bytes 786440 | tf_op jit(solution)/shard_map/ppermute | solution.py:271
  79.1 17.0 %collective-permute-start.13 = (bf16[512,256]{1,0:T(8,128)(2,1)S(1)}, bf16[512,256]{1,0:T(8,128)(2,1)S(1)}, u32[]{:S(2)}, u32[]{:S(2)}) collective-permute-start(bf16[512,256]{1,0:T(8,128)(2,1)S(1)} %get-tuple-element.48), channel_id=1, source_target_pairs={{8,4},{9,5},{10,6},{11,7},{12,0},{13,1},{14,2},{15,3},{16,12},{17,... | collective-permute-start | bytes 786440 | tf_op jit(solution)/shard_map/ppermute | solution.py:271
  81.1 5.1 %collective-permute-start.7 = (bf16[256,256]{1,0:T(8,128)(2,1)S(1)}, bf16[256,256]{1,0:T(8,128)(2,1)S(1)}, u32[]{:S(2)}, u32[]{:S(2)}) collective-permute-start(bf16[256,256]{1,0:T(8,128)(2,1)S(1)} %get-tuple-element.40), channel_id=1, source_target_pairs={{0,1},{1,2},{2,3},{3,0},{4,5},{5,6},{6,7},{7,4},{8,9},{9,10},{10,1... | collective-permute-start | bytes 393224 | tf_op jit(solution)/shard_map/ppermute | solution.py:271
  81.1 9.9 %collective-permute-start.8 = (bf16[256,256]{1,0:T(8,128)(2,1)S(1)}, bf16[256,256]{1,0:T(8,128)(2,1)S(1)}, u32[]{:S(2)}, u32[]{:S(2)}) collective-permute-start(bf16[256,256]{1,0:T(8,128)(2,1)S(1)} %get-tuple-element.41), channel_id=1, source_target_pairs={{0,2},{1,3},{2,0},{3,1},{4,6},{5,7},{6,4},{7,5},{8,10},{9,11},{10,... | collective-permute-start | bytes 393224 | tf_op jit(solution)/shard_map/ppermute | solution.py:271
  85.9 9.2 %collective-permute-start.9 = (bf16[256,256]{1,0:T(8,128)(2,1)S(1)}, bf16[256,256]{1,0:T(8,128)(2,1)S(1)}, u32[]{:S(2)}, u32[]{:S(2)}) collective-permute-start(bf16[256,256]{1,0:T(8,128)(2,1)S(1)} %get-tuple-element.42), channel_id=1, source_target_pairs={{0,3},{1,0},{2,1},{3,2},{4,7},{5,4},{6,5},{7,6},{8,11},{9,8},{10,9... | collective-permute-start | bytes 393224 | tf_op jit(solution)/shard_map/ppermute | solution.py:271
  95.6 16.7 %collective-permute-start.11 = (bf16[512,256]{1,0:T(8,128)(2,1)S(1)}, bf16[512,256]{1,0:T(8,128)(2,1)S(1)}, u32[]{:S(2)}, u32[]{:S(2)}) collective-permute-start(bf16[512,256]{1,0:T(8,128)(2,1)S(1)} %get-tuple-element.45), channel_id=1, source_target_pairs={{0,4},{1,5},{2,6},{3,7},{4,0},{5,1},{6,2},{7,3},{8,12},{9,13},{10,... | collective-permute-start | bytes 786440 | tf_op jit(solution)/shard_map/ppermute | solution.py:271
  96.8 5.1 %collective-permute-start.14 = (bf16[128,512]{1,0:T(8,128)(2,1)S(1)}, bf16[128,512]{1,0:T(8,128)(2,1)S(1)}, u32[]{:S(2)}, u32[]{:S(2)}) collective-permute-start(bf16[128,512]{1,0:T(8,128)(2,1)S(1)} %get-tuple-element.50), channel_id=1, source_target_pairs={{0,1},{1,2},{2,3},{3,0},{4,5},{5,6},{6,7},{7,4},{8,9},{9,10},{10,1... | collective-permute-start | bytes 393224 | tf_op jit(solution)/shard_map/ppermute | solution.py:271
  96.9 11.5 %collective-permute-start.15 = (bf16[128,512]{1,0:T(8,128)(2,1)S(1)}, bf16[128,512]{1,0:T(8,128)(2,1)S(1)}, u32[]{:S(2)}, u32[]{:S(2)}) collective-permute-start(bf16[128,512]{1,0:T(8,128)(2,1)S(1)} %get-tuple-element.51), channel_id=1, source_target_pairs={{0,2},{1,3},{2,0},{3,1},{4,6},{5,7},{6,4},{7,5},{8,10},{9,11},{10,... | collective-permute-start | bytes 393224 | tf_op jit(solution)/shard_map/ppermute | solution.py:271
  98.4 12.4 %collective-permute-start.16 = (bf16[128,512]{1,0:T(8,128)(2,1)S(1)}, bf16[128,512]{1,0:T(8,128)(2,1)S(1)}, u32[]{:S(2)}, u32[]{:S(2)}) collective-permute-start(bf16[128,512]{1,0:T(8,128)(2,1)S(1)} %get-tuple-element.52), channel_id=1, source_target_pairs={{0,3},{1,0},{2,1},{3,2},{4,7},{5,4},{6,5},{7,6},{8,11},{9,8},{10,9... | collective-permute-start | bytes 393224 | tf_op jit(solution)/shard_map/ppermute | solution.py:271

commit v9 on v7

--- a/solution.py
+++ b/solution.py
@@ -132,29 +132,34 @@
     copied(sems, pairs)
 
 
-def unpack_kv_kernel(heads, place_ref, *refs):
-    in_refs, (k_ref, v_ref) = refs[:heads], refs[heads:]
-    core, head = place_ref[1], place_ref[2]
+def sort_kv_kernel(heads, place_ref, *refs):
+    halves, (mine_ref, other_ref) = (refs[:heads], refs[heads : 2 * heads]), refs[2 * heads :]
+    core = place_ref[1]
+    for c in range(2):
+
+        @pl.when(core == c)
+        def _():
+            for k in range(heads):
+                mine_ref[k * BLOCK : (k + 1) * BLOCK] = halves[c][k][...]
+                other_ref[k * BLOCK : (k + 1) * BLOCK] = halves[1 - c][k][...]
+
+
+def unpack_kv_kernel(heads, place_ref, mine_ref, sibling_ref, k_ref, v_ref):
+    core = place_ref[1]
     d = HEAD_SIZE
-    for h in range(heads):
-        for c in range(2):
-
-            @pl.when((head == h) & (core == c))
-            def _():
-                for k, in_ref in enumerate(in_refs):
-                    z = (h - k) % heads
-                    for n, g in enumerate((2 * z + c, 2 * z + 1 - c)):
-                        k_ref[:, g * d : (g + 1) * d] = in_ref[:, 2 * n * d : (2 * n + 1) * d]
-                        v_ref[:, g * d : (g + 1) * d] = in_ref[:, (2 * n + 1) * d : (2 * n + 2) * d]
-
-
-def add_kernel(heads, place_ref, own_ref, near_ref, sibling_ref, far_ref, *out_refs):
-    width = 2 * HEAD_SIZE
+    for k in range(heads):
+        z = source(place_ref, heads, k)
+        rows = slice(k * BLOCK, (k + 1) * BLOCK)
+        for ref, c in ((mine_ref, core), (sibling_ref, 1 - core)):
+            columns = at((2 * z + c) * d, d)
+            k_ref[:, columns] = ref[rows, :d]
+            v_ref[:, columns] = ref[rows, d:]
+
+
+def add_kernel(heads, place_ref, own_ref, back_ref, after_ref, *out_refs):
     for k, out_ref in enumerate(out_refs):
         rows = at(onward(place_ref, heads, k) * BLOCK, BLOCK)
-        wide = lambda ref: ref[rows].astype(jnp.float32)
-        out_ref[:, :width] = (own_ref[rows] + wide(near_ref)).astype(jnp.bfloat16)
-        out_ref[:, width:] = (wide(sibling_ref) + wide(far_ref)).astype(jnp.bfloat16)
+        out_ref[...] = (own_ref[rows] + back_ref[rows].astype(jnp.float32)).astype(jnp.bfloat16)
 
 
 def attention_block(i, count, q, g, own_ref, prev_ref, own_kt_ref, prev_kt_ref, own_grad_ref, prev_grad_ref, bias):
@@ -196,42 +201,48 @@
     return dq_t * score_scale
 
 
-def attention_kernel(heads, steps, last, place_ref, own_ref, own_kt_ref, a_ref, b_ref, *refs):
+def attention_kernel(heads, steps, cores, phase, place_ref, own_ref, own_kt_ref, a_ref, b_ref, *refs):
     d = HEAD_SIZE
     count = 2 * heads
     half = heads * BLOCK
+    first, core, head = place_ref[0], place_ref[1], place_ref[2]
+    low_rows, high_rows = slice(0, half), slice(half, 2 * half)
     block_refs, refs = refs[: len(steps)], refs[len(steps) :]
-    if last:
-        own_so_far_ref, prev_so_far_ref = refs[:2]
-        own_mine_ref, own_other_ref, prev_mine_ref, prev_other_ref = refs[2:6]
-        dq_refs, (qd_ref, dq_ref, own_grad_ref, prev_grad_ref) = refs[6:-4], refs[-4:]
-        prev_ref, prev_kt_ref = a_ref, b_ref
-        own_grad_ref[...] = own_so_far_ref[...]
-        prev_grad_ref[...] = prev_so_far_ref[...]
-    else:
+    prev_ref, prev_kt_ref = a_ref, b_ref
+    if phase == 0:
         prev_ref, prev_kt_ref, own_grad_ref, prev_grad_ref = refs[:4]
         dq_refs, (qd_ref, dq_ref) = refs[4:-2], refs[-2:]
         own_grad_ref[...] = jnp.zeros_like(own_grad_ref)
         prev_grad_ref[...] = jnp.zeros_like(prev_grad_ref)
-    first, core, head = place_ref[0], place_ref[1], place_ref[2]
-    mine, other = at(core * half, half), at((1 - core) * half, half)
-    if not last:
-        prev_ref[mine] = a_ref[...]
-        prev_ref[other] = b_ref[...]
+        prev_ref[at(core * half, half)] = a_ref[...]
+        prev_ref[at((1 - core) * half, half)] = b_ref[...]
         prev_kt_ref[...] = prev_ref[:, :d].T
+    elif phase == 1:
+        own_sums_ref, prev_sums_ref, own_grad_ref, prev_high_ref, back_ref, dq_out_ref = refs[:6]
+        qd_ref, dq_ref, prev_grad_ref = refs[6:]
+        own_grad_ref[...] = own_sums_ref[low_rows]
+        prev_grad_ref[...] = prev_sums_ref[...]
+    else:
+        own_low_ref, own_sums_ref, prev_high_ref, dq_so_far_ref = refs[:4]
+        dq_early_refs, refs = refs[4 : 4 + heads - len(steps)], refs[4 + heads - len(steps) :]
+        own_a_ref, own_b_ref, back_ref = refs[:3]
+        dq_refs, (qd_ref, dq_ref, own_grad_ref, prev_grad_ref) = refs[3:-4], refs[-4:]
+        own_grad_ref[low_rows] = own_low_ref[...]
+        own_grad_ref[high_rows] = own_sums_ref[high_rows]
+        prev_grad_ref[high_rows] = prev_high_ref[...]
+        dq_ref[:, :BLOCK] = dq_so_far_ref[...]
     for n, block_ref in enumerate(block_refs):
         qd_ref[n] = block_ref[: 2 * BLOCK]
     bias = jnp.where(first == 1, masked_value, 0.0).astype(jnp.float32)
 
     @pl.loop(0, len(steps))
     def _(n):
-        step = steps[0] + n
-        z_here = lax.rem(head + heads - step, heads)
+        z_here = lax.rem(head + heads - (steps[0] + n), heads)
         for z in range(heads):
 
             @pl.when(z_here == z)
             def _():
-                for c in range(2):
+                for c in cores:
                     rows = slice(c * BLOCK, (c + 1) * BLOCK)
                     q = jnp.concatenate([qd_ref[n, rows, :d], qd_ref[n, rows, d : 2 * d]], 0)
                     g = jnp.concatenate([qd_ref[n, rows, 2 * d : 3 * d], qd_ref[n, rows, 3 * d :]], 0)
@@ -242,44 +253,61 @@
                     dq_ref[n, rows, :d] = dq_t[:, :BLOCK].T.astype(jnp.bfloat16)
                     dq_ref[n, rows, d:] = dq_t[:, BLOCK:].T.astype(jnp.bfloat16)
 
-    for n, ref in enumerate(dq_refs):
-        ref[...] = dq_ref[n]
-    if last:
-        for ref, grad_ref, rows in (
-            (prev_mine_ref, prev_grad_ref, mine),
-            (prev_other_ref, prev_grad_ref, other),
-            (own_other_ref, own_grad_ref, other),
-            (own_mine_ref, own_grad_ref, mine),
-        ):
-            ref[:, :d] = (grad_ref[rows, :d] * score_scale).astype(ref.dtype)
-            ref[:, d:] = grad_ref[rows, d:].astype(ref.dtype)
-
-
-def attention_backward(heads, steps, place, own, prev, blocks, so_far=()):
+    def finish(ref, grad_ref, rows):
+        ref[low_rows, :d] = (grad_ref[rows, :d] * score_scale).astype(ref.dtype)
+        ref[low_rows, d:] = grad_ref[rows, d:].astype(ref.dtype)
+
+    if phase == 0:
+        for n, ref in enumerate(dq_refs):
+            ref[...] = dq_ref[n]
+    elif phase == 1:
+        finish(back_ref, prev_grad_ref, low_rows)
+        prev_high_ref[...] = prev_grad_ref[high_rows]
+        dq_out_ref[...] = dq_ref[:, :BLOCK]
+    else:
+        finish(back_ref, prev_grad_ref, high_rows)
+        finish(own_a_ref, own_grad_ref, low_rows)
+        finish(own_b_ref, own_grad_ref, high_rows)
+        for ref, early_ref in zip(dq_refs, dq_early_refs):
+            ref[...] = early_ref[...]
+        for n, ref in enumerate(dq_refs[len(dq_early_refs) :]):
+            ref[...] = dq_ref[n]
+
+
+def attention_backward(heads, place, own, near, far, blocks):
     half, d = heads * BLOCK, HEAD_SIZE
     whole = 2 * half
     low, wide = jnp.bfloat16, jnp.float32
-    part = shape_of(low, half, 2 * d)
-    sums = shape_of(wide, whole, 2 * d)
-    scratch = (
-        pltpu.VMEM((len(steps), 2 * BLOCK, 4 * d), low),
-        pltpu.VMEM((len(steps), 2 * BLOCK, 2 * d), low),
-    )
-    if so_far:
-        outs = (shape_of(wide, half, 2 * d), part, part, part)
-        scratch += (pltpu.VMEM((whole, 2 * d), wide), pltpu.VMEM((whole, 2 * d), wide))
-    else:
-        outs = (shape_of(low, whole, 2 * d), shape_of(low, d, whole), sums, sums)
-    outs = call(
-        functools.partial(attention_kernel, heads, steps, bool(so_far)),
-        outs + (shape_of(low, 2 * BLOCK, 2 * d),) * len(steps),
-        (place,) + tuple(own) + tuple(prev) + tuple(blocks) + tuple(so_far),
-        scratch,
-        10 * whole * whole * d,
-        whole * whole,
-        32,
-    )
-    return outs[:4], outs[4:]
+    sums, half_sums, part = shape_of(wide, whole, 2 * d), shape_of(wide, half, 2 * d), shape_of(low, half, 2 * d)
+    block = shape_of(low, 2 * BLOCK, 2 * d)
+    early, late = tuple(range(heads // 2)), tuple(range(heads // 2, heads))
+
+    def run(steps, cores, phase, outs, operands, scratch):
+        scratch = (
+            pltpu.VMEM((len(steps), 2 * BLOCK, 4 * d), low),
+            pltpu.VMEM((len(steps), 2 * BLOCK, 2 * d), low),
+        ) + (pltpu.VMEM((whole, 2 * d), wide),) * scratch
+        kernel = functools.partial(attention_kernel, heads, steps, cores, phase)
+        return call(kernel, outs, (place,) + tuple(own) + tuple(operands), scratch, 1, 1, 32)
+
+    outs = (shape_of(low, whole, 2 * d), shape_of(low, d, whole), sums, sums) + (block,) * len(early)
+    outs = run(early, (0, 1), 0, outs, [near, far] + [blocks[k] for k in early], 0)
+    prev, (own_sums, prev_sums), dq_early = outs[:2], outs[2:4], outs[4:]
+    late_blocks = tuple(blocks[k] for k in late)
+    wide_part = shape_of(low, half + 32, 2 * d)
+    outs = (half_sums, half_sums, wide_part, shape_of(low, len(late), BLOCK, 2 * d))
+    own_low, prev_high, back_a, dq_so_far = run(
+        late, (0,), 1, outs, prev + late_blocks + (own_sums, prev_sums), 1
+    )
+    outs = run(
+        late,
+        (1,),
+        2,
+        (half_sums, half_sums, part) + (block,) * heads,
+        prev + late_blocks + (own_low, own_sums, prev_high, dq_so_far) + dq_early,
+        2,
+    )
+    return outs[:2], (back_a, outs[2]), outs[3:]
 
 
 def moved(value, chips, heads, chip_step, flip, head_step):
@@ -334,20 +362,17 @@
         (shape_of(low, 2 * heads * rows, 2 * d), shape_of(low, d, 2 * heads * rows)),
         (place, mine, sibling),
     )
-    early, late = tuple(range(heads // 2)), tuple(range(heads // 2, heads))
-    prev_and_sums, dq_early = attention_backward(heads, early, place, own, (near, far), [blocks[k] for k in early])
-    grads, dq_late = attention_backward(
-        heads, late, place, own, prev_and_sums[:2], [blocks[k] for k in late], prev_and_sums[2:]
-    )
-    own_mine, own_other, prev_mine, prev_other = grads
-    near_back = across(prev_mine, chip_step=-1, flip=0)
-    far_back = across(prev_other, chip_step=-1, flip=1)
-    sibling_back = across(own_other, chip_step=0, flip=1)
-    back = dict(zip(early + late, dq_early + dq_late))
-    dqs = [
-        send(back[heads - k], chip_step=0, flip=0, head_step=k) if k else back[0] for k in range(heads)
-    ]
-    totals = call(bind(add_kernel), (slab,) * heads, (place, own_mine, near_back, sibling_back, far_back))
+    own_sums, partial, dqs = attention_backward(heads, place, own, near, far, blocks)
+    back = [across(part, chip_step=-1, flip=0) for part in partial]
+    dqs = (dqs[0],) + tuple(send(dqs[heads - k], chip_step=0, flip=0, head_step=k) for k in range(1, heads))
+    piece = shape_of(low, rows, 2 * d)
+    total_a = call(bind(add_kernel), (piece,) * heads, (place, own_sums[0], back[0], mine[:8]))
+    total_b = call(bind(add_kernel), (piece,) * heads, (place, own_sums[1], back[1], total_a[0]))
+    totals = [spread(total_a), spread(total_b)]
+    kv_mine, kv_other = call(
+        bind(sort_kv_kernel), (shape_of(low, heads * rows, 2 * d),) * 2, (place,) + totals[0] + totals[1]
+    )
+    kv_sibling = across(kv_other, chip_step=0, flip=1)
     dq_mine, dq_other = call(
         bind(sort_dq_kernel), (shape_of(low, heads * rows, 2 * d),) * 2, (place,) + tuple(dqs)
     )
@@ -355,9 +380,8 @@
     query_grad = copy_call(
         bind(unpack_dq_kernel), 2 * heads, shape_of(low, *query_rows.shape), (place, dq_mine, dq_sibling)
     )
-    totals = spread(totals)
     key_grad, value_grad = call(
-        bind(unpack_kv_kernel), (shape_of(low, *key_rows.shape),) * 2, (place,) + totals
+        bind(unpack_kv_kernel), (shape_of(low, *key_rows.shape),) * 2, (place, kv_mine, kv_sibling)
     )
     return query_grad, key_grad, value_grad
 

time: 92.7 us -> 90.8 us (0.980)
  waiting for transfers between devices: 36.9 us -> 34.1 us
  Pallas kernels: 19.9 us -> 22.3 us
  starting transfers between devices: 31.5 us -> 30.5 us
    ppermute x20 -> x23, waiting for transfers between devices: 36.9 us -> 34.1 us  [moved(): return lax.ppermute(value, ('chip', 'core', 'head'), pairs)]
    pallas_call x11 -> x14, Pallas kernels: 19.9 us -> 22.3 us  [call(): pl.pallas_call(kernel, out_shape=out_shape, in_specs=[SMEM_SPEC] + [spec]...]
    ppermute x20 -> x23, starting transfers between devices: 31.5 us -> 30.5 us  [moved(): return lax.ppermute(value, ('chip', 'core', 'head'), pairs)]
  transfers between devices with their start and end apart: 20 -> 23, of which waited for: 10 -> 10; matrix products, arithmetic and copies ran while one was open for 0% -> 0% of each run, Pallas kernels for 19% -> 18%
where the time goes in v9:
time: 90.8 us; the launch traced here: 90 us
  waiting for transfers between devices  34.1 us (38%)
  starting transfers between devices  30.5 us (34%)
  Pallas kernels  22.3 us (25%)
  local copies, waits for them, and re-layouts  2.09 us (2%)
    ppermute x23, waiting for transfers between devices, moved(): return lax.ppermute(value, ('chip', 'core', 'head'), pairs)  34.1 us
    ppermute x23, starting transfers between devices, moved(): return lax.ppermute(value, ('chip', 'core', 'head'), pairs)  30.5 us
    pallas_call x14, Pallas kernels, call(): pl.pallas_call(kernel, out_shape=out_shape, in_specs=[SMEM_SPEC] + [spec]...  22.3 us
    unnamed x8, local copies, waits for them, and re-layouts  2.09 us
  transfers between devices with their start and end apart: 23, of which 10 were waited for; matrix products, arithmetic and copies ran while one was open for 0% of the time, Pallas kernels for 18%

profile of v9, /device:TPU:13, one launch (start us, length us, event | category | flops | bytes accessed | tf_op | source)
XLA Modules:
  0.0 90.0 jit_solution(5525682882734394756)
XLA Ops:
  0.6 0.1 pad_add_fusion.place_ref
  0.7 1.0 %copy-done = bf16[128,2048]{1,0:T(8,128)(2,1)S(1)} copy-done((bf16[128,2048]{1,0:T(8,128)(2,1)S(1)}, bf16[128,2048]{1,0:T(8,128)(2,1)}, u32[]{:S(2)}) %copy-start) | copy-done | bytes 524312
  1.8 1.0 %copy-done.1 = bf16[128,2048]{1,0:T(8,128)(2,1)S(1)} copy-done((bf16[128,2048]{1,0:T(8,128)(2,1)S(1)}, bf16[128,2048]{1,0:T(8,128)(2,1)}, u32[]{:S(2)}) %copy-start.1) | copy-done | bytes 524312
  2.8 0.9 shard_map.70
  3.7 0.7 collective-permute-start.6
  4.5 0.0 copy-done.2
  4.5 0.9 shard_map.67
  5.3 1.3 %collective-permute-start = (bf16[128,512]{1,0:T(8,128)(2,1)S(1)}, bf16[128,512]{1,0:T(8,128)(2,1)S(1)}, u32[]{:S(2)}, u32[]{:S(2)}) collective-permute-start(bf16[128,512]{1,0:T(8,128)(2,1)S(1)} %get-tuple-element.49), channel_id=1, source_target_pairs={{0,1},{1,2},{2,3},{3,0},{4,5},{5,6},{6,7},{7,4},{8,9},{9,10},{10,1... | collective-permute-start | bytes 393224 | tf_op jit(solution)/shard_map/ppermute | solution.py:322
  6.7 1.1 %collective-permute-start.1 = (bf16[128,512]{1,0:T(8,128)(2,1)S(1)}, bf16[128,512]{1,0:T(8,128)(2,1)S(1)}, u32[]{:S(2)}, u32[]{:S(2)}) collective-permute-start(bf16[128,512]{1,0:T(8,128)(2,1)S(1)} %get-tuple-element.50), channel_id=1, source_target_pairs={{0,2},{1,3},{2,0},{3,1},{4,6},{5,7},{6,4},{7,5},{8,10},{9,11},{10,... | collective-permute-start | bytes 393224 | tf_op jit(solution)/shard_map/ppermute | solution.py:322
  7.8 1.4 %collective-permute-start.2 = (bf16[128,512]{1,0:T(8,128)(2,1)S(1)}, bf16[128,512]{1,0:T(8,128)(2,1)S(1)}, u32[]{:S(2)}, u32[]{:S(2)}) collective-permute-start(bf16[128,512]{1,0:T(8,128)(2,1)S(1)} %get-tuple-element.51), channel_id=1, source_target_pairs={{0,3},{1,0},{2,1},{3,2},{4,7},{5,4},{6,5},{7,6},{8,11},{9,8},{10,9... | collective-permute-start | bytes 393224 | tf_op jit(solution)/shard_map/ppermute | solution.py:322
  9.2 1.3 %collective-permute-done.refs_1_ = bf16[128,512]{1,0:T(8,128)(2,1)S(1)} collective-permute-done((bf16[128,512]{1,0:T(8,128)(2,1)S(1)}, bf16[128,512]{1,0:T(8,128)(2,1)S(1)}, u32[]{:S(2)}, u32[]{:S(2)}) %collective-permute-start) | collective-permute-done | bytes 131104 | tf_op jit(solution)/shard_map/ppermute | solution.py:322
  10.5 7.5 %collective-permute-done.1.refs_2_ = bf16[128,512]{1,0:T(8,128)(2,1)S(1)} collective-permute-done((bf16[128,512]{1,0:T(8,128)(2,1)S(1)}, bf16[128,512]{1,0:T(8,128)(2,1)S(1)}, u32[]{:S(2)}, u32[]{:S(2)}) %collective-permute-start.1) | collective-permute-done | bytes 131104 | tf_op jit(solution)/shard_map/ppermute | solution.py:322
  18.0 2.1 %collective-permute-done.2.refs_3_ = bf16[128,512]{1,0:T(8,128)(2,1)S(1)} collective-permute-done((bf16[128,512]{1,0:T(8,128)(2,1)S(1)}, bf16[128,512]{1,0:T(8,128)(2,1)S(1)}, u32[]{:S(2)}, u32[]{:S(2)}) %collective-permute-start.2) | collective-permute-done | bytes 131104 | tf_op jit(solution)/shard_map/ppermute | solution.py:322
  20.1 0.6 shard_map.68
  20.7 0.5 collective-permute-start.3
  21.2 0.0 collective-permute-done.6.other_ref
  21.2 0.6 shard_map.71
  21.9 0.1 collective-permute-start.7
  21.9 1.4 %collective-permute-start.8 = (bf16[272,512]{1,0:T(8,128)(2,1)S(1)}, bf16[272,512]{1,0:T(8,128)(2,1)S(1)}, u32[]{:S(2)}, u32[]{:S(2)}) collective-permute-start(bf16[272,512]{1,0:T(8,128)(2,1)S(1)} %get-tuple-element.62), channel_id=1, source_target_pairs={{0,2},{1,3},{2,0},{3,1},{4,6},{5,7},{6,4},{7,5},{8,10},{9,11},{10,... | collective-permute-start | bytes 835592 | tf_op jit(solution)/shard_map/ppermute | solution.py:322
  23.4 1.4 %collective-permute-start.9 = (bf16[272,512]{1,0:T(8,128)(2,1)S(1)}, bf16[272,512]{1,0:T(8,128)(2,1)S(1)}, u32[]{:S(2)}, u32[]{:S(2)}) collective-permute-start(bf16[272,512]{1,0:T(8,128)(2,1)S(1)} %get-tuple-element.63), channel_id=1, source_target_pairs={{0,3},{1,0},{2,1},{3,2},{4,7},{5,4},{6,5},{7,6},{8,11},{9,8},{10,9... | collective-permute-start | bytes 835592 | tf_op jit(solution)/shard_map/ppermute | solution.py:322
  24.7 3.9 %collective-permute-start.5 = (bf16[512,256]{1,0:T(8,128)(2,1)S(1)}, bf16[512,256]{1,0:T(8,128)(2,1)S(1)}, u32[]{:S(2)}, u32[]{:S(2)}) collective-permute-start(bf16[512,256]{1,0:T(8,128)(2,1)S(1)} %get-tuple-element.53), channel_id=1, source_target_pairs={{0,12},{1,13},{2,14},{3,15},{4,8},{5,9},{6,10},{7,11},{8,20},{9,21... | collective-permute-start | bytes 786440 | tf_op jit(solution)/shard_map/ppermute | solution.py:322
  28.6 0.0 collective-permute-done.3.sibling_ref
  28.6 1.9 %collective-permute-start.4 = (bf16[512,256]{1,0:T(8,128)(2,1)S(1)}, bf16[512,256]{1,0:T(8,128)(2,1)S(1)}, u32[]{:S(2)}, u32[]{:S(2)}) collective-permute-start(bf16[512,256]{1,0:T(8,128)(2,1)S(1)} %get-tuple-element.52.mine_ref), channel_id=1, source_target_pairs={{0,8},{1,9},{2,10},{3,11},{4,12},{5,13},{6,14},{7,15},{8,16},{9,17... | collective-permute-start | bytes 786440 | tf_op jit(solution)/shard_map/ppermute | solution.py:322
  30.6 0.7 shard_map.69
  31.3 5.0 %collective-permute-done.5.b_ref = bf16[512,256]{1,0:T(8,128)(2,1)S(1)} collective-permute-done((bf16[512,256]{1,0:T(8,128)(2,1)S(1)}, bf16[512,256]{1,0:T(8,128)(2,1)S(1)}, u32[]{:S(2)}, u32[]{:S(2)}) %collective-permute-start.5) | collective-permute-done | bytes 262176 | tf_op jit(solution)/shard_map/ppermute | solution.py:322
  36.2 5.6 %collective-permute-done.4.a_ref = bf16[512,256]{1,0:T(8,128)(2,1)S(1)} collective-permute-done((bf16[512,256]{1,0:T(8,128)(2,1)S(1)}, bf16[512,256]{1,0:T(8,128)(2,1)S(1)}, u32[]{:S(2)}, u32[]{:S(2)}) %collective-permute-start.4) | collective-permute-done | bytes 262176 | tf_op jit(solution)/shard_map/ppermute | solution.py:322
  41.9 0.0 collective-permute-done.7.refs_1_
  41.9 6.1 %shard_map.72 = (bf16[1024,256]{1,0:T(8,128)(2,1)S(1)}, bf16[128,1024]{1,0:T(8,128)(2,1)S(1)}, f32[1024,256]{1,0:T(8,128)S(1)}, f32[1024,256]{1,0:T(8,128)S(1)},...) custom-call(s32[3]{0:T(128)S(1)} %pad_add_fusion.place_ref, bf16[1024,256]{1,0:T(8,128)(2,1)S(1)} %get-tuple-element.54.own_ref, ...), custom_call_target="tpu_custom_call" | custom-call | flops 1 | bytes 5013516 | tf_op jit(solution)/shard_map/pallas_call | solution.py:26
  47.9 0.0 collective-permute-done.8.refs_0_
  47.9 0.4 collective-permute-done.9.refs_1_
  48.4 3.7 %shard_map.73 = (f32[512,256]{1,0:T(8,128)S(1)}, f32[512,256]{1,0:T(8,128)S(1)}, bf16[544,256]{1,0:T(8,128)(2,1)S(1)}, bf16[2,128,256]{2,1,0:T(8,128)(2,1)S(1)}) custom-call(s32[3]{0:T(128)S(1)} %pad_add_fusion.place_ref, bf16[1024,256]{1,0:T(8,128)(2,1)S(1)} %get-tuple-element.54.own_ref, bf16[128,1024]{1,0:T(8,128)(2,1)S(1)} %get-tuple-element.55.own_kt_ref, ...), custom_call_target="tpu_custom_call" | custom-call | flops 1 | bytes 5685260 | tf_op jit(solution)/shard_map/pallas_call | solution.py:26
  52.1 3.1 %collective-permute-start.14 = (bf16[544,256]{1,0:T(8,128)(2,1)S(1)}, bf16[544,256]{1,0:T(8,128)(2,1)S(1)}, u32[]{:S(2)}, u32[]{:S(2)}) collective-permute-start(bf16[544,256]{1,0:T(8,128)(2,1)S(1)} %get-tuple-element.78), channel_id=1, source_target_pairs={{8,0},{9,1},{10,2},{11,3},{12,4},{13,5},{14,6},{15,7},{16,8},{17,9... | collective-permute-start | bytes 835592 | tf_op jit(solution)/shard_map/ppermute | solution.py:322
  55.1 3.6 %shard_map.74 = (f32[512,256]{1,0:T(8,128)S(1)}, f32[512,256]{1,0:T(8,128)S(1)}, bf16[512,256]{1,0:T(8,128)(2,1)S(1)}, bf16[256,256]{1,0:T(8,128)(2,1)S(1)}, bf1...) custom-call(s32[3]{0:T(128)S(1)} %pad_add_fusion.place_ref, ...), custom_call_target="tpu_custom_call" | custom-call | flops 1 | bytes 6455308 | tf_op jit(solution)/shard_map/pallas_call | solution.py:26
  58.8 2.2 %collective-permute-start.18 = (bf16[512,256]{1,0:T(8,128)(2,1)S(1)}, bf16[512,256]{1,0:T(8,128)(2,1)S(1)}, u32[]{:S(2)}, u32[]{:S(2)}) collective-permute-start(bf16[512,256]{1,0:T(8,128)(2,1)S(1)} %get-tuple-element.84), channel_id=1, source_target_pairs={{8,0},{9,1},{10,2},{11,3},{12,4},{13,5},{14,6},{15,7},{16,8},{17,9... | collective-permute-start | bytes 786440 | tf_op jit(solution)/shard_map/ppermute | solution.py:322
  60.9 0.1 collective-permute-start.10
  61.0 1.3 %collective-permute-start.11 = (bf16[256,256]{1,0:T(8,128)(2,1)S(1)}, bf16[256,256]{1,0:T(8,128)(2,1)S(1)}, u32[]{:S(2)}, u32[]{:S(2)}) collective-permute-start(bf16[256,256]{1,0:T(8,128)(2,1)S(1)} %get-tuple-element.73), channel_id=1, source_target_pairs={{0,2},{1,3},{2,0},{3,1},{4,6},{5,7},{6,4},{7,5},{8,10},{9,11},{10,... | collective-permute-start | bytes 393224 | tf_op jit(solution)/shard_map/ppermute | solution.py:322
  62.3 1.2 %collective-permute-start.12 = (bf16[256,256]{1,0:T(8,128)(2,1)S(1)}, bf16[256,256]{1,0:T(8,128)(2,1)S(1)}, u32[]{:S(2)}, u32[]{:S(2)}) collective-permute-start(bf16[256,256]{1,0:T(8,128)(2,1)S(1)} %get-tuple-element.74), channel_id=1, source_target_pairs={{0,3},{1,0},{2,1},{3,2},{4,7},{5,4},{6,5},{7,6},{8,11},{9,8},{10,9... | collective-permute-start | bytes 393224 | tf_op jit(solution)/shard_map/ppermute | solution.py:322
  63.5 0.0 collective-permute-done.14.back_ref
  63.5 0.6 shard_map.77
  64.1 0.3 collective-permute-start.15
  64.5 3.3 %collective-permute-done.18.back_ref = bf16[512,256]{1,0:T(8,128)(2,1)S(1)} collective-permute-done((bf16[512,256]{1,0:T(8,128)(2,1)S(1)}, bf16[512,256]{1,0:T(8,128)(2,1)S(1)}, u32[]{:S(2)}, u32[]{:S(2)}) %collective-permute-start.18) | collective-permute-done | bytes 262176 | tf_op jit(solution)/shard_map/ppermute | solution.py:322
  67.8 0.9 collective-permute-start.16
  68.7 0.6 shard_map.78
  69.3 0.0 collective-permute-done.10.refs_1_
  69.3 0.1 collective-permute-start.17
  69.3 0.5 collective-permute-done.11.refs_2_
  69.9 1.9 %collective-permute-start.19 = (bf16[128,256]{1,0:T(8,128)(2,1)S(1)}, bf16[128,256]{1,0:T(8,128)(2,1)S(1)}, u32[]{:S(2)}, u32[]{:S(2)}) collective-permute-start(bf16[128,256]{1,0:T(8,128)(2,1)S(1)} %get-tuple-element.86), channel_id=1, source_target_pairs={{0,1},{1,2},{2,3},{3,0},{4,5},{5,6},{6,7},{7,4},{8,9},{9,10},{10,1... | collective-permute-start | bytes 196616 | tf_op jit(solution)/shard_map/ppermute | solution.py:322
  71.8 5.7 %collective-permute-done.12.refs_3_ = bf16[256,256]{1,0:T(8,128)(2,1)S(1)} collective-permute-done((bf16[256,256]{1,0:T(8,128)(2,1)S(1)}, bf16[256,256]{1,0:T(8,128)(2,1)S(1)}, u32[]{:S(2)}, u32[]{:S(2)}) %collective-permute-start.12) | collective-permute-done | bytes 131104 | tf_op jit(solution)/shard_map/ppermute | solution.py:322
  77.5 0.0 collective-permute-start.20
  77.5 0.0 collective-permute-done.15.refs_1_
  77.5 0.4 collective-permute-start.21
  78.0 0.6 shard_map.75
  78.6 0.0 collective-permute-done.16.refs_2_
  78.6 4.7 %collective-permute-start.13 = (bf16[512,256]{1,0:T(8,128)(2,1)S(1)}, bf16[512,256]{1,0:T(8,128)(2,1)S(1)}, u32[]{:S(2)}, u32[]{:S(2)}) collective-permute-start(bf16[512,256]{1,0:T(8,128)(2,1)S(1)} %get-tuple-element.76), channel_id=1, source_target_pairs={{0,4},{1,5},{2,6},{3,7},{4,0},{5,1},{6,2},{7,3},{8,12},{9,13},{10,... | collective-permute-start | bytes 786440 | tf_op jit(solution)/shard_map/ppermute | solution.py:322
  83.3 0.0 collective-permute-done.17.refs_3_
  83.3 0.0 collective-permute-done.19.refs_5_
  83.3 0.0 collective-permute-done.20.refs_6_
  83.3 2.6 %collective-permute-done.21.refs_7_ = bf16[128,256]{1,0:T(8,128)(2,1)S(1)} collective-permute-done((bf16[128,256]{1,0:T(8,128)(2,1)S(1)}, bf16[128,256]{1,0:T(8,128)(2,1)S(1)}, u32[]{:S(2)}, u32[]{:S(2)}) %collective-permute-start.21) | collective-permute-done | bytes 65568 | tf_op jit(solution)/shard_map/ppermute | solution.py:322
  85.8 0.6 shard_map.79
  86.4 0.7 collective-permute-start.22
  87.1 0.0 collective-permute-done.13.sibling_ref
  87.1 1.4 %shard_map.76 = bf16[128,2048]{1,0:T(8,128)(2,1)} custom-call(s32[3]{0:T(128)S(1)} %pad_add_fusion.place_ref, bf16[512,256]{1,0:T(8,128)(2,1)S(1)} %get-tuple-element.75.mine_ref, bf16[512,256]{1,0:T(8,128)(2,1)S(1)} %collective-permute-done.13.sibling_ref), custom_call_target="tpu_custom_call" | custom-call | bytes 1048588 | tf_op jit(solution)/shard_map/pallas_call | solution.py:26
  88.5 0.0 collective-permute-done.22.sibling_ref
  88.5 1.5 %shard_map.80 = (bf16[128,1024]{1,0:T(8,128)(2,1)}, bf16[128,1024]{1,0:T(8,128)(2,1)}) custom-call(s32[3]{0:T(128)S(1)} %pad_add_fusion.place_ref, bf16[512,256]{1,0:T(8,128)(2,1)S(1)} %get-tuple-element.89.mine_ref, bf16[512,256]{1,0:T(8,128)(2,1)S(1)} %collective-permute-done.22.sibling_ref), custom_call_target="tpu_custom_call" | custom-call | bytes 1048588 | tf_op jit(solution)/shard_map/pallas_call | solution.py:26
  (6 shorter events, 0.0 us)
Async XLA Ops:
  0.7 1.0 %copy-start = (bf16[128,2048]{1,0:T(8,128)(2,1)S(1)}, bf16[128,2048]{1,0:T(8,128)(2,1)}, u32[]{:S(2)}) copy-start(bf16[128,2048]{1,0:T(8,128)(2,1)} %q_ref.1) | copy-start | bytes 1572868
  1.8 1.0 %copy-start.1 = (bf16[128,2048]{1,0:T(8,128)(2,1)S(1)}, bf16[128,2048]{1,0:T(8,128)(2,1)}, u32[]{:S(2)}) copy-start(bf16[128,2048]{1,0:T(8,128)(2,1)} %g_ref.1) | copy-start | bytes 1572868
  2.8 1.7 %copy-start.2 = (bf16[128,1024]{1,0:T(8,128)(2,1)S(1)}, bf16[128,1024]{1,0:T(8,128)(2,1)}, u32[]{:S(2)}) copy-start(bf16[128,1024]{1,0:T(8,128)(2,1)} %k_ref.1) | copy-start | bytes 786436
  2.8 1.7 %copy-start.3 = (bf16[128,1024]{1,0:T(8,128)(2,1)S(1)}, bf16[128,1024]{1,0:T(8,128)(2,1)}, u32[]{:S(2)}) copy-start(bf16[128,1024]{1,0:T(8,128)(2,1)} %v_ref.1) | copy-start | bytes 786436
  3.7 17.5 %collective-permute-start.6 = (bf16[4,128,512]{2,1,0:T(8,128)(2,1)S(1)}, bf16[4,128,512]{2,1,0:T(8,128)(2,1)S(1)}, u32[]{:S(2)}, u32[]{:S(2)}) collective-permute-start(bf16[4,128,512]{2,1,0:T(8,128)(2,1)S(1)} %get-tuple-element.57), channel_id=1, source_target_pairs={{0,4},{1,5},{2,6},{3,7},{4,0},{5,1},{6,2},{7,3},{8,12},{9,13},{10,... | collective-permute-start | bytes 1572872 | tf_op jit(solution)/shard_map/ppermute | solution.py:322
  5.3 5.1 %collective-permute-start = (bf16[128,512]{1,0:T(8,128)(2,1)S(1)}, bf16[128,512]{1,0:T(8,128)(2,1)S(1)}, u32[]{:S(2)}, u32[]{:S(2)}) collective-permute-start(bf16[128,512]{1,0:T(8,128)(2,1)S(1)} %get-tuple-element.49), channel_id=1, source_target_pairs={{0,1},{1,2},{2,3},{3,0},{4,5},{5,6},{6,7},{7,4},{8,9},{9,10},{10,1... | collective-permute-start | bytes 393224 | tf_op jit(solution)/shard_map/ppermute | solution.py:322
  6.7 11.3 %collective-permute-start.1 = (bf16[128,512]{1,0:T(8,128)(2,1)S(1)}, bf16[128,512]{1,0:T(8,128)(2,1)S(1)}, u32[]{:S(2)}, u32[]{:S(2)}) collective-permute-start(bf16[128,512]{1,0:T(8,128)(2,1)S(1)} %get-tuple-element.50), channel_id=1, source_target_pairs={{0,2},{1,3},{2,0},{3,1},{4,6},{5,7},{6,4},{7,5},{8,10},{9,11},{10,... | collective-permute-start | bytes 393224 | tf_op jit(solution)/shard_map/ppermute | solution.py:322
  7.8 12.3 %collective-permute-start.2 = (bf16[128,512]{1,0:T(8,128)(2,1)S(1)}, bf16[128,512]{1,0:T(8,128)(2,1)S(1)}, u32[]{:S(2)}, u32[]{:S(2)}) collective-permute-start(bf16[128,512]{1,0:T(8,128)(2,1)S(1)} %get-tuple-element.51), channel_id=1, source_target_pairs={{0,3},{1,0},{2,1},{3,2},{4,7},{5,4},{6,5},{7,6},{8,11},{9,8},{10,9... | collective-permute-start | bytes 393224 | tf_op jit(solution)/shard_map/ppermute | solution.py:322
  20.7 7.9 %collective-permute-start.3 = (bf16[512,256]{1,0:T(8,128)(2,1)S(1)}, bf16[512,256]{1,0:T(8,128)(2,1)S(1)}, u32[]{:S(2)}, u32[]{:S(2)}) collective-permute-start(bf16[512,256]{1,0:T(8,128)(2,1)S(1)} %get-tuple-element.53), channel_id=1, source_target_pairs={{0,4},{1,5},{2,6},{3,7},{4,0},{5,1},{6,2},{7,3},{8,12},{9,13},{10,... | collective-permute-start | bytes 786440 | tf_op jit(solution)/shard_map/ppermute | solution.py:322
  21.9 20.0 %collective-permute-start.7 = (bf16[272,512]{1,0:T(8,128)(2,1)S(1)}, bf16[272,512]{1,0:T(8,128)(2,1)S(1)}, u32[]{:S(2)}, u32[]{:S(2)}) collective-permute-start(bf16[272,512]{1,0:T(8,128)(2,1)S(1)} %get-tuple-element.59), channel_id=1, source_target_pairs={{0,1},{1,2},{2,3},{3,0},{4,5},{5,6},{6,7},{7,4},{8,9},{9,10},{10,1... | collective-permute-start | bytes 835592 | tf_op jit(solution)/shard_map/ppermute | solution.py:322
  21.9 26.0 %collective-permute-start.8 = (bf16[272,512]{1,0:T(8,128)(2,1)S(1)}, bf16[272,512]{1,0:T(8,128)(2,1)S(1)}, u32[]{:S(2)}, u32[]{:S(2)}) collective-permute-start(bf16[272,512]{1,0:T(8,128)(2,1)S(1)} %get-tuple-element.62), channel_id=1, source_target_pairs={{0,2},{1,3},{2,0},{3,1},{4,6},{5,7},{6,4},{7,5},{8,10},{9,11},{10,... | collective-permute-start | bytes 835592 | tf_op jit(solution)/shard_map/ppermute | solution.py:322
  23.4 25.0 %collective-permute-start.9 = (bf16[272,512]{1,0:T(8,128)(2,1)S(1)}, bf16[272,512]{1,0:T(8,128)(2,1)S(1)}, u32[]{:S(2)}, u32[]{:S(2)}) collective-permute-start(bf16[272,512]{1,0:T(8,128)(2,1)S(1)} %get-tuple-element.63), channel_id=1, source_target_pairs={{0,3},{1,0},{2,1},{3,2},{4,7},{5,4},{6,5},{7,6},{8,11},{9,8},{10,9... | collective-permute-start | bytes 835592 | tf_op jit(solution)/shard_map/ppermute | solution.py:322
  24.7 11.5 %collective-permute-start.5 = (bf16[512,256]{1,0:T(8,128)(2,1)S(1)}, bf16[512,256]{1,0:T(8,128)(2,1)S(1)}, u32[]{:S(2)}, u32[]{:S(2)}) collective-permute-start(bf16[512,256]{1,0:T(8,128)(2,1)S(1)} %get-tuple-element.53), channel_id=1, source_target_pairs={{0,12},{1,13},{2,14},{3,15},{4,8},{5,9},{6,10},{7,11},{8,20},{9,21... | collective-permute-start | bytes 786440 | tf_op jit(solution)/shard_map/ppermute | solution.py:322
  28.6 13.2 %collective-permute-start.4 = (bf16[512,256]{1,0:T(8,128)(2,1)S(1)}, bf16[512,256]{1,0:T(8,128)(2,1)S(1)}, u32[]{:S(2)}, u32[]{:S(2)}) collective-permute-start(bf16[512,256]{1,0:T(8,128)(2,1)S(1)} %get-tuple-element.52.mine_ref), channel_id=1, source_target_pairs={{0,8},{1,9},{2,10},{3,11},{4,12},{5,13},{6,14},{7,15},{8,16},{9,17... | collective-permute-start | bytes 786440 | tf_op jit(solution)/shard_map/ppermute | solution.py:322
  52.1 11.4 %collective-permute-start.14 = (bf16[544,256]{1,0:T(8,128)(2,1)S(1)}, bf16[544,256]{1,0:T(8,128)(2,1)S(1)}, u32[]{:S(2)}, u32[]{:S(2)}) collective-permute-start(bf16[544,256]{1,0:T(8,128)(2,1)S(1)} %get-tuple-element.78), channel_id=1, source_target_pairs={{8,0},{9,1},{10,2},{11,3},{12,4},{13,5},{14,6},{15,7},{16,8},{17,9... | collective-permute-start | bytes 835592 | tf_op jit(solution)/shard_map/ppermute | solution.py:322
  58.8 9.0 %collective-permute-start.18 = (bf16[512,256]{1,0:T(8,128)(2,1)S(1)}, bf16[512,256]{1,0:T(8,128)(2,1)S(1)}, u32[]{:S(2)}, u32[]{:S(2)}) collective-permute-start(bf16[512,256]{1,0:T(8,128)(2,1)S(1)} %get-tuple-element.84), channel_id=1, source_target_pairs={{8,0},{9,1},{10,2},{11,3},{12,4},{13,5},{14,6},{15,7},{16,8},{17,9... | collective-permute-start | bytes 786440 | tf_op jit(solution)/shard_map/ppermute | solution.py:322
  60.9 8.3 %collective-permute-start.10 = (bf16[256,256]{1,0:T(8,128)(2,1)S(1)}, bf16[256,256]{1,0:T(8,128)(2,1)S(1)}, u32[]{:S(2)}, u32[]{:S(2)}) collective-permute-start(bf16[256,256]{1,0:T(8,128)(2,1)S(1)} %get-tuple-element.72), channel_id=1, source_target_pairs={{0,1},{1,2},{2,3},{3,0},{4,5},{5,6},{6,7},{7,4},{8,9},{9,10},{10,1... | collective-permute-start | bytes 393224 | tf_op jit(solution)/shard_map/ppermute | solution.py:322
  61.0 8.9 %collective-permute-start.11 = (bf16[256,256]{1,0:T(8,128)(2,1)S(1)}, bf16[256,256]{1,0:T(8,128)(2,1)S(1)}, u32[]{:S(2)}, u32[]{:S(2)}) collective-permute-start(bf16[256,256]{1,0:T(8,128)(2,1)S(1)} %get-tuple-element.73), channel_id=1, source_target_pairs={{0,2},{1,3},{2,0},{3,1},{4,6},{5,7},{6,4},{7,5},{8,10},{9,11},{10,... | collective-permute-start | bytes 393224 | tf_op jit(solution)/shard_map/ppermute | solution.py:322
  62.3 15.2 %collective-permute-start.12 = (bf16[256,256]{1,0:T(8,128)(2,1)S(1)}, bf16[256,256]{1,0:T(8,128)(2,1)S(1)}, u32[]{:S(2)}, u32[]{:S(2)}) collective-permute-start(bf16[256,256]{1,0:T(8,128)(2,1)S(1)} %get-tuple-element.74), channel_id=1, source_target_pairs={{0,3},{1,0},{2,1},{3,2},{4,7},{5,4},{6,5},{7,6},{8,11},{9,8},{10,9... | collective-permute-start | bytes 393224 | tf_op jit(solution)/shard_map/ppermute | solution.py:322
  64.1 13.4 %collective-permute-start.15 = (bf16[128,256]{1,0:T(8,128)(2,1)S(1)}, bf16[128,256]{1,0:T(8,128)(2,1)S(1)}, u32[]{:S(2)}, u32[]{:S(2)}) collective-permute-start(bf16[128,256]{1,0:T(8,128)(2,1)S(1)} %get-tuple-element.80), channel_id=1, source_target_pairs={{0,1},{1,2},{2,3},{3,0},{4,5},{5,6},{6,7},{7,4},{8,9},{9,10},{10,1... | collective-permute-start | bytes 196616 | tf_op jit(solution)/shard_map/ppermute | solution.py:322
  67.8 10.8 %collective-permute-start.16 = (bf16[128,256]{1,0:T(8,128)(2,1)S(1)}, bf16[128,256]{1,0:T(8,128)(2,1)S(1)}, u32[]{:S(2)}, u32[]{:S(2)}) collective-permute-start(bf16[128,256]{1,0:T(8,128)(2,1)S(1)} %get-tuple-element.81), channel_id=1, source_target_pairs={{0,2},{1,3},{2,0},{3,1},{4,6},{5,7},{6,4},{7,5},{8,10},{9,11},{10,... | collective-permute-start | bytes 196616 | tf_op jit(solution)/shard_map/ppermute | solution.py:322
  69.3 14.0 %collective-permute-start.17 = (bf16[128,256]{1,0:T(8,128)(2,1)S(1)}, bf16[128,256]{1,0:T(8,128)(2,1)S(1)}, u32[]{:S(2)}, u32[]{:S(2)}) collective-permute-start(bf16[128,256]{1,0:T(8,128)(2,1)S(1)} %get-tuple-element.82), channel_id=1, source_target_pairs={{0,3},{1,0},{2,1},{3,2},{4,7},{5,4},{6,5},{7,6},{8,11},{9,8},{10,9... | collective-permute-start | bytes 196616 | tf_op jit(solution)/shard_map/ppermute | solution.py:322
  69.9 13.4 %collective-permute-start.19 = (bf16[128,256]{1,0:T(8,128)(2,1)S(1)}, bf16[128,256]{1,0:T(8,128)(2,1)S(1)}, u32[]{:S(2)}, u32[]{:S(2)}) collective-permute-start(bf16[128,256]{1,0:T(8,128)(2,1)S(1)} %get-tuple-element.86), channel_id=1, source_target_pairs={{0,1},{1,2},{2,3},{3,0},{4,5},{5,6},{6,7},{7,4},{8,9},{9,10},{10,1... | collective-permute-start | bytes 196616 | tf_op jit(solution)/shard_map/ppermute | solution.py:322
  77.5 5.7 %collective-permute-start.20 = (bf16[128,256]{1,0:T(8,128)(2,1)S(1)}, bf16[128,256]{1,0:T(8,128)(2,1)S(1)}, u32[]{:S(2)}, u32[]{:S(2)}) collective-permute-start(bf16[128,256]{1,0:T(8,128)(2,1)S(1)} %get-tuple-element.87), channel_id=1, source_target_pairs={{0,2},{1,3},{2,0},{3,1},{4,6},{5,7},{6,4},{7,5},{8,10},{9,11},{10,... | collective-permute-start | bytes 196616 | tf_op jit(solution)/shard_map/ppermute | solution.py:322
  77.5 8.3 %collective-permute-start.21 = (bf16[128,256]{1,0:T(8,128)(2,1)S(1)}, bf16[128,256]{1,0:T(8,128)(2,1)S(1)}, u32[]{:S(2)}, u32[]{:S(2)}) collective-permute-start(bf16[128,256]{1,0:T(8,128)(2,1)S(1)} %get-tuple-element.88), channel_id=1, source_target_pairs={{0,3},{1,0},{2,1},{3,2},{4,7},{5,4},{6,5},{7,6},{8,11},{9,8},{10,9... | collective-permute-start | bytes 196616 | tf_op jit(solution)/shard_map/ppermute | solution.py:322
  78.6 8.5 %collective-permute-start.13 = (bf16[512,256]{1,0:T(8,128)(2,1)S(1)}, bf16[512,256]{1,0:T(8,128)(2,1)S(1)}, u32[]{:S(2)}, u32[]{:S(2)}) collective-permute-start(bf16[512,256]{1,0:T(8,128)(2,1)S(1)} %get-tuple-element.76), channel_id=1, source_target_pairs={{0,4},{1,5},{2,6},{3,7},{4,0},{5,1},{6,2},{7,3},{8,12},{9,13},{10,... | collective-permute-start | bytes 786440 | tf_op jit(solution)/shard_map/ppermute | solution.py:322
  86.4 2.1 %collective-permute-start.22 = (bf16[512,256]{1,0:T(8,128)(2,1)S(1)}, bf16[512,256]{1,0:T(8,128)(2,1)S(1)}, u32[]{:S(2)}, u32[]{:S(2)}) collective-permute-start(bf16[512,256]{1,0:T(8,128)(2,1)S(1)} %get-tuple-element.90), channel_id=1, source_target_pairs={{0,4},{1,5},{2,6},{3,7},{4,0},{5,1},{6,2},{7,3},{8,12},{9,13},{10,... | collective-permute-start | bytes 786440 | tf_op jit(solution)/shard_map/ppermute | solution.py:322

commit v10 on v9

--- a/solution.py
+++ b/solution.py
@@ -54,32 +54,29 @@
         copy.wait()
 
 
-def onward(place_ref, heads, k):
-    return lax.rem(place_ref[2] + k, heads)
-
-
-def source(place_ref, heads, k):
-    return lax.rem(place_ref[2] + heads - k, heads)
-
-
-def pack_kv_kernel(heads, place_ref, k_ref, v_ref, *refs):
-    out_refs, sems = refs[:-1], refs[-1]
-    core = place_ref[1]
-    d = HEAD_SIZE
+def steps_of(heads):
+    return (0,) + tuple(sorted(range(1, heads), key=lambda k: -min(k, heads - k)))
+
+
+def onward(place_ref, heads, n):
+    return lax.rem(place_ref[2] + steps_of(heads)[n], heads)
+
+
+def source(place_ref, heads, n):
+    return lax.rem(place_ref[2] + heads - steps_of(heads)[n], heads)
+
+
+def pack_kernel(heads, place_ref, k_ref, v_ref, q_ref, g_ref, *refs):
+    kv_refs, (mine_ref, other_ref, sems) = refs[:heads], refs[heads:]
+    core = place_ref[1]
+    d, width = HEAD_SIZE, 2 * HEAD_SIZE
     pairs = []
-    for k, out_ref in enumerate(out_refs):
+    for k, out_ref in enumerate(kv_refs):
         z = onward(place_ref, heads, k)
         for n, g in enumerate((2 * z + core, 2 * z + 1 - core)):
             columns = at(g * d, d)
             pairs.append((k_ref.at[:, columns], out_ref.at[:, pl.ds(2 * n * d, d)]))
             pairs.append((v_ref.at[:, columns], out_ref.at[:, pl.ds((2 * n + 1) * d, d)]))
-    copied(sems, pairs)
-
-
-def pack_qd_kernel(heads, place_ref, q_ref, g_ref, mine_ref, other_ref, sems):
-    core = place_ref[1]
-    width = 2 * HEAD_SIZE
-    pairs = []
     for ref, c in ((other_ref, 1 - core), (mine_ref, core)):
         for k in range(heads):
             columns = at((2 * onward(place_ref, heads, k) + c) * width, width)
@@ -112,7 +109,7 @@
         out_ref[at((1 - core) * BLOCK, BLOCK)] = other_ref[k]
 
 
-def sort_dq_kernel(heads, place_ref, *refs):
+def sort_kernel(heads, place_ref, *refs):
     in_refs, (mine_ref, other_ref) = refs[:heads], refs[heads:]
     core = place_ref[1]
     for k, in_ref in enumerate(in_refs):
@@ -125,23 +122,11 @@
     width = 2 * HEAD_SIZE
     pairs = []
     for k in range(heads):
-        z = source(place_ref, heads, k)
+        z = onward(place_ref, heads, k)
         for ref, c in ((mine_ref, core), (sibling_ref, 1 - core)):
             rows = pl.ds(k * BLOCK, BLOCK)
             pairs.append((ref.at[rows], out_ref.at[:, at((2 * z + c) * width, width)]))
     copied(sems, pairs)
-
-
-def sort_kv_kernel(heads, place_ref, *refs):
-    halves, (mine_ref, other_ref) = (refs[:heads], refs[heads : 2 * heads]), refs[2 * heads :]
-    core = place_ref[1]
-    for c in range(2):
-
-        @pl.when(core == c)
-        def _():
-            for k in range(heads):
-                mine_ref[k * BLOCK : (k + 1) * BLOCK] = halves[c][k][...]
-                other_ref[k * BLOCK : (k + 1) * BLOCK] = halves[1 - c][k][...]
 
 
 def unpack_kv_kernel(heads, place_ref, mine_ref, sibling_ref, k_ref, v_ref):
@@ -156,10 +141,12 @@
             v_ref[:, columns] = ref[rows, d:]
 
 
-def add_kernel(heads, place_ref, own_ref, back_ref, after_ref, *out_refs):
+def add_kernel(heads, place_ref, own_a_ref, own_b_ref, back_a_ref, back_b_ref, *out_refs):
     for k, out_ref in enumerate(out_refs):
         rows = at(onward(place_ref, heads, k) * BLOCK, BLOCK)
-        out_ref[...] = (own_ref[rows] + back_ref[rows].astype(jnp.float32)).astype(jnp.bfloat16)
+        for c, (own_ref, back_ref) in enumerate(((own_a_ref, back_a_ref), (own_b_ref, back_b_ref))):
+            total = own_ref[rows] + back_ref[rows].astype(jnp.float32)
+            out_ref[c * BLOCK : (c + 1) * BLOCK] = total.astype(jnp.bfloat16)
 
 
 def attention_block(i, count, q, g, own_ref, prev_ref, own_kt_ref, prev_kt_ref, own_grad_ref, prev_grad_ref, bias):
@@ -237,7 +224,8 @@
 
     @pl.loop(0, len(steps))
     def _(n):
-        z_here = lax.rem(head + heads - (steps[0] + n), heads)
+        step = steps[0] + n * (steps[-1] - steps[0]) // max(len(steps) - 1, 1)
+        z_here = lax.rem(head + heads - step, heads)
         for z in range(heads):
 
             @pl.when(z_here == z)
@@ -280,7 +268,7 @@
     low, wide = jnp.bfloat16, jnp.float32
     sums, half_sums, part = shape_of(wide, whole, 2 * d), shape_of(wide, half, 2 * d), shape_of(low, half, 2 * d)
     block = shape_of(low, 2 * BLOCK, 2 * d)
-    early, late = tuple(range(heads // 2)), tuple(range(heads // 2, heads))
+    early, late = steps_of(heads)[: heads // 2], steps_of(heads)[heads // 2 :]
 
     def run(steps, cores, phase, outs, operands, scratch):
         scratch = (
@@ -291,9 +279,9 @@
         return call(kernel, outs, (place,) + tuple(own) + tuple(operands), scratch, 1, 1, 32)
 
     outs = (shape_of(low, whole, 2 * d), shape_of(low, d, whole), sums, sums) + (block,) * len(early)
-    outs = run(early, (0, 1), 0, outs, [near, far] + [blocks[k] for k in early], 0)
+    outs = run(early, (0, 1), 0, outs, [near, far] + list(blocks[: len(early)]), 0)
     prev, (own_sums, prev_sums), dq_early = outs[:2], outs[2:4], outs[4:]
-    late_blocks = tuple(blocks[k] for k in late)
+    late_blocks = tuple(blocks[len(early) :])
     wide_part = shape_of(low, half + 32, 2 * d)
     outs = (half_sums, half_sums, wide_part, shape_of(low, len(late), BLOCK, 2 * d))
     own_low, prev_high, back_a, dq_so_far = run(
@@ -331,21 +319,21 @@
         [(lax.axis_index("chip") == 0).astype(jnp.int32), lax.axis_index("core"), lax.axis_index("head")]
     ).astype(jnp.int32)
 
-    def spread(parts):
-        order = sorted(range(1, heads), key=lambda k: -min(k, heads - k))
-        out = {k: send(parts[k], chip_step=0, flip=0, head_step=k) for k in order}
-        return (parts[0],) + tuple(out[k] for k in range(1, heads))
+    def spread(parts, way=1):
+        steps = steps_of(heads)
+        return (parts[0],) + tuple(
+            send(parts[n], chip_step=0, flip=0, head_step=way * steps[n]) for n in range(1, heads)
+        )
 
     across = functools.partial(send, head_step=0)
     slab = shape_of(low, rows, 4 * d)
-    kvs = copy_call(bind(pack_kv_kernel), 4 * heads, (slab,) * heads, (place, key_rows, saved_value_rows))
-    qd_mine, qd_other = copy_call(
-        bind(pack_qd_kernel),
-        4 * heads,
-        (shape_of(low, heads, rows, 4 * d),) * 2,
-        (place, query_rows, out_grad),
-    )
-    kvs = spread(kvs)
+    packed = copy_call(
+        bind(pack_kernel),
+        8 * heads,
+        (slab,) * heads + (shape_of(low, heads, rows, 4 * d),) * 2,
+        (place, key_rows, saved_value_rows, query_rows, out_grad),
+    )
+    kvs, (qd_mine, qd_other) = spread(packed[:heads]), packed[heads:]
     qd_other = across(qd_other, chip_step=0, flip=1)
     mine, other = call(bind(gather_kv_kernel), (shape_of(low, heads * rows, 2 * d),) * 2, (place,) + kvs)
     near = across(mine, chip_step=1, flip=0)
@@ -364,17 +352,13 @@
     )
     own_sums, partial, dqs = attention_backward(heads, place, own, near, far, blocks)
     back = [across(part, chip_step=-1, flip=0) for part in partial]
-    dqs = (dqs[0],) + tuple(send(dqs[heads - k], chip_step=0, flip=0, head_step=k) for k in range(1, heads))
-    piece = shape_of(low, rows, 2 * d)
-    total_a = call(bind(add_kernel), (piece,) * heads, (place, own_sums[0], back[0], mine[:8]))
-    total_b = call(bind(add_kernel), (piece,) * heads, (place, own_sums[1], back[1], total_a[0]))
-    totals = [spread(total_a), spread(total_b)]
-    kv_mine, kv_other = call(
-        bind(sort_kv_kernel), (shape_of(low, heads * rows, 2 * d),) * 2, (place,) + totals[0] + totals[1]
-    )
+    dqs = spread(dqs, -1)
+    halves = shape_of(low, heads * rows, 2 * d)
+    totals = spread(call(bind(add_kernel), (shape_of(low, 2 * rows, 2 * d),) * heads, (place, *own_sums, *back)))
+    kv_mine, kv_other = call(bind(sort_kernel), (halves, halves), (place,) + totals)
     kv_sibling = across(kv_other, chip_step=0, flip=1)
     dq_mine, dq_other = call(
-        bind(sort_dq_kernel), (shape_of(low, heads * rows, 2 * d),) * 2, (place,) + tuple(dqs)
+        bind(sort_kernel), (shape_of(low, heads * rows, 2 * d),) * 2, (place,) + tuple(dqs)
     )
     dq_sibling = across(dq_other, chip_step=0, flip=1)
     query_grad = copy_call(

time: 90.8 us -> 92.7 us (1.021)
  waiting for transfers between devices: 34.1 us -> 38.2 us
  starting transfers between devices: 30.5 us -> 28.1 us
  local copies, waits for them, and re-layouts: 2.09 us -> 3.98 us
  Pallas kernels: 22.3 us -> 21.2 us
    ppermute x23 -> x20, waiting for transfers between devices: 34.1 us -> 38.2 us  [moved(): return lax.ppermute(value, ('chip', 'core', 'head'), pairs)]
    ppermute x23 -> x20, starting transfers between devices: 30.5 us -> 28.1 us  [moved(): return lax.ppermute(value, ('chip', 'core', 'head'), pairs)]
    unnamed x8, local copies, waits for them, and re-layouts: 2.09 us -> 3.98 us
    pallas_call x14 -> x12, Pallas kernels: 22.3 us -> 21.2 us  [call(): pl.pallas_call(kernel, out_shape=out_shape, in_specs=[SMEM_SPEC] + [spec]...]
  transfers between devices with their start and end apart: 23 -> 20, of which waited for: 10 -> 9; matrix products, arithmetic and copies ran while one was open for 0% -> 0% of each run, Pallas kernels for 18% -> 16%
where the time goes in v10:
time: 92.7 us; the launch traced here: 92.4 us
  waiting for transfers between devices  38.2 us (41%)
  starting transfers between devices  28.1 us (30%)
  Pallas kernels  21.2 us (23%)
  local copies, waits for them, and re-layouts  3.98 us (4%)
    ppermute x20, waiting for transfers between devices, moved(): return lax.ppermute(value, ('chip', 'core', 'head'), pairs)  38.2 us
    ppermute x20, starting transfers between devices, moved(): return lax.ppermute(value, ('chip', 'core', 'head'), pairs)  28.1 us
    pallas_call x12, Pallas kernels, call(): pl.pallas_call(kernel, out_shape=out_shape, in_specs=[SMEM_SPEC] + [spec]...  21.2 us
    unnamed x8, local copies, waits for them, and re-layouts  3.98 us
  transfers between devices with their start and end apart: 20, of which 9 were waited for; matrix products, arithmetic and copies ran while one was open for 0% of the time, Pallas kernels for 16%

profile of v10, /device:TPU:13, one launch (start us, length us, event | category | flops | bytes accessed | tf_op | source)
XLA Modules:
  0.0 92.4 jit_solution(17009254530729450827)
XLA Ops:
  0.6 0.1 pad_add_fusion.place_ref
  0.7 0.0 copy-start
  0.7 1.0 %copy-done = bf16[128,2048]{1,0:T(8,128)(2,1)S(1)} copy-done((bf16[128,2048]{1,0:T(8,128)(2,1)S(1)}, bf16[128,2048]{1,0:T(8,128)(2,1)}, u32[]{:S(2)}) %copy-start) | copy-done | bytes 524312
  1.8 0.0 copy-start.1
  1.8 1.0 %copy-done.1 = bf16[128,2048]{1,0:T(8,128)(2,1)S(1)} copy-done((bf16[128,2048]{1,0:T(8,128)(2,1)S(1)}, bf16[128,2048]{1,0:T(8,128)(2,1)}, u32[]{:S(2)}) %copy-start.1) | copy-done | bytes 524312
  2.8 0.0 copy-start.2
  2.8 0.9 %copy-done.2 = bf16[128,1024]{1,0:T(8,128)(2,1)S(1)} copy-done((bf16[128,1024]{1,0:T(8,128)(2,1)S(1)}, bf16[128,1024]{1,0:T(8,128)(2,1)}, u32[]{:S(2)}) %copy-start.2) | copy-done | bytes 262168
  3.8 0.0 copy-start.3
  3.8 0.9 %copy-done.3 = bf16[128,1024]{1,0:T(8,128)(2,1)S(1)} copy-done((bf16[128,1024]{1,0:T(8,128)(2,1)S(1)}, bf16[128,1024]{1,0:T(8,128)(2,1)}, u32[]{:S(2)}) %copy-start.3) | copy-done | bytes 262168
  4.7 1.3 %shard_map.67 = (bf16[128,512]{1,0:T(8,128)(2,1)S(1)}, bf16[128,512]{1,0:T(8,128)(2,1)S(1)}, bf16[128,512]{1,0:T(8,128)(2,1)S(1)}, bf16[128,512]{1,0:T(8,128)(2,...) custom-call(s32[3]{0:T(128)S(1)} %pad_add_fusion.place_ref, bf16[128,1024]{1,0:T(8,128)(2,1)S(1)} %copy-done.2, ...), custom_call_target="tpu_custom_call" | custom-call | bytes 3145740 | tf_op jit(solution)/shard_map/pallas_call | solution.py:26
  6.0 0.7 collective-permute-start.6
  6.7 2.3 %collective-permute-start = (bf16[128,512]{1,0:T(8,128)(2,1)S(1)}, bf16[128,512]{1,0:T(8,128)(2,1)S(1)}, u32[]{:S(2)}, u32[]{:S(2)}) collective-permute-start(bf16[128,512]{1,0:T(8,128)(2,1)S(1)} %get-tuple-element.45), channel_id=1, source_target_pairs={{0,2},{1,3},{2,0},{3,1},{4,6},{5,7},{6,4},{7,5},{8,10},{9,11},{10,... | collective-permute-start | bytes 393224 | tf_op jit(solution)/shard_map/ppermute | solution.py:310
  9.0 0.0 collective-permute-start.1
  9.1 1.5 %collective-permute-start.2 = (bf16[128,512]{1,0:T(8,128)(2,1)S(1)}, bf16[128,512]{1,0:T(8,128)(2,1)S(1)}, u32[]{:S(2)}, u32[]{:S(2)}) collective-permute-start(bf16[128,512]{1,0:T(8,128)(2,1)S(1)} %get-tuple-element.47), channel_id=1, source_target_pairs={{0,3},{1,0},{2,1},{3,2},{4,7},{5,4},{6,5},{7,6},{8,11},{9,8},{10,9... | collective-permute-start | bytes 393224 | tf_op jit(solution)/shard_map/ppermute | solution.py:310
  10.5 4.4 %collective-permute-done.refs_1_ = bf16[128,512]{1,0:T(8,128)(2,1)S(1)} collective-permute-done((bf16[128,512]{1,0:T(8,128)(2,1)S(1)}, bf16[128,512]{1,0:T(8,128)(2,1)S(1)}, u32[]{:S(2)}, u32[]{:S(2)}) %collective-permute-start) | collective-permute-done | bytes 131104 | tf_op jit(solution)/shard_map/ppermute | solution.py:310
  14.9 5.8 %collective-permute-done.1.refs_2_ = bf16[128,512]{1,0:T(8,128)(2,1)S(1)} collective-permute-done((bf16[128,512]{1,0:T(8,128)(2,1)S(1)}, bf16[128,512]{1,0:T(8,128)(2,1)S(1)}, u32[]{:S(2)}, u32[]{:S(2)}) %collective-permute-start.1) | collective-permute-done | bytes 131104 | tf_op jit(solution)/shard_map/ppermute | solution.py:310
  20.6 0.0 collective-permute-done.2.refs_3_
  20.6 0.6 shard_map.68
  21.2 0.5 collective-permute-start.3
  21.8 0.0 collective-permute-done.6.other_ref
  21.8 0.6 shard_map.70
  22.4 0.5 collective-permute-start.7
  22.9 1.8 %collective-permute-start.8 = (bf16[272,512]{1,0:T(8,128)(2,1)S(1)}, bf16[272,512]{1,0:T(8,128)(2,1)S(1)}, u32[]{:S(2)}, u32[]{:S(2)}) collective-permute-start(bf16[272,512]{1,0:T(8,128)(2,1)S(1)} %get-tuple-element.58), channel_id=1, source_target_pairs={{0,1},{1,2},{2,3},{3,0},{4,5},{5,6},{6,7},{7,4},{8,9},{9,10},{10,1... | collective-permute-start | bytes 835592 | tf_op jit(solution)/shard_map/ppermute | solution.py:310
  24.7 1.1 %collective-permute-start.9 = (bf16[272,512]{1,0:T(8,128)(2,1)S(1)}, bf16[272,512]{1,0:T(8,128)(2,1)S(1)}, u32[]{:S(2)}, u32[]{:S(2)}) collective-permute-start(bf16[272,512]{1,0:T(8,128)(2,1)S(1)} %get-tuple-element.59), channel_id=1, source_target_pairs={{0,3},{1,0},{2,1},{3,2},{4,7},{5,4},{6,5},{7,6},{8,11},{9,8},{10,9... | collective-permute-start | bytes 835592 | tf_op jit(solution)/shard_map/ppermute | solution.py:310
  25.8 3.6 %collective-permute-start.5 = (bf16[512,256]{1,0:T(8,128)(2,1)S(1)}, bf16[512,256]{1,0:T(8,128)(2,1)S(1)}, u32[]{:S(2)}, u32[]{:S(2)}) collective-permute-start(bf16[512,256]{1,0:T(8,128)(2,1)S(1)} %get-tuple-element.49), channel_id=1, source_target_pairs={{0,12},{1,13},{2,14},{3,15},{4,8},{5,9},{6,10},{7,11},{8,20},{9,21... | collective-permute-start | bytes 786440 | tf_op jit(solution)/shard_map/ppermute | solution.py:310
  29.4 0.0 collective-permute-done.3.sibling_ref
  29.4 1.9 %collective-permute-start.4 = (bf16[512,256]{1,0:T(8,128)(2,1)S(1)}, bf16[512,256]{1,0:T(8,128)(2,1)S(1)}, u32[]{:S(2)}, u32[]{:S(2)}) collective-permute-start(bf16[512,256]{1,0:T(8,128)(2,1)S(1)} %get-tuple-element.48.mine_ref), channel_id=1, source_target_pairs={{0,8},{1,9},{2,10},{3,11},{4,12},{5,13},{6,14},{7,15},{8,16},{9,17... | collective-permute-start | bytes 786440 | tf_op jit(solution)/shard_map/ppermute | solution.py:310
  31.4 0.7 shard_map.69
  32.1 5.3 %collective-permute-done.5.b_ref = bf16[512,256]{1,0:T(8,128)(2,1)S(1)} collective-permute-done((bf16[512,256]{1,0:T(8,128)(2,1)S(1)}, bf16[512,256]{1,0:T(8,128)(2,1)S(1)}, u32[]{:S(2)}, u32[]{:S(2)}) %collective-permute-start.5) | collective-permute-done | bytes 262176 | tf_op jit(solution)/shard_map/ppermute | solution.py:310
  37.4 5.6 %collective-permute-done.4.a_ref = bf16[512,256]{1,0:T(8,128)(2,1)S(1)} collective-permute-done((bf16[512,256]{1,0:T(8,128)(2,1)S(1)}, bf16[512,256]{1,0:T(8,128)(2,1)S(1)}, u32[]{:S(2)}, u32[]{:S(2)}) %collective-permute-start.4) | collective-permute-done | bytes 262176 | tf_op jit(solution)/shard_map/ppermute | solution.py:310
  43.0 0.0 collective-permute-done.7.refs_1_
  43.0 6.0 %shard_map.71 = (bf16[1024,256]{1,0:T(8,128)(2,1)S(1)}, bf16[128,1024]{1,0:T(8,128)(2,1)S(1)}, f32[1024,256]{1,0:T(8,128)S(1)}, f32[1024,256]{1,0:T(8,128)S(1)},...) custom-call(s32[3]{0:T(128)S(1)} %pad_add_fusion.place_ref, bf16[1024,256]{1,0:T(8,128)(2,1)S(1)} %get-tuple-element.50.own_ref, ...), custom_call_target="tpu_custom_call" | custom-call | flops 1 | bytes 5013516 | tf_op jit(solution)/shard_map/pallas_call | solution.py:26
  49.0 0.0 collective-permute-done.8.refs_0_
  49.0 0.6 collective-permute-done.9.refs_1_
  49.6 3.8 %shard_map.72 = (f32[512,256]{1,0:T(8,128)S(1)}, f32[512,256]{1,0:T(8,128)S(1)}, bf16[544,256]{1,0:T(8,128)(2,1)S(1)}, bf16[2,128,256]{2,1,0:T(8,128)(2,1)S(1)}) custom-call(s32[3]{0:T(128)S(1)} %pad_add_fusion.place_ref, bf16[1024,256]{1,0:T(8,128)(2,1)S(1)} %get-tuple-element.50.own_ref, bf16[128,1024]{1,0:T(8,128)(2,1)S(1)} %get-tuple-element.51.own_kt_ref, ...), custom_call_target="tpu_custom_call" | custom-call | flops 1 | bytes 5685260 | tf_op jit(solution)/shard_map/pallas_call | solution.py:26
  53.4 3.1 %collective-permute-start.14 = (bf16[544,256]{1,0:T(8,128)(2,1)S(1)}, bf16[544,256]{1,0:T(8,128)(2,1)S(1)}, u32[]{:S(2)}, u32[]{:S(2)}) collective-permute-start(bf16[544,256]{1,0:T(8,128)(2,1)S(1)} %get-tuple-element.75), channel_id=1, source_target_pairs={{8,0},{9,1},{10,2},{11,3},{12,4},{13,5},{14,6},{15,7},{16,8},{17,9... | collective-permute-start | bytes 835592 | tf_op jit(solution)/shard_map/ppermute | solution.py:310
  56.4 3.7 %shard_map.73 = (f32[512,256]{1,0:T(8,128)S(1)}, f32[512,256]{1,0:T(8,128)S(1)}, bf16[512,256]{1,0:T(8,128)(2,1)S(1)}, bf16[256,256]{1,0:T(8,128)(2,1)S(1)}, bf1...) custom-call(s32[3]{0:T(128)S(1)} %pad_add_fusion.place_ref, ...), custom_call_target="tpu_custom_call" | custom-call | flops 1 | bytes 6455308 | tf_op jit(solution)/shard_map/pallas_call | solution.py:26
  60.1 2.2 %collective-permute-start.15 = (bf16[512,256]{1,0:T(8,128)(2,1)S(1)}, bf16[512,256]{1,0:T(8,128)(2,1)S(1)}, u32[]{:S(2)}, u32[]{:S(2)}) collective-permute-start(bf16[512,256]{1,0:T(8,128)(2,1)S(1)} %get-tuple-element.76), channel_id=1, source_target_pairs={{8,0},{9,1},{10,2},{11,3},{12,4},{13,5},{14,6},{15,7},{16,8},{17,9... | collective-permute-start | bytes 786440 | tf_op jit(solution)/shard_map/ppermute | solution.py:310
  62.3 0.4 collective-permute-start.10
  62.7 1.4 %collective-permute-start.11 = (bf16[256,256]{1,0:T(8,128)(2,1)S(1)}, bf16[256,256]{1,0:T(8,128)(2,1)S(1)}, u32[]{:S(2)}, u32[]{:S(2)}) collective-permute-start(bf16[256,256]{1,0:T(8,128)(2,1)S(1)} %get-tuple-element.69), channel_id=1, source_target_pairs={{0,3},{1,0},{2,1},{3,2},{4,7},{5,4},{6,5},{7,6},{8,11},{9,8},{10,9... | collective-permute-start | bytes 393224 | tf_op jit(solution)/shard_map/ppermute | solution.py:310
  64.1 1.1 %collective-permute-start.12 = (bf16[256,256]{1,0:T(8,128)(2,1)S(1)}, bf16[256,256]{1,0:T(8,128)(2,1)S(1)}, u32[]{:S(2)}, u32[]{:S(2)}) collective-permute-start(bf16[256,256]{1,0:T(8,128)(2,1)S(1)} %get-tuple-element.70), channel_id=1, source_target_pairs={{0,1},{1,2},{2,3},{3,0},{4,5},{5,6},{6,7},{7,4},{8,9},{9,10},{10,1... | collective-permute-start | bytes 393224 | tf_op jit(solution)/shard_map/ppermute | solution.py:310
  65.2 3.7 %collective-permute-done.15.back_b_ref = bf16[512,256]{1,0:T(8,128)(2,1)S(1)} collective-permute-done((bf16[512,256]{1,0:T(8,128)(2,1)S(1)}, bf16[512,256]{1,0:T(8,128)(2,1)S(1)}, u32[]{:S(2)}, u32[]{:S(2)}) %collective-permute-start.15) | collective-permute-done | bytes 262176 | tf_op jit(solution)/shard_map/ppermute | solution.py:310
  68.9 0.0 collective-permute-done.14.back_a_ref
  68.9 0.6 shard_map.76
  69.6 1.1 %collective-permute-start.16 = (bf16[256,256]{1,0:T(8,128)(2,1)S(1)}, bf16[256,256]{1,0:T(8,128)(2,1)S(1)}, u32[]{:S(2)}, u32[]{:S(2)}) collective-permute-start(bf16[256,256]{1,0:T(8,128)(2,1)S(1)} %get-tuple-element.78), channel_id=1, source_target_pairs={{0,2},{1,3},{2,0},{3,1},{4,6},{5,7},{6,4},{7,5},{8,10},{9,11},{10,... | collective-permute-start | bytes 393224 | tf_op jit(solution)/shard_map/ppermute | solution.py:310
  70.7 2.6 %collective-permute-start.17 = (bf16[256,256]{1,0:T(8,128)(2,1)S(1)}, bf16[256,256]{1,0:T(8,128)(2,1)S(1)}, u32[]{:S(2)}, u32[]{:S(2)}) collective-permute-start(bf16[256,256]{1,0:T(8,128)(2,1)S(1)} %get-tuple-element.79), channel_id=1, source_target_pairs={{0,1},{1,2},{2,3},{3,0},{4,5},{5,6},{6,7},{7,4},{8,9},{9,10},{10,1... | collective-permute-start | bytes 393224 | tf_op jit(solution)/shard_map/ppermute | solution.py:310
  73.2 0.0 collective-permute-done.10.refs_1_
  73.2 0.0 collective-permute-start.18
  73.2 9.1 %collective-permute-done.11.refs_2_ = bf16[256,256]{1,0:T(8,128)(2,1)S(1)} collective-permute-done((bf16[256,256]{1,0:T(8,128)(2,1)S(1)}, bf16[256,256]{1,0:T(8,128)(2,1)S(1)}, u32[]{:S(2)}, u32[]{:S(2)}) %collective-permute-start.11) | collective-permute-done | bytes 131104 | tf_op jit(solution)/shard_map/ppermute | solution.py:310
  82.4 0.0 collective-permute-done.12.refs_3_
  82.4 0.6 shard_map.74
  82.9 1.3 %collective-permute-start.13 = (bf16[512,256]{1,0:T(8,128)(2,1)S(1)}, bf16[512,256]{1,0:T(8,128)(2,1)S(1)}, u32[]{:S(2)}, u32[]{:S(2)}) collective-permute-start(bf16[512,256]{1,0:T(8,128)(2,1)S(1)} %get-tuple-element.72), channel_id=1, source_target_pairs={{0,4},{1,5},{2,6},{3,7},{4,0},{5,1},{6,2},{7,3},{8,12},{9,13},{10,... | collective-permute-start | bytes 786440 | tf_op jit(solution)/shard_map/ppermute | solution.py:310
  84.2 0.0 collective-permute-done.16.refs_1_
  84.3 0.2 collective-permute-done.17.refs_2_
  84.4 3.6 %collective-permute-done.18.refs_3_ = bf16[256,256]{1,0:T(8,128)(2,1)S(1)} collective-permute-done((bf16[256,256]{1,0:T(8,128)(2,1)S(1)}, bf16[256,256]{1,0:T(8,128)(2,1)S(1)}, u32[]{:S(2)}, u32[]{:S(2)}) %collective-permute-start.18) | collective-permute-done | bytes 131104 | tf_op jit(solution)/shard_map/ppermute | solution.py:310
  88.0 0.6 shard_map.77
  88.6 0.9 collective-permute-start.19
  89.5 0.0 collective-permute-done.13.sibling_ref
  89.5 1.4 %shard_map.75 = bf16[128,2048]{1,0:T(8,128)(2,1)} custom-call(s32[3]{0:T(128)S(1)} %pad_add_fusion.place_ref, bf16[512,256]{1,0:T(8,128)(2,1)S(1)} %get-tuple-element.71.mine_ref, bf16[512,256]{1,0:T(8,128)(2,1)S(1)} %collective-permute-done.13.sibling_ref), custom_call_target="tpu_custom_call" | custom-call | bytes 1048588 | tf_op jit(solution)/shard_map/pallas_call | solution.py:26
  90.9 0.0 collective-permute-done.19.sibling_ref
  90.9 1.5 %shard_map.78 = (bf16[128,1024]{1,0:T(8,128)(2,1)}, bf16[128,1024]{1,0:T(8,128)(2,1)}) custom-call(s32[3]{0:T(128)S(1)} %pad_add_fusion.place_ref, bf16[512,256]{1,0:T(8,128)(2,1)S(1)} %get-tuple-element.81.mine_ref, bf16[512,256]{1,0:T(8,128)(2,1)S(1)} %collective-permute-done.19.sibling_ref), custom_call_target="tpu_custom_call" | custom-call | bytes 1048588 | tf_op jit(solution)/shard_map/pallas_call | solution.py:26
  (1 shorter events, 0.0 us)
Async XLA Ops:
  0.7 1.0 %copy-start = (bf16[128,2048]{1,0:T(8,128)(2,1)S(1)}, bf16[128,2048]{1,0:T(8,128)(2,1)}, u32[]{:S(2)}) copy-start(bf16[128,2048]{1,0:T(8,128)(2,1)} %q_ref.1) | copy-start | bytes 1572868
  1.8 1.0 %copy-start.1 = (bf16[128,2048]{1,0:T(8,128)(2,1)S(1)}, bf16[128,2048]{1,0:T(8,128)(2,1)}, u32[]{:S(2)}) copy-start(bf16[128,2048]{1,0:T(8,128)(2,1)} %g_ref.1) | copy-start | bytes 1572868
  2.8 0.9 %copy-start.2 = (bf16[128,1024]{1,0:T(8,128)(2,1)S(1)}, bf16[128,1024]{1,0:T(8,128)(2,1)}, u32[]{:S(2)}) copy-start(bf16[128,1024]{1,0:T(8,128)(2,1)} %k_ref.1) | copy-start | bytes 786436
  3.8 0.9 %copy-start.3 = (bf16[128,1024]{1,0:T(8,128)(2,1)S(1)}, bf16[128,1024]{1,0:T(8,128)(2,1)}, u32[]{:S(2)}) copy-start(bf16[128,1024]{1,0:T(8,128)(2,1)} %v_ref.1) | copy-start | bytes 786436
  6.0 15.8 %collective-permute-start.6 = (bf16[4,128,512]{2,1,0:T(8,128)(2,1)S(1)}, bf16[4,128,512]{2,1,0:T(8,128)(2,1)S(1)}, u32[]{:S(2)}, u32[]{:S(2)}) collective-permute-start(bf16[4,128,512]{2,1,0:T(8,128)(2,1)S(1)} %get-tuple-element.53), channel_id=1, source_target_pairs={{0,4},{1,5},{2,6},{3,7},{4,0},{5,1},{6,2},{7,3},{8,12},{9,13},{10,... | collective-permute-start | bytes 1572872 | tf_op jit(solution)/shard_map/ppermute | solution.py:310
  6.7 8.1 %collective-permute-start = (bf16[128,512]{1,0:T(8,128)(2,1)S(1)}, bf16[128,512]{1,0:T(8,128)(2,1)S(1)}, u32[]{:S(2)}, u32[]{:S(2)}) collective-permute-start(bf16[128,512]{1,0:T(8,128)(2,1)S(1)} %get-tuple-element.45), channel_id=1, source_target_pairs={{0,2},{1,3},{2,0},{3,1},{4,6},{5,7},{6,4},{7,5},{8,10},{9,11},{10,... | collective-permute-start | bytes 393224 | tf_op jit(solution)/shard_map/ppermute | solution.py:310
  9.0 11.6 %collective-permute-start.1 = (bf16[128,512]{1,0:T(8,128)(2,1)S(1)}, bf16[128,512]{1,0:T(8,128)(2,1)S(1)}, u32[]{:S(2)}, u32[]{:S(2)}) collective-permute-start(bf16[128,512]{1,0:T(8,128)(2,1)S(1)} %get-tuple-element.46), channel_id=1, source_target_pairs={{0,1},{1,2},{2,3},{3,0},{4,5},{5,6},{6,7},{7,4},{8,9},{9,10},{10,1... | collective-permute-start | bytes 393224 | tf_op jit(solution)/shard_map/ppermute | solution.py:310
  9.1 11.6 %collective-permute-start.2 = (bf16[128,512]{1,0:T(8,128)(2,1)S(1)}, bf16[128,512]{1,0:T(8,128)(2,1)S(1)}, u32[]{:S(2)}, u32[]{:S(2)}) collective-permute-start(bf16[128,512]{1,0:T(8,128)(2,1)S(1)} %get-tuple-element.47), channel_id=1, source_target_pairs={{0,3},{1,0},{2,1},{3,2},{4,7},{5,4},{6,5},{7,6},{8,11},{9,8},{10,9... | collective-permute-start | bytes 393224 | tf_op jit(solution)/shard_map/ppermute | solution.py:310
  21.2 8.2 %collective-permute-start.3 = (bf16[512,256]{1,0:T(8,128)(2,1)S(1)}, bf16[512,256]{1,0:T(8,128)(2,1)S(1)}, u32[]{:S(2)}, u32[]{:S(2)}) collective-permute-start(bf16[512,256]{1,0:T(8,128)(2,1)S(1)} %get-tuple-element.49), channel_id=1, source_target_pairs={{0,4},{1,5},{2,6},{3,7},{4,0},{5,1},{6,2},{7,3},{8,12},{9,13},{10,... | collective-permute-start | bytes 786440 | tf_op jit(solution)/shard_map/ppermute | solution.py:310
  22.4 20.6 %collective-permute-start.7 = (bf16[272,512]{1,0:T(8,128)(2,1)S(1)}, bf16[272,512]{1,0:T(8,128)(2,1)S(1)}, u32[]{:S(2)}, u32[]{:S(2)}) collective-permute-start(bf16[272,512]{1,0:T(8,128)(2,1)S(1)} %get-tuple-element.55), channel_id=1, source_target_pairs={{0,2},{1,3},{2,0},{3,1},{4,6},{5,7},{6,4},{7,5},{8,10},{9,11},{10,... | collective-permute-start | bytes 835592 | tf_op jit(solution)/shard_map/ppermute | solution.py:310
  22.9 26.1 %collective-permute-start.8 = (bf16[272,512]{1,0:T(8,128)(2,1)S(1)}, bf16[272,512]{1,0:T(8,128)(2,1)S(1)}, u32[]{:S(2)}, u32[]{:S(2)}) collective-permute-start(bf16[272,512]{1,0:T(8,128)(2,1)S(1)} %get-tuple-element.58), channel_id=1, source_target_pairs={{0,1},{1,2},{2,3},{3,0},{4,5},{5,6},{6,7},{7,4},{8,9},{9,10},{10,1... | collective-permute-start | bytes 835592 | tf_op jit(solution)/shard_map/ppermute | solution.py:310
  24.7 24.9 %collective-permute-start.9 = (bf16[272,512]{1,0:T(8,128)(2,1)S(1)}, bf16[272,512]{1,0:T(8,128)(2,1)S(1)}, u32[]{:S(2)}, u32[]{:S(2)}) collective-permute-start(bf16[272,512]{1,0:T(8,128)(2,1)S(1)} %get-tuple-element.59), channel_id=1, source_target_pairs={{0,3},{1,0},{2,1},{3,2},{4,7},{5,4},{6,5},{7,6},{8,11},{9,8},{10,9... | collective-permute-start | bytes 835592 | tf_op jit(solution)/shard_map/ppermute | solution.py:310
  25.8 11.6 %collective-permute-start.5 = (bf16[512,256]{1,0:T(8,128)(2,1)S(1)}, bf16[512,256]{1,0:T(8,128)(2,1)S(1)}, u32[]{:S(2)}, u32[]{:S(2)}) collective-permute-start(bf16[512,256]{1,0:T(8,128)(2,1)S(1)} %get-tuple-element.49), channel_id=1, source_target_pairs={{0,12},{1,13},{2,14},{3,15},{4,8},{5,9},{6,10},{7,11},{8,20},{9,21... | collective-permute-start | bytes 786440 | tf_op jit(solution)/shard_map/ppermute | solution.py:310
  29.4 13.5 %collective-permute-start.4 = (bf16[512,256]{1,0:T(8,128)(2,1)S(1)}, bf16[512,256]{1,0:T(8,128)(2,1)S(1)}, u32[]{:S(2)}, u32[]{:S(2)}) collective-permute-start(bf16[512,256]{1,0:T(8,128)(2,1)S(1)} %get-tuple-element.48.mine_ref), channel_id=1, source_target_pairs={{0,8},{1,9},{2,10},{3,11},{4,12},{5,13},{6,14},{7,15},{8,16},{9,17... | collective-permute-start | bytes 786440 | tf_op jit(solution)/shard_map/ppermute | solution.py:310
  53.4 15.6 %collective-permute-start.14 = (bf16[544,256]{1,0:T(8,128)(2,1)S(1)}, bf16[544,256]{1,0:T(8,128)(2,1)S(1)}, u32[]{:S(2)}, u32[]{:S(2)}) collective-permute-start(bf16[544,256]{1,0:T(8,128)(2,1)S(1)} %get-tuple-element.75), channel_id=1, source_target_pairs={{8,0},{9,1},{10,2},{11,3},{12,4},{13,5},{14,6},{15,7},{16,8},{17,9... | collective-permute-start | bytes 835592 | tf_op jit(solution)/shard_map/ppermute | solution.py:310
  60.1 8.8 %collective-permute-start.15 = (bf16[512,256]{1,0:T(8,128)(2,1)S(1)}, bf16[512,256]{1,0:T(8,128)(2,1)S(1)}, u32[]{:S(2)}, u32[]{:S(2)}) collective-permute-start(bf16[512,256]{1,0:T(8,128)(2,1)S(1)} %get-tuple-element.76), channel_id=1, source_target_pairs={{8,0},{9,1},{10,2},{11,3},{12,4},{13,5},{14,6},{15,7},{16,8},{17,9... | collective-permute-start | bytes 786440 | tf_op jit(solution)/shard_map/ppermute | solution.py:310
  62.3 11.0 %collective-permute-start.10 = (bf16[256,256]{1,0:T(8,128)(2,1)S(1)}, bf16[256,256]{1,0:T(8,128)(2,1)S(1)}, u32[]{:S(2)}, u32[]{:S(2)}) collective-permute-start(bf16[256,256]{1,0:T(8,128)(2,1)S(1)} %get-tuple-element.68), channel_id=1, source_target_pairs={{0,2},{1,3},{2,0},{3,1},{4,6},{5,7},{6,4},{7,5},{8,10},{9,11},{10,... | collective-permute-start | bytes 393224 | tf_op jit(solution)/shard_map/ppermute | solution.py:310
  62.7 19.7 %collective-permute-start.11 = (bf16[256,256]{1,0:T(8,128)(2,1)S(1)}, bf16[256,256]{1,0:T(8,128)(2,1)S(1)}, u32[]{:S(2)}, u32[]{:S(2)}) collective-permute-start(bf16[256,256]{1,0:T(8,128)(2,1)S(1)} %get-tuple-element.69), channel_id=1, source_target_pairs={{0,3},{1,0},{2,1},{3,2},{4,7},{5,4},{6,5},{7,6},{8,11},{9,8},{10,9... | collective-permute-start | bytes 393224 | tf_op jit(solution)/shard_map/ppermute | solution.py:310
  64.1 18.3 %collective-permute-start.12 = (bf16[256,256]{1,0:T(8,128)(2,1)S(1)}, bf16[256,256]{1,0:T(8,128)(2,1)S(1)}, u32[]{:S(2)}, u32[]{:S(2)}) collective-permute-start(bf16[256,256]{1,0:T(8,128)(2,1)S(1)} %get-tuple-element.70), channel_id=1, source_target_pairs={{0,1},{1,2},{2,3},{3,0},{4,5},{5,6},{6,7},{7,4},{8,9},{9,10},{10,1... | collective-permute-start | bytes 393224 | tf_op jit(solution)/shard_map/ppermute | solution.py:310
  69.6 14.7 %collective-permute-start.16 = (bf16[256,256]{1,0:T(8,128)(2,1)S(1)}, bf16[256,256]{1,0:T(8,128)(2,1)S(1)}, u32[]{:S(2)}, u32[]{:S(2)}) collective-permute-start(bf16[256,256]{1,0:T(8,128)(2,1)S(1)} %get-tuple-element.78), channel_id=1, source_target_pairs={{0,2},{1,3},{2,0},{3,1},{4,6},{5,7},{6,4},{7,5},{8,10},{9,11},{10,... | collective-permute-start | bytes 393224 | tf_op jit(solution)/shard_map/ppermute | solution.py:310
  70.7 13.8 %collective-permute-start.17 = (bf16[256,256]{1,0:T(8,128)(2,1)S(1)}, bf16[256,256]{1,0:T(8,128)(2,1)S(1)}, u32[]{:S(2)}, u32[]{:S(2)}) collective-permute-start(bf16[256,256]{1,0:T(8,128)(2,1)S(1)} %get-tuple-element.79), channel_id=1, source_target_pairs={{0,1},{1,2},{2,3},{3,0},{4,5},{5,6},{6,7},{7,4},{8,9},{9,10},{10,1... | collective-permute-start | bytes 393224 | tf_op jit(solution)/shard_map/ppermute | solution.py:310
  73.2 14.8 %collective-permute-start.18 = (bf16[256,256]{1,0:T(8,128)(2,1)S(1)}, bf16[256,256]{1,0:T(8,128)(2,1)S(1)}, u32[]{:S(2)}, u32[]{:S(2)}) collective-permute-start(bf16[256,256]{1,0:T(8,128)(2,1)S(1)} %get-tuple-element.80), channel_id=1, source_target_pairs={{0,3},{1,0},{2,1},{3,2},{4,7},{5,4},{6,5},{7,6},{8,11},{9,8},{10,9... | collective-permute-start | bytes 393224 | tf_op jit(solution)/shard_map/ppermute | solution.py:310
  82.9 6.5 %collective-permute-start.13 = (bf16[512,256]{1,0:T(8,128)(2,1)S(1)}, bf16[512,256]{1,0:T(8,128)(2,1)S(1)}, u32[]{:S(2)}, u32[]{:S(2)}) collective-permute-start(bf16[512,256]{1,0:T(8,128)(2,1)S(1)} %get-tuple-element.72), channel_id=1, source_target_pairs={{0,4},{1,5},{2,6},{3,7},{4,0},{5,1},{6,2},{7,3},{8,12},{9,13},{10,... | collective-permute-start | bytes 786440 | tf_op jit(solution)/shard_map/ppermute | solution.py:310
  88.6 2.3 %collective-permute-start.19 = (bf16[512,256]{1,0:T(8,128)(2,1)S(1)}, bf16[512,256]{1,0:T(8,128)(2,1)S(1)}, u32[]{:S(2)}, u32[]{:S(2)}) collective-permute-start(bf16[512,256]{1,0:T(8,128)(2,1)S(1)} %get-tuple-element.82), channel_id=1, source_target_pairs={{0,4},{1,5},{2,6},{3,7},{4,0},{5,1},{6,2},{7,3},{8,12},{9,13},{10,... | collective-permute-start | bytes 786440 | tf_op jit(solution)/shard_map/ppermute | solution.py:310

commit v11 on v10

--- a/solution.py
+++ b/solution.py
@@ -66,17 +66,24 @@
     return lax.rem(place_ref[2] + heads - steps_of(heads)[n], heads)
 
 
-def pack_kernel(heads, place_ref, k_ref, v_ref, q_ref, g_ref, *refs):
-    kv_refs, (mine_ref, other_ref, sems) = refs[:heads], refs[heads:]
-    core = place_ref[1]
-    d, width = HEAD_SIZE, 2 * HEAD_SIZE
+def pack_kv_kernel(heads, place_ref, k_ref, v_ref, *refs):
+    out_refs, sems = refs[:-1], refs[-1]
+    core = place_ref[1]
+    d = HEAD_SIZE
     pairs = []
-    for k, out_ref in enumerate(kv_refs):
+    for k, out_ref in enumerate(out_refs):
         z = onward(place_ref, heads, k)
         for n, g in enumerate((2 * z + core, 2 * z + 1 - core)):
             columns = at(g * d, d)
             pairs.append((k_ref.at[:, columns], out_ref.at[:, pl.ds(2 * n * d, d)]))
             pairs.append((v_ref.at[:, columns], out_ref.at[:, pl.ds((2 * n + 1) * d, d)]))
+    copied(sems, pairs)
+
+
+def pack_qd_kernel(heads, place_ref, q_ref, g_ref, mine_ref, other_ref, sems):
+    core = place_ref[1]
+    width = 2 * HEAD_SIZE
+    pairs = []
     for ref, c in ((other_ref, 1 - core), (mine_ref, core)):
         for k in range(heads):
             columns = at((2 * onward(place_ref, heads, k) + c) * width, width)
@@ -210,10 +217,9 @@
         own_grad_ref[...] = own_sums_ref[low_rows]
         prev_grad_ref[...] = prev_sums_ref[...]
     else:
-        own_low_ref, own_sums_ref, prev_high_ref, dq_so_far_ref = refs[:4]
-        dq_early_refs, refs = refs[4 : 4 + heads - len(steps)], refs[4 + heads - len(steps) :]
-        own_a_ref, own_b_ref, back_ref = refs[:3]
-        dq_refs, (qd_ref, dq_ref, own_grad_ref, prev_grad_ref) = refs[3:-4], refs[-4:]
+        own_low_ref, own_sums_ref, prev_high_ref, dq_so_far_ref, after_ref = refs[:5]
+        own_a_ref, own_b_ref, back_ref = refs[5:8]
+        dq_refs, (qd_ref, dq_ref, own_grad_ref, prev_grad_ref) = refs[8:-4], refs[-4:]
         own_grad_ref[low_rows] = own_low_ref[...]
         own_grad_ref[high_rows] = own_sums_ref[high_rows]
         prev_grad_ref[high_rows] = prev_high_ref[...]
@@ -256,13 +262,11 @@
         finish(back_ref, prev_grad_ref, high_rows)
         finish(own_a_ref, own_grad_ref, low_rows)
         finish(own_b_ref, own_grad_ref, high_rows)
-        for ref, early_ref in zip(dq_refs, dq_early_refs):
-            ref[...] = early_ref[...]
-        for n, ref in enumerate(dq_refs[len(dq_early_refs) :]):
+        for n, ref in enumerate(dq_refs):
             ref[...] = dq_ref[n]
 
 
-def attention_backward(heads, place, own, near, far, blocks):
+def attention_backward(heads, place, own, near, far, blocks, home):
     half, d = heads * BLOCK, HEAD_SIZE
     whole = 2 * half
     low, wide = jnp.bfloat16, jnp.float32
@@ -281,6 +285,7 @@
     outs = (shape_of(low, whole, 2 * d), shape_of(low, d, whole), sums, sums) + (block,) * len(early)
     outs = run(early, (0, 1), 0, outs, [near, far] + list(blocks[: len(early)]), 0)
     prev, (own_sums, prev_sums), dq_early = outs[:2], outs[2:4], outs[4:]
+    dq_early = (dq_early[0],) + tuple(home(dq_early[n], early[n]) for n in range(1, len(early)))
     late_blocks = tuple(blocks[len(early) :])
     wide_part = shape_of(low, half + 32, 2 * d)
     outs = (half_sums, half_sums, wide_part, shape_of(low, len(late), BLOCK, 2 * d))
@@ -291,11 +296,12 @@
         late,
         (1,),
         2,
-        (half_sums, half_sums, part) + (block,) * heads,
-        prev + late_blocks + (own_low, own_sums, prev_high, dq_so_far) + dq_early,
+        (half_sums, half_sums, part) + (block,) * len(late),
+        prev + late_blocks + (own_low, own_sums, prev_high, dq_so_far, dq_early[-1][:16]),
         2,
     )
-    return outs[:2], (back_a, outs[2]), outs[3:]
+    dq_late = tuple(home(dq, step) for dq, step in zip(outs[3:], late))
+    return outs[:2], (back_a, outs[2]), dq_early + dq_late
 
 
 def moved(value, chips, heads, chip_step, flip, head_step):
@@ -319,21 +325,23 @@
         [(lax.axis_index("chip") == 0).astype(jnp.int32), lax.axis_index("core"), lax.axis_index("head")]
     ).astype(jnp.int32)
 
-    def spread(parts, way=1):
-        steps = steps_of(heads)
-        return (parts[0],) + tuple(
-            send(parts[n], chip_step=0, flip=0, head_step=way * steps[n]) for n in range(1, heads)
-        )
+    def ship(value, head_step):
+        return send(value, chip_step=0, flip=0, head_step=head_step)
+
+    def spread(parts):
+        return (parts[0],) + tuple(ship(parts[n], steps_of(heads)[n]) for n in range(1, heads))
 
     across = functools.partial(send, head_step=0)
     slab = shape_of(low, rows, 4 * d)
-    packed = copy_call(
-        bind(pack_kernel),
-        8 * heads,
-        (slab,) * heads + (shape_of(low, heads, rows, 4 * d),) * 2,
-        (place, key_rows, saved_value_rows, query_rows, out_grad),
-    )
-    kvs, (qd_mine, qd_other) = spread(packed[:heads]), packed[heads:]
+    kvs = spread(
+        copy_call(bind(pack_kv_kernel), 4 * heads, (slab,) * heads, (place, key_rows, saved_value_rows))
+    )
+    qd_mine, qd_other = copy_call(
+        bind(pack_qd_kernel),
+        4 * heads,
+        (shape_of(low, heads, rows, 4 * d),) * 2,
+        (place, query_rows, out_grad),
+    )
     qd_other = across(qd_other, chip_step=0, flip=1)
     mine, other = call(bind(gather_kv_kernel), (shape_of(low, heads * rows, 2 * d),) * 2, (place,) + kvs)
     near = across(mine, chip_step=1, flip=0)
@@ -350,9 +358,10 @@
         (shape_of(low, 2 * heads * rows, 2 * d), shape_of(low, d, 2 * heads * rows)),
         (place, mine, sibling),
     )
-    own_sums, partial, dqs = attention_backward(heads, place, own, near, far, blocks)
+    own_sums, partial, dqs = attention_backward(
+        heads, place, own, near, far, blocks, lambda dq, step: ship(dq, -step)
+    )
     back = [across(part, chip_step=-1, flip=0) for part in partial]
-    dqs = spread(dqs, -1)
     halves = shape_of(low, heads * rows, 2 * d)
     totals = spread(call(bind(add_kernel), (shape_of(low, 2 * rows, 2 * d),) * heads, (place, *own_sums, *back)))
     kv_mine, kv_other = call(bind(sort_kernel), (halves, halves), (place,) + totals)

time: 92.7 us -> 88.5 us (0.955)
  waiting for transfers between devices: 38.2 us -> 35.2 us
  local copies, waits for them, and re-layouts: 3.98 us -> 2.1 us
    ppermute x20, waiting for transfers between devices: 38.2 us -> 35.2 us  [moved(): return lax.ppermute(value, ('chip', 'core', 'head'), pairs)]
    unnamed x8, local copies, waits for them, and re-layouts: 3.98 us -> 2.09 us
    pallas_call x12 -> x13, Pallas kernels: 21.2 us -> 21.8 us  [call(): pl.pallas_call(kernel, out_shape=out_shape, in_specs=[SMEM_SPEC] + [spec]...]
  transfers between devices with their start and end apart: 20 -> 20, of which waited for: 9 -> 9; matrix products, arithmetic and copies ran while one was open for 0% -> 0% of each run, Pallas kernels for 16% -> 22%
where the time goes in v11:
time: 88.5 us; the launch traced here: 88.1 us
  waiting for transfers between devices  35.2 us (40%)
  starting transfers between devices  28.2 us (32%)
  Pallas kernels  21.8 us (25%)
  local copies, waits for them, and re-layouts  2.1 us (2%)
    ppermute x20, waiting for transfers between devices, moved(): return lax.ppermute(value, ('chip', 'core', 'head'), pairs)  35.2 us
    ppermute x20, starting transfers between devices, moved(): return lax.ppermute(value, ('chip', 'core', 'head'), pairs)  28.2 us
    pallas_call x13, Pallas kernels, call(): pl.pallas_call(kernel, out_shape=out_shape, in_specs=[SMEM_SPEC] + [spec]...  21.8 us
    unnamed x8, local copies, waits for them, and re-layouts  2.09 us
  transfers between devices with their start and end apart: 20, of which 9 were waited for; matrix products, arithmetic and copies ran while one was open for 0% of the time, Pallas kernels for 22%

profile of v11, /device:TPU:13, one launch (start us, length us, event | category | flops | bytes accessed | tf_op | source)
XLA Modules:
  0.0 88.1 jit_solution(15624060863888623422)
XLA Ops:
  0.6 0.1 pad_add_fusion.place_ref
  0.7 0.0 copy-start
  0.7 1.0 %copy-done = bf16[128,2048]{1,0:T(8,128)(2,1)S(1)} copy-done((bf16[128,2048]{1,0:T(8,128)(2,1)S(1)}, bf16[128,2048]{1,0:T(8,128)(2,1)}, u32[]{:S(2)}) %copy-start) | copy-done | bytes 524312
  1.8 0.0 copy-start.1
  1.8 1.0 %copy-done.1 = bf16[128,2048]{1,0:T(8,128)(2,1)S(1)} copy-done((bf16[128,2048]{1,0:T(8,128)(2,1)S(1)}, bf16[128,2048]{1,0:T(8,128)(2,1)}, u32[]{:S(2)}) %copy-start.1) | copy-done | bytes 524312
  2.8 0.0 copy-start.2
  2.8 0.0 copy-start.3
  2.8 0.9 %shard_map.70 = (bf16[4,128,512]{2,1,0:T(8,128)(2,1)S(1)}, bf16[4,128,512]{2,1,0:T(8,128)(2,1)S(1)}) custom-call(s32[3]{0:T(128)S(1)} %pad_add_fusion.place_ref, bf16[128,2048]{1,0:T(8,128)(2,1)S(1)} %copy-done, bf16[128,2048]{1,0:T(8,128)(2,1)S(1)} %copy-done.1), custom_call_target="tpu_custom_call" | custom-call | bytes 2097164 | tf_op jit(solution)/shard_map/pallas_call | solution.py:26
  3.7 0.7 collective-permute-start.6
  4.5 0.0 copy-done.2
  4.5 0.0 copy-done.3
  4.5 0.9 %shard_map.67 = (bf16[128,512]{1,0:T(8,128)(2,1)S(1)}, bf16[128,512]{1,0:T(8,128)(2,1)S(1)}, bf16[128,512]{1,0:T(8,128)(2,1)S(1)}, bf16[128,512]{1,0:T(8,128)(2,1)S(1)}) custom-call(s32[3]{0:T(128)S(1)} %pad_add_fusion.place_ref, bf16[128,1024]{1,0:T(8,128)(2,1)S(1)} %copy-done.2, bf16[128,1024]{1,0:T(8,128)(2,1)S(1)} %copy-done.3), custom_call_target="tpu_custom_call" | custom-call | bytes 1048588 | tf_op jit(solution)/shard_map/pallas_call | solution.py:26
  5.3 2.4 %collective-permute-start = (bf16[128,512]{1,0:T(8,128)(2,1)S(1)}, bf16[128,512]{1,0:T(8,128)(2,1)S(1)}, u32[]{:S(2)}, u32[]{:S(2)}) collective-permute-start(bf16[128,512]{1,0:T(8,128)(2,1)S(1)} %get-tuple-element.43), channel_id=1, source_target_pairs={{0,2},{1,3},{2,0},{3,1},{4,6},{5,7},{6,4},{7,5},{8,10},{9,11},{10,... | collective-permute-start | bytes 393224 | tf_op jit(solution)/shard_map/ppermute | solution.py:316
  7.7 0.0 collective-permute-start.1
  7.7 1.5 %collective-permute-start.2 = (bf16[128,512]{1,0:T(8,128)(2,1)S(1)}, bf16[128,512]{1,0:T(8,128)(2,1)S(1)}, u32[]{:S(2)}, u32[]{:S(2)}) collective-permute-start(bf16[128,512]{1,0:T(8,128)(2,1)S(1)} %get-tuple-element.45), channel_id=1, source_target_pairs={{0,3},{1,0},{2,1},{3,2},{4,7},{5,4},{6,5},{7,6},{8,11},{9,8},{10,9... | collective-permute-start | bytes 393224 | tf_op jit(solution)/shard_map/ppermute | solution.py:316
  9.2 4.4 %collective-permute-done.refs_1_ = bf16[128,512]{1,0:T(8,128)(2,1)S(1)} collective-permute-done((bf16[128,512]{1,0:T(8,128)(2,1)S(1)}, bf16[128,512]{1,0:T(8,128)(2,1)S(1)}, u32[]{:S(2)}, u32[]{:S(2)}) %collective-permute-start) | collective-permute-done | bytes 131104 | tf_op jit(solution)/shard_map/ppermute | solution.py:316
  13.6 5.7 %collective-permute-done.1.refs_2_ = bf16[128,512]{1,0:T(8,128)(2,1)S(1)} collective-permute-done((bf16[128,512]{1,0:T(8,128)(2,1)S(1)}, bf16[128,512]{1,0:T(8,128)(2,1)S(1)}, u32[]{:S(2)}, u32[]{:S(2)}) %collective-permute-start.1) | collective-permute-done | bytes 131104 | tf_op jit(solution)/shard_map/ppermute | solution.py:316
  19.3 0.0 collective-permute-done.2.refs_3_
  19.3 0.6 shard_map.68
  19.9 0.5 collective-permute-start.3
  20.4 0.0 collective-permute-done.6.other_ref
  20.4 0.6 shard_map.71
  21.0 0.5 collective-permute-start.7
  21.5 3.3 %collective-permute-start.5 = (bf16[512,256]{1,0:T(8,128)(2,1)S(1)}, bf16[512,256]{1,0:T(8,128)(2,1)S(1)}, u32[]{:S(2)}, u32[]{:S(2)}) collective-permute-start(bf16[512,256]{1,0:T(8,128)(2,1)S(1)} %get-tuple-element.47), channel_id=1, source_target_pairs={{0,12},{1,13},{2,14},{3,15},{4,8},{5,9},{6,10},{7,11},{8,20},{9,21... | collective-permute-start | bytes 786440 | tf_op jit(solution)/shard_map/ppermute | solution.py:316
  24.8 1.9 %collective-permute-start.4 = (bf16[512,256]{1,0:T(8,128)(2,1)S(1)}, bf16[512,256]{1,0:T(8,128)(2,1)S(1)}, u32[]{:S(2)}, u32[]{:S(2)}) collective-permute-start(bf16[512,256]{1,0:T(8,128)(2,1)S(1)} %get-tuple-element.46.mine_ref), channel_id=1, source_target_pairs={{0,8},{1,9},{2,10},{3,11},{4,12},{5,13},{6,14},{7,15},{8,16},{9,17... | collective-permute-start | bytes 786440 | tf_op jit(solution)/shard_map/ppermute | solution.py:316
  26.8 1.6 %collective-permute-start.9 = (bf16[272,512]{1,0:T(8,128)(2,1)S(1)}, bf16[272,512]{1,0:T(8,128)(2,1)S(1)}, u32[]{:S(2)}, u32[]{:S(2)}) collective-permute-start(bf16[272,512]{1,0:T(8,128)(2,1)S(1)} %get-tuple-element.58), channel_id=1, source_target_pairs={{0,1},{1,2},{2,3},{3,0},{4,5},{5,6},{6,7},{7,4},{8,9},{9,10},{10,1... | collective-permute-start | bytes 835592 | tf_op jit(solution)/shard_map/ppermute | solution.py:316
  28.4 0.0 collective-permute-done.3.sibling_ref
  28.4 1.5 %collective-permute-start.10 = (bf16[272,512]{1,0:T(8,128)(2,1)S(1)}, bf16[272,512]{1,0:T(8,128)(2,1)S(1)}, u32[]{:S(2)}, u32[]{:S(2)}) collective-permute-start(bf16[272,512]{1,0:T(8,128)(2,1)S(1)} %get-tuple-element.59), channel_id=1, source_target_pairs={{0,3},{1,0},{2,1},{3,2},{4,7},{5,4},{6,5},{7,6},{8,11},{9,8},{10,9... | collective-permute-start | bytes 835592 | tf_op jit(solution)/shard_map/ppermute | solution.py:316
  29.9 0.7 shard_map.69
  30.6 2.2 %collective-permute-done.5.b_ref = bf16[512,256]{1,0:T(8,128)(2,1)S(1)} collective-permute-done((bf16[512,256]{1,0:T(8,128)(2,1)S(1)}, bf16[512,256]{1,0:T(8,128)(2,1)S(1)}, u32[]{:S(2)}, u32[]{:S(2)}) %collective-permute-start.5) | collective-permute-done | bytes 262176 | tf_op jit(solution)/shard_map/ppermute | solution.py:316
  32.8 5.3 %collective-permute-done.4.a_ref = bf16[512,256]{1,0:T(8,128)(2,1)S(1)} collective-permute-done((bf16[512,256]{1,0:T(8,128)(2,1)S(1)}, bf16[512,256]{1,0:T(8,128)(2,1)S(1)}, u32[]{:S(2)}, u32[]{:S(2)}) %collective-permute-start.4) | collective-permute-done | bytes 262176 | tf_op jit(solution)/shard_map/ppermute | solution.py:316
  38.2 0.0 collective-permute-done.7.refs_1_
  38.2 6.0 %shard_map.72 = (bf16[1024,256]{1,0:T(8,128)(2,1)S(1)}, bf16[128,1024]{1,0:T(8,128)(2,1)S(1)}, f32[1024,256]{1,0:T(8,128)S(1)}, f32[1024,256]{1,0:T(8,128)S(1)},...) custom-call(s32[3]{0:T(128)S(1)} %pad_add_fusion.place_ref, bf16[1024,256]{1,0:T(8,128)(2,1)S(1)} %get-tuple-element.48.own_ref, ...), custom_call_target="tpu_custom_call" | custom-call | flops 1 | bytes 5013516 | tf_op jit(solution)/shard_map/pallas_call | solution.py:26
  44.2 2.0 %collective-permute-start.8 = (bf16[256,256]{1,0:T(8,128)(2,1)S(1)}, bf16[256,256]{1,0:T(8,128)(2,1)S(1)}, u32[]{:S(2)}, u32[]{:S(2)}) collective-permute-start(bf16[256,256]{1,0:T(8,128)(2,1)S(1)} %get-tuple-element.55), channel_id=1, source_target_pairs={{0,2},{1,3},{2,0},{3,1},{4,6},{5,7},{6,4},{7,5},{8,10},{9,11},{10,... | collective-permute-start | bytes 393224 | tf_op jit(solution)/shard_map/ppermute | solution.py:316
  46.2 0.0 collective-permute-done.9.refs_0_
  46.2 4.8 %collective-permute-done.10.refs_1_ = bf16[272,512]{1,0:T(8,128)(2,1)S(1)} collective-permute-done((bf16[272,512]{1,0:T(8,128)(2,1)S(1)}, bf16[272,512]{1,0:T(8,128)(2,1)S(1)}, u32[]{:S(2)}, u32[]{:S(2)}) %collective-permute-start.10) | collective-permute-done | bytes 278560 | tf_op jit(solution)/shard_map/ppermute | solution.py:316
  51.0 3.8 %shard_map.73 = (f32[512,256]{1,0:T(8,128)S(1)}, f32[512,256]{1,0:T(8,128)S(1)}, bf16[544,256]{1,0:T(8,128)(2,1)S(1)}, bf16[2,128,256]{2,1,0:T(8,128)(2,1)S(1)}) custom-call(s32[3]{0:T(128)S(1)} %pad_add_fusion.place_ref, bf16[1024,256]{1,0:T(8,128)(2,1)S(1)} %get-tuple-element.48.own_ref, bf16[128,1024]{1,0:T(8,128)(2,1)S(1)} %get-tuple-element.49.own_kt_ref, ...), custom_call_target="tpu_custom_call" | custom-call | flops 1 | bytes 5685260 | tf_op jit(solution)/shard_map/pallas_call | solution.py:26
  54.8 3.1 %collective-permute-start.14 = (bf16[544,256]{1,0:T(8,128)(2,1)S(1)}, bf16[544,256]{1,0:T(8,128)(2,1)S(1)}, u32[]{:S(2)}, u32[]{:S(2)}) collective-permute-start(bf16[544,256]{1,0:T(8,128)(2,1)S(1)} %get-tuple-element.71), channel_id=1, source_target_pairs={{8,0},{9,1},{10,2},{11,3},{12,4},{13,5},{14,6},{15,7},{16,8},{17,9... | collective-permute-start | bytes 835592 | tf_op jit(solution)/shard_map/ppermute | solution.py:316
  57.9 0.0 collective-permute-done.8.refs_1_
  57.9 3.6 %shard_map.74 = (f32[512,256]{1,0:T(8,128)S(1)}, f32[512,256]{1,0:T(8,128)S(1)}, bf16[512,256]{1,0:T(8,128)(2,1)S(1)}, bf16[256,256]{1,0:T(8,128)(2,1)S(1)}, bf16[256,256]{1,0:T(8,128)(2,1)S(1)}) custom-call(s32[3]{0:T(128)S(1)} %pad_add_fusion.place_ref, bf16[1024,256]{1,0:T(8,128)(2,1)S(1)} %get-tuple-element.48.own_ref, ...), custom_call_target="tpu_custom_call" | custom-call | flops 1 | bytes 5939212 | tf_op jit(solution)/shard_map/pallas_call | solution.py:26
  61.6 2.2 %collective-permute-start.15 = (bf16[512,256]{1,0:T(8,128)(2,1)S(1)}, bf16[512,256]{1,0:T(8,128)(2,1)S(1)}, u32[]{:S(2)}, u32[]{:S(2)}) collective-permute-start(bf16[512,256]{1,0:T(8,128)(2,1)S(1)} %get-tuple-element.72), channel_id=1, source_target_pairs={{8,0},{9,1},{10,2},{11,3},{12,4},{13,5},{14,6},{15,7},{16,8},{17,9... | collective-permute-start | bytes 786440 | tf_op jit(solution)/shard_map/ppermute | solution.py:316
  63.7 0.1 collective-permute-start.11
  63.8 1.5 %collective-permute-start.12 = (bf16[256,256]{1,0:T(8,128)(2,1)S(1)}, bf16[256,256]{1,0:T(8,128)(2,1)S(1)}, u32[]{:S(2)}, u32[]{:S(2)}) collective-permute-start(bf16[256,256]{1,0:T(8,128)(2,1)S(1)} %get-tuple-element.66), channel_id=1, source_target_pairs={{0,1},{1,2},{2,3},{3,0},{4,5},{5,6},{6,7},{7,4},{8,9},{9,10},{10,1... | collective-permute-start | bytes 393224 | tf_op jit(solution)/shard_map/ppermute | solution.py:316
  65.2 0.0 collective-permute-done.14.back_a_ref
  65.3 5.1 %collective-permute-done.15.back_b_ref = bf16[512,256]{1,0:T(8,128)(2,1)S(1)} collective-permute-done((bf16[512,256]{1,0:T(8,128)(2,1)S(1)}, bf16[512,256]{1,0:T(8,128)(2,1)S(1)}, u32[]{:S(2)}, u32[]{:S(2)}) %collective-permute-start.15) | collective-permute-done | bytes 262176 | tf_op jit(solution)/shard_map/ppermute | solution.py:316
  70.3 0.7 shard_map.77
  71.0 0.1 collective-permute-start.16
  71.1 0.1 collective-permute-start.17
  71.2 1.5 %collective-permute-start.18 = (bf16[256,256]{1,0:T(8,128)(2,1)S(1)}, bf16[256,256]{1,0:T(8,128)(2,1)S(1)}, u32[]{:S(2)}, u32[]{:S(2)}) collective-permute-start(bf16[256,256]{1,0:T(8,128)(2,1)S(1)} %get-tuple-element.76), channel_id=1, source_target_pairs={{0,3},{1,0},{2,1},{3,2},{4,7},{5,4},{6,5},{7,6},{8,11},{9,8},{10,9... | collective-permute-start | bytes 393224 | tf_op jit(solution)/shard_map/ppermute | solution.py:316
  72.6 0.0 collective-permute-done.11.refs_2_
  72.6 0.0 collective-permute-done.12.refs_3_
  72.6 0.6 shard_map.75
  73.2 2.4 %collective-permute-start.13 = (bf16[512,256]{1,0:T(8,128)(2,1)S(1)}, bf16[512,256]{1,0:T(8,128)(2,1)S(1)}, u32[]{:S(2)}, u32[]{:S(2)}) collective-permute-start(bf16[512,256]{1,0:T(8,128)(2,1)S(1)} %get-tuple-element.68), channel_id=1, source_target_pairs={{0,4},{1,5},{2,6},{3,7},{4,0},{5,1},{6,2},{7,3},{8,12},{9,13},{10,... | collective-permute-start | bytes 786440 | tf_op jit(solution)/shard_map/ppermute | solution.py:316
  75.7 2.1 %collective-permute-done.16.refs_1_ = bf16[256,256]{1,0:T(8,128)(2,1)S(1)} collective-permute-done((bf16[256,256]{1,0:T(8,128)(2,1)S(1)}, bf16[256,256]{1,0:T(8,128)(2,1)S(1)}, u32[]{:S(2)}, u32[]{:S(2)}) %collective-permute-start.16) | collective-permute-done | bytes 131104 | tf_op jit(solution)/shard_map/ppermute | solution.py:316
  77.8 4.4 %collective-permute-done.17.refs_2_ = bf16[256,256]{1,0:T(8,128)(2,1)S(1)} collective-permute-done((bf16[256,256]{1,0:T(8,128)(2,1)S(1)}, bf16[256,256]{1,0:T(8,128)(2,1)S(1)}, u32[]{:S(2)}, u32[]{:S(2)}) %collective-permute-start.17) | collective-permute-done | bytes 131104 | tf_op jit(solution)/shard_map/ppermute | solution.py:316
  82.2 1.0 %collective-permute-done.18.refs_3_ = bf16[256,256]{1,0:T(8,128)(2,1)S(1)} collective-permute-done((bf16[256,256]{1,0:T(8,128)(2,1)S(1)}, bf16[256,256]{1,0:T(8,128)(2,1)S(1)}, u32[]{:S(2)}, u32[]{:S(2)}) %collective-permute-start.18) | collective-permute-done | bytes 131104 | tf_op jit(solution)/shard_map/ppermute | solution.py:316
  83.2 0.6 shard_map.78
  83.8 1.5 %collective-permute-start.19 = (bf16[512,256]{1,0:T(8,128)(2,1)S(1)}, bf16[512,256]{1,0:T(8,128)(2,1)S(1)}, u32[]{:S(2)}, u32[]{:S(2)}) collective-permute-start(bf16[512,256]{1,0:T(8,128)(2,1)S(1)} %get-tuple-element.78), channel_id=1, source_target_pairs={{0,4},{1,5},{2,6},{3,7},{4,0},{5,1},{6,2},{7,3},{8,12},{9,13},{10,... | collective-permute-start | bytes 786440 | tf_op jit(solution)/shard_map/ppermute | solution.py:316
  85.2 0.0 collective-permute-done.13.sibling_ref
  85.2 1.4 %shard_map.76 = bf16[128,2048]{1,0:T(8,128)(2,1)} custom-call(s32[3]{0:T(128)S(1)} %pad_add_fusion.place_ref, bf16[512,256]{1,0:T(8,128)(2,1)S(1)} %get-tuple-element.67.mine_ref, bf16[512,256]{1,0:T(8,128)(2,1)S(1)} %collective-permute-done.13.sibling_ref), custom_call_target="tpu_custom_call" | custom-call | bytes 1048588 | tf_op jit(solution)/shard_map/pallas_call | solution.py:26
  86.6 0.0 collective-permute-done.19.sibling_ref
  86.6 1.5 %shard_map.79 = (bf16[128,1024]{1,0:T(8,128)(2,1)}, bf16[128,1024]{1,0:T(8,128)(2,1)}) custom-call(s32[3]{0:T(128)S(1)} %pad_add_fusion.place_ref, bf16[512,256]{1,0:T(8,128)(2,1)S(1)} %get-tuple-element.77.mine_ref, bf16[512,256]{1,0:T(8,128)(2,1)S(1)} %collective-permute-done.19.sibling_ref), custom_call_target="tpu_custom_call" | custom-call | bytes 1048588 | tf_op jit(solution)/shard_map/pallas_call | solution.py:26
  (2 shorter events, 0.0 us)
Async XLA Ops:
  0.7 1.0 %copy-start = (bf16[128,2048]{1,0:T(8,128)(2,1)S(1)}, bf16[128,2048]{1,0:T(8,128)(2,1)}, u32[]{:S(2)}) copy-start(bf16[128,2048]{1,0:T(8,128)(2,1)} %q_ref.1) | copy-start | bytes 1572868
  1.8 1.0 %copy-start.1 = (bf16[128,2048]{1,0:T(8,128)(2,1)S(1)}, bf16[128,2048]{1,0:T(8,128)(2,1)}, u32[]{:S(2)}) copy-start(bf16[128,2048]{1,0:T(8,128)(2,1)} %g_ref.1) | copy-start | bytes 1572868
  2.8 1.7 %copy-start.2 = (bf16[128,1024]{1,0:T(8,128)(2,1)S(1)}, bf16[128,1024]{1,0:T(8,128)(2,1)}, u32[]{:S(2)}) copy-start(bf16[128,1024]{1,0:T(8,128)(2,1)} %k_ref.1) | copy-start | bytes 786436
  2.8 1.7 %copy-start.3 = (bf16[128,1024]{1,0:T(8,128)(2,1)S(1)}, bf16[128,1024]{1,0:T(8,128)(2,1)}, u32[]{:S(2)}) copy-start(bf16[128,1024]{1,0:T(8,128)(2,1)} %v_ref.1) | copy-start | bytes 786436
  3.7 16.7 %collective-permute-start.6 = (bf16[4,128,512]{2,1,0:T(8,128)(2,1)S(1)}, bf16[4,128,512]{2,1,0:T(8,128)(2,1)S(1)}, u32[]{:S(2)}, u32[]{:S(2)}) collective-permute-start(bf16[4,128,512]{2,1,0:T(8,128)(2,1)S(1)} %get-tuple-element.51), channel_id=1, source_target_pairs={{0,4},{1,5},{2,6},{3,7},{4,0},{5,1},{6,2},{7,3},{8,12},{9,13},{10,... | collective-permute-start | bytes 1572872 | tf_op jit(solution)/shard_map/ppermute | solution.py:316
  5.3 8.2 %collective-permute-start = (bf16[128,512]{1,0:T(8,128)(2,1)S(1)}, bf16[128,512]{1,0:T(8,128)(2,1)S(1)}, u32[]{:S(2)}, u32[]{:S(2)}) collective-permute-start(bf16[128,512]{1,0:T(8,128)(2,1)S(1)} %get-tuple-element.43), channel_id=1, source_target_pairs={{0,2},{1,3},{2,0},{3,1},{4,6},{5,7},{6,4},{7,5},{8,10},{9,11},{10,... | collective-permute-start | bytes 393224 | tf_op jit(solution)/shard_map/ppermute | solution.py:316
  7.7 11.6 %collective-permute-start.1 = (bf16[128,512]{1,0:T(8,128)(2,1)S(1)}, bf16[128,512]{1,0:T(8,128)(2,1)S(1)}, u32[]{:S(2)}, u32[]{:S(2)}) collective-permute-start(bf16[128,512]{1,0:T(8,128)(2,1)S(1)} %get-tuple-element.44), channel_id=1, source_target_pairs={{0,1},{1,2},{2,3},{3,0},{4,5},{5,6},{6,7},{7,4},{8,9},{9,10},{10,1... | collective-permute-start | bytes 393224 | tf_op jit(solution)/shard_map/ppermute | solution.py:316
  7.7 11.6 %collective-permute-start.2 = (bf16[128,512]{1,0:T(8,128)(2,1)S(1)}, bf16[128,512]{1,0:T(8,128)(2,1)S(1)}, u32[]{:S(2)}, u32[]{:S(2)}) collective-permute-start(bf16[128,512]{1,0:T(8,128)(2,1)S(1)} %get-tuple-element.45), channel_id=1, source_target_pairs={{0,3},{1,0},{2,1},{3,2},{4,7},{5,4},{6,5},{7,6},{8,11},{9,8},{10,9... | collective-permute-start | bytes 393224 | tf_op jit(solution)/shard_map/ppermute | solution.py:316
  19.9 8.5 %collective-permute-start.3 = (bf16[512,256]{1,0:T(8,128)(2,1)S(1)}, bf16[512,256]{1,0:T(8,128)(2,1)S(1)}, u32[]{:S(2)}, u32[]{:S(2)}) collective-permute-start(bf16[512,256]{1,0:T(8,128)(2,1)S(1)} %get-tuple-element.47), channel_id=1, source_target_pairs={{0,4},{1,5},{2,6},{3,7},{4,0},{5,1},{6,2},{7,3},{8,12},{9,13},{10,... | collective-permute-start | bytes 786440 | tf_op jit(solution)/shard_map/ppermute | solution.py:316
  21.0 17.1 %collective-permute-start.7 = (bf16[272,512]{1,0:T(8,128)(2,1)S(1)}, bf16[272,512]{1,0:T(8,128)(2,1)S(1)}, u32[]{:S(2)}, u32[]{:S(2)}) collective-permute-start(bf16[272,512]{1,0:T(8,128)(2,1)S(1)} %get-tuple-element.53), channel_id=1, source_target_pairs={{0,2},{1,3},{2,0},{3,1},{4,6},{5,7},{6,4},{7,5},{8,10},{9,11},{10,... | collective-permute-start | bytes 835592 | tf_op jit(solution)/shard_map/ppermute | solution.py:316
  21.5 11.3 %collective-permute-start.5 = (bf16[512,256]{1,0:T(8,128)(2,1)S(1)}, bf16[512,256]{1,0:T(8,128)(2,1)S(1)}, u32[]{:S(2)}, u32[]{:S(2)}) collective-permute-start(bf16[512,256]{1,0:T(8,128)(2,1)S(1)} %get-tuple-element.47), channel_id=1, source_target_pairs={{0,12},{1,13},{2,14},{3,15},{4,8},{5,9},{6,10},{7,11},{8,20},{9,21... | collective-permute-start | bytes 786440 | tf_op jit(solution)/shard_map/ppermute | solution.py:316
  24.8 13.3 %collective-permute-start.4 = (bf16[512,256]{1,0:T(8,128)(2,1)S(1)}, bf16[512,256]{1,0:T(8,128)(2,1)S(1)}, u32[]{:S(2)}, u32[]{:S(2)}) collective-permute-start(bf16[512,256]{1,0:T(8,128)(2,1)S(1)} %get-tuple-element.46.mine_ref), channel_id=1, source_target_pairs={{0,8},{1,9},{2,10},{3,11},{4,12},{5,13},{6,14},{7,15},{8,16},{9,17... | collective-permute-start | bytes 786440 | tf_op jit(solution)/shard_map/ppermute | solution.py:316
  26.8 19.4 %collective-permute-start.9 = (bf16[272,512]{1,0:T(8,128)(2,1)S(1)}, bf16[272,512]{1,0:T(8,128)(2,1)S(1)}, u32[]{:S(2)}, u32[]{:S(2)}) collective-permute-start(bf16[272,512]{1,0:T(8,128)(2,1)S(1)} %get-tuple-element.58), channel_id=1, source_target_pairs={{0,1},{1,2},{2,3},{3,0},{4,5},{5,6},{6,7},{7,4},{8,9},{9,10},{10,1... | collective-permute-start | bytes 835592 | tf_op jit(solution)/shard_map/ppermute | solution.py:316
  28.4 22.7 %collective-permute-start.10 = (bf16[272,512]{1,0:T(8,128)(2,1)S(1)}, bf16[272,512]{1,0:T(8,128)(2,1)S(1)}, u32[]{:S(2)}, u32[]{:S(2)}) collective-permute-start(bf16[272,512]{1,0:T(8,128)(2,1)S(1)} %get-tuple-element.59), channel_id=1, source_target_pairs={{0,3},{1,0},{2,1},{3,2},{4,7},{5,4},{6,5},{7,6},{8,11},{9,8},{10,9... | collective-permute-start | bytes 835592 | tf_op jit(solution)/shard_map/ppermute | solution.py:316
  44.2 13.7 %collective-permute-start.8 = (bf16[256,256]{1,0:T(8,128)(2,1)S(1)}, bf16[256,256]{1,0:T(8,128)(2,1)S(1)}, u32[]{:S(2)}, u32[]{:S(2)}) collective-permute-start(bf16[256,256]{1,0:T(8,128)(2,1)S(1)} %get-tuple-element.55), channel_id=1, source_target_pairs={{0,2},{1,3},{2,0},{3,1},{4,6},{5,7},{6,4},{7,5},{8,10},{9,11},{10,... | collective-permute-start | bytes 393224 | tf_op jit(solution)/shard_map/ppermute | solution.py:316
  54.8 10.4 %collective-permute-start.14 = (bf16[544,256]{1,0:T(8,128)(2,1)S(1)}, bf16[544,256]{1,0:T(8,128)(2,1)S(1)}, u32[]{:S(2)}, u32[]{:S(2)}) collective-permute-start(bf16[544,256]{1,0:T(8,128)(2,1)S(1)} %get-tuple-element.71), channel_id=1, source_target_pairs={{8,0},{9,1},{10,2},{11,3},{12,4},{13,5},{14,6},{15,7},{16,8},{17,9... | collective-permute-start | bytes 835592 | tf_op jit(solution)/shard_map/ppermute | solution.py:316
  61.6 8.8 %collective-permute-start.15 = (bf16[512,256]{1,0:T(8,128)(2,1)S(1)}, bf16[512,256]{1,0:T(8,128)(2,1)S(1)}, u32[]{:S(2)}, u32[]{:S(2)}) collective-permute-start(bf16[512,256]{1,0:T(8,128)(2,1)S(1)} %get-tuple-element.72), channel_id=1, source_target_pairs={{8,0},{9,1},{10,2},{11,3},{12,4},{13,5},{14,6},{15,7},{16,8},{17,9... | collective-permute-start | bytes 786440 | tf_op jit(solution)/shard_map/ppermute | solution.py:316
  63.7 8.9 %collective-permute-start.11 = (bf16[256,256]{1,0:T(8,128)(2,1)S(1)}, bf16[256,256]{1,0:T(8,128)(2,1)S(1)}, u32[]{:S(2)}, u32[]{:S(2)}) collective-permute-start(bf16[256,256]{1,0:T(8,128)(2,1)S(1)} %get-tuple-element.65), channel_id=1, source_target_pairs={{0,3},{1,0},{2,1},{3,2},{4,7},{5,4},{6,5},{7,6},{8,11},{9,8},{10,9... | collective-permute-start | bytes 393224 | tf_op jit(solution)/shard_map/ppermute | solution.py:316
  63.8 8.8 %collective-permute-start.12 = (bf16[256,256]{1,0:T(8,128)(2,1)S(1)}, bf16[256,256]{1,0:T(8,128)(2,1)S(1)}, u32[]{:S(2)}, u32[]{:S(2)}) collective-permute-start(bf16[256,256]{1,0:T(8,128)(2,1)S(1)} %get-tuple-element.66), channel_id=1, source_target_pairs={{0,1},{1,2},{2,3},{3,0},{4,5},{5,6},{6,7},{7,4},{8,9},{9,10},{10,1... | collective-permute-start | bytes 393224 | tf_op jit(solution)/shard_map/ppermute | solution.py:316
  71.0 6.8 %collective-permute-start.16 = (bf16[256,256]{1,0:T(8,128)(2,1)S(1)}, bf16[256,256]{1,0:T(8,128)(2,1)S(1)}, u32[]{:S(2)}, u32[]{:S(2)}) collective-permute-start(bf16[256,256]{1,0:T(8,128)(2,1)S(1)} %get-tuple-element.74), channel_id=1, source_target_pairs={{0,2},{1,3},{2,0},{3,1},{4,6},{5,7},{6,4},{7,5},{8,10},{9,11},{10,... | collective-permute-start | bytes 393224 | tf_op jit(solution)/shard_map/ppermute | solution.py:316
  71.1 11.1 %collective-permute-start.17 = (bf16[256,256]{1,0:T(8,128)(2,1)S(1)}, bf16[256,256]{1,0:T(8,128)(2,1)S(1)}, u32[]{:S(2)}, u32[]{:S(2)}) collective-permute-start(bf16[256,256]{1,0:T(8,128)(2,1)S(1)} %get-tuple-element.75), channel_id=1, source_target_pairs={{0,1},{1,2},{2,3},{3,0},{4,5},{5,6},{6,7},{7,4},{8,9},{9,10},{10,1... | collective-permute-start | bytes 393224 | tf_op jit(solution)/shard_map/ppermute | solution.py:316
  71.2 12.0 %collective-permute-start.18 = (bf16[256,256]{1,0:T(8,128)(2,1)S(1)}, bf16[256,256]{1,0:T(8,128)(2,1)S(1)}, u32[]{:S(2)}, u32[]{:S(2)}) collective-permute-start(bf16[256,256]{1,0:T(8,128)(2,1)S(1)} %get-tuple-element.76), channel_id=1, source_target_pairs={{0,3},{1,0},{2,1},{3,2},{4,7},{5,4},{6,5},{7,6},{8,11},{9,8},{10,9... | collective-permute-start | bytes 393224 | tf_op jit(solution)/shard_map/ppermute | solution.py:316
  73.2 12.0 %collective-permute-start.13 = (bf16[512,256]{1,0:T(8,128)(2,1)S(1)}, bf16[512,256]{1,0:T(8,128)(2,1)S(1)}, u32[]{:S(2)}, u32[]{:S(2)}) collective-permute-start(bf16[512,256]{1,0:T(8,128)(2,1)S(1)} %get-tuple-element.68), channel_id=1, source_target_pairs={{0,4},{1,5},{2,6},{3,7},{4,0},{5,1},{6,2},{7,3},{8,12},{9,13},{10,... | collective-permute-start | bytes 786440 | tf_op jit(solution)/shard_map/ppermute | solution.py:316
  83.8 2.9 %collective-permute-start.19 = (bf16[512,256]{1,0:T(8,128)(2,1)S(1)}, bf16[512,256]{1,0:T(8,128)(2,1)S(1)}, u32[]{:S(2)}, u32[]{:S(2)}) collective-permute-start(bf16[512,256]{1,0:T(8,128)(2,1)S(1)} %get-tuple-element.78), channel_id=1, source_target_pairs={{0,4},{1,5},{2,6},{3,7},{4,0},{5,1},{6,2},{7,3},{8,12},{9,13},{10,... | collective-permute-start | bytes 786440 | tf_op jit(solution)/shard_map/ppermute | solution.py:316

commit v12 on v11

--- a/solution.py
+++ b/solution.py
@@ -80,15 +80,16 @@
     copied(sems, pairs)
 
 
-def pack_qd_kernel(heads, place_ref, q_ref, g_ref, mine_ref, other_ref, sems):
+def pack_qd_kernel(heads, place_ref, q_ref, g_ref, mine_ref, *refs):
+    other_refs, sems = refs[:heads], refs[heads]
     core = place_ref[1]
     width = 2 * HEAD_SIZE
     pairs = []
-    for ref, c in ((other_ref, 1 - core), (mine_ref, core)):
-        for k in range(heads):
+    for k in range(heads):
+        for ref, c in ((other_refs[k], 1 - core), (mine_ref.at[k], core)):
             columns = at((2 * onward(place_ref, heads, k) + c) * width, width)
-            pairs.append((q_ref.at[:, columns], ref.at[k, :, pl.ds(0, width)]))
-            pairs.append((g_ref.at[:, columns], ref.at[k, :, pl.ds(width, width)]))
+            pairs.append((q_ref.at[:, columns], ref.at[:, pl.ds(0, width)]))
+            pairs.append((g_ref.at[:, columns], ref.at[:, pl.ds(width, width)]))
     copied(sems, pairs)
 
 
@@ -109,11 +110,12 @@
     kt_ref[...] = out_ref[:, :HEAD_SIZE].T
 
 
-def merge_rows_kernel(heads, place_ref, mine_ref, other_ref, after_ref, *out_refs):
+def merge_rows_kernel(heads, place_ref, mine_ref, *refs):
+    other_refs, out_refs = refs[:heads], refs[heads + 1 :]
     core = place_ref[1]
     for k, out_ref in enumerate(out_refs):
         out_ref[at(core * BLOCK, BLOCK)] = mine_ref[k]
-        out_ref[at((1 - core) * BLOCK, BLOCK)] = other_ref[k]
+        out_ref[at((1 - core) * BLOCK, BLOCK)] = other_refs[k][...]
 
 
 def sort_kernel(heads, place_ref, *refs):
@@ -287,7 +289,7 @@
     prev, (own_sums, prev_sums), dq_early = outs[:2], outs[2:4], outs[4:]
     dq_early = (dq_early[0],) + tuple(home(dq_early[n], early[n]) for n in range(1, len(early)))
     late_blocks = tuple(blocks[len(early) :])
-    wide_part = shape_of(low, half + 32, 2 * d)
+    wide_part = shape_of(low, half + 16, 2 * d)
     outs = (half_sums, half_sums, wide_part, shape_of(low, len(late), BLOCK, 2 * d))
     own_low, prev_high, back_a, dq_so_far = run(
         late, (0,), 1, outs, prev + late_blocks + (own_sums, prev_sums), 1
@@ -336,20 +338,20 @@
     kvs = spread(
         copy_call(bind(pack_kv_kernel), 4 * heads, (slab,) * heads, (place, key_rows, saved_value_rows))
     )
-    qd_mine, qd_other = copy_call(
+    qd_mine, *qd_other = copy_call(
         bind(pack_qd_kernel),
         4 * heads,
-        (shape_of(low, heads, rows, 4 * d),) * 2,
+        (shape_of(low, heads, rows, 4 * d),) + (slab,) * heads,
         (place, query_rows, out_grad),
     )
-    qd_other = across(qd_other, chip_step=0, flip=1)
+    qd_other = [across(part, chip_step=0, flip=1) for part in qd_other]
     mine, other = call(bind(gather_kv_kernel), (shape_of(low, heads * rows, 2 * d),) * 2, (place,) + kvs)
     near = across(mine, chip_step=1, flip=0)
     far = across(other, chip_step=1, flip=1)
     blocks = call(
         bind(merge_rows_kernel),
-        (shape_of(low, 2 * rows + 16, 4 * d),) * heads,
-        (place, qd_mine, qd_other, mine[:8]),
+        tuple(shape_of(low, 2 * rows + 16 * (n == 1), 4 * d) for n in range(heads)),
+        (place, qd_mine, *qd_other, mine[:8]),
     )
     blocks = spread(blocks)
     sibling = across(other, chip_step=0, flip=1)

time: 88.5 us -> 86.5 us (0.977)
  waiting for transfers between devices: 35.2 us -> 26.2 us
  starting transfers between devices: 28.2 us -> 34.3 us
  local copies, waits for them, and re-layouts: 2.1 us -> 3 us
    ppermute x20 -> x23, waiting for transfers between devices: 35.2 us -> 26.2 us  [moved(): return lax.ppermute(value, ('chip', 'core', 'head'), pairs)]
    ppermute x20 -> x23, starting transfers between devices: 28.2 us -> 34.3 us  [moved(): return lax.ppermute(value, ('chip', 'core', 'head'), pairs)]
    unnamed x8, local copies, waits for them, and re-layouts: 2.09 us -> 2.99 us
  transfers between devices with their start and end apart: 20 -> 23, of which waited for: 9 -> 10; matrix products, arithmetic and copies ran while one was open for 0% -> 0% of each run, Pallas kernels for 22% -> 22%
where the time goes in v12:
time: 86.5 us; the launch traced here: 86.2 us
  starting transfers between devices  34.3 us (40%)
  waiting for transfers between devices  26.2 us (30%)
  Pallas kernels  21.7 us (25%)
  local copies, waits for them, and re-layouts  3 us (3%)
    ppermute x23, starting transfers between devices, moved(): return lax.ppermute(value, ('chip', 'core', 'head'), pairs)  34.3 us
    ppermute x23, waiting for transfers between devices, moved(): return lax.ppermute(value, ('chip', 'core', 'head'), pairs)  26.2 us
    pallas_call x13, Pallas kernels, call(): pl.pallas_call(kernel, out_shape=out_shape, in_specs=[SMEM_SPEC] + [spec]...  21.7 us
    unnamed x8, local copies, waits for them, and re-layouts  2.99 us
  transfers between devices with their start and end apart: 23, of which 10 were waited for; matrix products, arithmetic and copies ran while one was open for 0% of the time, Pallas kernels for 22%

profile of v12, /device:TPU:13, one launch (start us, length us, event | category | flops | bytes accessed | tf_op | source)
XLA Modules:
  0.0 86.2 jit_solution(13439045553917575131)
XLA Ops:
  0.6 0.0 copy-start
  0.6 0.1 pad_add_fusion.place_ref
  0.7 1.0 %copy-done.2 = bf16[128,1024]{1,0:T(8,128)(2,1)S(1)} copy-done((bf16[128,1024]{1,0:T(8,128)(2,1)S(1)}, bf16[128,1024]{1,0:T(8,128)(2,1)}, u32[]{:S(2)}) %copy-start.2) | copy-done | bytes 262168
  1.7 0.9 %copy-done.3 = bf16[128,1024]{1,0:T(8,128)(2,1)S(1)} copy-done((bf16[128,1024]{1,0:T(8,128)(2,1)S(1)}, bf16[128,1024]{1,0:T(8,128)(2,1)}, u32[]{:S(2)}) %copy-start.3) | copy-done | bytes 262168
  2.7 0.9 %shard_map.67 = (bf16[128,512]{1,0:T(8,128)(2,1)S(1)}, bf16[128,512]{1,0:T(8,128)(2,1)S(1)}, bf16[128,512]{1,0:T(8,128)(2,1)S(1)}, bf16[128,512]{1,0:T(8,128)(2,1)S(1)}) custom-call(s32[3]{0:T(128)S(1)} %pad_add_fusion.place_ref, bf16[128,1024]{1,0:T(8,128)(2,1)S(1)} %copy-done.2, bf16[128,1024]{1,0:T(8,128)(2,1)S(1)} %copy-done.3), custom_call_target="tpu_custom_call" | custom-call | bytes 1048588 | tf_op jit(solution)/shard_map/pallas_call | solution.py:26
  3.6 2.4 %collective-permute-start = (bf16[128,512]{1,0:T(8,128)(2,1)S(1)}, bf16[128,512]{1,0:T(8,128)(2,1)S(1)}, u32[]{:S(2)}, u32[]{:S(2)}) collective-permute-start(bf16[128,512]{1,0:T(8,128)(2,1)S(1)} %get-tuple-element.46), channel_id=1, source_target_pairs={{0,2},{1,3},{2,0},{3,1},{4,6},{5,7},{6,4},{7,5},{8,10},{9,11},{10,... | collective-permute-start | bytes 393224 | tf_op jit(solution)/shard_map/ppermute | solution.py:318
  5.9 0.0 collective-permute-start.1
  5.9 1.5 %collective-permute-start.2 = (bf16[128,512]{1,0:T(8,128)(2,1)S(1)}, bf16[128,512]{1,0:T(8,128)(2,1)S(1)}, u32[]{:S(2)}, u32[]{:S(2)}) collective-permute-start(bf16[128,512]{1,0:T(8,128)(2,1)S(1)} %get-tuple-element.48), channel_id=1, source_target_pairs={{0,3},{1,0},{2,1},{3,2},{4,7},{5,4},{6,5},{7,6},{8,11},{9,8},{10,9... | collective-permute-start | bytes 393224 | tf_op jit(solution)/shard_map/ppermute | solution.py:318
  7.4 1.0 %copy-done.1 = bf16[128,2048]{1,0:T(8,128)(2,1)S(1)} copy-done((bf16[128,2048]{1,0:T(8,128)(2,1)S(1)}, bf16[128,2048]{1,0:T(8,128)(2,1)}, u32[]{:S(2)}) %copy-start.1) | copy-done | bytes 524312
  8.5 0.9 %shard_map.70 = (bf16[4,128,512]{2,1,0:T(8,128)(2,1)S(1)}, bf16[128,512]{1,0:T(8,128)(2,1)S(1)}, bf16[128,512]{1,0:T(8,128)(2,1)S(1)}, bf16[128,512]{1,0:T(8,128)(2,1)S(1)}, bf16[128,512]{1,0:T(8,128)(2,1)S(1)}) custom-call(s32[3]{0:T(128)S(1)} %pad_add_fusion.place_ref, bf16[128,2048]{1,0:T(8,128)(2,1)S(1)} %copy-done, bf16[128,2048]{1,0:T(8,128)(2,1)S(1)} %copy-done.1), custom_call_target="tpu_custom_call" | custom-call | bytes 2097164 | tf_op jit(solution)/shard_map/pallas_call | solution.py:26
  9.4 1.6 %collective-permute-start.6 = (bf16[128,512]{1,0:T(8,128)(2,1)S(1)}, bf16[128,512]{1,0:T(8,128)(2,1)S(1)}, u32[]{:S(2)}, u32[]{:S(2)}) collective-permute-start(bf16[128,512]{1,0:T(8,128)(2,1)S(1)} %get-tuple-element.54), channel_id=1, source_target_pairs={{0,4},{1,5},{2,6},{3,7},{4,0},{5,1},{6,2},{7,3},{8,12},{9,13},{10,... | collective-permute-start | bytes 393224 | tf_op jit(solution)/shard_map/ppermute | solution.py:318
  10.9 0.1 collective-permute-start.7
  11.0 1.4 %collective-permute-done.refs_1_ = bf16[128,512]{1,0:T(8,128)(2,1)S(1)} collective-permute-done((bf16[128,512]{1,0:T(8,128)(2,1)S(1)}, bf16[128,512]{1,0:T(8,128)(2,1)S(1)}, u32[]{:S(2)}, u32[]{:S(2)}) %collective-permute-start) | collective-permute-done | bytes 131104 | tf_op jit(solution)/shard_map/ppermute | solution.py:318
  12.4 0.9 %collective-permute-start.8 = (bf16[128,512]{1,0:T(8,128)(2,1)S(1)}, bf16[128,512]{1,0:T(8,128)(2,1)S(1)}, u32[]{:S(2)}, u32[]{:S(2)}) collective-permute-start(bf16[128,512]{1,0:T(8,128)(2,1)S(1)} %get-tuple-element.56), channel_id=1, source_target_pairs={{0,4},{1,5},{2,6},{3,7},{4,0},{5,1},{6,2},{7,3},{8,12},{9,13},{10,... | collective-permute-start | bytes 393224 | tf_op jit(solution)/shard_map/ppermute | solution.py:318
  13.3 4.1 %collective-permute-done.1.refs_2_ = bf16[128,512]{1,0:T(8,128)(2,1)S(1)} collective-permute-done((bf16[128,512]{1,0:T(8,128)(2,1)S(1)}, bf16[128,512]{1,0:T(8,128)(2,1)S(1)}, u32[]{:S(2)}, u32[]{:S(2)}) %collective-permute-start.1) | collective-permute-done | bytes 131104 | tf_op jit(solution)/shard_map/ppermute | solution.py:318
  17.5 0.5 collective-permute-start.9
  18.0 0.0 collective-permute-done.2.refs_3_
  18.0 0.6 shard_map.68
  18.6 0.1 collective-permute-start.3
  18.6 0.0 collective-permute-done.6.refs_0_
  18.7 0.0 collective-permute-done.7.refs_1_
  18.7 0.0 collective-permute-done.8.refs_2_
  18.7 0.3 collective-permute-done.9.refs_3_
  19.0 0.6 shard_map.71
  19.6 0.2 collective-permute-start.10
  19.7 3.3 %collective-permute-start.5 = (bf16[512,256]{1,0:T(8,128)(2,1)S(1)}, bf16[512,256]{1,0:T(8,128)(2,1)S(1)}, u32[]{:S(2)}, u32[]{:S(2)}) collective-permute-start(bf16[512,256]{1,0:T(8,128)(2,1)S(1)} %get-tuple-element.50), channel_id=1, source_target_pairs={{0,12},{1,13},{2,14},{3,15},{4,8},{5,9},{6,10},{7,11},{8,20},{9,21... | collective-permute-start | bytes 786440 | tf_op jit(solution)/shard_map/ppermute | solution.py:318
  23.1 1.9 %collective-permute-start.4 = (bf16[512,256]{1,0:T(8,128)(2,1)S(1)}, bf16[512,256]{1,0:T(8,128)(2,1)S(1)}, u32[]{:S(2)}, u32[]{:S(2)}) collective-permute-start(bf16[512,256]{1,0:T(8,128)(2,1)S(1)} %get-tuple-element.49.mine_ref), channel_id=1, source_target_pairs={{0,8},{1,9},{2,10},{3,11},{4,12},{5,13},{6,14},{7,15},{8,16},{9,17... | collective-permute-start | bytes 786440 | tf_op jit(solution)/shard_map/ppermute | solution.py:318
  25.0 2.2 %collective-permute-start.12 = (bf16[256,512]{1,0:T(8,128)(2,1)S(1)}, bf16[256,512]{1,0:T(8,128)(2,1)S(1)}, u32[]{:S(2)}, u32[]{:S(2)}) collective-permute-start(bf16[256,512]{1,0:T(8,128)(2,1)S(1)} %get-tuple-element.64), channel_id=1, source_target_pairs={{0,1},{1,2},{2,3},{3,0},{4,5},{5,6},{6,7},{7,4},{8,9},{9,10},{10,1... | collective-permute-start | bytes 786440 | tf_op jit(solution)/shard_map/ppermute | solution.py:318
  27.2 0.0 collective-permute-done.3.sibling_ref
  27.2 1.5 %collective-permute-start.13 = (bf16[256,512]{1,0:T(8,128)(2,1)S(1)}, bf16[256,512]{1,0:T(8,128)(2,1)S(1)}, u32[]{:S(2)}, u32[]{:S(2)}) collective-permute-start(bf16[256,512]{1,0:T(8,128)(2,1)S(1)} %get-tuple-element.65), channel_id=1, source_target_pairs={{0,3},{1,0},{2,1},{3,2},{4,7},{5,4},{6,5},{7,6},{8,11},{9,8},{10,9... | collective-permute-start | bytes 786440 | tf_op jit(solution)/shard_map/ppermute | solution.py:318
  28.7 0.7 shard_map.69
  29.4 1.6 %collective-permute-done.5.b_ref = bf16[512,256]{1,0:T(8,128)(2,1)S(1)} collective-permute-done((bf16[512,256]{1,0:T(8,128)(2,1)S(1)}, bf16[512,256]{1,0:T(8,128)(2,1)S(1)}, u32[]{:S(2)}, u32[]{:S(2)}) %collective-permute-start.5) | collective-permute-done | bytes 262176 | tf_op jit(solution)/shard_map/ppermute | solution.py:318
  31.0 5.3 %collective-permute-done.4.a_ref = bf16[512,256]{1,0:T(8,128)(2,1)S(1)} collective-permute-done((bf16[512,256]{1,0:T(8,128)(2,1)S(1)}, bf16[512,256]{1,0:T(8,128)(2,1)S(1)}, u32[]{:S(2)}, u32[]{:S(2)}) %collective-permute-start.4) | collective-permute-done | bytes 262176 | tf_op jit(solution)/shard_map/ppermute | solution.py:318
  36.4 0.0 collective-permute-done.10.refs_1_
  36.4 6.0 %shard_map.72 = (bf16[1024,256]{1,0:T(8,128)(2,1)S(1)}, bf16[128,1024]{1,0:T(8,128)(2,1)S(1)}, f32[1024,256]{1,0:T(8,128)S(1)}, f32[1024,256]{1,0:T(8,128)S(1)},...) custom-call(s32[3]{0:T(128)S(1)} %pad_add_fusion.place_ref, bf16[1024,256]{1,0:T(8,128)(2,1)S(1)} %get-tuple-element.51.own_ref, ...), custom_call_target="tpu_custom_call" | custom-call | flops 1 | bytes 4997132 | tf_op jit(solution)/shard_map/pallas_call | solution.py:26
  42.4 2.9 %collective-permute-start.11 = (bf16[256,256]{1,0:T(8,128)(2,1)S(1)}, bf16[256,256]{1,0:T(8,128)(2,1)S(1)}, u32[]{:S(2)}, u32[]{:S(2)}) collective-permute-start(bf16[256,256]{1,0:T(8,128)(2,1)S(1)} %get-tuple-element.61), channel_id=1, source_target_pairs={{0,2},{1,3},{2,0},{3,1},{4,6},{5,7},{6,4},{7,5},{8,10},{9,11},{10,... | collective-permute-start | bytes 393224 | tf_op jit(solution)/shard_map/ppermute | solution.py:318
  45.2 0.0 collective-permute-done.12.refs_0_
  45.2 0.8 collective-permute-done.13.refs_1_
  46.0 3.8 %shard_map.73 = (f32[512,256]{1,0:T(8,128)S(1)}, f32[512,256]{1,0:T(8,128)S(1)}, bf16[528,256]{1,0:T(8,128)(2,1)S(1)}, bf16[2,128,256]{2,1,0:T(8,128)(2,1)S(1)}) custom-call(s32[3]{0:T(128)S(1)} %pad_add_fusion.place_ref, bf16[1024,256]{1,0:T(8,128)(2,1)S(1)} %get-tuple-element.51.own_ref, bf16[128,1024]{1,0:T(8,128)(2,1)S(1)} %get-tuple-element.52.own_kt_ref, ...), custom_call_target="tpu_custom_call" | custom-call | flops 1 | bytes 5644300 | tf_op jit(solution)/shard_map/pallas_call | solution.py:26
  49.8 5.9 %collective-permute-start.17 = (bf16[528,256]{1,0:T(8,128)(2,1)S(1)}, bf16[528,256]{1,0:T(8,128)(2,1)S(1)}, u32[]{:S(2)}, u32[]{:S(2)}) collective-permute-start(bf16[528,256]{1,0:T(8,128)(2,1)S(1)} %get-tuple-element.77), channel_id=1, source_target_pairs={{8,0},{9,1},{10,2},{11,3},{12,4},{13,5},{14,6},{15,7},{16,8},{17,9... | collective-permute-start | bytes 811016 | tf_op jit(solution)/shard_map/ppermute | solution.py:318
  55.7 0.0 collective-permute-done.11.refs_1_
  55.8 3.6 %shard_map.74 = (f32[512,256]{1,0:T(8,128)S(1)}, f32[512,256]{1,0:T(8,128)S(1)}, bf16[512,256]{1,0:T(8,128)(2,1)S(1)}, bf16[256,256]{1,0:T(8,128)(2,1)S(1)}, bf16[256,256]{1,0:T(8,128)(2,1)S(1)}) custom-call(s32[3]{0:T(128)S(1)} %pad_add_fusion.place_ref, bf16[1024,256]{1,0:T(8,128)(2,1)S(1)} %get-tuple-element.51.own_ref, ...), custom_call_target="tpu_custom_call" | custom-call | flops 1 | bytes 5906444 | tf_op jit(solution)/shard_map/pallas_call | solution.py:26
  59.4 2.1 %collective-permute-start.18 = (bf16[512,256]{1,0:T(8,128)(2,1)S(1)}, bf16[512,256]{1,0:T(8,128)(2,1)S(1)}, u32[]{:S(2)}, u32[]{:S(2)}) collective-permute-start(bf16[512,256]{1,0:T(8,128)(2,1)S(1)} %get-tuple-element.78), channel_id=1, source_target_pairs={{8,0},{9,1},{10,2},{11,3},{12,4},{13,5},{14,6},{15,7},{16,8},{17,9... | collective-permute-start | bytes 786440 | tf_op jit(solution)/shard_map/ppermute | solution.py:318
  61.5 0.1 collective-permute-start.14
  61.6 1.5 %collective-permute-start.15 = (bf16[256,256]{1,0:T(8,128)(2,1)S(1)}, bf16[256,256]{1,0:T(8,128)(2,1)S(1)}, u32[]{:S(2)}, u32[]{:S(2)}) collective-permute-start(bf16[256,256]{1,0:T(8,128)(2,1)S(1)} %get-tuple-element.72), channel_id=1, source_target_pairs={{0,1},{1,2},{2,3},{3,0},{4,5},{5,6},{6,7},{7,4},{8,9},{9,10},{10,1... | collective-permute-start | bytes 393224 | tf_op jit(solution)/shard_map/ppermute | solution.py:318
  63.1 0.0 collective-permute-done.17.back_a_ref
  63.1 5.1 %collective-permute-done.18.back_b_ref = bf16[512,256]{1,0:T(8,128)(2,1)S(1)} collective-permute-done((bf16[512,256]{1,0:T(8,128)(2,1)S(1)}, bf16[512,256]{1,0:T(8,128)(2,1)S(1)}, u32[]{:S(2)}, u32[]{:S(2)}) %collective-permute-start.18) | collective-permute-done | bytes 262176 | tf_op jit(solution)/shard_map/ppermute | solution.py:318
  68.2 0.7 shard_map.77
  68.8 0.1 collective-permute-start.19
  68.9 0.1 collective-permute-start.20
  69.0 1.5 %collective-permute-start.21 = (bf16[256,256]{1,0:T(8,128)(2,1)S(1)}, bf16[256,256]{1,0:T(8,128)(2,1)S(1)}, u32[]{:S(2)}, u32[]{:S(2)}) collective-permute-start(bf16[256,256]{1,0:T(8,128)(2,1)S(1)} %get-tuple-element.82), channel_id=1, source_target_pairs={{0,3},{1,0},{2,1},{3,2},{4,7},{5,4},{6,5},{7,6},{8,11},{9,8},{10,9... | collective-permute-start | bytes 393224 | tf_op jit(solution)/shard_map/ppermute | solution.py:318
  70.4 0.0 collective-permute-done.14.refs_2_
  70.4 0.0 collective-permute-done.15.refs_3_
  70.4 0.6 shard_map.75
  71.0 2.4 %collective-permute-start.16 = (bf16[512,256]{1,0:T(8,128)(2,1)S(1)}, bf16[512,256]{1,0:T(8,128)(2,1)S(1)}, u32[]{:S(2)}, u32[]{:S(2)}) collective-permute-start(bf16[512,256]{1,0:T(8,128)(2,1)S(1)} %get-tuple-element.74), channel_id=1, source_target_pairs={{0,4},{1,5},{2,6},{3,7},{4,0},{5,1},{6,2},{7,3},{8,12},{9,13},{10,... | collective-permute-start | bytes 786440 | tf_op jit(solution)/shard_map/ppermute | solution.py:318
  73.5 0.2 collective-permute-done.19.refs_1_
  73.7 6.3 %collective-permute-done.20.refs_2_ = bf16[256,256]{1,0:T(8,128)(2,1)S(1)} collective-permute-done((bf16[256,256]{1,0:T(8,128)(2,1)S(1)}, bf16[256,256]{1,0:T(8,128)(2,1)S(1)}, u32[]{:S(2)}, u32[]{:S(2)}) %collective-permute-start.20) | collective-permute-done | bytes 131104 | tf_op jit(solution)/shard_map/ppermute | solution.py:318
  80.0 1.0 %collective-permute-done.21.refs_3_ = bf16[256,256]{1,0:T(8,128)(2,1)S(1)} collective-permute-done((bf16[256,256]{1,0:T(8,128)(2,1)S(1)}, bf16[256,256]{1,0:T(8,128)(2,1)S(1)}, u32[]{:S(2)}, u32[]{:S(2)}) %collective-permute-start.21) | collective-permute-done | bytes 131104 | tf_op jit(solution)/shard_map/ppermute | solution.py:318
  81.0 0.6 shard_map.78
  81.6 1.7 %collective-permute-start.22 = (bf16[512,256]{1,0:T(8,128)(2,1)S(1)}, bf16[512,256]{1,0:T(8,128)(2,1)S(1)}, u32[]{:S(2)}, u32[]{:S(2)}) collective-permute-start(bf16[512,256]{1,0:T(8,128)(2,1)S(1)} %get-tuple-element.84), channel_id=1, source_target_pairs={{0,4},{1,5},{2,6},{3,7},{4,0},{5,1},{6,2},{7,3},{8,12},{9,13},{10,... | collective-permute-start | bytes 786440 | tf_op jit(solution)/shard_map/ppermute | solution.py:318
  83.3 0.0 collective-permute-done.16.sibling_ref
  83.4 1.4 %shard_map.76 = bf16[128,2048]{1,0:T(8,128)(2,1)} custom-call(s32[3]{0:T(128)S(1)} %pad_add_fusion.place_ref, bf16[512,256]{1,0:T(8,128)(2,1)S(1)} %get-tuple-element.73.mine_ref, bf16[512,256]{1,0:T(8,128)(2,1)S(1)} %collective-permute-done.16.sibling_ref), custom_call_target="tpu_custom_call" | custom-call | bytes 1048588 | tf_op jit(solution)/shard_map/pallas_call | solution.py:26
  84.8 0.0 collective-permute-done.22.sibling_ref
  84.8 1.5 %shard_map.79 = (bf16[128,1024]{1,0:T(8,128)(2,1)}, bf16[128,1024]{1,0:T(8,128)(2,1)}) custom-call(s32[3]{0:T(128)S(1)} %pad_add_fusion.place_ref, bf16[512,256]{1,0:T(8,128)(2,1)S(1)} %get-tuple-element.83.mine_ref, bf16[512,256]{1,0:T(8,128)(2,1)S(1)} %collective-permute-done.22.sibling_ref), custom_call_target="tpu_custom_call" | custom-call | bytes 1048588 | tf_op jit(solution)/shard_map/pallas_call | solution.py:26
  (6 shorter events, 0.0 us)
Async XLA Ops:
  0.6 6.8 %copy-start = (bf16[128,2048]{1,0:T(8,128)(2,1)S(1)}, bf16[128,2048]{1,0:T(8,128)(2,1)}, u32[]{:S(2)}) copy-start(bf16[128,2048]{1,0:T(8,128)(2,1)} %q_ref.1) | copy-start | bytes 1572868
  0.7 1.0 %copy-start.2 = (bf16[128,1024]{1,0:T(8,128)(2,1)S(1)}, bf16[128,1024]{1,0:T(8,128)(2,1)}, u32[]{:S(2)}) copy-start(bf16[128,1024]{1,0:T(8,128)(2,1)} %k_ref.1) | copy-start | bytes 786436
  1.7 0.9 %copy-start.3 = (bf16[128,1024]{1,0:T(8,128)(2,1)S(1)}, bf16[128,1024]{1,0:T(8,128)(2,1)}, u32[]{:S(2)}) copy-start(bf16[128,1024]{1,0:T(8,128)(2,1)} %v_ref.1) | copy-start | bytes 786436
  3.6 8.8 %collective-permute-start = (bf16[128,512]{1,0:T(8,128)(2,1)S(1)}, bf16[128,512]{1,0:T(8,128)(2,1)S(1)}, u32[]{:S(2)}, u32[]{:S(2)}) collective-permute-start(bf16[128,512]{1,0:T(8,128)(2,1)S(1)} %get-tuple-element.46), channel_id=1, source_target_pairs={{0,2},{1,3},{2,0},{3,1},{4,6},{5,7},{6,4},{7,5},{8,10},{9,11},{10,... | collective-permute-start | bytes 393224 | tf_op jit(solution)/shard_map/ppermute | solution.py:318
  5.9 11.5 %collective-permute-start.1 = (bf16[128,512]{1,0:T(8,128)(2,1)S(1)}, bf16[128,512]{1,0:T(8,128)(2,1)S(1)}, u32[]{:S(2)}, u32[]{:S(2)}) collective-permute-start(bf16[128,512]{1,0:T(8,128)(2,1)S(1)} %get-tuple-element.47), channel_id=1, source_target_pairs={{0,1},{1,2},{2,3},{3,0},{4,5},{5,6},{6,7},{7,4},{8,9},{9,10},{10,1... | collective-permute-start | bytes 393224 | tf_op jit(solution)/shard_map/ppermute | solution.py:318
  5.9 12.0 %collective-permute-start.2 = (bf16[128,512]{1,0:T(8,128)(2,1)S(1)}, bf16[128,512]{1,0:T(8,128)(2,1)S(1)}, u32[]{:S(2)}, u32[]{:S(2)}) collective-permute-start(bf16[128,512]{1,0:T(8,128)(2,1)S(1)} %get-tuple-element.48), channel_id=1, source_target_pairs={{0,3},{1,0},{2,1},{3,2},{4,7},{5,4},{6,5},{7,6},{8,11},{9,8},{10,9... | collective-permute-start | bytes 393224 | tf_op jit(solution)/shard_map/ppermute | solution.py:318
  7.4 1.0 %copy-start.1 = (bf16[128,2048]{1,0:T(8,128)(2,1)S(1)}, bf16[128,2048]{1,0:T(8,128)(2,1)}, u32[]{:S(2)}) copy-start(bf16[128,2048]{1,0:T(8,128)(2,1)} %g_ref.1) | copy-start | bytes 1572868
  9.4 9.3 %collective-permute-start.6 = (bf16[128,512]{1,0:T(8,128)(2,1)S(1)}, bf16[128,512]{1,0:T(8,128)(2,1)S(1)}, u32[]{:S(2)}, u32[]{:S(2)}) collective-permute-start(bf16[128,512]{1,0:T(8,128)(2,1)S(1)} %get-tuple-element.54), channel_id=1, source_target_pairs={{0,4},{1,5},{2,6},{3,7},{4,0},{5,1},{6,2},{7,3},{8,12},{9,13},{10,... | collective-permute-start | bytes 393224 | tf_op jit(solution)/shard_map/ppermute | solution.py:318
  10.9 7.7 %collective-permute-start.7 = (bf16[128,512]{1,0:T(8,128)(2,1)S(1)}, bf16[128,512]{1,0:T(8,128)(2,1)S(1)}, u32[]{:S(2)}, u32[]{:S(2)}) collective-permute-start(bf16[128,512]{1,0:T(8,128)(2,1)S(1)} %get-tuple-element.55), channel_id=1, source_target_pairs={{0,4},{1,5},{2,6},{3,7},{4,0},{5,1},{6,2},{7,3},{8,12},{9,13},{10,... | collective-permute-start | bytes 393224 | tf_op jit(solution)/shard_map/ppermute | solution.py:318
  12.4 6.3 %collective-permute-start.8 = (bf16[128,512]{1,0:T(8,128)(2,1)S(1)}, bf16[128,512]{1,0:T(8,128)(2,1)S(1)}, u32[]{:S(2)}, u32[]{:S(2)}) collective-permute-start(bf16[128,512]{1,0:T(8,128)(2,1)S(1)} %get-tuple-element.56), channel_id=1, source_target_pairs={{0,4},{1,5},{2,6},{3,7},{4,0},{5,1},{6,2},{7,3},{8,12},{9,13},{10,... | collective-permute-start | bytes 393224 | tf_op jit(solution)/shard_map/ppermute | solution.py:318
  17.5 1.5 %collective-permute-start.9 = (bf16[128,512]{1,0:T(8,128)(2,1)S(1)}, bf16[128,512]{1,0:T(8,128)(2,1)S(1)}, u32[]{:S(2)}, u32[]{:S(2)}) collective-permute-start(bf16[128,512]{1,0:T(8,128)(2,1)S(1)} %get-tuple-element.57), channel_id=1, source_target_pairs={{0,4},{1,5},{2,6},{3,7},{4,0},{5,1},{6,2},{7,3},{8,12},{9,13},{10,... | collective-permute-start | bytes 393224 | tf_op jit(solution)/shard_map/ppermute | solution.py:318
  18.6 8.7 %collective-permute-start.3 = (bf16[512,256]{1,0:T(8,128)(2,1)S(1)}, bf16[512,256]{1,0:T(8,128)(2,1)S(1)}, u32[]{:S(2)}, u32[]{:S(2)}) collective-permute-start(bf16[512,256]{1,0:T(8,128)(2,1)S(1)} %get-tuple-element.50), channel_id=1, source_target_pairs={{0,4},{1,5},{2,6},{3,7},{4,0},{5,1},{6,2},{7,3},{8,12},{9,13},{10,... | collective-permute-start | bytes 786440 | tf_op jit(solution)/shard_map/ppermute | solution.py:318
  19.6 16.8 %collective-permute-start.10 = (bf16[272,512]{1,0:T(8,128)(2,1)S(1)}, bf16[272,512]{1,0:T(8,128)(2,1)S(1)}, u32[]{:S(2)}, u32[]{:S(2)}) collective-permute-start(bf16[272,512]{1,0:T(8,128)(2,1)S(1)} %get-tuple-element.59), channel_id=1, source_target_pairs={{0,2},{1,3},{2,0},{3,1},{4,6},{5,7},{6,4},{7,5},{8,10},{9,11},{10,... | collective-permute-start | bytes 835592 | tf_op jit(solution)/shard_map/ppermute | solution.py:318
  19.7 11.3 %collective-permute-start.5 = (bf16[512,256]{1,0:T(8,128)(2,1)S(1)}, bf16[512,256]{1,0:T(8,128)(2,1)S(1)}, u32[]{:S(2)}, u32[]{:S(2)}) collective-permute-start(bf16[512,256]{1,0:T(8,128)(2,1)S(1)} %get-tuple-element.50), channel_id=1, source_target_pairs={{0,12},{1,13},{2,14},{3,15},{4,8},{5,9},{6,10},{7,11},{8,20},{9,21... | collective-permute-start | bytes 786440 | tf_op jit(solution)/shard_map/ppermute | solution.py:318
  23.1 13.3 %collective-permute-start.4 = (bf16[512,256]{1,0:T(8,128)(2,1)S(1)}, bf16[512,256]{1,0:T(8,128)(2,1)S(1)}, u32[]{:S(2)}, u32[]{:S(2)}) collective-permute-start(bf16[512,256]{1,0:T(8,128)(2,1)S(1)} %get-tuple-element.49.mine_ref), channel_id=1, source_target_pairs={{0,8},{1,9},{2,10},{3,11},{4,12},{5,13},{6,14},{7,15},{8,16},{9,17... | collective-permute-start | bytes 786440 | tf_op jit(solution)/shard_map/ppermute | solution.py:318
  25.0 20.3 %collective-permute-start.12 = (bf16[256,512]{1,0:T(8,128)(2,1)S(1)}, bf16[256,512]{1,0:T(8,128)(2,1)S(1)}, u32[]{:S(2)}, u32[]{:S(2)}) collective-permute-start(bf16[256,512]{1,0:T(8,128)(2,1)S(1)} %get-tuple-element.64), channel_id=1, source_target_pairs={{0,1},{1,2},{2,3},{3,0},{4,5},{5,6},{6,7},{7,4},{8,9},{9,10},{10,1... | collective-permute-start | bytes 786440 | tf_op jit(solution)/shard_map/ppermute | solution.py:318
  27.2 18.8 %collective-permute-start.13 = (bf16[256,512]{1,0:T(8,128)(2,1)S(1)}, bf16[256,512]{1,0:T(8,128)(2,1)S(1)}, u32[]{:S(2)}, u32[]{:S(2)}) collective-permute-start(bf16[256,512]{1,0:T(8,128)(2,1)S(1)} %get-tuple-element.65), channel_id=1, source_target_pairs={{0,3},{1,0},{2,1},{3,2},{4,7},{5,4},{6,5},{7,6},{8,11},{9,8},{10,9... | collective-permute-start | bytes 786440 | tf_op jit(solution)/shard_map/ppermute | solution.py:318
  42.4 13.4 %collective-permute-start.11 = (bf16[256,256]{1,0:T(8,128)(2,1)S(1)}, bf16[256,256]{1,0:T(8,128)(2,1)S(1)}, u32[]{:S(2)}, u32[]{:S(2)}) collective-permute-start(bf16[256,256]{1,0:T(8,128)(2,1)S(1)} %get-tuple-element.61), channel_id=1, source_target_pairs={{0,2},{1,3},{2,0},{3,1},{4,6},{5,7},{6,4},{7,5},{8,10},{9,11},{10,... | collective-permute-start | bytes 393224 | tf_op jit(solution)/shard_map/ppermute | solution.py:318
  49.8 13.2 %collective-permute-start.17 = (bf16[528,256]{1,0:T(8,128)(2,1)S(1)}, bf16[528,256]{1,0:T(8,128)(2,1)S(1)}, u32[]{:S(2)}, u32[]{:S(2)}) collective-permute-start(bf16[528,256]{1,0:T(8,128)(2,1)S(1)} %get-tuple-element.77), channel_id=1, source_target_pairs={{8,0},{9,1},{10,2},{11,3},{12,4},{13,5},{14,6},{15,7},{16,8},{17,9... | collective-permute-start | bytes 811016 | tf_op jit(solution)/shard_map/ppermute | solution.py:318
  59.4 8.8 %collective-permute-start.18 = (bf16[512,256]{1,0:T(8,128)(2,1)S(1)}, bf16[512,256]{1,0:T(8,128)(2,1)S(1)}, u32[]{:S(2)}, u32[]{:S(2)}) collective-permute-start(bf16[512,256]{1,0:T(8,128)(2,1)S(1)} %get-tuple-element.78), channel_id=1, source_target_pairs={{8,0},{9,1},{10,2},{11,3},{12,4},{13,5},{14,6},{15,7},{16,8},{17,9... | collective-permute-start | bytes 786440 | tf_op jit(solution)/shard_map/ppermute | solution.py:318
  61.5 8.9 %collective-permute-start.14 = (bf16[256,256]{1,0:T(8,128)(2,1)S(1)}, bf16[256,256]{1,0:T(8,128)(2,1)S(1)}, u32[]{:S(2)}, u32[]{:S(2)}) collective-permute-start(bf16[256,256]{1,0:T(8,128)(2,1)S(1)} %get-tuple-element.71), channel_id=1, source_target_pairs={{0,3},{1,0},{2,1},{3,2},{4,7},{5,4},{6,5},{7,6},{8,11},{9,8},{10,9... | collective-permute-start | bytes 393224 | tf_op jit(solution)/shard_map/ppermute | solution.py:318
  61.6 8.8 %collective-permute-start.15 = (bf16[256,256]{1,0:T(8,128)(2,1)S(1)}, bf16[256,256]{1,0:T(8,128)(2,1)S(1)}, u32[]{:S(2)}, u32[]{:S(2)}) collective-permute-start(bf16[256,256]{1,0:T(8,128)(2,1)S(1)} %get-tuple-element.72), channel_id=1, source_target_pairs={{0,1},{1,2},{2,3},{3,0},{4,5},{5,6},{6,7},{7,4},{8,9},{9,10},{10,1... | collective-permute-start | bytes 393224 | tf_op jit(solution)/shard_map/ppermute | solution.py:318
  68.8 4.9 %collective-permute-start.19 = (bf16[256,256]{1,0:T(8,128)(2,1)S(1)}, bf16[256,256]{1,0:T(8,128)(2,1)S(1)}, u32[]{:S(2)}, u32[]{:S(2)}) collective-permute-start(bf16[256,256]{1,0:T(8,128)(2,1)S(1)} %get-tuple-element.80), channel_id=1, source_target_pairs={{0,2},{1,3},{2,0},{3,1},{4,6},{5,7},{6,4},{7,5},{8,10},{9,11},{10,... | collective-permute-start | bytes 393224 | tf_op jit(solution)/shard_map/ppermute | solution.py:318
  68.9 11.1 %collective-permute-start.20 = (bf16[256,256]{1,0:T(8,128)(2,1)S(1)}, bf16[256,256]{1,0:T(8,128)(2,1)S(1)}, u32[]{:S(2)}, u32[]{:S(2)}) collective-permute-start(bf16[256,256]{1,0:T(8,128)(2,1)S(1)} %get-tuple-element.81), channel_id=1, source_target_pairs={{0,1},{1,2},{2,3},{3,0},{4,5},{5,6},{6,7},{7,4},{8,9},{9,10},{10,1... | collective-permute-start | bytes 393224 | tf_op jit(solution)/shard_map/ppermute | solution.py:318
  69.0 12.0 %collective-permute-start.21 = (bf16[256,256]{1,0:T(8,128)(2,1)S(1)}, bf16[256,256]{1,0:T(8,128)(2,1)S(1)}, u32[]{:S(2)}, u32[]{:S(2)}) collective-permute-start(bf16[256,256]{1,0:T(8,128)(2,1)S(1)} %get-tuple-element.82), channel_id=1, source_target_pairs={{0,3},{1,0},{2,1},{3,2},{4,7},{5,4},{6,5},{7,6},{8,11},{9,8},{10,9... | collective-permute-start | bytes 393224 | tf_op jit(solution)/shard_map/ppermute | solution.py:318
  71.0 12.3 %collective-permute-start.16 = (bf16[512,256]{1,0:T(8,128)(2,1)S(1)}, bf16[512,256]{1,0:T(8,128)(2,1)S(1)}, u32[]{:S(2)}, u32[]{:S(2)}) collective-permute-start(bf16[512,256]{1,0:T(8,128)(2,1)S(1)} %get-tuple-element.74), channel_id=1, source_target_pairs={{0,4},{1,5},{2,6},{3,7},{4,0},{5,1},{6,2},{7,3},{8,12},{9,13},{10,... | collective-permute-start | bytes 786440 | tf_op jit(solution)/shard_map/ppermute | solution.py:318
  81.6 3.1 %collective-permute-start.22 = (bf16[512,256]{1,0:T(8,128)(2,1)S(1)}, bf16[512,256]{1,0:T(8,128)(2,1)S(1)}, u32[]{:S(2)}, u32[]{:S(2)}) collective-permute-start(bf16[512,256]{1,0:T(8,128)(2,1)S(1)} %get-tuple-element.84), channel_id=1, source_target_pairs={{0,4},{1,5},{2,6},{3,7},{4,0},{5,1},{6,2},{7,3},{8,12},{9,13},{10,... | collective-permute-start | bytes 786440 | tf_op jit(solution)/shard_map/ppermute | solution.py:318

commit v13 on v12

--- a/solution.py
+++ b/solution.py
@@ -350,7 +350,7 @@
     far = across(other, chip_step=1, flip=1)
     blocks = call(
         bind(merge_rows_kernel),
-        tuple(shape_of(low, 2 * rows + 16 * (n == 1), 4 * d) for n in range(heads)),
+        tuple(shape_of(low, 2 * rows + 16 * (n > 0), 4 * d) for n in range(heads)),
         (place, qd_mine, *qd_other, mine[:8]),
     )
     blocks = spread(blocks)

time: 86.5 us -> 89.5 us (1.035)
  waiting for transfers between devices: 26.2 us -> 33 us
  starting transfers between devices: 34.3 us -> 31.7 us
  local copies, waits for them, and re-layouts: 3 us -> 1.91 us
    ppermute x23, waiting for transfers between devices: 26.2 us -> 33 us  [moved(): return lax.ppermute(value, ('chip', 'core', 'head'), pairs)]
    ppermute x23, starting transfers between devices: 34.3 us -> 31.7 us  [moved(): return lax.ppermute(value, ('chip', 'core', 'head'), pairs)]
    unnamed x8, local copies, waits for them, and re-layouts: 2.99 us -> 1.91 us
  transfers between devices with their start and end apart: 23 -> 23, of which waited for: 10 -> 13; matrix products, arithmetic and copies ran while one was open for 0% -> 0% of each run, Pallas kernels for 22% -> 21%
where the time goes in v13:
time: 89.5 us; the launch traced here: 89.3 us
  waiting for transfers between devices  33 us (37%)
  starting transfers between devices  31.7 us (35%)
  Pallas kernels  21.8 us (24%)
  local copies, waits for them, and re-layouts  1.91 us (2%)
    ppermute x23, waiting for transfers between devices, moved(): return lax.ppermute(value, ('chip', 'core', 'head'), pairs)  33 us
    ppermute x23, starting transfers between devices, moved(): return lax.ppermute(value, ('chip', 'core', 'head'), pairs)  31.7 us
    pallas_call x13, Pallas kernels, call(): pl.pallas_call(kernel, out_shape=out_shape, in_specs=[SMEM_SPEC] + [spec]...  21.8 us
    unnamed x8, local copies, waits for them, and re-layouts  1.91 us
  transfers between devices with their start and end apart: 23, of which 13 were waited for; matrix products, arithmetic and copies ran while one was open for 0% of the time, Pallas kernels for 21%

profile of v13, /device:TPU:13, one launch (start us, length us, event | category | flops | bytes accessed | tf_op | source)
XLA Modules:
  0.0 89.3 jit_solution(15873488829583515806)
XLA Ops:
  0.6 0.1 pad_add_fusion.place_ref
  0.7 0.9 %copy-done.2 = bf16[128,1024]{1,0:T(8,128)(2,1)S(1)} copy-done((bf16[128,1024]{1,0:T(8,128)(2,1)S(1)}, bf16[128,1024]{1,0:T(8,128)(2,1)}, u32[]{:S(2)}) %copy-start.2) | copy-done | bytes 262168
  1.7 0.9 %copy-done.3 = bf16[128,1024]{1,0:T(8,128)(2,1)S(1)} copy-done((bf16[128,1024]{1,0:T(8,128)(2,1)S(1)}, bf16[128,1024]{1,0:T(8,128)(2,1)}, u32[]{:S(2)}) %copy-start.3) | copy-done | bytes 262168
  2.6 0.9 shard_map.67
  3.5 2.4 %collective-permute-start = (bf16[128,512]{1,0:T(8,128)(2,1)S(1)}, bf16[128,512]{1,0:T(8,128)(2,1)S(1)}, u32[]{:S(2)}, u32[]{:S(2)}) collective-permute-start(bf16[128,512]{1,0:T(8,128)(2,1)S(1)} %get-tuple-element.46), channel_id=1, source_target_pairs={{0,2},{1,3},{2,0},{3,1},{4,6},{5,7},{6,4},{7,5},{8,10},{9,11},{10,... | collective-permute-start | bytes 393224 | tf_op jit(solution)/shard_map/ppermute | solution.py:318
  5.9 0.0 collective-permute-start.1
  5.9 1.5 %collective-permute-start.2 = (bf16[128,512]{1,0:T(8,128)(2,1)S(1)}, bf16[128,512]{1,0:T(8,128)(2,1)S(1)}, u32[]{:S(2)}, u32[]{:S(2)}) collective-permute-start(bf16[128,512]{1,0:T(8,128)(2,1)S(1)} %get-tuple-element.48), channel_id=1, source_target_pairs={{0,3},{1,0},{2,1},{3,2},{4,7},{5,4},{6,5},{7,6},{8,11},{9,8},{10,9... | collective-permute-start | bytes 393224 | tf_op jit(solution)/shard_map/ppermute | solution.py:318
  7.4 5.0 %collective-permute-done.refs_1_ = bf16[128,512]{1,0:T(8,128)(2,1)S(1)} collective-permute-done((bf16[128,512]{1,0:T(8,128)(2,1)S(1)}, bf16[128,512]{1,0:T(8,128)(2,1)S(1)}, u32[]{:S(2)}, u32[]{:S(2)}) %collective-permute-start) | collective-permute-done | bytes 131104 | tf_op jit(solution)/shard_map/ppermute | solution.py:318
  12.3 5.1 %collective-permute-done.1.refs_2_ = bf16[128,512]{1,0:T(8,128)(2,1)S(1)} collective-permute-done((bf16[128,512]{1,0:T(8,128)(2,1)S(1)}, bf16[128,512]{1,0:T(8,128)(2,1)S(1)}, u32[]{:S(2)}, u32[]{:S(2)}) %collective-permute-start.1) | collective-permute-done | bytes 131104 | tf_op jit(solution)/shard_map/ppermute | solution.py:318
  17.4 0.0 collective-permute-done.2.refs_3_
  17.4 0.6 shard_map.68
  18.0 0.6 collective-permute-start.3
  18.6 0.0 copy-done
  18.6 0.0 copy-done.1
  18.6 0.9 %shard_map.70 = (bf16[4,128,512]{2,1,0:T(8,128)(2,1)S(1)}, bf16[128,512]{1,0:T(8,128)(2,1)S(1)}, bf16[128,512]{1,0:T(8,128)(2,1)S(1)}, bf16[128,512]{1,0:T(8,128)(2,1)S(1)}, bf16[128,512]{1,0:T(8,128)(2,1)S(1)}) custom-call(s32[3]{0:T(128)S(1)} %pad_add_fusion.place_ref, bf16[128,2048]{1,0:T(8,128)(2,1)S(1)} %copy-done, bf16[128,2048]{1,0:T(8,128)(2,1)S(1)} %copy-done.1), custom_call_target="tpu_custom_call" | custom-call | bytes 2097164 | tf_op jit(solution)/shard_map/pallas_call | solution.py:26
  19.5 0.1 collective-permute-start.6
  19.6 0.5 collective-permute-start.7
  20.1 0.1 collective-permute-start.8
  20.1 0.4 collective-permute-start.9
  20.6 0.3 collective-permute-done.6.refs_0_
  20.9 0.2 collective-permute-done.7.refs_1_
  21.1 0.3 collective-permute-done.8.refs_2_
  21.4 0.2 collective-permute-done.9.refs_3_
  21.6 0.6 shard_map.71
  22.2 0.5 collective-permute-start.10
  22.7 3.6 %collective-permute-start.5 = (bf16[512,256]{1,0:T(8,128)(2,1)S(1)}, bf16[512,256]{1,0:T(8,128)(2,1)S(1)}, u32[]{:S(2)}, u32[]{:S(2)}) collective-permute-start(bf16[512,256]{1,0:T(8,128)(2,1)S(1)} %get-tuple-element.50), channel_id=1, source_target_pairs={{0,12},{1,13},{2,14},{3,15},{4,8},{5,9},{6,10},{7,11},{8,20},{9,21... | collective-permute-start | bytes 786440 | tf_op jit(solution)/shard_map/ppermute | solution.py:318
  26.3 1.9 %collective-permute-start.4 = (bf16[512,256]{1,0:T(8,128)(2,1)S(1)}, bf16[512,256]{1,0:T(8,128)(2,1)S(1)}, u32[]{:S(2)}, u32[]{:S(2)}) collective-permute-start(bf16[512,256]{1,0:T(8,128)(2,1)S(1)} %get-tuple-element.49.mine_ref), channel_id=1, source_target_pairs={{0,8},{1,9},{2,10},{3,11},{4,12},{5,13},{6,14},{7,15},{8,16},{9,17... | collective-permute-start | bytes 786440 | tf_op jit(solution)/shard_map/ppermute | solution.py:318
  28.2 1.6 %collective-permute-start.12 = (bf16[272,512]{1,0:T(8,128)(2,1)S(1)}, bf16[272,512]{1,0:T(8,128)(2,1)S(1)}, u32[]{:S(2)}, u32[]{:S(2)}) collective-permute-start(bf16[272,512]{1,0:T(8,128)(2,1)S(1)} %get-tuple-element.64), channel_id=1, source_target_pairs={{0,1},{1,2},{2,3},{3,0},{4,5},{5,6},{6,7},{7,4},{8,9},{9,10},{10,1... | collective-permute-start | bytes 835592 | tf_op jit(solution)/shard_map/ppermute | solution.py:318
  29.8 0.0 collective-permute-done.3.sibling_ref
  29.8 1.5 %collective-permute-start.13 = (bf16[272,512]{1,0:T(8,128)(2,1)S(1)}, bf16[272,512]{1,0:T(8,128)(2,1)S(1)}, u32[]{:S(2)}, u32[]{:S(2)}) collective-permute-start(bf16[272,512]{1,0:T(8,128)(2,1)S(1)} %get-tuple-element.65), channel_id=1, source_target_pairs={{0,3},{1,0},{2,1},{3,2},{4,7},{5,4},{6,5},{7,6},{8,11},{9,8},{10,9... | collective-permute-start | bytes 835592 | tf_op jit(solution)/shard_map/ppermute | solution.py:318
  31.3 0.7 shard_map.69
  32.0 2.2 %collective-permute-done.5.b_ref = bf16[512,256]{1,0:T(8,128)(2,1)S(1)} collective-permute-done((bf16[512,256]{1,0:T(8,128)(2,1)S(1)}, bf16[512,256]{1,0:T(8,128)(2,1)S(1)}, u32[]{:S(2)}, u32[]{:S(2)}) %collective-permute-start.5) | collective-permute-done | bytes 262176 | tf_op jit(solution)/shard_map/ppermute | solution.py:318
  34.2 5.6 %collective-permute-done.4.a_ref = bf16[512,256]{1,0:T(8,128)(2,1)S(1)} collective-permute-done((bf16[512,256]{1,0:T(8,128)(2,1)S(1)}, bf16[512,256]{1,0:T(8,128)(2,1)S(1)}, u32[]{:S(2)}, u32[]{:S(2)}) %collective-permute-start.4) | collective-permute-done | bytes 262176 | tf_op jit(solution)/shard_map/ppermute | solution.py:318
  39.8 0.0 collective-permute-done.10.refs_1_
  39.8 6.0 %shard_map.72 = (bf16[1024,256]{1,0:T(8,128)(2,1)S(1)}, bf16[128,1024]{1,0:T(8,128)(2,1)S(1)}, f32[1024,256]{1,0:T(8,128)S(1)}, f32[1024,256]{1,0:T(8,128)S(1)},...) custom-call(s32[3]{0:T(128)S(1)} %pad_add_fusion.place_ref, bf16[1024,256]{1,0:T(8,128)(2,1)S(1)} %get-tuple-element.51.own_ref, ...), custom_call_target="tpu_custom_call" | custom-call | flops 1 | bytes 4997132 | tf_op jit(solution)/shard_map/pallas_call | solution.py:26
  45.8 2.0 %collective-permute-start.11 = (bf16[256,256]{1,0:T(8,128)(2,1)S(1)}, bf16[256,256]{1,0:T(8,128)(2,1)S(1)}, u32[]{:S(2)}, u32[]{:S(2)}) collective-permute-start(bf16[256,256]{1,0:T(8,128)(2,1)S(1)} %get-tuple-element.61), channel_id=1, source_target_pairs={{0,2},{1,3},{2,0},{3,1},{4,6},{5,7},{6,4},{7,5},{8,10},{9,11},{10,... | collective-permute-start | bytes 393224 | tf_op jit(solution)/shard_map/ppermute | solution.py:318
  47.8 0.0 collective-permute-done.12.refs_0_
  47.8 1.6 %collective-permute-done.13.refs_1_ = bf16[272,512]{1,0:T(8,128)(2,1)S(1)} collective-permute-done((bf16[272,512]{1,0:T(8,128)(2,1)S(1)}, bf16[272,512]{1,0:T(8,128)(2,1)S(1)}, u32[]{:S(2)}, u32[]{:S(2)}) %collective-permute-start.13) | collective-permute-done | bytes 278560 | tf_op jit(solution)/shard_map/ppermute | solution.py:318
  49.4 3.8 %shard_map.73 = (f32[512,256]{1,0:T(8,128)S(1)}, f32[512,256]{1,0:T(8,128)S(1)}, bf16[528,256]{1,0:T(8,128)(2,1)S(1)}, bf16[2,128,256]{2,1,0:T(8,128)(2,1)S(1)}) custom-call(s32[3]{0:T(128)S(1)} %pad_add_fusion.place_ref, bf16[1024,256]{1,0:T(8,128)(2,1)S(1)} %get-tuple-element.51.own_ref, bf16[128,1024]{1,0:T(8,128)(2,1)S(1)} %get-tuple-element.52.own_kt_ref, ...), custom_call_target="tpu_custom_call" | custom-call | flops 1 | bytes 5677068 | tf_op jit(solution)/shard_map/pallas_call | solution.py:26
  53.2 5.9 %collective-permute-start.17 = (bf16[528,256]{1,0:T(8,128)(2,1)S(1)}, bf16[528,256]{1,0:T(8,128)(2,1)S(1)}, u32[]{:S(2)}, u32[]{:S(2)}) collective-permute-start(bf16[528,256]{1,0:T(8,128)(2,1)S(1)} %get-tuple-element.77), channel_id=1, source_target_pairs={{8,0},{9,1},{10,2},{11,3},{12,4},{13,5},{14,6},{15,7},{16,8},{17,9... | collective-permute-start | bytes 811016 | tf_op jit(solution)/shard_map/ppermute | solution.py:318
  59.1 0.0 collective-permute-done.11.refs_1_
  59.1 3.6 %shard_map.74 = (f32[512,256]{1,0:T(8,128)S(1)}, f32[512,256]{1,0:T(8,128)S(1)}, bf16[512,256]{1,0:T(8,128)(2,1)S(1)}, bf16[256,256]{1,0:T(8,128)(2,1)S(1)}, bf16[256,256]{1,0:T(8,128)(2,1)S(1)}) custom-call(s32[3]{0:T(128)S(1)} %pad_add_fusion.place_ref, bf16[1024,256]{1,0:T(8,128)(2,1)S(1)} %get-tuple-element.51.own_ref, ...), custom_call_target="tpu_custom_call" | custom-call | flops 1 | bytes 5939212 | tf_op jit(solution)/shard_map/pallas_call | solution.py:26
  62.7 2.2 %collective-permute-start.18 = (bf16[512,256]{1,0:T(8,128)(2,1)S(1)}, bf16[512,256]{1,0:T(8,128)(2,1)S(1)}, u32[]{:S(2)}, u32[]{:S(2)}) collective-permute-start(bf16[512,256]{1,0:T(8,128)(2,1)S(1)} %get-tuple-element.78), channel_id=1, source_target_pairs={{8,0},{9,1},{10,2},{11,3},{12,4},{13,5},{14,6},{15,7},{16,8},{17,9... | collective-permute-start | bytes 786440 | tf_op jit(solution)/shard_map/ppermute | solution.py:318
  64.9 0.1 collective-permute-start.14
  65.0 1.5 %collective-permute-start.15 = (bf16[256,256]{1,0:T(8,128)(2,1)S(1)}, bf16[256,256]{1,0:T(8,128)(2,1)S(1)}, u32[]{:S(2)}, u32[]{:S(2)}) collective-permute-start(bf16[256,256]{1,0:T(8,128)(2,1)S(1)} %get-tuple-element.72), channel_id=1, source_target_pairs={{0,1},{1,2},{2,3},{3,0},{4,5},{5,6},{6,7},{7,4},{8,9},{9,10},{10,1... | collective-permute-start | bytes 393224 | tf_op jit(solution)/shard_map/ppermute | solution.py:318
  66.4 0.0 collective-permute-done.17.back_a_ref
  66.4 5.0 %collective-permute-done.18.back_b_ref = bf16[512,256]{1,0:T(8,128)(2,1)S(1)} collective-permute-done((bf16[512,256]{1,0:T(8,128)(2,1)S(1)}, bf16[512,256]{1,0:T(8,128)(2,1)S(1)}, u32[]{:S(2)}, u32[]{:S(2)}) %collective-permute-start.18) | collective-permute-done | bytes 262176 | tf_op jit(solution)/shard_map/ppermute | solution.py:318
  71.5 0.7 shard_map.77
  72.1 0.1 collective-permute-start.19
  72.2 0.1 collective-permute-start.20
  72.3 1.5 %collective-permute-start.21 = (bf16[256,256]{1,0:T(8,128)(2,1)S(1)}, bf16[256,256]{1,0:T(8,128)(2,1)S(1)}, u32[]{:S(2)}, u32[]{:S(2)}) collective-permute-start(bf16[256,256]{1,0:T(8,128)(2,1)S(1)} %get-tuple-element.82), channel_id=1, source_target_pairs={{0,3},{1,0},{2,1},{3,2},{4,7},{5,4},{6,5},{7,6},{8,11},{9,8},{10,9... | collective-permute-start | bytes 393224 | tf_op jit(solution)/shard_map/ppermute | solution.py:318
  73.7 0.0 collective-permute-done.14.refs_2_
  73.7 0.0 collective-permute-done.15.refs_3_
  73.8 0.6 shard_map.75
  74.3 2.5 %collective-permute-start.16 = (bf16[512,256]{1,0:T(8,128)(2,1)S(1)}, bf16[512,256]{1,0:T(8,128)(2,1)S(1)}, u32[]{:S(2)}, u32[]{:S(2)}) collective-permute-start(bf16[512,256]{1,0:T(8,128)(2,1)S(1)} %get-tuple-element.74), channel_id=1, source_target_pairs={{0,4},{1,5},{2,6},{3,7},{4,0},{5,1},{6,2},{7,3},{8,12},{9,13},{10,... | collective-permute-start | bytes 786440 | tf_op jit(solution)/shard_map/ppermute | solution.py:318
  76.8 2.1 %collective-permute-done.19.refs_1_ = bf16[256,256]{1,0:T(8,128)(2,1)S(1)} collective-permute-done((bf16[256,256]{1,0:T(8,128)(2,1)S(1)}, bf16[256,256]{1,0:T(8,128)(2,1)S(1)}, u32[]{:S(2)}, u32[]{:S(2)}) %collective-permute-start.19) | collective-permute-done | bytes 131104 | tf_op jit(solution)/shard_map/ppermute | solution.py:318
  78.9 4.4 %collective-permute-done.20.refs_2_ = bf16[256,256]{1,0:T(8,128)(2,1)S(1)} collective-permute-done((bf16[256,256]{1,0:T(8,128)(2,1)S(1)}, bf16[256,256]{1,0:T(8,128)(2,1)S(1)}, u32[]{:S(2)}, u32[]{:S(2)}) %collective-permute-start.20) | collective-permute-done | bytes 131104 | tf_op jit(solution)/shard_map/ppermute | solution.py:318
  83.3 1.0 %collective-permute-done.21.refs_3_ = bf16[256,256]{1,0:T(8,128)(2,1)S(1)} collective-permute-done((bf16[256,256]{1,0:T(8,128)(2,1)S(1)}, bf16[256,256]{1,0:T(8,128)(2,1)S(1)}, u32[]{:S(2)}, u32[]{:S(2)}) %collective-permute-start.21) | collective-permute-done | bytes 131104 | tf_op jit(solution)/shard_map/ppermute | solution.py:318
  84.3 0.6 shard_map.78
  84.9 1.5 %collective-permute-start.22 = (bf16[512,256]{1,0:T(8,128)(2,1)S(1)}, bf16[512,256]{1,0:T(8,128)(2,1)S(1)}, u32[]{:S(2)}, u32[]{:S(2)}) collective-permute-start(bf16[512,256]{1,0:T(8,128)(2,1)S(1)} %get-tuple-element.84), channel_id=1, source_target_pairs={{0,4},{1,5},{2,6},{3,7},{4,0},{5,1},{6,2},{7,3},{8,12},{9,13},{10,... | collective-permute-start | bytes 786440 | tf_op jit(solution)/shard_map/ppermute | solution.py:318
  86.4 0.0 collective-permute-done.16.sibling_ref
  86.4 1.4 %shard_map.76 = bf16[128,2048]{1,0:T(8,128)(2,1)} custom-call(s32[3]{0:T(128)S(1)} %pad_add_fusion.place_ref, bf16[512,256]{1,0:T(8,128)(2,1)S(1)} %get-tuple-element.73.mine_ref, bf16[512,256]{1,0:T(8,128)(2,1)S(1)} %collective-permute-done.16.sibling_ref), custom_call_target="tpu_custom_call" | custom-call | bytes 1048588 | tf_op jit(solution)/shard_map/pallas_call | solution.py:26
  87.8 0.0 collective-permute-done.22.sibling_ref
  87.8 1.5 %shard_map.79 = (bf16[128,1024]{1,0:T(8,128)(2,1)}, bf16[128,1024]{1,0:T(8,128)(2,1)}) custom-call(s32[3]{0:T(128)S(1)} %pad_add_fusion.place_ref, bf16[512,256]{1,0:T(8,128)(2,1)S(1)} %get-tuple-element.83.mine_ref, bf16[512,256]{1,0:T(8,128)(2,1)S(1)} %collective-permute-done.22.sibling_ref), custom_call_target="tpu_custom_call" | custom-call | bytes 1048588 | tf_op jit(solution)/shard_map/pallas_call | solution.py:26
  (6 shorter events, 0.0 us)
Async XLA Ops:
  0.7 1.0 %copy-start.2 = (bf16[128,1024]{1,0:T(8,128)(2,1)S(1)}, bf16[128,1024]{1,0:T(8,128)(2,1)}, u32[]{:S(2)}) copy-start(bf16[128,1024]{1,0:T(8,128)(2,1)} %k_ref.1) | copy-start | bytes 786436
  1.7 0.9 %copy-start.3 = (bf16[128,1024]{1,0:T(8,128)(2,1)S(1)}, bf16[128,1024]{1,0:T(8,128)(2,1)}, u32[]{:S(2)}) copy-start(bf16[128,1024]{1,0:T(8,128)(2,1)} %v_ref.1) | copy-start | bytes 786436
  2.6 16.0 %copy-start = (bf16[128,2048]{1,0:T(8,128)(2,1)S(1)}, bf16[128,2048]{1,0:T(8,128)(2,1)}, u32[]{:S(2)}) copy-start(bf16[128,2048]{1,0:T(8,128)(2,1)} %q_ref.1) | copy-start | bytes 1572868
  2.6 16.0 %copy-start.1 = (bf16[128,2048]{1,0:T(8,128)(2,1)S(1)}, bf16[128,2048]{1,0:T(8,128)(2,1)}, u32[]{:S(2)}) copy-start(bf16[128,2048]{1,0:T(8,128)(2,1)} %g_ref.1) | copy-start | bytes 1572868
  3.5 8.8 %collective-permute-start = (bf16[128,512]{1,0:T(8,128)(2,1)S(1)}, bf16[128,512]{1,0:T(8,128)(2,1)S(1)}, u32[]{:S(2)}, u32[]{:S(2)}) collective-permute-start(bf16[128,512]{1,0:T(8,128)(2,1)S(1)} %get-tuple-element.46), channel_id=1, source_target_pairs={{0,2},{1,3},{2,0},{3,1},{4,6},{5,7},{6,4},{7,5},{8,10},{9,11},{10,... | collective-permute-start | bytes 393224 | tf_op jit(solution)/shard_map/ppermute | solution.py:318
  5.9 11.5 %collective-permute-start.1 = (bf16[128,512]{1,0:T(8,128)(2,1)S(1)}, bf16[128,512]{1,0:T(8,128)(2,1)S(1)}, u32[]{:S(2)}, u32[]{:S(2)}) collective-permute-start(bf16[128,512]{1,0:T(8,128)(2,1)S(1)} %get-tuple-element.47), channel_id=1, source_target_pairs={{0,1},{1,2},{2,3},{3,0},{4,5},{5,6},{6,7},{7,4},{8,9},{9,10},{10,1... | collective-permute-start | bytes 393224 | tf_op jit(solution)/shard_map/ppermute | solution.py:318
  5.9 11.5 %collective-permute-start.2 = (bf16[128,512]{1,0:T(8,128)(2,1)S(1)}, bf16[128,512]{1,0:T(8,128)(2,1)S(1)}, u32[]{:S(2)}, u32[]{:S(2)}) collective-permute-start(bf16[128,512]{1,0:T(8,128)(2,1)S(1)} %get-tuple-element.48), channel_id=1, source_target_pairs={{0,3},{1,0},{2,1},{3,2},{4,7},{5,4},{6,5},{7,6},{8,11},{9,8},{10,9... | collective-permute-start | bytes 393224 | tf_op jit(solution)/shard_map/ppermute | solution.py:318
  18.0 11.8 %collective-permute-start.3 = (bf16[512,256]{1,0:T(8,128)(2,1)S(1)}, bf16[512,256]{1,0:T(8,128)(2,1)S(1)}, u32[]{:S(2)}, u32[]{:S(2)}) collective-permute-start(bf16[512,256]{1,0:T(8,128)(2,1)S(1)} %get-tuple-element.50), channel_id=1, source_target_pairs={{0,4},{1,5},{2,6},{3,7},{4,0},{5,1},{6,2},{7,3},{8,12},{9,13},{10,... | collective-permute-start | bytes 786440 | tf_op jit(solution)/shard_map/ppermute | solution.py:318
  19.5 1.4 %collective-permute-start.6 = (bf16[128,512]{1,0:T(8,128)(2,1)S(1)}, bf16[128,512]{1,0:T(8,128)(2,1)S(1)}, u32[]{:S(2)}, u32[]{:S(2)}) collective-permute-start(bf16[128,512]{1,0:T(8,128)(2,1)S(1)} %get-tuple-element.54), channel_id=1, source_target_pairs={{0,4},{1,5},{2,6},{3,7},{4,0},{5,1},{6,2},{7,3},{8,12},{9,13},{10,... | collective-permute-start | bytes 393224 | tf_op jit(solution)/shard_map/ppermute | solution.py:318
  19.6 1.5 %collective-permute-start.7 = (bf16[128,512]{1,0:T(8,128)(2,1)S(1)}, bf16[128,512]{1,0:T(8,128)(2,1)S(1)}, u32[]{:S(2)}, u32[]{:S(2)}) collective-permute-start(bf16[128,512]{1,0:T(8,128)(2,1)S(1)} %get-tuple-element.55), channel_id=1, source_target_pairs={{0,4},{1,5},{2,6},{3,7},{4,0},{5,1},{6,2},{7,3},{8,12},{9,13},{10,... | collective-permute-start | bytes 393224 | tf_op jit(solution)/shard_map/ppermute | solution.py:318
  20.1 1.3 %collective-permute-start.8 = (bf16[128,512]{1,0:T(8,128)(2,1)S(1)}, bf16[128,512]{1,0:T(8,128)(2,1)S(1)}, u32[]{:S(2)}, u32[]{:S(2)}) collective-permute-start(bf16[128,512]{1,0:T(8,128)(2,1)S(1)} %get-tuple-element.56), channel_id=1, source_target_pairs={{0,4},{1,5},{2,6},{3,7},{4,0},{5,1},{6,2},{7,3},{8,12},{9,13},{10,... | collective-permute-start | bytes 393224 | tf_op jit(solution)/shard_map/ppermute | solution.py:318
  20.1 1.5 %collective-permute-start.9 = (bf16[128,512]{1,0:T(8,128)(2,1)S(1)}, bf16[128,512]{1,0:T(8,128)(2,1)S(1)}, u32[]{:S(2)}, u32[]{:S(2)}) collective-permute-start(bf16[128,512]{1,0:T(8,128)(2,1)S(1)} %get-tuple-element.57), channel_id=1, source_target_pairs={{0,4},{1,5},{2,6},{3,7},{4,0},{5,1},{6,2},{7,3},{8,12},{9,13},{10,... | collective-permute-start | bytes 393224 | tf_op jit(solution)/shard_map/ppermute | solution.py:318
  22.2 17.6 %collective-permute-start.10 = (bf16[272,512]{1,0:T(8,128)(2,1)S(1)}, bf16[272,512]{1,0:T(8,128)(2,1)S(1)}, u32[]{:S(2)}, u32[]{:S(2)}) collective-permute-start(bf16[272,512]{1,0:T(8,128)(2,1)S(1)} %get-tuple-element.59), channel_id=1, source_target_pairs={{0,2},{1,3},{2,0},{3,1},{4,6},{5,7},{6,4},{7,5},{8,10},{9,11},{10,... | collective-permute-start | bytes 835592 | tf_op jit(solution)/shard_map/ppermute | solution.py:318
  22.7 11.5 %collective-permute-start.5 = (bf16[512,256]{1,0:T(8,128)(2,1)S(1)}, bf16[512,256]{1,0:T(8,128)(2,1)S(1)}, u32[]{:S(2)}, u32[]{:S(2)}) collective-permute-start(bf16[512,256]{1,0:T(8,128)(2,1)S(1)} %get-tuple-element.50), channel_id=1, source_target_pairs={{0,12},{1,13},{2,14},{3,15},{4,8},{5,9},{6,10},{7,11},{8,20},{9,21... | collective-permute-start | bytes 786440 | tf_op jit(solution)/shard_map/ppermute | solution.py:318
  26.3 13.5 %collective-permute-start.4 = (bf16[512,256]{1,0:T(8,128)(2,1)S(1)}, bf16[512,256]{1,0:T(8,128)(2,1)S(1)}, u32[]{:S(2)}, u32[]{:S(2)}) collective-permute-start(bf16[512,256]{1,0:T(8,128)(2,1)S(1)} %get-tuple-element.49.mine_ref), channel_id=1, source_target_pairs={{0,8},{1,9},{2,10},{3,11},{4,12},{5,13},{6,14},{7,15},{8,16},{9,17... | collective-permute-start | bytes 786440 | tf_op jit(solution)/shard_map/ppermute | solution.py:318
  28.2 19.6 %collective-permute-start.12 = (bf16[272,512]{1,0:T(8,128)(2,1)S(1)}, bf16[272,512]{1,0:T(8,128)(2,1)S(1)}, u32[]{:S(2)}, u32[]{:S(2)}) collective-permute-start(bf16[272,512]{1,0:T(8,128)(2,1)S(1)} %get-tuple-element.64), channel_id=1, source_target_pairs={{0,1},{1,2},{2,3},{3,0},{4,5},{5,6},{6,7},{7,4},{8,9},{9,10},{10,1... | collective-permute-start | bytes 835592 | tf_op jit(solution)/shard_map/ppermute | solution.py:318
  29.8 19.6 %collective-permute-start.13 = (bf16[272,512]{1,0:T(8,128)(2,1)S(1)}, bf16[272,512]{1,0:T(8,128)(2,1)S(1)}, u32[]{:S(2)}, u32[]{:S(2)}) collective-permute-start(bf16[272,512]{1,0:T(8,128)(2,1)S(1)} %get-tuple-element.65), channel_id=1, source_target_pairs={{0,3},{1,0},{2,1},{3,2},{4,7},{5,4},{6,5},{7,6},{8,11},{9,8},{10,9... | collective-permute-start | bytes 835592 | tf_op jit(solution)/shard_map/ppermute | solution.py:318
  45.8 13.3 %collective-permute-start.11 = (bf16[256,256]{1,0:T(8,128)(2,1)S(1)}, bf16[256,256]{1,0:T(8,128)(2,1)S(1)}, u32[]{:S(2)}, u32[]{:S(2)}) collective-permute-start(bf16[256,256]{1,0:T(8,128)(2,1)S(1)} %get-tuple-element.61), channel_id=1, source_target_pairs={{0,2},{1,3},{2,0},{3,1},{4,6},{5,7},{6,4},{7,5},{8,10},{9,11},{10,... | collective-permute-start | bytes 393224 | tf_op jit(solution)/shard_map/ppermute | solution.py:318
  53.2 13.3 %collective-permute-start.17 = (bf16[528,256]{1,0:T(8,128)(2,1)S(1)}, bf16[528,256]{1,0:T(8,128)(2,1)S(1)}, u32[]{:S(2)}, u32[]{:S(2)}) collective-permute-start(bf16[528,256]{1,0:T(8,128)(2,1)S(1)} %get-tuple-element.77), channel_id=1, source_target_pairs={{8,0},{9,1},{10,2},{11,3},{12,4},{13,5},{14,6},{15,7},{16,8},{17,9... | collective-permute-start | bytes 811016 | tf_op jit(solution)/shard_map/ppermute | solution.py:318
  62.7 8.8 %collective-permute-start.18 = (bf16[512,256]{1,0:T(8,128)(2,1)S(1)}, bf16[512,256]{1,0:T(8,128)(2,1)S(1)}, u32[]{:S(2)}, u32[]{:S(2)}) collective-permute-start(bf16[512,256]{1,0:T(8,128)(2,1)S(1)} %get-tuple-element.78), channel_id=1, source_target_pairs={{8,0},{9,1},{10,2},{11,3},{12,4},{13,5},{14,6},{15,7},{16,8},{17,9... | collective-permute-start | bytes 786440 | tf_op jit(solution)/shard_map/ppermute | solution.py:318
  64.9 8.8 %collective-permute-start.14 = (bf16[256,256]{1,0:T(8,128)(2,1)S(1)}, bf16[256,256]{1,0:T(8,128)(2,1)S(1)}, u32[]{:S(2)}, u32[]{:S(2)}) collective-permute-start(bf16[256,256]{1,0:T(8,128)(2,1)S(1)} %get-tuple-element.71), channel_id=1, source_target_pairs={{0,3},{1,0},{2,1},{3,2},{4,7},{5,4},{6,5},{7,6},{8,11},{9,8},{10,9... | collective-permute-start | bytes 393224 | tf_op jit(solution)/shard_map/ppermute | solution.py:318
  65.0 8.8 %collective-permute-start.15 = (bf16[256,256]{1,0:T(8,128)(2,1)S(1)}, bf16[256,256]{1,0:T(8,128)(2,1)S(1)}, u32[]{:S(2)}, u32[]{:S(2)}) collective-permute-start(bf16[256,256]{1,0:T(8,128)(2,1)S(1)} %get-tuple-element.72), channel_id=1, source_target_pairs={{0,1},{1,2},{2,3},{3,0},{4,5},{5,6},{6,7},{7,4},{8,9},{9,10},{10,1... | collective-permute-start | bytes 393224 | tf_op jit(solution)/shard_map/ppermute | solution.py:318
  72.1 6.7 %collective-permute-start.19 = (bf16[256,256]{1,0:T(8,128)(2,1)S(1)}, bf16[256,256]{1,0:T(8,128)(2,1)S(1)}, u32[]{:S(2)}, u32[]{:S(2)}) collective-permute-start(bf16[256,256]{1,0:T(8,128)(2,1)S(1)} %get-tuple-element.80), channel_id=1, source_target_pairs={{0,2},{1,3},{2,0},{3,1},{4,6},{5,7},{6,4},{7,5},{8,10},{9,11},{10,... | collective-permute-start | bytes 393224 | tf_op jit(solution)/shard_map/ppermute | solution.py:318
  72.2 11.1 %collective-permute-start.20 = (bf16[256,256]{1,0:T(8,128)(2,1)S(1)}, bf16[256,256]{1,0:T(8,128)(2,1)S(1)}, u32[]{:S(2)}, u32[]{:S(2)}) collective-permute-start(bf16[256,256]{1,0:T(8,128)(2,1)S(1)} %get-tuple-element.81), channel_id=1, source_target_pairs={{0,1},{1,2},{2,3},{3,0},{4,5},{5,6},{6,7},{7,4},{8,9},{9,10},{10,1... | collective-permute-start | bytes 393224 | tf_op jit(solution)/shard_map/ppermute | solution.py:318
  72.3 12.0 %collective-permute-start.21 = (bf16[256,256]{1,0:T(8,128)(2,1)S(1)}, bf16[256,256]{1,0:T(8,128)(2,1)S(1)}, u32[]{:S(2)}, u32[]{:S(2)}) collective-permute-start(bf16[256,256]{1,0:T(8,128)(2,1)S(1)} %get-tuple-element.82), channel_id=1, source_target_pairs={{0,3},{1,0},{2,1},{3,2},{4,7},{5,4},{6,5},{7,6},{8,11},{9,8},{10,9... | collective-permute-start | bytes 393224 | tf_op jit(solution)/shard_map/ppermute | solution.py:318
  74.3 12.0 %collective-permute-start.16 = (bf16[512,256]{1,0:T(8,128)(2,1)S(1)}, bf16[512,256]{1,0:T(8,128)(2,1)S(1)}, u32[]{:S(2)}, u32[]{:S(2)}) collective-permute-start(bf16[512,256]{1,0:T(8,128)(2,1)S(1)} %get-tuple-element.74), channel_id=1, source_target_pairs={{0,4},{1,5},{2,6},{3,7},{4,0},{5,1},{6,2},{7,3},{8,12},{9,13},{10,... | collective-permute-start | bytes 786440 | tf_op jit(solution)/shard_map/ppermute | solution.py:318
  84.9 2.9 %collective-permute-start.22 = (bf16[512,256]{1,0:T(8,128)(2,1)S(1)}, bf16[512,256]{1,0:T(8,128)(2,1)S(1)}, u32[]{:S(2)}, u32[]{:S(2)}) collective-permute-start(bf16[512,256]{1,0:T(8,128)(2,1)S(1)} %get-tuple-element.84), channel_id=1, source_target_pairs={{0,4},{1,5},{2,6},{3,7},{4,0},{5,1},{6,2},{7,3},{8,12},{9,13},{10,... | collective-permute-start | bytes 786440 | tf_op jit(solution)/shard_map/ppermute | solution.py:318

commit v14 on v12

--- a/solution.py
+++ b/solution.py
@@ -309,11 +309,10 @@
 def moved(value, chips, heads, chip_step, flip, head_step):
     index = lambda chip, core, head: (chip * 2 + core) * heads + head
     pairs = [
-        (index(chip, core, head), index(chip + chip_step, core ^ flip, (head + head_step) % heads))
+        (index(chip, core, head), index((chip + chip_step) % chips, core ^ flip, (head + head_step) % heads))
         for chip in range(chips)
         for core in range(2)
         for head in range(heads)
-        if 0 <= chip + chip_step < chips
     ]
     return lax.ppermute(value, ("chip", "core", "head"), pairs)
 

time: 86.5 us -> 84.6 us (0.978); the launches traced: 86.2 us -> 83.5 us
  starting transfers between devices: 34.3 us -> 23 us
  waiting for transfers between devices: 26.2 us -> 34.9 us
    ppermute x23, starting transfers between devices: 34.3 us -> 23 us  [moved(): return lax.ppermute(value, ('chip', 'core', 'head'), pairs)]
    ppermute x23, waiting for transfers between devices: 26.2 us -> 34.9 us  [moved(): return lax.ppermute(value, ('chip', 'core', 'head'), pairs)]
  transfers between devices with their start and end apart: 23 -> 23, of which waited for: 10 -> 11; matrix products, arithmetic and copies ran while one was open for 0% -> 0% of each run, Pallas kernels for 22% -> 23%
where the time goes in v14:
time: 84.6 us; the launch traced here: 83.5 us
  waiting for transfers between devices  34.9 us (41%)
  starting transfers between devices  23 us (27%)
  Pallas kernels  21.7 us (26%)
  local copies, waits for them, and re-layouts  3 us (4%)
    ppermute x23, waiting for transfers between devices, moved(): return lax.ppermute(value, ('chip', 'core', 'head'), pairs)  34.9 us
    ppermute x23, starting transfers between devices, moved(): return lax.ppermute(value, ('chip', 'core', 'head'), pairs)  23 us
    pallas_call x13, Pallas kernels, call(): pl.pallas_call(kernel, out_shape=out_shape, in_specs=[SMEM_SPEC] + [spec]...  21.7 us
    unnamed x8, local copies, waits for them, and re-layouts  2.99 us
  transfers between devices with their start and end apart: 23, of which 11 were waited for; matrix products, arithmetic and copies ran while one was open for 0% of the time, Pallas kernels for 23%

profile of v14, /device:TPU:13, one launch (start us, length us, event | category | flops | bytes accessed | tf_op | source)
XLA Modules:
  0.0 83.5 jit_solution(18426082165016713606)
XLA Ops:
  0.6 0.0 copy-start
  0.6 0.1 pad_add_fusion.place_ref
  0.7 1.0 %copy-done.2 = bf16[128,1024]{1,0:T(8,128)(2,1)S(1)} copy-done((bf16[128,1024]{1,0:T(8,128)(2,1)S(1)}, bf16[128,1024]{1,0:T(8,128)(2,1)}, u32[]{:S(2)}) %copy-start.2) | copy-done | bytes 262168
  1.7 0.9 %copy-done.3 = bf16[128,1024]{1,0:T(8,128)(2,1)S(1)} copy-done((bf16[128,1024]{1,0:T(8,128)(2,1)S(1)}, bf16[128,1024]{1,0:T(8,128)(2,1)}, u32[]{:S(2)}) %copy-start.3) | copy-done | bytes 262168
  2.7 0.9 %shard_map.67 = (bf16[128,512]{1,0:T(8,128)(2,1)S(1)}, bf16[128,512]{1,0:T(8,128)(2,1)S(1)}, bf16[128,512]{1,0:T(8,128)(2,1)S(1)}, bf16[128,512]{1,0:T(8,128)(2,1)S(1)}) custom-call(s32[3]{0:T(128)S(1)} %pad_add_fusion.place_ref, bf16[128,1024]{1,0:T(8,128)(2,1)S(1)} %copy-done.2, bf16[128,1024]{1,0:T(8,128)(2,1)S(1)} %copy-done.3), custom_call_target="tpu_custom_call" | custom-call | bytes 1048588 | tf_op jit(solution)/shard_map/pallas_call | solution.py:26
  3.6 2.4 %collective-permute-start = (bf16[128,512]{1,0:T(8,128)(2,1)S(1)}, bf16[128,512]{1,0:T(8,128)(2,1)S(1)}, u32[]{:S(2)}, u32[]{:S(2)}) collective-permute-start(bf16[128,512]{1,0:T(8,128)(2,1)S(1)} %get-tuple-element.46), channel_id=1, source_target_pairs={{0,2},{1,3},{2,0},{3,1},{4,6},{5,7},{6,4},{7,5},{8,10},{9,11},{10,... | collective-permute-start | bytes 393224 | tf_op jit(solution)/shard_map/ppermute | solution.py:317
  5.9 0.0 collective-permute-start.1
  5.9 1.5 %collective-permute-start.2 = (bf16[128,512]{1,0:T(8,128)(2,1)S(1)}, bf16[128,512]{1,0:T(8,128)(2,1)S(1)}, u32[]{:S(2)}, u32[]{:S(2)}) collective-permute-start(bf16[128,512]{1,0:T(8,128)(2,1)S(1)} %get-tuple-element.48), channel_id=1, source_target_pairs={{0,3},{1,0},{2,1},{3,2},{4,7},{5,4},{6,5},{7,6},{8,11},{9,8},{10,9... | collective-permute-start | bytes 393224 | tf_op jit(solution)/shard_map/ppermute | solution.py:317
  7.4 1.0 %copy-done.1 = bf16[128,2048]{1,0:T(8,128)(2,1)S(1)} copy-done((bf16[128,2048]{1,0:T(8,128)(2,1)S(1)}, bf16[128,2048]{1,0:T(8,128)(2,1)}, u32[]{:S(2)}) %copy-start.1) | copy-done | bytes 524312
  8.5 0.9 %shard_map.70 = (bf16[4,128,512]{2,1,0:T(8,128)(2,1)S(1)}, bf16[128,512]{1,0:T(8,128)(2,1)S(1)}, bf16[128,512]{1,0:T(8,128)(2,1)S(1)}, bf16[128,512]{1,0:T(8,128)(2,1)S(1)}, bf16[128,512]{1,0:T(8,128)(2,1)S(1)}) custom-call(s32[3]{0:T(128)S(1)} %pad_add_fusion.place_ref, bf16[128,2048]{1,0:T(8,128)(2,1)S(1)} %copy-done, bf16[128,2048]{1,0:T(8,128)(2,1)S(1)} %copy-done.1), custom_call_target="tpu_custom_call" | custom-call | bytes 2097164 | tf_op jit(solution)/shard_map/pallas_call | solution.py:26
  9.4 1.6 %collective-permute-start.6 = (bf16[128,512]{1,0:T(8,128)(2,1)S(1)}, bf16[128,512]{1,0:T(8,128)(2,1)S(1)}, u32[]{:S(2)}, u32[]{:S(2)}) collective-permute-start(bf16[128,512]{1,0:T(8,128)(2,1)S(1)} %get-tuple-element.54), channel_id=1, source_target_pairs={{0,4},{1,5},{2,6},{3,7},{4,0},{5,1},{6,2},{7,3},{8,12},{9,13},{10,... | collective-permute-start | bytes 393224 | tf_op jit(solution)/shard_map/ppermute | solution.py:317
  10.9 0.1 collective-permute-start.7
  11.0 1.4 %collective-permute-done.refs_1_ = bf16[128,512]{1,0:T(8,128)(2,1)S(1)} collective-permute-done((bf16[128,512]{1,0:T(8,128)(2,1)S(1)}, bf16[128,512]{1,0:T(8,128)(2,1)S(1)}, u32[]{:S(2)}, u32[]{:S(2)}) %collective-permute-start) | collective-permute-done | bytes 131104 | tf_op jit(solution)/shard_map/ppermute | solution.py:317
  12.4 0.9 %collective-permute-start.8 = (bf16[128,512]{1,0:T(8,128)(2,1)S(1)}, bf16[128,512]{1,0:T(8,128)(2,1)S(1)}, u32[]{:S(2)}, u32[]{:S(2)}) collective-permute-start(bf16[128,512]{1,0:T(8,128)(2,1)S(1)} %get-tuple-element.56), channel_id=1, source_target_pairs={{0,4},{1,5},{2,6},{3,7},{4,0},{5,1},{6,2},{7,3},{8,12},{9,13},{10,... | collective-permute-start | bytes 393224 | tf_op jit(solution)/shard_map/ppermute | solution.py:317
  13.3 4.1 %collective-permute-done.1.refs_2_ = bf16[128,512]{1,0:T(8,128)(2,1)S(1)} collective-permute-done((bf16[128,512]{1,0:T(8,128)(2,1)S(1)}, bf16[128,512]{1,0:T(8,128)(2,1)S(1)}, u32[]{:S(2)}, u32[]{:S(2)}) %collective-permute-start.1) | collective-permute-done | bytes 131104 | tf_op jit(solution)/shard_map/ppermute | solution.py:317
  17.5 0.5 collective-permute-start.9
  18.0 0.0 collective-permute-done.2.refs_3_
  18.0 0.6 shard_map.68
  18.6 0.1 collective-permute-start.3
  18.6 0.0 collective-permute-done.6.refs_0_
  18.7 0.0 collective-permute-done.7.refs_1_
  18.7 0.0 collective-permute-done.8.refs_2_
  18.7 0.3 collective-permute-done.9.refs_3_
  19.0 0.6 shard_map.71
  19.6 0.2 collective-permute-start.10
  19.7 1.4 %collective-permute-start.5 = (bf16[512,256]{1,0:T(8,128)(2,1)S(1)}, bf16[512,256]{1,0:T(8,128)(2,1)S(1)}, u32[]{:S(2)}, u32[]{:S(2)}) collective-permute-start(bf16[512,256]{1,0:T(8,128)(2,1)S(1)} %get-tuple-element.50), channel_id=1, source_target_pairs={{0,12},{1,13},{2,14},{3,15},{4,8},{5,9},{6,10},{7,11},{8,20},{9,21... | collective-permute-start | bytes 786440 | tf_op jit(solution)/shard_map/ppermute | solution.py:317
  21.2 0.2 collective-permute-start.4
  21.4 2.2 %collective-permute-start.12 = (bf16[256,512]{1,0:T(8,128)(2,1)S(1)}, bf16[256,512]{1,0:T(8,128)(2,1)S(1)}, u32[]{:S(2)}, u32[]{:S(2)}) collective-permute-start(bf16[256,512]{1,0:T(8,128)(2,1)S(1)} %get-tuple-element.64), channel_id=1, source_target_pairs={{0,1},{1,2},{2,3},{3,0},{4,5},{5,6},{6,7},{7,4},{8,9},{9,10},{10,1... | collective-permute-start | bytes 786440 | tf_op jit(solution)/shard_map/ppermute | solution.py:317
  23.6 0.0 collective-permute-done.3.sibling_ref
  23.6 1.4 %collective-permute-start.13 = (bf16[256,512]{1,0:T(8,128)(2,1)S(1)}, bf16[256,512]{1,0:T(8,128)(2,1)S(1)}, u32[]{:S(2)}, u32[]{:S(2)}) collective-permute-start(bf16[256,512]{1,0:T(8,128)(2,1)S(1)} %get-tuple-element.65), channel_id=1, source_target_pairs={{0,3},{1,0},{2,1},{3,2},{4,7},{5,4},{6,5},{7,6},{8,11},{9,8},{10,9... | collective-permute-start | bytes 786440 | tf_op jit(solution)/shard_map/ppermute | solution.py:317
  25.0 0.7 shard_map.69
  25.7 3.8 %collective-permute-done.5.b_ref = bf16[512,256]{1,0:T(8,128)(2,1)S(1)} collective-permute-done((bf16[512,256]{1,0:T(8,128)(2,1)S(1)}, bf16[512,256]{1,0:T(8,128)(2,1)S(1)}, u32[]{:S(2)}, u32[]{:S(2)}) %collective-permute-start.5) | collective-permute-done | bytes 262176 | tf_op jit(solution)/shard_map/ppermute | solution.py:317
  29.4 5.1 %collective-permute-done.4.a_ref = bf16[512,256]{1,0:T(8,128)(2,1)S(1)} collective-permute-done((bf16[512,256]{1,0:T(8,128)(2,1)S(1)}, bf16[512,256]{1,0:T(8,128)(2,1)S(1)}, u32[]{:S(2)}, u32[]{:S(2)}) %collective-permute-start.4) | collective-permute-done | bytes 262176 | tf_op jit(solution)/shard_map/ppermute | solution.py:317
  34.5 0.0 collective-permute-done.10.refs_1_
  34.5 6.0 %shard_map.72 = (bf16[1024,256]{1,0:T(8,128)(2,1)S(1)}, bf16[128,1024]{1,0:T(8,128)(2,1)S(1)}, f32[1024,256]{1,0:T(8,128)S(1)}, f32[1024,256]{1,0:T(8,128)S(1)},...) custom-call(s32[3]{0:T(128)S(1)} %pad_add_fusion.place_ref, bf16[1024,256]{1,0:T(8,128)(2,1)S(1)} %get-tuple-element.51.own_ref, ...), custom_call_target="tpu_custom_call" | custom-call | flops 1 | bytes 4997132 | tf_op jit(solution)/shard_map/pallas_call | solution.py:26
  40.5 2.9 %collective-permute-start.11 = (bf16[256,256]{1,0:T(8,128)(2,1)S(1)}, bf16[256,256]{1,0:T(8,128)(2,1)S(1)}, u32[]{:S(2)}, u32[]{:S(2)}) collective-permute-start(bf16[256,256]{1,0:T(8,128)(2,1)S(1)} %get-tuple-element.61), channel_id=1, source_target_pairs={{0,2},{1,3},{2,0},{3,1},{4,6},{5,7},{6,4},{7,5},{8,10},{9,11},{10,... | collective-permute-start | bytes 393224 | tf_op jit(solution)/shard_map/ppermute | solution.py:317
  43.4 0.0 collective-permute-done.12.refs_0_
  43.4 5.5 %collective-permute-done.13.refs_1_ = bf16[256,512]{1,0:T(8,128)(2,1)S(1)} collective-permute-done((bf16[256,512]{1,0:T(8,128)(2,1)S(1)}, bf16[256,512]{1,0:T(8,128)(2,1)S(1)}, u32[]{:S(2)}, u32[]{:S(2)}) %collective-permute-start.13) | collective-permute-done | bytes 262176 | tf_op jit(solution)/shard_map/ppermute | solution.py:317
  48.9 3.8 %shard_map.73 = (f32[512,256]{1,0:T(8,128)S(1)}, f32[512,256]{1,0:T(8,128)S(1)}, bf16[528,256]{1,0:T(8,128)(2,1)S(1)}, bf16[2,128,256]{2,1,0:T(8,128)(2,1)S(1)}) custom-call(s32[3]{0:T(128)S(1)} %pad_add_fusion.place_ref, bf16[1024,256]{1,0:T(8,128)(2,1)S(1)} %get-tuple-element.51.own_ref, bf16[128,1024]{1,0:T(8,128)(2,1)S(1)} %get-tuple-element.52.own_kt_ref, ...), custom_call_target="tpu_custom_call" | custom-call | flops 1 | bytes 5644300 | tf_op jit(solution)/shard_map/pallas_call | solution.py:26
  52.6 1.2 %collective-permute-start.17 = (bf16[528,256]{1,0:T(8,128)(2,1)S(1)}, bf16[528,256]{1,0:T(8,128)(2,1)S(1)}, u32[]{:S(2)}, u32[]{:S(2)}) collective-permute-start(bf16[528,256]{1,0:T(8,128)(2,1)S(1)} %get-tuple-element.77), channel_id=1, source_target_pairs={{0,24},{1,25},{2,26},{3,27},{4,28},{5,29},{6,30},{7,31},{8,0},{9,1... | collective-permute-start | bytes 811016 | tf_op jit(solution)/shard_map/ppermute | solution.py:317
  53.9 0.0 collective-permute-done.11.refs_1_
  53.9 3.6 %shard_map.74 = (f32[512,256]{1,0:T(8,128)S(1)}, f32[512,256]{1,0:T(8,128)S(1)}, bf16[512,256]{1,0:T(8,128)(2,1)S(1)}, bf16[256,256]{1,0:T(8,128)(2,1)S(1)}, bf16[256,256]{1,0:T(8,128)(2,1)S(1)}) custom-call(s32[3]{0:T(128)S(1)} %pad_add_fusion.place_ref, bf16[1024,256]{1,0:T(8,128)(2,1)S(1)} %get-tuple-element.51.own_ref, ...), custom_call_target="tpu_custom_call" | custom-call | flops 1 | bytes 5906444 | tf_op jit(solution)/shard_map/pallas_call | solution.py:26
  57.5 0.3 collective-permute-start.18
  57.8 0.0 collective-permute-start.14
  57.8 1.5 %collective-permute-start.15 = (bf16[256,256]{1,0:T(8,128)(2,1)S(1)}, bf16[256,256]{1,0:T(8,128)(2,1)S(1)}, u32[]{:S(2)}, u32[]{:S(2)}) collective-permute-start(bf16[256,256]{1,0:T(8,128)(2,1)S(1)} %get-tuple-element.72), channel_id=1, source_target_pairs={{0,1},{1,2},{2,3},{3,0},{4,5},{5,6},{6,7},{7,4},{8,9},{9,10},{10,1... | collective-permute-start | bytes 393224 | tf_op jit(solution)/shard_map/ppermute | solution.py:317
  59.3 0.8 collective-permute-done.17.back_a_ref
  60.1 5.9 %collective-permute-done.18.back_b_ref = bf16[512,256]{1,0:T(8,128)(2,1)S(1)} collective-permute-done((bf16[512,256]{1,0:T(8,128)(2,1)S(1)}, bf16[512,256]{1,0:T(8,128)(2,1)S(1)}, u32[]{:S(2)}, u32[]{:S(2)}) %collective-permute-start.18) | collective-permute-done | bytes 262176 | tf_op jit(solution)/shard_map/ppermute | solution.py:317
  65.9 0.7 shard_map.77
  66.6 0.1 collective-permute-start.19
  66.7 0.1 collective-permute-start.20
  66.7 1.5 %collective-permute-start.21 = (bf16[256,256]{1,0:T(8,128)(2,1)S(1)}, bf16[256,256]{1,0:T(8,128)(2,1)S(1)}, u32[]{:S(2)}, u32[]{:S(2)}) collective-permute-start(bf16[256,256]{1,0:T(8,128)(2,1)S(1)} %get-tuple-element.82), channel_id=1, source_target_pairs={{0,3},{1,0},{2,1},{3,2},{4,7},{5,4},{6,5},{7,6},{8,11},{9,8},{10,9... | collective-permute-start | bytes 393224 | tf_op jit(solution)/shard_map/ppermute | solution.py:317
  68.2 0.0 collective-permute-done.14.refs_2_
  68.2 0.0 collective-permute-done.15.refs_3_
  68.2 0.6 shard_map.75
  68.8 1.9 %collective-permute-start.16 = (bf16[512,256]{1,0:T(8,128)(2,1)S(1)}, bf16[512,256]{1,0:T(8,128)(2,1)S(1)}, u32[]{:S(2)}, u32[]{:S(2)}) collective-permute-start(bf16[512,256]{1,0:T(8,128)(2,1)S(1)} %get-tuple-element.74), channel_id=1, source_target_pairs={{0,4},{1,5},{2,6},{3,7},{4,0},{5,1},{6,2},{7,3},{8,12},{9,13},{10,... | collective-permute-start | bytes 786440 | tf_op jit(solution)/shard_map/ppermute | solution.py:317
  70.7 0.8 collective-permute-done.19.refs_1_
  71.5 6.0 %collective-permute-done.20.refs_2_ = bf16[256,256]{1,0:T(8,128)(2,1)S(1)} collective-permute-done((bf16[256,256]{1,0:T(8,128)(2,1)S(1)}, bf16[256,256]{1,0:T(8,128)(2,1)S(1)}, u32[]{:S(2)}, u32[]{:S(2)}) %collective-permute-start.20) | collective-permute-done | bytes 131104 | tf_op jit(solution)/shard_map/ppermute | solution.py:317
  77.5 1.3 %collective-permute-done.21.refs_3_ = bf16[256,256]{1,0:T(8,128)(2,1)S(1)} collective-permute-done((bf16[256,256]{1,0:T(8,128)(2,1)S(1)}, bf16[256,256]{1,0:T(8,128)(2,1)S(1)}, u32[]{:S(2)}, u32[]{:S(2)}) %collective-permute-start.21) | collective-permute-done | bytes 131104 | tf_op jit(solution)/shard_map/ppermute | solution.py:317
  78.8 0.6 shard_map.78
  79.4 1.2 %collective-permute-start.22 = (bf16[512,256]{1,0:T(8,128)(2,1)S(1)}, bf16[512,256]{1,0:T(8,128)(2,1)S(1)}, u32[]{:S(2)}, u32[]{:S(2)}) collective-permute-start(bf16[512,256]{1,0:T(8,128)(2,1)S(1)} %get-tuple-element.84), channel_id=1, source_target_pairs={{0,4},{1,5},{2,6},{3,7},{4,0},{5,1},{6,2},{7,3},{8,12},{9,13},{10,... | collective-permute-start | bytes 786440 | tf_op jit(solution)/shard_map/ppermute | solution.py:317
  80.6 0.0 collective-permute-done.16.sibling_ref
  80.6 1.4 %shard_map.76 = bf16[128,2048]{1,0:T(8,128)(2,1)} custom-call(s32[3]{0:T(128)S(1)} %pad_add_fusion.place_ref, bf16[512,256]{1,0:T(8,128)(2,1)S(1)} %get-tuple-element.73.mine_ref, bf16[512,256]{1,0:T(8,128)(2,1)S(1)} %collective-permute-done.16.sibling_ref), custom_call_target="tpu_custom_call" | custom-call | bytes 1048588 | tf_op jit(solution)/shard_map/pallas_call | solution.py:26
  82.0 0.0 collective-permute-done.22.sibling_ref
  82.0 1.5 %shard_map.79 = (bf16[128,1024]{1,0:T(8,128)(2,1)}, bf16[128,1024]{1,0:T(8,128)(2,1)}) custom-call(s32[3]{0:T(128)S(1)} %pad_add_fusion.place_ref, bf16[512,256]{1,0:T(8,128)(2,1)S(1)} %get-tuple-element.83.mine_ref, bf16[512,256]{1,0:T(8,128)(2,1)S(1)} %collective-permute-done.22.sibling_ref), custom_call_target="tpu_custom_call" | custom-call | bytes 1048588 | tf_op jit(solution)/shard_map/pallas_call | solution.py:26
  (6 shorter events, 0.0 us)
Async XLA Ops:
  0.6 6.8 %copy-start = (bf16[128,2048]{1,0:T(8,128)(2,1)S(1)}, bf16[128,2048]{1,0:T(8,128)(2,1)}, u32[]{:S(2)}) copy-start(bf16[128,2048]{1,0:T(8,128)(2,1)} %q_ref.1) | copy-start | bytes 1572868
  0.7 1.0 %copy-start.2 = (bf16[128,1024]{1,0:T(8,128)(2,1)S(1)}, bf16[128,1024]{1,0:T(8,128)(2,1)}, u32[]{:S(2)}) copy-start(bf16[128,1024]{1,0:T(8,128)(2,1)} %k_ref.1) | copy-start | bytes 786436
  1.7 0.9 %copy-start.3 = (bf16[128,1024]{1,0:T(8,128)(2,1)S(1)}, bf16[128,1024]{1,0:T(8,128)(2,1)}, u32[]{:S(2)}) copy-start(bf16[128,1024]{1,0:T(8,128)(2,1)} %v_ref.1) | copy-start | bytes 786436
  3.6 8.8 %collective-permute-start = (bf16[128,512]{1,0:T(8,128)(2,1)S(1)}, bf16[128,512]{1,0:T(8,128)(2,1)S(1)}, u32[]{:S(2)}, u32[]{:S(2)}) collective-permute-start(bf16[128,512]{1,0:T(8,128)(2,1)S(1)} %get-tuple-element.46), channel_id=1, source_target_pairs={{0,2},{1,3},{2,0},{3,1},{4,6},{5,7},{6,4},{7,5},{8,10},{9,11},{10,... | collective-permute-start | bytes 393224 | tf_op jit(solution)/shard_map/ppermute | solution.py:317
  5.9 11.5 %collective-permute-start.1 = (bf16[128,512]{1,0:T(8,128)(2,1)S(1)}, bf16[128,512]{1,0:T(8,128)(2,1)S(1)}, u32[]{:S(2)}, u32[]{:S(2)}) collective-permute-start(bf16[128,512]{1,0:T(8,128)(2,1)S(1)} %get-tuple-element.47), channel_id=1, source_target_pairs={{0,1},{1,2},{2,3},{3,0},{4,5},{5,6},{6,7},{7,4},{8,9},{9,10},{10,1... | collective-permute-start | bytes 393224 | tf_op jit(solution)/shard_map/ppermute | solution.py:317
  5.9 12.0 %collective-permute-start.2 = (bf16[128,512]{1,0:T(8,128)(2,1)S(1)}, bf16[128,512]{1,0:T(8,128)(2,1)S(1)}, u32[]{:S(2)}, u32[]{:S(2)}) collective-permute-start(bf16[128,512]{1,0:T(8,128)(2,1)S(1)} %get-tuple-element.48), channel_id=1, source_target_pairs={{0,3},{1,0},{2,1},{3,2},{4,7},{5,4},{6,5},{7,6},{8,11},{9,8},{10,9... | collective-permute-start | bytes 393224 | tf_op jit(solution)/shard_map/ppermute | solution.py:317
  7.4 1.0 %copy-start.1 = (bf16[128,2048]{1,0:T(8,128)(2,1)S(1)}, bf16[128,2048]{1,0:T(8,128)(2,1)}, u32[]{:S(2)}) copy-start(bf16[128,2048]{1,0:T(8,128)(2,1)} %g_ref.1) | copy-start | bytes 1572868
  9.4 9.3 %collective-permute-start.6 = (bf16[128,512]{1,0:T(8,128)(2,1)S(1)}, bf16[128,512]{1,0:T(8,128)(2,1)S(1)}, u32[]{:S(2)}, u32[]{:S(2)}) collective-permute-start(bf16[128,512]{1,0:T(8,128)(2,1)S(1)} %get-tuple-element.54), channel_id=1, source_target_pairs={{0,4},{1,5},{2,6},{3,7},{4,0},{5,1},{6,2},{7,3},{8,12},{9,13},{10,... | collective-permute-start | bytes 393224 | tf_op jit(solution)/shard_map/ppermute | solution.py:317
  10.9 7.7 %collective-permute-start.7 = (bf16[128,512]{1,0:T(8,128)(2,1)S(1)}, bf16[128,512]{1,0:T(8,128)(2,1)S(1)}, u32[]{:S(2)}, u32[]{:S(2)}) collective-permute-start(bf16[128,512]{1,0:T(8,128)(2,1)S(1)} %get-tuple-element.55), channel_id=1, source_target_pairs={{0,4},{1,5},{2,6},{3,7},{4,0},{5,1},{6,2},{7,3},{8,12},{9,13},{10,... | collective-permute-start | bytes 393224 | tf_op jit(solution)/shard_map/ppermute | solution.py:317
  12.4 6.3 %collective-permute-start.8 = (bf16[128,512]{1,0:T(8,128)(2,1)S(1)}, bf16[128,512]{1,0:T(8,128)(2,1)S(1)}, u32[]{:S(2)}, u32[]{:S(2)}) collective-permute-start(bf16[128,512]{1,0:T(8,128)(2,1)S(1)} %get-tuple-element.56), channel_id=1, source_target_pairs={{0,4},{1,5},{2,6},{3,7},{4,0},{5,1},{6,2},{7,3},{8,12},{9,13},{10,... | collective-permute-start | bytes 393224 | tf_op jit(solution)/shard_map/ppermute | solution.py:317
  17.5 1.5 %collective-permute-start.9 = (bf16[128,512]{1,0:T(8,128)(2,1)S(1)}, bf16[128,512]{1,0:T(8,128)(2,1)S(1)}, u32[]{:S(2)}, u32[]{:S(2)}) collective-permute-start(bf16[128,512]{1,0:T(8,128)(2,1)S(1)} %get-tuple-element.57), channel_id=1, source_target_pairs={{0,4},{1,5},{2,6},{3,7},{4,0},{5,1},{6,2},{7,3},{8,12},{9,13},{10,... | collective-permute-start | bytes 393224 | tf_op jit(solution)/shard_map/ppermute | solution.py:317
  18.6 5.0 %collective-permute-start.3 = (bf16[512,256]{1,0:T(8,128)(2,1)S(1)}, bf16[512,256]{1,0:T(8,128)(2,1)S(1)}, u32[]{:S(2)}, u32[]{:S(2)}) collective-permute-start(bf16[512,256]{1,0:T(8,128)(2,1)S(1)} %get-tuple-element.50), channel_id=1, source_target_pairs={{0,4},{1,5},{2,6},{3,7},{4,0},{5,1},{6,2},{7,3},{8,12},{9,13},{10,... | collective-permute-start | bytes 786440 | tf_op jit(solution)/shard_map/ppermute | solution.py:317
  19.6 15.0 %collective-permute-start.10 = (bf16[272,512]{1,0:T(8,128)(2,1)S(1)}, bf16[272,512]{1,0:T(8,128)(2,1)S(1)}, u32[]{:S(2)}, u32[]{:S(2)}) collective-permute-start(bf16[272,512]{1,0:T(8,128)(2,1)S(1)} %get-tuple-element.59), channel_id=1, source_target_pairs={{0,2},{1,3},{2,0},{3,1},{4,6},{5,7},{6,4},{7,5},{8,10},{9,11},{10,... | collective-permute-start | bytes 835592 | tf_op jit(solution)/shard_map/ppermute | solution.py:317
  19.7 9.7 %collective-permute-start.5 = (bf16[512,256]{1,0:T(8,128)(2,1)S(1)}, bf16[512,256]{1,0:T(8,128)(2,1)S(1)}, u32[]{:S(2)}, u32[]{:S(2)}) collective-permute-start(bf16[512,256]{1,0:T(8,128)(2,1)S(1)} %get-tuple-element.50), channel_id=1, source_target_pairs={{0,12},{1,13},{2,14},{3,15},{4,8},{5,9},{6,10},{7,11},{8,20},{9,21... | collective-permute-start | bytes 786440 | tf_op jit(solution)/shard_map/ppermute | solution.py:317
  21.2 13.4 %collective-permute-start.4 = (bf16[512,256]{1,0:T(8,128)(2,1)S(1)}, bf16[512,256]{1,0:T(8,128)(2,1)S(1)}, u32[]{:S(2)}, u32[]{:S(2)}) collective-permute-start(bf16[512,256]{1,0:T(8,128)(2,1)S(1)} %get-tuple-element.49.mine_ref), channel_id=1, source_target_pairs={{0,8},{1,9},{2,10},{3,11},{4,12},{5,13},{6,14},{7,15},{8,16},{9,17... | collective-permute-start | bytes 786440 | tf_op jit(solution)/shard_map/ppermute | solution.py:317
  21.4 22.0 %collective-permute-start.12 = (bf16[256,512]{1,0:T(8,128)(2,1)S(1)}, bf16[256,512]{1,0:T(8,128)(2,1)S(1)}, u32[]{:S(2)}, u32[]{:S(2)}) collective-permute-start(bf16[256,512]{1,0:T(8,128)(2,1)S(1)} %get-tuple-element.64), channel_id=1, source_target_pairs={{0,1},{1,2},{2,3},{3,0},{4,5},{5,6},{6,7},{7,4},{8,9},{9,10},{10,1... | collective-permute-start | bytes 786440 | tf_op jit(solution)/shard_map/ppermute | solution.py:317
  23.6 25.3 %collective-permute-start.13 = (bf16[256,512]{1,0:T(8,128)(2,1)S(1)}, bf16[256,512]{1,0:T(8,128)(2,1)S(1)}, u32[]{:S(2)}, u32[]{:S(2)}) collective-permute-start(bf16[256,512]{1,0:T(8,128)(2,1)S(1)} %get-tuple-element.65), channel_id=1, source_target_pairs={{0,3},{1,0},{2,1},{3,2},{4,7},{5,4},{6,5},{7,6},{8,11},{9,8},{10,9... | collective-permute-start | bytes 786440 | tf_op jit(solution)/shard_map/ppermute | solution.py:317
  40.5 13.3 %collective-permute-start.11 = (bf16[256,256]{1,0:T(8,128)(2,1)S(1)}, bf16[256,256]{1,0:T(8,128)(2,1)S(1)}, u32[]{:S(2)}, u32[]{:S(2)}) collective-permute-start(bf16[256,256]{1,0:T(8,128)(2,1)S(1)} %get-tuple-element.61), channel_id=1, source_target_pairs={{0,2},{1,3},{2,0},{3,1},{4,6},{5,7},{6,4},{7,5},{8,10},{9,11},{10,... | collective-permute-start | bytes 393224 | tf_op jit(solution)/shard_map/ppermute | solution.py:317
  52.6 7.4 %collective-permute-start.17 = (bf16[528,256]{1,0:T(8,128)(2,1)S(1)}, bf16[528,256]{1,0:T(8,128)(2,1)S(1)}, u32[]{:S(2)}, u32[]{:S(2)}) collective-permute-start(bf16[528,256]{1,0:T(8,128)(2,1)S(1)} %get-tuple-element.77), channel_id=1, source_target_pairs={{0,24},{1,25},{2,26},{3,27},{4,28},{5,29},{6,30},{7,31},{8,0},{9,1... | collective-permute-start | bytes 811016 | tf_op jit(solution)/shard_map/ppermute | solution.py:317
  57.5 8.4 %collective-permute-start.18 = (bf16[512,256]{1,0:T(8,128)(2,1)S(1)}, bf16[512,256]{1,0:T(8,128)(2,1)S(1)}, u32[]{:S(2)}, u32[]{:S(2)}) collective-permute-start(bf16[512,256]{1,0:T(8,128)(2,1)S(1)} %get-tuple-element.78), channel_id=1, source_target_pairs={{0,24},{1,25},{2,26},{3,27},{4,28},{5,29},{6,30},{7,31},{8,0},{9,1... | collective-permute-start | bytes 786440 | tf_op jit(solution)/shard_map/ppermute | solution.py:317
  57.8 10.4 %collective-permute-start.14 = (bf16[256,256]{1,0:T(8,128)(2,1)S(1)}, bf16[256,256]{1,0:T(8,128)(2,1)S(1)}, u32[]{:S(2)}, u32[]{:S(2)}) collective-permute-start(bf16[256,256]{1,0:T(8,128)(2,1)S(1)} %get-tuple-element.71), channel_id=1, source_target_pairs={{0,3},{1,0},{2,1},{3,2},{4,7},{5,4},{6,5},{7,6},{8,11},{9,8},{10,9... | collective-permute-start | bytes 393224 | tf_op jit(solution)/shard_map/ppermute | solution.py:317
  57.8 10.4 %collective-permute-start.15 = (bf16[256,256]{1,0:T(8,128)(2,1)S(1)}, bf16[256,256]{1,0:T(8,128)(2,1)S(1)}, u32[]{:S(2)}, u32[]{:S(2)}) collective-permute-start(bf16[256,256]{1,0:T(8,128)(2,1)S(1)} %get-tuple-element.72), channel_id=1, source_target_pairs={{0,1},{1,2},{2,3},{3,0},{4,5},{5,6},{6,7},{7,4},{8,9},{9,10},{10,1... | collective-permute-start | bytes 393224 | tf_op jit(solution)/shard_map/ppermute | solution.py:317
  66.6 4.9 %collective-permute-start.19 = (bf16[256,256]{1,0:T(8,128)(2,1)S(1)}, bf16[256,256]{1,0:T(8,128)(2,1)S(1)}, u32[]{:S(2)}, u32[]{:S(2)}) collective-permute-start(bf16[256,256]{1,0:T(8,128)(2,1)S(1)} %get-tuple-element.80), channel_id=1, source_target_pairs={{0,2},{1,3},{2,0},{3,1},{4,6},{5,7},{6,4},{7,5},{8,10},{9,11},{10,... | collective-permute-start | bytes 393224 | tf_op jit(solution)/shard_map/ppermute | solution.py:317
  66.7 10.8 %collective-permute-start.20 = (bf16[256,256]{1,0:T(8,128)(2,1)S(1)}, bf16[256,256]{1,0:T(8,128)(2,1)S(1)}, u32[]{:S(2)}, u32[]{:S(2)}) collective-permute-start(bf16[256,256]{1,0:T(8,128)(2,1)S(1)} %get-tuple-element.81), channel_id=1, source_target_pairs={{0,1},{1,2},{2,3},{3,0},{4,5},{5,6},{6,7},{7,4},{8,9},{9,10},{10,1... | collective-permute-start | bytes 393224 | tf_op jit(solution)/shard_map/ppermute | solution.py:317
  66.7 12.0 %collective-permute-start.21 = (bf16[256,256]{1,0:T(8,128)(2,1)S(1)}, bf16[256,256]{1,0:T(8,128)(2,1)S(1)}, u32[]{:S(2)}, u32[]{:S(2)}) collective-permute-start(bf16[256,256]{1,0:T(8,128)(2,1)S(1)} %get-tuple-element.82), channel_id=1, source_target_pairs={{0,3},{1,0},{2,1},{3,2},{4,7},{5,4},{6,5},{7,6},{8,11},{9,8},{10,9... | collective-permute-start | bytes 393224 | tf_op jit(solution)/shard_map/ppermute | solution.py:317
  68.8 11.8 %collective-permute-start.16 = (bf16[512,256]{1,0:T(8,128)(2,1)S(1)}, bf16[512,256]{1,0:T(8,128)(2,1)S(1)}, u32[]{:S(2)}, u32[]{:S(2)}) collective-permute-start(bf16[512,256]{1,0:T(8,128)(2,1)S(1)} %get-tuple-element.74), channel_id=1, source_target_pairs={{0,4},{1,5},{2,6},{3,7},{4,0},{5,1},{6,2},{7,3},{8,12},{9,13},{10,... | collective-permute-start | bytes 786440 | tf_op jit(solution)/shard_map/ppermute | solution.py:317
  79.4 2.6 %collective-permute-start.22 = (bf16[512,256]{1,0:T(8,128)(2,1)S(1)}, bf16[512,256]{1,0:T(8,128)(2,1)S(1)}, u32[]{:S(2)}, u32[]{:S(2)}) collective-permute-start(bf16[512,256]{1,0:T(8,128)(2,1)S(1)} %get-tuple-element.84), channel_id=1, source_target_pairs={{0,4},{1,5},{2,6},{3,7},{4,0},{5,1},{6,2},{7,3},{8,12},{9,13},{10,... | collective-permute-start | bytes 786440 | tf_op jit(solution)/shard_map/ppermute | solution.py:317

commit v15 on v14

--- a/solution.py
+++ b/solution.py
@@ -287,8 +287,9 @@
     outs = (shape_of(low, whole, 2 * d), shape_of(low, d, whole), sums, sums) + (block,) * len(early)
     outs = run(early, (0, 1), 0, outs, [near, far] + list(blocks[: len(early)]), 0)
     prev, (own_sums, prev_sums), dq_early = outs[:2], outs[2:4], outs[4:]
-    dq_early = (dq_early[0],) + tuple(home(dq_early[n], early[n]) for n in range(1, len(early)))
     late_blocks = tuple(blocks[len(early) :])
+    tied, late_blocks = lax.optimization_barrier((dq_early[1:], late_blocks))
+    dq_early = (dq_early[0],) + tuple(home(dq, step) for dq, step in zip(tied, early[1:]))
     wide_part = shape_of(low, half + 16, 2 * d)
     outs = (half_sums, half_sums, wide_part, shape_of(low, len(late), BLOCK, 2 * d))
     own_low, prev_high, back_a, dq_so_far = run(

time: 84.6 us -> 87.9 us (1.039)
  the two profiles are of different devices: /device:TPU:13 before, /device:TPU:0 now
where the time goes in v15:
time: 87.9 us; the launch traced here: 87.7 us
  waiting for transfers between devices  32.6 us (37%)
  starting transfers between devices  30.6 us (35%)
  Pallas kernels  21.8 us (25%)
  local copies, waits for them, and re-layouts  1.91 us (2%)
    ppermute x23, waiting for transfers between devices, moved(): return lax.ppermute(value, ('chip', 'core', 'head'), pairs)  32.6 us
    ppermute x23, starting transfers between devices, moved(): return lax.ppermute(value, ('chip', 'core', 'head'), pairs)  30.6 us
    pallas_call x13, Pallas kernels, call(): pl.pallas_call(kernel, out_shape=out_shape, in_specs=[SMEM_SPEC] + [spec]...  21.8 us
    unnamed x8, local copies, waits for them, and re-layouts  1.91 us
  transfers between devices with their start and end apart: 23, of which 14 were waited for; matrix products, arithmetic and copies ran while one was open for 0% of the time, Pallas kernels for 21%

profile of v15, /device:TPU:0, one launch (start us, length us, event | category | flops | bytes accessed | tf_op | source)
XLA Modules:
  0.0 87.7 jit_solution(5470915007767258511)
XLA Ops:
  0.6 0.1 pad_add_fusion.place_ref
  0.7 0.9 %copy-done.2 = bf16[128,1024]{1,0:T(8,128)(2,1)S(1)} copy-done((bf16[128,1024]{1,0:T(8,128)(2,1)S(1)}, bf16[128,1024]{1,0:T(8,128)(2,1)}, u32[]{:S(2)}) %copy-start.2) | copy-done | bytes 262168
  1.7 0.9 %copy-done.3 = bf16[128,1024]{1,0:T(8,128)(2,1)S(1)} copy-done((bf16[128,1024]{1,0:T(8,128)(2,1)S(1)}, bf16[128,1024]{1,0:T(8,128)(2,1)}, u32[]{:S(2)}) %copy-start.3) | copy-done | bytes 262168
  2.6 0.9 %shard_map.67 = (bf16[128,512]{1,0:T(8,128)(2,1)S(1)}, bf16[128,512]{1,0:T(8,128)(2,1)S(1)}, bf16[128,512]{1,0:T(8,128)(2,1)S(1)}, bf16[128,512]{1,0:T(8,128)(2,1)S(1)}) custom-call(s32[3]{0:T(128)S(1)} %pad_add_fusion.place_ref, bf16[128,1024]{1,0:T(8,128)(2,1)S(1)} %copy-done.2, bf16[128,1024]{1,0:T(8,128)(2,1)S(1)} %copy-done.3), custom_call_target="tpu_custom_call" | custom-call | bytes 1048588 | tf_op jit(solution)/shard_map/pallas_call | solution.py:26
  3.5 4.1 %collective-permute-start = (bf16[128,512]{1,0:T(8,128)(2,1)S(1)}, bf16[128,512]{1,0:T(8,128)(2,1)S(1)}, u32[]{:S(2)}, u32[]{:S(2)}) collective-permute-start(bf16[128,512]{1,0:T(8,128)(2,1)S(1)} %get-tuple-element.49), channel_id=1, source_target_pairs={{0,2},{1,3},{2,0},{3,1},{4,6},{5,7},{6,4},{7,5},{8,10},{9,11},{10,... | collective-permute-start | bytes 393224 | tf_op jit(solution)/shard_map/ppermute | solution.py:318
  7.6 1.6 %collective-permute-start.1 = (bf16[128,512]{1,0:T(8,128)(2,1)S(1)}, bf16[128,512]{1,0:T(8,128)(2,1)S(1)}, u32[]{:S(2)}, u32[]{:S(2)}) collective-permute-start(bf16[128,512]{1,0:T(8,128)(2,1)S(1)} %get-tuple-element.50), channel_id=1, source_target_pairs={{0,1},{1,2},{2,3},{3,0},{4,5},{5,6},{6,7},{7,4},{8,9},{9,10},{10,1... | collective-permute-start | bytes 393224 | tf_op jit(solution)/shard_map/ppermute | solution.py:318
  9.2 2.2 %collective-permute-start.2 = (bf16[128,512]{1,0:T(8,128)(2,1)S(1)}, bf16[128,512]{1,0:T(8,128)(2,1)S(1)}, u32[]{:S(2)}, u32[]{:S(2)}) collective-permute-start(bf16[128,512]{1,0:T(8,128)(2,1)S(1)} %get-tuple-element.51), channel_id=1, source_target_pairs={{0,3},{1,0},{2,1},{3,2},{4,7},{5,4},{6,5},{7,6},{8,11},{9,8},{10,9... | collective-permute-start | bytes 393224 | tf_op jit(solution)/shard_map/ppermute | solution.py:318
  11.4 6.2 %collective-permute-done.refs_1_ = bf16[128,512]{1,0:T(8,128)(2,1)S(1)} collective-permute-done((bf16[128,512]{1,0:T(8,128)(2,1)S(1)}, bf16[128,512]{1,0:T(8,128)(2,1)S(1)}, u32[]{:S(2)}, u32[]{:S(2)}) %collective-permute-start) | collective-permute-done | bytes 131104 | tf_op jit(solution)/shard_map/ppermute | solution.py:318
  17.6 0.0 collective-permute-done.1.refs_2_
  17.6 0.7 collective-permute-done.2.refs_3_
  18.3 0.6 shard_map.68
  18.9 0.1 collective-permute-start.3
  19.0 0.0 copy-done
  19.0 0.0 copy-done.1
  19.0 0.9 %shard_map.70 = (bf16[4,128,512]{2,1,0:T(8,128)(2,1)S(1)}, bf16[128,512]{1,0:T(8,128)(2,1)S(1)}, bf16[128,512]{1,0:T(8,128)(2,1)S(1)}, bf16[128,512]{1,0:T(8,128)(2,1)S(1)}, bf16[128,512]{1,0:T(8,128)(2,1)S(1)}) custom-call(s32[3]{0:T(128)S(1)} %pad_add_fusion.place_ref, bf16[128,2048]{1,0:T(8,128)(2,1)S(1)} %copy-done, bf16[128,2048]{1,0:T(8,128)(2,1)S(1)} %copy-done.1), custom_call_target="tpu_custom_call" | custom-call | bytes 2097164 | tf_op jit(solution)/shard_map/pallas_call | solution.py:26
  19.9 0.5 collective-permute-start.6
  20.5 0.1 collective-permute-start.7
  20.5 0.4 collective-permute-start.8
  21.0 0.1 collective-permute-start.9
  21.1 0.4 collective-permute-done.6.refs_0_
  21.5 0.4 collective-permute-done.7.refs_1_
  21.8 0.2 collective-permute-done.8.refs_2_
  22.0 0.3 collective-permute-done.9.refs_3_
  22.3 0.6 shard_map.71
  22.9 3.9 %collective-permute-start.10 = (bf16[272,512]{1,0:T(8,128)(2,1)S(1)}, bf16[272,512]{1,0:T(8,128)(2,1)S(1)}, u32[]{:S(2)}, u32[]{:S(2)}) collective-permute-start(bf16[272,512]{1,0:T(8,128)(2,1)S(1)} %get-tuple-element.62), channel_id=1, source_target_pairs={{0,2},{1,3},{2,0},{3,1},{4,6},{5,7},{6,4},{7,5},{8,10},{9,11},{10,... | collective-permute-start | bytes 835592 | tf_op jit(solution)/shard_map/ppermute | solution.py:318
  26.9 1.0 %collective-permute-start.5 = (bf16[512,256]{1,0:T(8,128)(2,1)S(1)}, bf16[512,256]{1,0:T(8,128)(2,1)S(1)}, u32[]{:S(2)}, u32[]{:S(2)}) collective-permute-start(bf16[512,256]{1,0:T(8,128)(2,1)S(1)} %get-tuple-element.53), channel_id=1, source_target_pairs={{0,12},{1,13},{2,14},{3,15},{4,8},{5,9},{6,10},{7,11},{8,20},{9,21... | collective-permute-start | bytes 786440 | tf_op jit(solution)/shard_map/ppermute | solution.py:318
  27.9 1.5 %collective-permute-start.4 = (bf16[512,256]{1,0:T(8,128)(2,1)S(1)}, bf16[512,256]{1,0:T(8,128)(2,1)S(1)}, u32[]{:S(2)}, u32[]{:S(2)}) collective-permute-start(bf16[512,256]{1,0:T(8,128)(2,1)S(1)} %get-tuple-element.52.mine_ref), channel_id=1, source_target_pairs={{0,8},{1,9},{2,10},{3,11},{4,12},{5,13},{6,14},{7,15},{8,16},{9,17... | collective-permute-start | bytes 786440 | tf_op jit(solution)/shard_map/ppermute | solution.py:318
  29.4 0.0 collective-permute-start.11
  29.4 0.0 collective-permute-done.3.sibling_ref
  29.4 3.8 %collective-permute-start.12 = (bf16[256,512]{1,0:T(8,128)(2,1)S(1)}, bf16[256,512]{1,0:T(8,128)(2,1)S(1)}, u32[]{:S(2)}, u32[]{:S(2)}) collective-permute-start(bf16[256,512]{1,0:T(8,128)(2,1)S(1)} %get-tuple-element.66), channel_id=1, source_target_pairs={{0,3},{1,0},{2,1},{3,2},{4,7},{5,4},{6,5},{7,6},{8,11},{9,8},{10,9... | collective-permute-start | bytes 786440 | tf_op jit(solution)/shard_map/ppermute | solution.py:318
  33.2 0.7 shard_map.69
  33.9 2.4 %collective-permute-done.5.b_ref = bf16[512,256]{1,0:T(8,128)(2,1)S(1)} collective-permute-done((bf16[512,256]{1,0:T(8,128)(2,1)S(1)}, bf16[512,256]{1,0:T(8,128)(2,1)S(1)}, u32[]{:S(2)}, u32[]{:S(2)}) %collective-permute-start.5) | collective-permute-done | bytes 262176 | tf_op jit(solution)/shard_map/ppermute | solution.py:318
  36.3 5.7 %collective-permute-done.4.a_ref = bf16[512,256]{1,0:T(8,128)(2,1)S(1)} collective-permute-done((bf16[512,256]{1,0:T(8,128)(2,1)S(1)}, bf16[512,256]{1,0:T(8,128)(2,1)S(1)}, u32[]{:S(2)}, u32[]{:S(2)}) %collective-permute-start.4) | collective-permute-done | bytes 262176 | tf_op jit(solution)/shard_map/ppermute | solution.py:318
  42.0 3.8 %collective-permute-done.10.refs_1_ = bf16[272,512]{1,0:T(8,128)(2,1)S(1)} collective-permute-done((bf16[272,512]{1,0:T(8,128)(2,1)S(1)}, bf16[272,512]{1,0:T(8,128)(2,1)S(1)}, u32[]{:S(2)}, u32[]{:S(2)}) %collective-permute-start.10) | collective-permute-done | bytes 278560 | tf_op jit(solution)/shard_map/ppermute | solution.py:318
  45.8 6.0 %shard_map.72 = (bf16[1024,256]{1,0:T(8,128)(2,1)S(1)}, bf16[128,1024]{1,0:T(8,128)(2,1)S(1)}, f32[1024,256]{1,0:T(8,128)S(1)}, f32[1024,256]{1,0:T(8,128)S(1)},...) custom-call(s32[3]{0:T(128)S(1)} %pad_add_fusion.place_ref, bf16[1024,256]{1,0:T(8,128)(2,1)S(1)} %get-tuple-element.54.own_ref, ...), custom_call_target="tpu_custom_call" | custom-call | flops 1 | bytes 4997132 | tf_op jit(solution)/shard_map/pallas_call | solution.py:26
  51.8 0.0 collective-permute-done.11.refs_0_
  51.8 0.0 collective-permute-done.12.refs_1_
  51.8 0.1 collective-permute-start.13
  51.9 3.8 %shard_map.73 = (f32[512,256]{1,0:T(8,128)S(1)}, f32[512,256]{1,0:T(8,128)S(1)}, bf16[528,256]{1,0:T(8,128)(2,1)S(1)}, bf16[2,128,256]{2,1,0:T(8,128)(2,1)S(1)}) custom-call(s32[3]{0:T(128)S(1)} %pad_add_fusion.place_ref, bf16[1024,256]{1,0:T(8,128)(2,1)S(1)} %get-tuple-element.54.own_ref, bf16[128,1024]{1,0:T(8,128)(2,1)S(1)} %get-tuple-element.55.own_kt_ref, ...), custom_call_target="tpu_custom_call" | custom-call | flops 1 | bytes 5644300 | tf_op jit(solution)/shard_map/pallas_call | solution.py:26
  55.7 2.5 %collective-permute-start.17 = (bf16[528,256]{1,0:T(8,128)(2,1)S(1)}, bf16[528,256]{1,0:T(8,128)(2,1)S(1)}, u32[]{:S(2)}, u32[]{:S(2)}) collective-permute-start(bf16[528,256]{1,0:T(8,128)(2,1)S(1)} %get-tuple-element.83), channel_id=1, source_target_pairs={{0,24},{1,25},{2,26},{3,27},{4,28},{5,29},{6,30},{7,31},{8,0},{9,1... | collective-permute-start | bytes 811016 | tf_op jit(solution)/shard_map/ppermute | solution.py:318
  58.2 1.9 %collective-permute-done.13.refs_1_ = bf16[256,256]{1,0:T(8,128)(2,1)S(1)} collective-permute-done((bf16[256,256]{1,0:T(8,128)(2,1)S(1)}, bf16[256,256]{1,0:T(8,128)(2,1)S(1)}, u32[]{:S(2)}, u32[]{:S(2)}) %collective-permute-start.13) | collective-permute-done | bytes 131104 | tf_op jit(solution)/shard_map/ppermute | solution.py:318
  60.1 3.6 %shard_map.74 = (f32[512,256]{1,0:T(8,128)S(1)}, f32[512,256]{1,0:T(8,128)S(1)}, bf16[512,256]{1,0:T(8,128)(2,1)S(1)}, bf16[256,256]{1,0:T(8,128)(2,1)S(1)}, bf16[256,256]{1,0:T(8,128)(2,1)S(1)}) custom-call(s32[3]{0:T(128)S(1)} %pad_add_fusion.place_ref, bf16[1024,256]{1,0:T(8,128)(2,1)S(1)} %get-tuple-element.54.own_ref, ...), custom_call_target="tpu_custom_call" | custom-call | flops 1 | bytes 5906444 | tf_op jit(solution)/shard_map/pallas_call | solution.py:26
  63.7 2.5 %collective-permute-start.18 = (bf16[512,256]{1,0:T(8,128)(2,1)S(1)}, bf16[512,256]{1,0:T(8,128)(2,1)S(1)}, u32[]{:S(2)}, u32[]{:S(2)}) collective-permute-start(bf16[512,256]{1,0:T(8,128)(2,1)S(1)} %get-tuple-element.84), channel_id=1, source_target_pairs={{0,24},{1,25},{2,26},{3,27},{4,28},{5,29},{6,30},{7,31},{8,0},{9,1... | collective-permute-start | bytes 786440 | tf_op jit(solution)/shard_map/ppermute | solution.py:318
  66.2 0.3 collective-permute-start.14
  66.5 1.8 %collective-permute-start.15 = (bf16[256,256]{1,0:T(8,128)(2,1)S(1)}, bf16[256,256]{1,0:T(8,128)(2,1)S(1)}, u32[]{:S(2)}, u32[]{:S(2)}) collective-permute-start(bf16[256,256]{1,0:T(8,128)(2,1)S(1)} %get-tuple-element.78), channel_id=1, source_target_pairs={{0,1},{1,2},{2,3},{3,0},{4,5},{5,6},{6,7},{7,4},{8,9},{9,10},{10,1... | collective-permute-start | bytes 393224 | tf_op jit(solution)/shard_map/ppermute | solution.py:318
  68.3 0.0 collective-permute-done.17.back_a_ref
  68.3 3.7 %collective-permute-done.18.back_b_ref = bf16[512,256]{1,0:T(8,128)(2,1)S(1)} collective-permute-done((bf16[512,256]{1,0:T(8,128)(2,1)S(1)}, bf16[512,256]{1,0:T(8,128)(2,1)S(1)}, u32[]{:S(2)}, u32[]{:S(2)}) %collective-permute-start.18) | collective-permute-done | bytes 262176 | tf_op jit(solution)/shard_map/ppermute | solution.py:318
  72.0 0.7 shard_map.77
  72.7 0.1 collective-permute-start.19
  72.7 0.1 collective-permute-start.20
  72.9 3.8 %collective-permute-start.21 = (bf16[256,256]{1,0:T(8,128)(2,1)S(1)}, bf16[256,256]{1,0:T(8,128)(2,1)S(1)}, u32[]{:S(2)}, u32[]{:S(2)}) collective-permute-start(bf16[256,256]{1,0:T(8,128)(2,1)S(1)} %get-tuple-element.88), channel_id=1, source_target_pairs={{0,3},{1,0},{2,1},{3,2},{4,7},{5,4},{6,5},{7,6},{8,11},{9,8},{10,9... | collective-permute-start | bytes 393224 | tf_op jit(solution)/shard_map/ppermute | solution.py:318
  76.6 0.0 collective-permute-done.14.refs_2_
  76.6 0.0 collective-permute-done.15.refs_3_
  76.6 0.6 shard_map.75
  77.2 0.1 collective-permute-start.16
  77.3 4.7 %collective-permute-done.19.refs_1_ = bf16[256,256]{1,0:T(8,128)(2,1)S(1)} collective-permute-done((bf16[256,256]{1,0:T(8,128)(2,1)S(1)}, bf16[256,256]{1,0:T(8,128)(2,1)S(1)}, u32[]{:S(2)}, u32[]{:S(2)}) %collective-permute-start.19) | collective-permute-done | bytes 131104 | tf_op jit(solution)/shard_map/ppermute | solution.py:318
  82.0 0.0 collective-permute-done.20.refs_2_
  82.0 2.1 %collective-permute-done.21.refs_3_ = bf16[256,256]{1,0:T(8,128)(2,1)S(1)} collective-permute-done((bf16[256,256]{1,0:T(8,128)(2,1)S(1)}, bf16[256,256]{1,0:T(8,128)(2,1)S(1)}, u32[]{:S(2)}, u32[]{:S(2)}) %collective-permute-start.21) | collective-permute-done | bytes 131104 | tf_op jit(solution)/shard_map/ppermute | solution.py:318
  84.1 0.6 shard_map.78
  84.6 0.1 collective-permute-start.22
  84.7 0.0 collective-permute-done.16.sibling_ref
  84.7 1.4 %shard_map.76 = bf16[128,2048]{1,0:T(8,128)(2,1)} custom-call(s32[3]{0:T(128)S(1)} %pad_add_fusion.place_ref, bf16[512,256]{1,0:T(8,128)(2,1)S(1)} %get-tuple-element.79.mine_ref, bf16[512,256]{1,0:T(8,128)(2,1)S(1)} %collective-permute-done.16.sibling_ref), custom_call_target="tpu_custom_call" | custom-call | bytes 1048588 | tf_op jit(solution)/shard_map/pallas_call | solution.py:26
  86.1 0.1 collective-permute-done.22.sibling_ref
  86.2 1.5 %shard_map.79 = (bf16[128,1024]{1,0:T(8,128)(2,1)}, bf16[128,1024]{1,0:T(8,128)(2,1)}) custom-call(s32[3]{0:T(128)S(1)} %pad_add_fusion.place_ref, bf16[512,256]{1,0:T(8,128)(2,1)S(1)} %get-tuple-element.89.mine_ref, bf16[512,256]{1,0:T(8,128)(2,1)S(1)} %collective-permute-done.22.sibling_ref), custom_call_target="tpu_custom_call" | custom-call | bytes 1048588 | tf_op jit(solution)/shard_map/pallas_call | solution.py:26
  (6 shorter events, 0.0 us)
Async XLA Ops:
  0.7 1.0 %copy-start.2 = (bf16[128,1024]{1,0:T(8,128)(2,1)S(1)}, bf16[128,1024]{1,0:T(8,128)(2,1)}, u32[]{:S(2)}) copy-start(bf16[128,1024]{1,0:T(8,128)(2,1)} %k_ref.1) | copy-start | bytes 786436
  1.7 0.9 %copy-start.3 = (bf16[128,1024]{1,0:T(8,128)(2,1)S(1)}, bf16[128,1024]{1,0:T(8,128)(2,1)}, u32[]{:S(2)}) copy-start(bf16[128,1024]{1,0:T(8,128)(2,1)} %v_ref.1) | copy-start | bytes 786436
  2.6 16.4 %copy-start = (bf16[128,2048]{1,0:T(8,128)(2,1)S(1)}, bf16[128,2048]{1,0:T(8,128)(2,1)}, u32[]{:S(2)}) copy-start(bf16[128,2048]{1,0:T(8,128)(2,1)} %q_ref.1) | copy-start | bytes 1572868
  2.6 16.4 %copy-start.1 = (bf16[128,2048]{1,0:T(8,128)(2,1)S(1)}, bf16[128,2048]{1,0:T(8,128)(2,1)}, u32[]{:S(2)}) copy-start(bf16[128,2048]{1,0:T(8,128)(2,1)} %g_ref.1) | copy-start | bytes 1572868
  3.5 14.1 %collective-permute-start = (bf16[128,512]{1,0:T(8,128)(2,1)S(1)}, bf16[128,512]{1,0:T(8,128)(2,1)S(1)}, u32[]{:S(2)}, u32[]{:S(2)}) collective-permute-start(bf16[128,512]{1,0:T(8,128)(2,1)S(1)} %get-tuple-element.49), channel_id=1, source_target_pairs={{0,2},{1,3},{2,0},{3,1},{4,6},{5,7},{6,4},{7,5},{8,10},{9,11},{10,... | collective-permute-start | bytes 393224 | tf_op jit(solution)/shard_map/ppermute | solution.py:318
  7.6 10.0 %collective-permute-start.1 = (bf16[128,512]{1,0:T(8,128)(2,1)S(1)}, bf16[128,512]{1,0:T(8,128)(2,1)S(1)}, u32[]{:S(2)}, u32[]{:S(2)}) collective-permute-start(bf16[128,512]{1,0:T(8,128)(2,1)S(1)} %get-tuple-element.50), channel_id=1, source_target_pairs={{0,1},{1,2},{2,3},{3,0},{4,5},{5,6},{6,7},{7,4},{8,9},{9,10},{10,1... | collective-permute-start | bytes 393224 | tf_op jit(solution)/shard_map/ppermute | solution.py:318
  9.2 9.1 %collective-permute-start.2 = (bf16[128,512]{1,0:T(8,128)(2,1)S(1)}, bf16[128,512]{1,0:T(8,128)(2,1)S(1)}, u32[]{:S(2)}, u32[]{:S(2)}) collective-permute-start(bf16[128,512]{1,0:T(8,128)(2,1)S(1)} %get-tuple-element.51), channel_id=1, source_target_pairs={{0,3},{1,0},{2,1},{3,2},{4,7},{5,4},{6,5},{7,6},{8,11},{9,8},{10,9... | collective-permute-start | bytes 393224 | tf_op jit(solution)/shard_map/ppermute | solution.py:318
  18.9 10.5 %collective-permute-start.3 = (bf16[512,256]{1,0:T(8,128)(2,1)S(1)}, bf16[512,256]{1,0:T(8,128)(2,1)S(1)}, u32[]{:S(2)}, u32[]{:S(2)}) collective-permute-start(bf16[512,256]{1,0:T(8,128)(2,1)S(1)} %get-tuple-element.53), channel_id=1, source_target_pairs={{0,4},{1,5},{2,6},{3,7},{4,0},{5,1},{6,2},{7,3},{8,12},{9,13},{10,... | collective-permute-start | bytes 786440 | tf_op jit(solution)/shard_map/ppermute | solution.py:318
  19.9 1.5 %collective-permute-start.6 = (bf16[128,512]{1,0:T(8,128)(2,1)S(1)}, bf16[128,512]{1,0:T(8,128)(2,1)S(1)}, u32[]{:S(2)}, u32[]{:S(2)}) collective-permute-start(bf16[128,512]{1,0:T(8,128)(2,1)S(1)} %get-tuple-element.57), channel_id=1, source_target_pairs={{0,4},{1,5},{2,6},{3,7},{4,0},{5,1},{6,2},{7,3},{8,12},{9,13},{10,... | collective-permute-start | bytes 393224 | tf_op jit(solution)/shard_map/ppermute | solution.py:318
  20.5 1.3 %collective-permute-start.7 = (bf16[128,512]{1,0:T(8,128)(2,1)S(1)}, bf16[128,512]{1,0:T(8,128)(2,1)S(1)}, u32[]{:S(2)}, u32[]{:S(2)}) collective-permute-start(bf16[128,512]{1,0:T(8,128)(2,1)S(1)} %get-tuple-element.58), channel_id=1, source_target_pairs={{0,4},{1,5},{2,6},{3,7},{4,0},{5,1},{6,2},{7,3},{8,12},{9,13},{10,... | collective-permute-start | bytes 393224 | tf_op jit(solution)/shard_map/ppermute | solution.py:318
  20.5 1.5 %collective-permute-start.8 = (bf16[128,512]{1,0:T(8,128)(2,1)S(1)}, bf16[128,512]{1,0:T(8,128)(2,1)S(1)}, u32[]{:S(2)}, u32[]{:S(2)}) collective-permute-start(bf16[128,512]{1,0:T(8,128)(2,1)S(1)} %get-tuple-element.59), channel_id=1, source_target_pairs={{0,4},{1,5},{2,6},{3,7},{4,0},{5,1},{6,2},{7,3},{8,12},{9,13},{10,... | collective-permute-start | bytes 393224 | tf_op jit(solution)/shard_map/ppermute | solution.py:318
  21.0 1.3 %collective-permute-start.9 = (bf16[128,512]{1,0:T(8,128)(2,1)S(1)}, bf16[128,512]{1,0:T(8,128)(2,1)S(1)}, u32[]{:S(2)}, u32[]{:S(2)}) collective-permute-start(bf16[128,512]{1,0:T(8,128)(2,1)S(1)} %get-tuple-element.60), channel_id=1, source_target_pairs={{0,4},{1,5},{2,6},{3,7},{4,0},{5,1},{6,2},{7,3},{8,12},{9,13},{10,... | collective-permute-start | bytes 393224 | tf_op jit(solution)/shard_map/ppermute | solution.py:318
  22.9 22.8 %collective-permute-start.10 = (bf16[272,512]{1,0:T(8,128)(2,1)S(1)}, bf16[272,512]{1,0:T(8,128)(2,1)S(1)}, u32[]{:S(2)}, u32[]{:S(2)}) collective-permute-start(bf16[272,512]{1,0:T(8,128)(2,1)S(1)} %get-tuple-element.62), channel_id=1, source_target_pairs={{0,2},{1,3},{2,0},{3,1},{4,6},{5,7},{6,4},{7,5},{8,10},{9,11},{10,... | collective-permute-start | bytes 835592 | tf_op jit(solution)/shard_map/ppermute | solution.py:318
  26.9 9.4 %collective-permute-start.5 = (bf16[512,256]{1,0:T(8,128)(2,1)S(1)}, bf16[512,256]{1,0:T(8,128)(2,1)S(1)}, u32[]{:S(2)}, u32[]{:S(2)}) collective-permute-start(bf16[512,256]{1,0:T(8,128)(2,1)S(1)} %get-tuple-element.53), channel_id=1, source_target_pairs={{0,12},{1,13},{2,14},{3,15},{4,8},{5,9},{6,10},{7,11},{8,20},{9,21... | collective-permute-start | bytes 786440 | tf_op jit(solution)/shard_map/ppermute | solution.py:318
  27.9 14.1 %collective-permute-start.4 = (bf16[512,256]{1,0:T(8,128)(2,1)S(1)}, bf16[512,256]{1,0:T(8,128)(2,1)S(1)}, u32[]{:S(2)}, u32[]{:S(2)}) collective-permute-start(bf16[512,256]{1,0:T(8,128)(2,1)S(1)} %get-tuple-element.52.mine_ref), channel_id=1, source_target_pairs={{0,8},{1,9},{2,10},{3,11},{4,12},{5,13},{6,14},{7,15},{8,16},{9,17... | collective-permute-start | bytes 786440 | tf_op jit(solution)/shard_map/ppermute | solution.py:318
  29.4 22.4 %collective-permute-start.11 = (bf16[256,512]{1,0:T(8,128)(2,1)S(1)}, bf16[256,512]{1,0:T(8,128)(2,1)S(1)}, u32[]{:S(2)}, u32[]{:S(2)}) collective-permute-start(bf16[256,512]{1,0:T(8,128)(2,1)S(1)} %get-tuple-element.65), channel_id=1, source_target_pairs={{0,1},{1,2},{2,3},{3,0},{4,5},{5,6},{6,7},{7,4},{8,9},{9,10},{10,1... | collective-permute-start | bytes 786440 | tf_op jit(solution)/shard_map/ppermute | solution.py:318
  29.4 22.4 %collective-permute-start.12 = (bf16[256,512]{1,0:T(8,128)(2,1)S(1)}, bf16[256,512]{1,0:T(8,128)(2,1)S(1)}, u32[]{:S(2)}, u32[]{:S(2)}) collective-permute-start(bf16[256,512]{1,0:T(8,128)(2,1)S(1)} %get-tuple-element.66), channel_id=1, source_target_pairs={{0,3},{1,0},{2,1},{3,2},{4,7},{5,4},{6,5},{7,6},{8,11},{9,8},{10,9... | collective-permute-start | bytes 786440 | tf_op jit(solution)/shard_map/ppermute | solution.py:318
  51.8 8.3 %collective-permute-start.13 = (bf16[256,256]{1,0:T(8,128)(2,1)S(1)}, bf16[256,256]{1,0:T(8,128)(2,1)S(1)}, u32[]{:S(2)}, u32[]{:S(2)}) collective-permute-start(bf16[256,256]{1,0:T(8,128)(2,1)S(1)} %get-tuple-element.67), channel_id=1, source_target_pairs={{0,2},{1,3},{2,0},{3,1},{4,6},{5,7},{6,4},{7,5},{8,10},{9,11},{10,... | collective-permute-start | bytes 393224 | tf_op jit(solution)/shard_map/ppermute | solution.py:318
  55.7 12.6 %collective-permute-start.17 = (bf16[528,256]{1,0:T(8,128)(2,1)S(1)}, bf16[528,256]{1,0:T(8,128)(2,1)S(1)}, u32[]{:S(2)}, u32[]{:S(2)}) collective-permute-start(bf16[528,256]{1,0:T(8,128)(2,1)S(1)} %get-tuple-element.83), channel_id=1, source_target_pairs={{0,24},{1,25},{2,26},{3,27},{4,28},{5,29},{6,30},{7,31},{8,0},{9,1... | collective-permute-start | bytes 811016 | tf_op jit(solution)/shard_map/ppermute | solution.py:318
  63.7 8.3 %collective-permute-start.18 = (bf16[512,256]{1,0:T(8,128)(2,1)S(1)}, bf16[512,256]{1,0:T(8,128)(2,1)S(1)}, u32[]{:S(2)}, u32[]{:S(2)}) collective-permute-start(bf16[512,256]{1,0:T(8,128)(2,1)S(1)} %get-tuple-element.84), channel_id=1, source_target_pairs={{0,24},{1,25},{2,26},{3,27},{4,28},{5,29},{6,30},{7,31},{8,0},{9,1... | collective-permute-start | bytes 786440 | tf_op jit(solution)/shard_map/ppermute | solution.py:318
  66.2 10.4 %collective-permute-start.14 = (bf16[256,256]{1,0:T(8,128)(2,1)S(1)}, bf16[256,256]{1,0:T(8,128)(2,1)S(1)}, u32[]{:S(2)}, u32[]{:S(2)}) collective-permute-start(bf16[256,256]{1,0:T(8,128)(2,1)S(1)} %get-tuple-element.77), channel_id=1, source_target_pairs={{0,3},{1,0},{2,1},{3,2},{4,7},{5,4},{6,5},{7,6},{8,11},{9,8},{10,9... | collective-permute-start | bytes 393224 | tf_op jit(solution)/shard_map/ppermute | solution.py:318
  66.5 10.1 %collective-permute-start.15 = (bf16[256,256]{1,0:T(8,128)(2,1)S(1)}, bf16[256,256]{1,0:T(8,128)(2,1)S(1)}, u32[]{:S(2)}, u32[]{:S(2)}) collective-permute-start(bf16[256,256]{1,0:T(8,128)(2,1)S(1)} %get-tuple-element.78), channel_id=1, source_target_pairs={{0,1},{1,2},{2,3},{3,0},{4,5},{5,6},{6,7},{7,4},{8,9},{9,10},{10,1... | collective-permute-start | bytes 393224 | tf_op jit(solution)/shard_map/ppermute | solution.py:318
  72.7 9.3 %collective-permute-start.19 = (bf16[256,256]{1,0:T(8,128)(2,1)S(1)}, bf16[256,256]{1,0:T(8,128)(2,1)S(1)}, u32[]{:S(2)}, u32[]{:S(2)}) collective-permute-start(bf16[256,256]{1,0:T(8,128)(2,1)S(1)} %get-tuple-element.86), channel_id=1, source_target_pairs={{0,2},{1,3},{2,0},{3,1},{4,6},{5,7},{6,4},{7,5},{8,10},{9,11},{10,... | collective-permute-start | bytes 393224 | tf_op jit(solution)/shard_map/ppermute | solution.py:318
  72.7 9.3 %collective-permute-start.20 = (bf16[256,256]{1,0:T(8,128)(2,1)S(1)}, bf16[256,256]{1,0:T(8,128)(2,1)S(1)}, u32[]{:S(2)}, u32[]{:S(2)}) collective-permute-start(bf16[256,256]{1,0:T(8,128)(2,1)S(1)} %get-tuple-element.87), channel_id=1, source_target_pairs={{0,1},{1,2},{2,3},{3,0},{4,5},{5,6},{6,7},{7,4},{8,9},{9,10},{10,1... | collective-permute-start | bytes 393224 | tf_op jit(solution)/shard_map/ppermute | solution.py:318
  72.9 11.2 %collective-permute-start.21 = (bf16[256,256]{1,0:T(8,128)(2,1)S(1)}, bf16[256,256]{1,0:T(8,128)(2,1)S(1)}, u32[]{:S(2)}, u32[]{:S(2)}) collective-permute-start(bf16[256,256]{1,0:T(8,128)(2,1)S(1)} %get-tuple-element.88), channel_id=1, source_target_pairs={{0,3},{1,0},{2,1},{3,2},{4,7},{5,4},{6,5},{7,6},{8,11},{9,8},{10,9... | collective-permute-start | bytes 393224 | tf_op jit(solution)/shard_map/ppermute | solution.py:318
  77.2 7.5 %collective-permute-start.16 = (bf16[512,256]{1,0:T(8,128)(2,1)S(1)}, bf16[512,256]{1,0:T(8,128)(2,1)S(1)}, u32[]{:S(2)}, u32[]{:S(2)}) collective-permute-start(bf16[512,256]{1,0:T(8,128)(2,1)S(1)} %get-tuple-element.80), channel_id=1, source_target_pairs={{0,4},{1,5},{2,6},{3,7},{4,0},{5,1},{6,2},{7,3},{8,12},{9,13},{10,... | collective-permute-start | bytes 786440 | tf_op jit(solution)/shard_map/ppermute | solution.py:318
  84.6 1.6 %collective-permute-start.22 = (bf16[512,256]{1,0:T(8,128)(2,1)S(1)}, bf16[512,256]{1,0:T(8,128)(2,1)S(1)}, u32[]{:S(2)}, u32[]{:S(2)}) collective-permute-start(bf16[512,256]{1,0:T(8,128)(2,1)S(1)} %get-tuple-element.90), channel_id=1, source_target_pairs={{0,4},{1,5},{2,6},{3,7},{4,0},{5,1},{6,2},{7,3},{8,12},{9,13},{10,... | collective-permute-start | bytes 786440 | tf_op jit(solution)/shard_map/ppermute | solution.py:318

commit v16 on v14

--- a/solution.py
+++ b/solution.py
@@ -119,7 +119,7 @@
 
 
 def sort_kernel(heads, place_ref, *refs):
-    in_refs, (mine_ref, other_ref) = refs[:heads], refs[heads:]
+    in_refs, (after_ref, mine_ref, other_ref) = refs[:heads], refs[heads:]
     core = place_ref[1]
     for k, in_ref in enumerate(in_refs):
         mine_ref[k * BLOCK : (k + 1) * BLOCK] = in_ref[at(core * BLOCK, BLOCK)]
@@ -289,7 +289,7 @@
     prev, (own_sums, prev_sums), dq_early = outs[:2], outs[2:4], outs[4:]
     dq_early = (dq_early[0],) + tuple(home(dq_early[n], early[n]) for n in range(1, len(early)))
     late_blocks = tuple(blocks[len(early) :])
-    wide_part = shape_of(low, half + 16, 2 * d)
+    wide_part = shape_of(low, half + 32, 2 * d)
     outs = (half_sums, half_sums, wide_part, shape_of(low, len(late), BLOCK, 2 * d))
     own_low, prev_high, back_a, dq_so_far = run(
         late, (0,), 1, outs, prev + late_blocks + (own_sums, prev_sums), 1
@@ -298,7 +298,7 @@
         late,
         (1,),
         2,
-        (half_sums, half_sums, part) + (block,) * len(late),
+        (half_sums, half_sums, shape_of(low, half + 16, 2 * d)) + (block,) * len(late),
         prev + late_blocks + (own_low, own_sums, prev_high, dq_so_far, dq_early[-1][:16]),
         2,
     )
@@ -365,15 +365,15 @@
     back = [across(part, chip_step=-1, flip=0) for part in partial]
     halves = shape_of(low, heads * rows, 2 * d)
     totals = spread(call(bind(add_kernel), (shape_of(low, 2 * rows, 2 * d),) * heads, (place, *own_sums, *back)))
-    kv_mine, kv_other = call(bind(sort_kernel), (halves, halves), (place,) + totals)
-    kv_sibling = across(kv_other, chip_step=0, flip=1)
     dq_mine, dq_other = call(
-        bind(sort_kernel), (shape_of(low, heads * rows, 2 * d),) * 2, (place,) + tuple(dqs)
+        bind(sort_kernel), (halves, halves), (place,) + tuple(dqs) + (near[:16, :d],)
     )
     dq_sibling = across(dq_other, chip_step=0, flip=1)
     query_grad = copy_call(
         bind(unpack_dq_kernel), 2 * heads, shape_of(low, *query_rows.shape), (place, dq_mine, dq_sibling)
     )
+    kv_mine, kv_other = call(bind(sort_kernel), (halves, halves), (place,) + totals + (query_grad[:16, :d],))
+    kv_sibling = across(kv_other, chip_step=0, flip=1)
     key_grad, value_grad = call(
         bind(unpack_kv_kernel), (shape_of(low, *key_rows.shape),) * 2, (place, kv_mine, kv_sibling)
     )

time: 84.6 us -> 87.6 us (1.035)
  starting transfers between devices: 23 us -> 24.6 us
    ppermute x23, starting transfers between devices: 23 us -> 24.6 us  [moved(): return lax.ppermute(value, ('chip', 'core', 'head'), pairs)]
  transfers between devices with their start and end apart: 23 -> 23, of which waited for: 11 -> 11; matrix products, arithmetic and copies ran while one was open for 0% -> 1% of each run, Pallas kernels for 23% -> 22%
where the time goes in v16:
time: 87.6 us; the launch traced here: 86.3 us
  waiting for transfers between devices  35.4 us (40%)
  starting transfers between devices  24.6 us (28%)
  Pallas kernels  21.8 us (25%)
  local copies, waits for them, and re-layouts  3.69 us (4%)
    ppermute x23, waiting for transfers between devices, moved(): return lax.ppermute(value, ('chip', 'core', 'head'), pairs)  35.4 us
    ppermute x23, starting transfers between devices, moved(): return lax.ppermute(value, ('chip', 'core', 'head'), pairs)  24.6 us
    pallas_call x13, Pallas kernels, call(): pl.pallas_call(kernel, out_shape=out_shape, in_specs=[SMEM_SPEC] + [spec]...  21.8 us
    unnamed x8, local copies, waits for them, and re-layouts  2.99 us
  transfers between devices with their start and end apart: 23, of which 11 were waited for; matrix products, arithmetic and copies ran while one was open for 1% of the time, Pallas kernels for 22%

profile of v16, /device:TPU:13, one launch (start us, length us, event | category | flops | bytes accessed | tf_op | source)
XLA Modules:
  0.0 86.3 jit_solution(2513885607682522676)
XLA Ops:
  0.6 0.1 pad_add_fusion.place_ref
  0.7 1.0 %copy-done.2 = bf16[128,1024]{1,0:T(8,128)(2,1)S(1)} copy-done((bf16[128,1024]{1,0:T(8,128)(2,1)S(1)}, bf16[128,1024]{1,0:T(8,128)(2,1)}, u32[]{:S(2)}) %copy-start.2) | copy-done | bytes 262168
  1.7 0.9 %copy-done.3 = bf16[128,1024]{1,0:T(8,128)(2,1)S(1)} copy-done((bf16[128,1024]{1,0:T(8,128)(2,1)S(1)}, bf16[128,1024]{1,0:T(8,128)(2,1)}, u32[]{:S(2)}) %copy-start.3) | copy-done | bytes 262168
  2.7 0.9 %shard_map.67 = (bf16[128,512]{1,0:T(8,128)(2,1)S(1)}, bf16[128,512]{1,0:T(8,128)(2,1)S(1)}, bf16[128,512]{1,0:T(8,128)(2,1)S(1)}, bf16[128,512]{1,0:T(8,128)(2,1)S(1)}) custom-call(s32[3]{0:T(128)S(1)} %pad_add_fusion.place_ref, bf16[128,1024]{1,0:T(8,128)(2,1)S(1)} %copy-done.2, bf16[128,1024]{1,0:T(8,128)(2,1)S(1)} %copy-done.3), custom_call_target="tpu_custom_call" | custom-call | bytes 1048588 | tf_op jit(solution)/shard_map/pallas_call | solution.py:26
  3.6 2.4 %collective-permute-start = (bf16[128,512]{1,0:T(8,128)(2,1)S(1)}, bf16[128,512]{1,0:T(8,128)(2,1)S(1)}, u32[]{:S(2)}, u32[]{:S(2)}) collective-permute-start(bf16[128,512]{1,0:T(8,128)(2,1)S(1)} %get-tuple-element.46), channel_id=1, source_target_pairs={{0,2},{1,3},{2,0},{3,1},{4,6},{5,7},{6,4},{7,5},{8,10},{9,11},{10,... | collective-permute-start | bytes 393224 | tf_op jit(solution)/shard_map/ppermute | solution.py:317
  5.9 0.0 collective-permute-start.1
  5.9 1.5 %collective-permute-start.2 = (bf16[128,512]{1,0:T(8,128)(2,1)S(1)}, bf16[128,512]{1,0:T(8,128)(2,1)S(1)}, u32[]{:S(2)}, u32[]{:S(2)}) collective-permute-start(bf16[128,512]{1,0:T(8,128)(2,1)S(1)} %get-tuple-element.48), channel_id=1, source_target_pairs={{0,3},{1,0},{2,1},{3,2},{4,7},{5,4},{6,5},{7,6},{8,11},{9,8},{10,9... | collective-permute-start | bytes 393224 | tf_op jit(solution)/shard_map/ppermute | solution.py:317
  7.4 1.0 %copy-done.1 = bf16[128,2048]{1,0:T(8,128)(2,1)S(1)} copy-done((bf16[128,2048]{1,0:T(8,128)(2,1)S(1)}, bf16[128,2048]{1,0:T(8,128)(2,1)}, u32[]{:S(2)}) %copy-start.1) | copy-done | bytes 524312
  8.5 0.9 %shard_map.70 = (bf16[4,128,512]{2,1,0:T(8,128)(2,1)S(1)}, bf16[128,512]{1,0:T(8,128)(2,1)S(1)}, bf16[128,512]{1,0:T(8,128)(2,1)S(1)}, bf16[128,512]{1,0:T(8,128)(2,1)S(1)}, bf16[128,512]{1,0:T(8,128)(2,1)S(1)}) custom-call(s32[3]{0:T(128)S(1)} %pad_add_fusion.place_ref, bf16[128,2048]{1,0:T(8,128)(2,1)S(1)} %copy-done, bf16[128,2048]{1,0:T(8,128)(2,1)S(1)} %copy-done.1), custom_call_target="tpu_custom_call" | custom-call | bytes 2097164 | tf_op jit(solution)/shard_map/pallas_call | solution.py:26
  9.4 1.6 %collective-permute-start.6 = (bf16[128,512]{1,0:T(8,128)(2,1)S(1)}, bf16[128,512]{1,0:T(8,128)(2,1)S(1)}, u32[]{:S(2)}, u32[]{:S(2)}) collective-permute-start(bf16[128,512]{1,0:T(8,128)(2,1)S(1)} %get-tuple-element.54), channel_id=1, source_target_pairs={{0,4},{1,5},{2,6},{3,7},{4,0},{5,1},{6,2},{7,3},{8,12},{9,13},{10,... | collective-permute-start | bytes 393224 | tf_op jit(solution)/shard_map/ppermute | solution.py:317
  10.9 0.1 collective-permute-start.7
  11.0 1.4 %collective-permute-done.refs_1_ = bf16[128,512]{1,0:T(8,128)(2,1)S(1)} collective-permute-done((bf16[128,512]{1,0:T(8,128)(2,1)S(1)}, bf16[128,512]{1,0:T(8,128)(2,1)S(1)}, u32[]{:S(2)}, u32[]{:S(2)}) %collective-permute-start) | collective-permute-done | bytes 131104 | tf_op jit(solution)/shard_map/ppermute | solution.py:317
  12.4 0.9 %collective-permute-start.8 = (bf16[128,512]{1,0:T(8,128)(2,1)S(1)}, bf16[128,512]{1,0:T(8,128)(2,1)S(1)}, u32[]{:S(2)}, u32[]{:S(2)}) collective-permute-start(bf16[128,512]{1,0:T(8,128)(2,1)S(1)} %get-tuple-element.56), channel_id=1, source_target_pairs={{0,4},{1,5},{2,6},{3,7},{4,0},{5,1},{6,2},{7,3},{8,12},{9,13},{10,... | collective-permute-start | bytes 393224 | tf_op jit(solution)/shard_map/ppermute | solution.py:317
  13.3 4.1 %collective-permute-done.1.refs_2_ = bf16[128,512]{1,0:T(8,128)(2,1)S(1)} collective-permute-done((bf16[128,512]{1,0:T(8,128)(2,1)S(1)}, bf16[128,512]{1,0:T(8,128)(2,1)S(1)}, u32[]{:S(2)}, u32[]{:S(2)}) %collective-permute-start.1) | collective-permute-done | bytes 131104 | tf_op jit(solution)/shard_map/ppermute | solution.py:317
  17.5 0.5 collective-permute-start.9
  18.0 0.0 collective-permute-done.2.refs_3_
  18.0 0.6 shard_map.68
  18.6 0.1 collective-permute-start.3
  18.6 0.0 collective-permute-done.6.refs_0_
  18.7 0.0 collective-permute-done.7.refs_1_
  18.7 0.0 collective-permute-done.8.refs_2_
  18.7 0.3 collective-permute-done.9.refs_3_
  19.0 0.6 shard_map.71
  19.6 0.2 collective-permute-start.10
  19.7 1.4 %collective-permute-start.5 = (bf16[512,256]{1,0:T(8,128)(2,1)S(1)}, bf16[512,256]{1,0:T(8,128)(2,1)S(1)}, u32[]{:S(2)}, u32[]{:S(2)}) collective-permute-start(bf16[512,256]{1,0:T(8,128)(2,1)S(1)} %get-tuple-element.50), channel_id=1, source_target_pairs={{0,12},{1,13},{2,14},{3,15},{4,8},{5,9},{6,10},{7,11},{8,20},{9,21... | collective-permute-start | bytes 786440 | tf_op jit(solution)/shard_map/ppermute | solution.py:317
  21.2 0.2 collective-permute-start.4
  21.4 2.2 %collective-permute-start.12 = (bf16[256,512]{1,0:T(8,128)(2,1)S(1)}, bf16[256,512]{1,0:T(8,128)(2,1)S(1)}, u32[]{:S(2)}, u32[]{:S(2)}) collective-permute-start(bf16[256,512]{1,0:T(8,128)(2,1)S(1)} %get-tuple-element.64), channel_id=1, source_target_pairs={{0,1},{1,2},{2,3},{3,0},{4,5},{5,6},{6,7},{7,4},{8,9},{9,10},{10,1... | collective-permute-start | bytes 786440 | tf_op jit(solution)/shard_map/ppermute | solution.py:317
  23.6 0.0 collective-permute-done.3.sibling_ref
  23.6 1.4 %collective-permute-start.13 = (bf16[256,512]{1,0:T(8,128)(2,1)S(1)}, bf16[256,512]{1,0:T(8,128)(2,1)S(1)}, u32[]{:S(2)}, u32[]{:S(2)}) collective-permute-start(bf16[256,512]{1,0:T(8,128)(2,1)S(1)} %get-tuple-element.65), channel_id=1, source_target_pairs={{0,3},{1,0},{2,1},{3,2},{4,7},{5,4},{6,5},{7,6},{8,11},{9,8},{10,9... | collective-permute-start | bytes 786440 | tf_op jit(solution)/shard_map/ppermute | solution.py:317
  25.0 0.7 shard_map.69
  25.7 3.8 %collective-permute-done.5.b_ref = bf16[512,256]{1,0:T(8,128)(2,1)S(1)} collective-permute-done((bf16[512,256]{1,0:T(8,128)(2,1)S(1)}, bf16[512,256]{1,0:T(8,128)(2,1)S(1)}, u32[]{:S(2)}, u32[]{:S(2)}) %collective-permute-start.5) | collective-permute-done | bytes 262176 | tf_op jit(solution)/shard_map/ppermute | solution.py:317
  29.4 5.1 %collective-permute-done.4.a_ref = bf16[512,256]{1,0:T(8,128)(2,1)S(1)} collective-permute-done((bf16[512,256]{1,0:T(8,128)(2,1)S(1)}, bf16[512,256]{1,0:T(8,128)(2,1)S(1)}, u32[]{:S(2)}, u32[]{:S(2)}) %collective-permute-start.4) | collective-permute-done | bytes 262176 | tf_op jit(solution)/shard_map/ppermute | solution.py:317
  34.5 0.0 collective-permute-done.10.refs_1_
  34.5 6.0 %shard_map.72 = (bf16[1024,256]{1,0:T(8,128)(2,1)S(1)}, bf16[128,1024]{1,0:T(8,128)(2,1)S(1)}, f32[1024,256]{1,0:T(8,128)S(1)}, f32[1024,256]{1,0:T(8,128)S(1)},...) custom-call(s32[3]{0:T(128)S(1)} %pad_add_fusion.place_ref, bf16[1024,256]{1,0:T(8,128)(2,1)S(1)} %get-tuple-element.51.own_ref, ...), custom_call_target="tpu_custom_call" | custom-call | flops 1 | bytes 4997132 | tf_op jit(solution)/shard_map/pallas_call | solution.py:26
  40.5 2.9 %collective-permute-start.11 = (bf16[256,256]{1,0:T(8,128)(2,1)S(1)}, bf16[256,256]{1,0:T(8,128)(2,1)S(1)}, u32[]{:S(2)}, u32[]{:S(2)}) collective-permute-start(bf16[256,256]{1,0:T(8,128)(2,1)S(1)} %get-tuple-element.61), channel_id=1, source_target_pairs={{0,2},{1,3},{2,0},{3,1},{4,6},{5,7},{6,4},{7,5},{8,10},{9,11},{10,... | collective-permute-start | bytes 393224 | tf_op jit(solution)/shard_map/ppermute | solution.py:317
  43.4 0.0 collective-permute-done.12.refs_0_
  43.4 5.5 %collective-permute-done.13.refs_1_ = bf16[256,512]{1,0:T(8,128)(2,1)S(1)} collective-permute-done((bf16[256,512]{1,0:T(8,128)(2,1)S(1)}, bf16[256,512]{1,0:T(8,128)(2,1)S(1)}, u32[]{:S(2)}, u32[]{:S(2)}) %collective-permute-start.13) | collective-permute-done | bytes 262176 | tf_op jit(solution)/shard_map/ppermute | solution.py:317
  48.9 3.8 %shard_map.73 = (f32[512,256]{1,0:T(8,128)S(1)}, f32[512,256]{1,0:T(8,128)S(1)}, bf16[544,256]{1,0:T(8,128)(2,1)S(1)}, bf16[2,128,256]{2,1,0:T(8,128)(2,1)S(1)}) custom-call(s32[3]{0:T(128)S(1)} %pad_add_fusion.place_ref, bf16[1024,256]{1,0:T(8,128)(2,1)S(1)} %get-tuple-element.51.own_ref, bf16[128,1024]{1,0:T(8,128)(2,1)S(1)} %get-tuple-element.52.own_kt_ref, ...), custom_call_target="tpu_custom_call" | custom-call | flops 1 | bytes 5652492 | tf_op jit(solution)/shard_map/pallas_call | solution.py:26
  52.7 1.2 %collective-permute-start.17 = (bf16[544,256]{1,0:T(8,128)(2,1)S(1)}, bf16[544,256]{1,0:T(8,128)(2,1)S(1)}, u32[]{:S(2)}, u32[]{:S(2)}) collective-permute-start(bf16[544,256]{1,0:T(8,128)(2,1)S(1)} %get-tuple-element.77), channel_id=1, source_target_pairs={{0,24},{1,25},{2,26},{3,27},{4,28},{5,29},{6,30},{7,31},{8,0},{9,1... | collective-permute-start | bytes 835592 | tf_op jit(solution)/shard_map/ppermute | solution.py:317
  53.9 0.0 collective-permute-done.11.refs_1_
  53.9 3.6 %shard_map.74 = (f32[512,256]{1,0:T(8,128)S(1)}, f32[512,256]{1,0:T(8,128)S(1)}, bf16[528,256]{1,0:T(8,128)(2,1)S(1)}, bf16[256,256]{1,0:T(8,128)(2,1)S(1)}, bf16[256,256]{1,0:T(8,128)(2,1)S(1)}) custom-call(s32[3]{0:T(128)S(1)} %pad_add_fusion.place_ref, bf16[1024,256]{1,0:T(8,128)(2,1)S(1)} %get-tuple-element.51.own_ref, ...), custom_call_target="tpu_custom_call" | custom-call | flops 1 | bytes 5914636 | tf_op jit(solution)/shard_map/pallas_call | solution.py:26
  57.5 0.3 collective-permute-start.18
  57.8 0.0 collective-permute-start.14
  57.8 1.5 %collective-permute-start.15 = (bf16[256,256]{1,0:T(8,128)(2,1)S(1)}, bf16[256,256]{1,0:T(8,128)(2,1)S(1)}, u32[]{:S(2)}, u32[]{:S(2)}) collective-permute-start(bf16[256,256]{1,0:T(8,128)(2,1)S(1)} %get-tuple-element.72), channel_id=1, source_target_pairs={{0,1},{1,2},{2,3},{3,0},{4,5},{5,6},{6,7},{7,4},{8,9},{9,10},{10,1... | collective-permute-start | bytes 393224 | tf_op jit(solution)/shard_map/ppermute | solution.py:317
  59.3 3.9 %collective-permute-done.14.refs_2_ = bf16[256,256]{1,0:T(8,128)(2,1)S(1)} collective-permute-done((bf16[256,256]{1,0:T(8,128)(2,1)S(1)}, bf16[256,256]{1,0:T(8,128)(2,1)S(1)}, u32[]{:S(2)}, u32[]{:S(2)}) %collective-permute-start.14) | collective-permute-done | bytes 131104 | tf_op jit(solution)/shard_map/ppermute | solution.py:317
  63.3 0.0 collective-permute-done.15.refs_3_
  63.3 0.6 shard_map.75
  63.8 3.4 %collective-permute-start.16 = (bf16[512,256]{1,0:T(8,128)(2,1)S(1)}, bf16[512,256]{1,0:T(8,128)(2,1)S(1)}, u32[]{:S(2)}, u32[]{:S(2)}) collective-permute-start(bf16[512,256]{1,0:T(8,128)(2,1)S(1)} %get-tuple-element.74), channel_id=1, source_target_pairs={{0,4},{1,5},{2,6},{3,7},{4,0},{5,1},{6,2},{7,3},{8,12},{9,13},{10,... | collective-permute-start | bytes 786440 | tf_op jit(solution)/shard_map/ppermute | solution.py:317
  67.2 0.0 collective-permute-done.17.back_a_ref
  67.2 0.0 collective-permute-done.18.back_b_ref
  67.2 0.6 shard_map.77
  67.9 0.4 collective-permute-start.19
  68.2 1.9 %collective-permute-start.20 = (bf16[256,256]{1,0:T(8,128)(2,1)S(1)}, bf16[256,256]{1,0:T(8,128)(2,1)S(1)}, u32[]{:S(2)}, u32[]{:S(2)}) collective-permute-start(bf16[256,256]{1,0:T(8,128)(2,1)S(1)} %get-tuple-element.81), channel_id=1, source_target_pairs={{0,1},{1,2},{2,3},{3,0},{4,5},{5,6},{6,7},{7,4},{8,9},{9,10},{10,1... | collective-permute-start | bytes 393224 | tf_op jit(solution)/shard_map/ppermute | solution.py:317
  70.1 0.0 collective-permute-start.21
  70.2 0.0 collective-permute-done.16.sibling_ref
  70.2 1.4 %shard_map.76 = bf16[128,2048]{1,0:T(8,128)(2,1)} custom-call(s32[3]{0:T(128)S(1)} %pad_add_fusion.place_ref, bf16[512,256]{1,0:T(8,128)(2,1)S(1)} %get-tuple-element.73.mine_ref, bf16[512,256]{1,0:T(8,128)(2,1)S(1)} %collective-permute-done.16.sibling_ref), custom_call_target="tpu_custom_call" | custom-call | bytes 1048588 | tf_op jit(solution)/shard_map/pallas_call | solution.py:26
  71.6 0.7 slice.18.refs_4_
  72.2 1.7 %collective-permute-done.19.refs_1_ = bf16[256,256]{1,0:T(8,128)(2,1)S(1)} collective-permute-done((bf16[256,256]{1,0:T(8,128)(2,1)S(1)}, bf16[256,256]{1,0:T(8,128)(2,1)S(1)}, u32[]{:S(2)}, u32[]{:S(2)}) %collective-permute-start.19) | collective-permute-done | bytes 131104 | tf_op jit(solution)/shard_map/ppermute | solution.py:317
  74.0 5.6 %collective-permute-done.20.refs_2_ = bf16[256,256]{1,0:T(8,128)(2,1)S(1)} collective-permute-done((bf16[256,256]{1,0:T(8,128)(2,1)S(1)}, bf16[256,256]{1,0:T(8,128)(2,1)S(1)}, u32[]{:S(2)}, u32[]{:S(2)}) %collective-permute-start.20) | collective-permute-done | bytes 131104 | tf_op jit(solution)/shard_map/ppermute | solution.py:317
  79.6 2.8 %collective-permute-done.21.refs_3_ = bf16[256,256]{1,0:T(8,128)(2,1)S(1)} collective-permute-done((bf16[256,256]{1,0:T(8,128)(2,1)S(1)}, bf16[256,256]{1,0:T(8,128)(2,1)S(1)}, u32[]{:S(2)}, u32[]{:S(2)}) %collective-permute-start.21) | collective-permute-done | bytes 131104 | tf_op jit(solution)/shard_map/ppermute | solution.py:317
  82.4 0.6 shard_map.78
  83.0 0.7 collective-permute-start.22
  83.7 1.2 %collective-permute-done.22.sibling_ref = bf16[512,256]{1,0:T(8,128)(2,1)S(1)} collective-permute-done((bf16[512,256]{1,0:T(8,128)(2,1)S(1)}, bf16[512,256]{1,0:T(8,128)(2,1)S(1)}, u32[]{:S(2)}, u32[]{:S(2)}) %collective-permute-start.22) | collective-permute-done | bytes 262176 | tf_op jit(solution)/shard_map/ppermute | solution.py:317
  84.8 1.5 %shard_map.79 = (bf16[128,1024]{1,0:T(8,128)(2,1)}, bf16[128,1024]{1,0:T(8,128)(2,1)}) custom-call(s32[3]{0:T(128)S(1)} %pad_add_fusion.place_ref, bf16[512,256]{1,0:T(8,128)(2,1)S(1)} %get-tuple-element.83.mine_ref, bf16[512,256]{1,0:T(8,128)(2,1)S(1)} %collective-permute-done.22.sibling_ref), custom_call_target="tpu_custom_call" | custom-call | bytes 1048588 | tf_op jit(solution)/shard_map/pallas_call | solution.py:26
  (8 shorter events, 0.0 us)
Async XLA Ops:
  0.6 6.8 %copy-start = (bf16[128,2048]{1,0:T(8,128)(2,1)S(1)}, bf16[128,2048]{1,0:T(8,128)(2,1)}, u32[]{:S(2)}) copy-start(bf16[128,2048]{1,0:T(8,128)(2,1)} %q_ref.1) | copy-start | bytes 1572868
  0.7 1.0 %copy-start.2 = (bf16[128,1024]{1,0:T(8,128)(2,1)S(1)}, bf16[128,1024]{1,0:T(8,128)(2,1)}, u32[]{:S(2)}) copy-start(bf16[128,1024]{1,0:T(8,128)(2,1)} %k_ref.1) | copy-start | bytes 786436
  1.7 0.9 %copy-start.3 = (bf16[128,1024]{1,0:T(8,128)(2,1)S(1)}, bf16[128,1024]{1,0:T(8,128)(2,1)}, u32[]{:S(2)}) copy-start(bf16[128,1024]{1,0:T(8,128)(2,1)} %v_ref.1) | copy-start | bytes 786436
  3.6 8.8 %collective-permute-start = (bf16[128,512]{1,0:T(8,128)(2,1)S(1)}, bf16[128,512]{1,0:T(8,128)(2,1)S(1)}, u32[]{:S(2)}, u32[]{:S(2)}) collective-permute-start(bf16[128,512]{1,0:T(8,128)(2,1)S(1)} %get-tuple-element.46), channel_id=1, source_target_pairs={{0,2},{1,3},{2,0},{3,1},{4,6},{5,7},{6,4},{7,5},{8,10},{9,11},{10,... | collective-permute-start | bytes 393224 | tf_op jit(solution)/shard_map/ppermute | solution.py:317
  5.9 11.5 %collective-permute-start.1 = (bf16[128,512]{1,0:T(8,128)(2,1)S(1)}, bf16[128,512]{1,0:T(8,128)(2,1)S(1)}, u32[]{:S(2)}, u32[]{:S(2)}) collective-permute-start(bf16[128,512]{1,0:T(8,128)(2,1)S(1)} %get-tuple-element.47), channel_id=1, source_target_pairs={{0,1},{1,2},{2,3},{3,0},{4,5},{5,6},{6,7},{7,4},{8,9},{9,10},{10,1... | collective-permute-start | bytes 393224 | tf_op jit(solution)/shard_map/ppermute | solution.py:317
  5.9 12.0 %collective-permute-start.2 = (bf16[128,512]{1,0:T(8,128)(2,1)S(1)}, bf16[128,512]{1,0:T(8,128)(2,1)S(1)}, u32[]{:S(2)}, u32[]{:S(2)}) collective-permute-start(bf16[128,512]{1,0:T(8,128)(2,1)S(1)} %get-tuple-element.48), channel_id=1, source_target_pairs={{0,3},{1,0},{2,1},{3,2},{4,7},{5,4},{6,5},{7,6},{8,11},{9,8},{10,9... | collective-permute-start | bytes 393224 | tf_op jit(solution)/shard_map/ppermute | solution.py:317
  7.4 1.0 %copy-start.1 = (bf16[128,2048]{1,0:T(8,128)(2,1)S(1)}, bf16[128,2048]{1,0:T(8,128)(2,1)}, u32[]{:S(2)}) copy-start(bf16[128,2048]{1,0:T(8,128)(2,1)} %g_ref.1) | copy-start | bytes 1572868
  9.4 9.3 %collective-permute-start.6 = (bf16[128,512]{1,0:T(8,128)(2,1)S(1)}, bf16[128,512]{1,0:T(8,128)(2,1)S(1)}, u32[]{:S(2)}, u32[]{:S(2)}) collective-permute-start(bf16[128,512]{1,0:T(8,128)(2,1)S(1)} %get-tuple-element.54), channel_id=1, source_target_pairs={{0,4},{1,5},{2,6},{3,7},{4,0},{5,1},{6,2},{7,3},{8,12},{9,13},{10,... | collective-permute-start | bytes 393224 | tf_op jit(solution)/shard_map/ppermute | solution.py:317
  10.9 7.7 %collective-permute-start.7 = (bf16[128,512]{1,0:T(8,128)(2,1)S(1)}, bf16[128,512]{1,0:T(8,128)(2,1)S(1)}, u32[]{:S(2)}, u32[]{:S(2)}) collective-permute-start(bf16[128,512]{1,0:T(8,128)(2,1)S(1)} %get-tuple-element.55), channel_id=1, source_target_pairs={{0,4},{1,5},{2,6},{3,7},{4,0},{5,1},{6,2},{7,3},{8,12},{9,13},{10,... | collective-permute-start | bytes 393224 | tf_op jit(solution)/shard_map/ppermute | solution.py:317
  12.4 6.3 %collective-permute-start.8 = (bf16[128,512]{1,0:T(8,128)(2,1)S(1)}, bf16[128,512]{1,0:T(8,128)(2,1)S(1)}, u32[]{:S(2)}, u32[]{:S(2)}) collective-permute-start(bf16[128,512]{1,0:T(8,128)(2,1)S(1)} %get-tuple-element.56), channel_id=1, source_target_pairs={{0,4},{1,5},{2,6},{3,7},{4,0},{5,1},{6,2},{7,3},{8,12},{9,13},{10,... | collective-permute-start | bytes 393224 | tf_op jit(solution)/shard_map/ppermute | solution.py:317
  17.5 1.5 %collective-permute-start.9 = (bf16[128,512]{1,0:T(8,128)(2,1)S(1)}, bf16[128,512]{1,0:T(8,128)(2,1)S(1)}, u32[]{:S(2)}, u32[]{:S(2)}) collective-permute-start(bf16[128,512]{1,0:T(8,128)(2,1)S(1)} %get-tuple-element.57), channel_id=1, source_target_pairs={{0,4},{1,5},{2,6},{3,7},{4,0},{5,1},{6,2},{7,3},{8,12},{9,13},{10,... | collective-permute-start | bytes 393224 | tf_op jit(solution)/shard_map/ppermute | solution.py:317
  18.6 5.0 %collective-permute-start.3 = (bf16[512,256]{1,0:T(8,128)(2,1)S(1)}, bf16[512,256]{1,0:T(8,128)(2,1)S(1)}, u32[]{:S(2)}, u32[]{:S(2)}) collective-permute-start(bf16[512,256]{1,0:T(8,128)(2,1)S(1)} %get-tuple-element.50), channel_id=1, source_target_pairs={{0,4},{1,5},{2,6},{3,7},{4,0},{5,1},{6,2},{7,3},{8,12},{9,13},{10,... | collective-permute-start | bytes 786440 | tf_op jit(solution)/shard_map/ppermute | solution.py:317
  19.6 15.0 %collective-permute-start.10 = (bf16[272,512]{1,0:T(8,128)(2,1)S(1)}, bf16[272,512]{1,0:T(8,128)(2,1)S(1)}, u32[]{:S(2)}, u32[]{:S(2)}) collective-permute-start(bf16[272,512]{1,0:T(8,128)(2,1)S(1)} %get-tuple-element.59), channel_id=1, source_target_pairs={{0,2},{1,3},{2,0},{3,1},{4,6},{5,7},{6,4},{7,5},{8,10},{9,11},{10,... | collective-permute-start | bytes 835592 | tf_op jit(solution)/shard_map/ppermute | solution.py:317
  19.7 9.7 %collective-permute-start.5 = (bf16[512,256]{1,0:T(8,128)(2,1)S(1)}, bf16[512,256]{1,0:T(8,128)(2,1)S(1)}, u32[]{:S(2)}, u32[]{:S(2)}) collective-permute-start(bf16[512,256]{1,0:T(8,128)(2,1)S(1)} %get-tuple-element.50), channel_id=1, source_target_pairs={{0,12},{1,13},{2,14},{3,15},{4,8},{5,9},{6,10},{7,11},{8,20},{9,21... | collective-permute-start | bytes 786440 | tf_op jit(solution)/shard_map/ppermute | solution.py:317
  21.2 13.4 %collective-permute-start.4 = (bf16[512,256]{1,0:T(8,128)(2,1)S(1)}, bf16[512,256]{1,0:T(8,128)(2,1)S(1)}, u32[]{:S(2)}, u32[]{:S(2)}) collective-permute-start(bf16[512,256]{1,0:T(8,128)(2,1)S(1)} %get-tuple-element.49.mine_ref), channel_id=1, source_target_pairs={{0,8},{1,9},{2,10},{3,11},{4,12},{5,13},{6,14},{7,15},{8,16},{9,17... | collective-permute-start | bytes 786440 | tf_op jit(solution)/shard_map/ppermute | solution.py:317
  21.4 22.0 %collective-permute-start.12 = (bf16[256,512]{1,0:T(8,128)(2,1)S(1)}, bf16[256,512]{1,0:T(8,128)(2,1)S(1)}, u32[]{:S(2)}, u32[]{:S(2)}) collective-permute-start(bf16[256,512]{1,0:T(8,128)(2,1)S(1)} %get-tuple-element.64), channel_id=1, source_target_pairs={{0,1},{1,2},{2,3},{3,0},{4,5},{5,6},{6,7},{7,4},{8,9},{9,10},{10,1... | collective-permute-start | bytes 786440 | tf_op jit(solution)/shard_map/ppermute | solution.py:317
  23.6 25.3 %collective-permute-start.13 = (bf16[256,512]{1,0:T(8,128)(2,1)S(1)}, bf16[256,512]{1,0:T(8,128)(2,1)S(1)}, u32[]{:S(2)}, u32[]{:S(2)}) collective-permute-start(bf16[256,512]{1,0:T(8,128)(2,1)S(1)} %get-tuple-element.65), channel_id=1, source_target_pairs={{0,3},{1,0},{2,1},{3,2},{4,7},{5,4},{6,5},{7,6},{8,11},{9,8},{10,9... | collective-permute-start | bytes 786440 | tf_op jit(solution)/shard_map/ppermute | solution.py:317
  40.5 13.4 %collective-permute-start.11 = (bf16[256,256]{1,0:T(8,128)(2,1)S(1)}, bf16[256,256]{1,0:T(8,128)(2,1)S(1)}, u32[]{:S(2)}, u32[]{:S(2)}) collective-permute-start(bf16[256,256]{1,0:T(8,128)(2,1)S(1)} %get-tuple-element.61), channel_id=1, source_target_pairs={{0,2},{1,3},{2,0},{3,1},{4,6},{5,7},{6,4},{7,5},{8,10},{9,11},{10,... | collective-permute-start | bytes 393224 | tf_op jit(solution)/shard_map/ppermute | solution.py:317
  52.7 14.6 %collective-permute-start.17 = (bf16[544,256]{1,0:T(8,128)(2,1)S(1)}, bf16[544,256]{1,0:T(8,128)(2,1)S(1)}, u32[]{:S(2)}, u32[]{:S(2)}) collective-permute-start(bf16[544,256]{1,0:T(8,128)(2,1)S(1)} %get-tuple-element.77), channel_id=1, source_target_pairs={{0,24},{1,25},{2,26},{3,27},{4,28},{5,29},{6,30},{7,31},{8,0},{9,1... | collective-permute-start | bytes 835592 | tf_op jit(solution)/shard_map/ppermute | solution.py:317
  57.5 9.7 %collective-permute-start.18 = (bf16[528,256]{1,0:T(8,128)(2,1)S(1)}, bf16[528,256]{1,0:T(8,128)(2,1)S(1)}, u32[]{:S(2)}, u32[]{:S(2)}) collective-permute-start(bf16[528,256]{1,0:T(8,128)(2,1)S(1)} %get-tuple-element.78), channel_id=1, source_target_pairs={{0,24},{1,25},{2,26},{3,27},{4,28},{5,29},{6,30},{7,31},{8,0},{9,1... | collective-permute-start | bytes 811016 | tf_op jit(solution)/shard_map/ppermute | solution.py:317
  57.8 5.4 %collective-permute-start.14 = (bf16[256,256]{1,0:T(8,128)(2,1)S(1)}, bf16[256,256]{1,0:T(8,128)(2,1)S(1)}, u32[]{:S(2)}, u32[]{:S(2)}) collective-permute-start(bf16[256,256]{1,0:T(8,128)(2,1)S(1)} %get-tuple-element.71), channel_id=1, source_target_pairs={{0,3},{1,0},{2,1},{3,2},{4,7},{5,4},{6,5},{7,6},{8,11},{9,8},{10,9... | collective-permute-start | bytes 393224 | tf_op jit(solution)/shard_map/ppermute | solution.py:317
  57.8 5.4 %collective-permute-start.15 = (bf16[256,256]{1,0:T(8,128)(2,1)S(1)}, bf16[256,256]{1,0:T(8,128)(2,1)S(1)}, u32[]{:S(2)}, u32[]{:S(2)}) collective-permute-start(bf16[256,256]{1,0:T(8,128)(2,1)S(1)} %get-tuple-element.72), channel_id=1, source_target_pairs={{0,1},{1,2},{2,3},{3,0},{4,5},{5,6},{6,7},{7,4},{8,9},{9,10},{10,1... | collective-permute-start | bytes 393224 | tf_op jit(solution)/shard_map/ppermute | solution.py:317
  63.8 6.3 %collective-permute-start.16 = (bf16[512,256]{1,0:T(8,128)(2,1)S(1)}, bf16[512,256]{1,0:T(8,128)(2,1)S(1)}, u32[]{:S(2)}, u32[]{:S(2)}) collective-permute-start(bf16[512,256]{1,0:T(8,128)(2,1)S(1)} %get-tuple-element.74), channel_id=1, source_target_pairs={{0,4},{1,5},{2,6},{3,7},{4,0},{5,1},{6,2},{7,3},{8,12},{9,13},{10,... | collective-permute-start | bytes 786440 | tf_op jit(solution)/shard_map/ppermute | solution.py:317
  67.9 6.1 %collective-permute-start.19 = (bf16[256,256]{1,0:T(8,128)(2,1)S(1)}, bf16[256,256]{1,0:T(8,128)(2,1)S(1)}, u32[]{:S(2)}, u32[]{:S(2)}) collective-permute-start(bf16[256,256]{1,0:T(8,128)(2,1)S(1)} %get-tuple-element.80), channel_id=1, source_target_pairs={{0,2},{1,3},{2,0},{3,1},{4,6},{5,7},{6,4},{7,5},{8,10},{9,11},{10,... | collective-permute-start | bytes 393224 | tf_op jit(solution)/shard_map/ppermute | solution.py:317
  68.2 11.3 %collective-permute-start.20 = (bf16[256,256]{1,0:T(8,128)(2,1)S(1)}, bf16[256,256]{1,0:T(8,128)(2,1)S(1)}, u32[]{:S(2)}, u32[]{:S(2)}) collective-permute-start(bf16[256,256]{1,0:T(8,128)(2,1)S(1)} %get-tuple-element.81), channel_id=1, source_target_pairs={{0,1},{1,2},{2,3},{3,0},{4,5},{5,6},{6,7},{7,4},{8,9},{9,10},{10,1... | collective-permute-start | bytes 393224 | tf_op jit(solution)/shard_map/ppermute | solution.py:317
  70.1 12.2 %collective-permute-start.21 = (bf16[256,256]{1,0:T(8,128)(2,1)S(1)}, bf16[256,256]{1,0:T(8,128)(2,1)S(1)}, u32[]{:S(2)}, u32[]{:S(2)}) collective-permute-start(bf16[256,256]{1,0:T(8,128)(2,1)S(1)} %get-tuple-element.82), channel_id=1, source_target_pairs={{0,3},{1,0},{2,1},{3,2},{4,7},{5,4},{6,5},{7,6},{8,11},{9,8},{10,9... | collective-permute-start | bytes 393224 | tf_op jit(solution)/shard_map/ppermute | solution.py:317
  83.0 1.9 %collective-permute-start.22 = (bf16[512,256]{1,0:T(8,128)(2,1)S(1)}, bf16[512,256]{1,0:T(8,128)(2,1)S(1)}, u32[]{:S(2)}, u32[]{:S(2)}) collective-permute-start(bf16[512,256]{1,0:T(8,128)(2,1)S(1)} %get-tuple-element.84), channel_id=1, source_target_pairs={{0,4},{1,5},{2,6},{3,7},{4,0},{5,1},{6,2},{7,3},{8,12},{9,13},{10,... | collective-permute-start | bytes 786440 | tf_op jit(solution)/shard_map/ppermute | solution.py:317
